TPU v7x, 32 devices: a whole 2x2x4 slice. The times are simulated.
32 devices in a mesh: dp: 8 (over y, x, core), mp: 4 (over z).
Axes of the slice: x: 2, y: 2, z: 4, core: 2. Of those that a mesh axis runs over, the one named last changes fastest.
Arguments:
- tokens: bfloat16 [2, 8, 1536, 1024], P(None, 'dp', 'mp'), may hold values from -6 to 6
- views: int32 [2, 8], P(None, 'dp'), may hold values from 1 to 3
- norm_gains: float32 [1, 2, 1024], replicated, may hold values from 0.25 to 1.75
- norm_biases: float32 [1, 2, 1024], replicated, may hold values from -1.8 to 1.8
- w_proj: bfloat16 [1, 3, 1024, 1024], P(None, None, 'dp', 'mp'), may hold values from -0.1875 to 0.1875
- w_out: bfloat16 [1, 1024, 1024], P(None, 'dp', 'mp'), may hold values from -3 to 3
- w_up: bfloat16 [1, 1024, 4096], P(None, 'dp', 'mp'), may hold values from -0.1875 to 0.1875
- w_down: bfloat16 [1, 1024, 4096], P(None, 'dp', 'mp'), may hold values from -0.09375 to 0.09375
- cotangent: bfloat16 [2, 8, 1536, 1024], P(None, 'dp', 'mp'), may hold values from -6 to 6
Outputs:
- output: bfloat16 [2, 8, 1536, 1024], P(None, 'dp', 'mp')
- grad_tokens: bfloat16 [2, 8, 1536, 1024], P(None, 'dp', 'mp')
- grad_proj: float32 [1, 3, 1024, 1024], P(None, None, 'dp', 'mp')
- grad_out: float32 [1, 1024, 1024], P(None, 'dp', 'mp')
- grad_up: float32 [1, 1024, 4096], P(None, 'dp', 'mp')
- grad_down: float32 [1, 1024, 4096], P(None, 'dp', 'mp')
- grad_gains: float32 [1, 2, 1024], P(None, None, ('dp', 'mp'))
- grad_biases: float32 [1, 1024], P(None, ('dp', 'mp'))
- grad_biases_second: float32 [1, 1024], P(None, ('dp', 'mp'))
Inputs may be any that keep to these rules, and one draw needn't show every extreme that they name: Number of views of each scene; its live tokens are the first 768 + views * 256.
All inputs are finite; a program needn't handle non-finite values.
Results may differ from a plain program's by a relative error of at most 0.02.
Values may be sent and summed in bfloat16 or wider, within the bound.
No kernel may reach another device: no remote copies, remote signals or barrier semaphores. Data moves between devices by JAX's collectives and lax.ppermute only.
A program may use at most 192 MiB of HBM per device.

v0:
```python
import jax
import jax.numpy as jnp
from jax import lax
from jax.sharding import PartitionSpec as P

HDIM = 64
VIEW_TOK = 256
TRI = 768
QBLOCK = 512
SEQ = 1536


EPSILON = 1e-05
MASKED = -1000000000.0


def gelu_exact(values):
    return jax.nn.gelu(values, approximate=False)


def normalize(state, gain, bias):
    centre = jnp.mean(state, axis=-1, keepdims=True)
    centred = state - centre
    spread = jnp.mean(centred * centred, axis=-1, keepdims=True)
    inverse = lax.rsqrt(spread + EPSILON)
    scaled = centred * inverse
    return (scaled * gain + bias, scaled, inverse)


def normalize_back(grad, scaled, inverse, gain):
    weighted = grad * gain
    first = jnp.mean(weighted, axis=-1, keepdims=True)
    second = jnp.mean(weighted * scaled, axis=-1, keepdims=True)
    return (
        inverse * (weighted - first - scaled * second),
        jnp.sum(grad * scaled, axis=0),
        jnp.sum(grad, axis=0),
    )


def spread_attn(normed):
    return lax.all_gather(normed, "mp", axis=0, tiled=True)


def spread_mlp(normed):
    return lax.all_gather(normed, "mp", axis=0, tiled=True)


def block_scores(query_part, keys, live):
    scale = HDIM ** (-0.5)
    scores = (
        jnp.einsum("qhd,khd->hqk", query_part, keys, preferred_element_type=jnp.float32) * scale
    )
    return jnp.where(live[None, None, :], scores, MASKED)


def attend_forward(queries, keys, values, live):
    count = queries.shape[1]

    def block(query_part):
        scores = block_scores(query_part, keys, live)
        top = jnp.max(scores, axis=-1, keepdims=True)
        expo = jnp.exp(scores - top)
        total = jnp.sum(expo, axis=-1, keepdims=True)
        probs = (expo / total).astype(jnp.bfloat16)
        mixed = jnp.einsum("hqk,khd->qhd", probs, values, preferred_element_type=jnp.float32)
        return (mixed, (top + jnp.log(total))[..., 0])

    blocks = queries.reshape(SEQ // QBLOCK, QBLOCK, count, HDIM)
    mixed, log_total = lax.map(block, blocks)
    return (mixed.reshape(SEQ, count * HDIM), log_total)


def attend_backward(queries, keys, values, live, log_total, grad_mixed):
    count = queries.shape[1]
    scale = HDIM ** (-0.5)

    def block(carry, item):
        query_part, grad_part, total_part = item
        scores = block_scores(query_part, keys, live)
        probs = jnp.exp(scores - total_part[..., None])
        upstream = jnp.einsum("qhd,khd->hqk", grad_part, values, preferred_element_type=jnp.float32)
        delta = jnp.sum(probs * upstream, axis=-1, keepdims=True)
        grad_scores = (probs * (upstream - delta)).astype(jnp.bfloat16)
        grad_query = (
            jnp.einsum("hqk,khd->qhd", grad_scores, keys, preferred_element_type=jnp.float32)
            * scale
        )
        grad_key = (
            carry[0]
            + jnp.einsum(
                "hqk,qhd->khd", grad_scores, query_part, preferred_element_type=jnp.float32
            )
            * scale
        )
        grad_value = carry[1] + jnp.einsum(
            "hqk,qhd->khd",
            probs.astype(jnp.bfloat16),
            grad_part,
            preferred_element_type=jnp.float32,
        )
        return ((grad_key, grad_value), grad_query)

    shape = (SEQ // QBLOCK, QBLOCK, count, HDIM)
    empty = jnp.zeros((SEQ, count, HDIM), jnp.float32)
    (grad_key, grad_value), grad_query = lax.scan(
        block, (empty, empty), (queries.reshape(shape), grad_mixed.reshape(shape), log_total)
    )
    width = count * HDIM
    return jnp.stack(
        [
            grad_query.reshape(SEQ, width),
            grad_key.reshape(SEQ, width),
            grad_value.reshape(SEQ, width),
        ]
    )


def layer_forward(state, live, gains, biases, weights):
    w_proj, w_out, w_up, w_down = weights
    normed, scaled_one, inverse_one = normalize(state, gains[0], biases[0])
    full_in = spread_attn(normed.astype(jnp.bfloat16))
    projected = jnp.einsum(
        "sd,ide->ise", full_in, w_proj, preferred_element_type=jnp.float32
    ).astype(jnp.bfloat16)
    count = projected.shape[2] // HDIM
    heads = projected.reshape(3, SEQ, count, HDIM)
    mixed, log_total = attend_forward(heads[0], heads[1], heads[2], live)
    mixed = mixed.astype(jnp.bfloat16)
    part = mixed
    middle = state + lax.psum_scatter(
        lax.dot_general(
            part, w_out, (((1,), (1,)), ((), ())), preferred_element_type=jnp.float32
        ).astype(jnp.bfloat16),
        "mp",
        scatter_dimension=0,
        tiled=True,
    ).astype(jnp.float32)
    normed_two, scaled_two, inverse_two = normalize(middle, gains[1], biases[1])
    up_used, down_used = (w_up, w_down)
    full_mid = spread_mlp(normed_two.astype(jnp.bfloat16))
    hidden_pre = jnp.dot(full_mid, w_up, preferred_element_type=jnp.float32)
    activation = gelu_exact(hidden_pre).astype(jnp.bfloat16)
    part = activation
    result = middle + lax.psum_scatter(
        lax.dot_general(
            part, w_down, (((1,), (1,)), ((), ())), preferred_element_type=jnp.float32
        ).astype(jnp.bfloat16),
        "mp",
        scatter_dimension=0,
        tiled=True,
    ).astype(jnp.float32)
    saved = (
        state,
        scaled_one,
        inverse_one,
        full_in,
        projected,
        log_total,
        mixed,
        middle,
        scaled_two,
        inverse_two,
        full_mid,
        hidden_pre,
        activation,
        (up_used, down_used),
    )
    return (result, saved)


def layer_backward(grad_state, live, gains, weights, saved):
    w_proj, w_out, w_up, w_down = weights
    (
        state,
        scaled_one,
        inverse_one,
        full_in,
        projected,
        log_total,
        mixed,
        middle,
        scaled_two,
        inverse_two,
        full_mid,
        hidden_pre,
        activation,
        mlp_weights,
    ) = saved
    up_used, down_used = mlp_weights
    contract_rows = (((0,), (0,)), ((), ()))
    full_grad = lax.all_gather(grad_state.astype(jnp.bfloat16), "mp", axis=0, tiled=True)
    grad_down = lax.dot_general(
        full_grad, activation, contract_rows, preferred_element_type=jnp.float32
    )
    grad_act = jnp.dot(full_grad, down_used, preferred_element_type=jnp.float32)
    unused, pull = jax.vjp(gelu_exact, hidden_pre)
    grad_hidden = pull(grad_act)[0].astype(jnp.bfloat16)
    grad_up = lax.dot_general(
        full_mid, grad_hidden, contract_rows, preferred_element_type=jnp.float32
    )
    part = grad_hidden
    grad_normed_two = lax.psum_scatter(
        lax.dot_general(
            part, w_up, (((1,), (1,)), ((), ())), preferred_element_type=jnp.float32
        ).astype(jnp.bfloat16),
        "mp",
        scatter_dimension=0,
        tiled=True,
    ).astype(jnp.float32)
    grad_norm_two, gain_two, bias_two = normalize_back(
        grad_normed_two, scaled_two, inverse_two, gains[1]
    )
    grad_middle = grad_state + grad_norm_two
    full_attn = lax.all_gather(grad_middle.astype(jnp.bfloat16), "mp", axis=0, tiled=True)
    grad_out = lax.dot_general(full_attn, mixed, contract_rows, preferred_element_type=jnp.float32)
    grad_mixed = jnp.dot(full_attn, w_out, preferred_element_type=jnp.float32).astype(jnp.bfloat16)
    count = projected.shape[2] // HDIM
    heads = projected.reshape(3, SEQ, count, HDIM)
    grad_projected = attend_backward(
        heads[0], heads[1], heads[2], live, log_total, grad_mixed.reshape(SEQ, count, HDIM)
    ).astype(jnp.bfloat16)
    grad_proj = jnp.einsum(
        "sd,ise->ide", full_in, grad_projected, preferred_element_type=jnp.float32
    )
    part = grad_projected
    grad_normed_one = lax.psum_scatter(
        jnp.einsum("ise,ide->sd", part, w_proj, preferred_element_type=jnp.float32).astype(
            jnp.bfloat16
        ),
        "mp",
        scatter_dimension=0,
        tiled=True,
    ).astype(jnp.float32)
    grad_norm_one, gain_one, bias_one = normalize_back(
        grad_normed_one, scaled_one, inverse_one, gains[0]
    )
    grad_result = grad_middle + grad_norm_one
    return (
        grad_result,
        (grad_proj, grad_out, grad_up, grad_down),
        jnp.stack([gain_one, gain_two]),
        jnp.stack([bias_one, bias_two]),
    )


def fetch(parts):
    return (
        lax.all_gather(parts[0], "dp", axis=2, tiled=True),
        lax.all_gather(parts[1], "dp", axis=1, tiled=True),
        lax.all_gather(parts[2], "dp", axis=1, tiled=True),
        lax.all_gather(parts[3], "dp", axis=1, tiled=True),
    )


def settle(parts):
    return (
        lax.psum_scatter(
            parts[0].astype(jnp.bfloat16), "dp", scatter_dimension=2, tiled=True
        ).astype(jnp.float32),
        lax.psum_scatter(
            parts[1].astype(jnp.bfloat16), "dp", scatter_dimension=1, tiled=True
        ).astype(jnp.float32),
        lax.psum_scatter(
            parts[2].astype(jnp.bfloat16), "dp", scatter_dimension=1, tiled=True
        ).astype(jnp.float32),
        lax.psum_scatter(
            parts[3].astype(jnp.bfloat16), "dp", scatter_dimension=1, tiled=True
        ).astype(jnp.float32),
    )


def shards(tokens, views, norm_gains, norm_biases, w_proj, w_out, w_up, w_down, cotangent):
    layers = w_proj.shape[0]
    micro = tokens.shape[0]
    positions = jnp.arange(SEQ, dtype=jnp.int32)
    stacked = (w_proj, w_out, w_up, w_down)
    shard_sums = tuple((jnp.zeros(w.shape, jnp.float32) for w in stacked))
    gain_sums = jnp.zeros(norm_gains.shape, jnp.float32)
    bias_sums = jnp.zeros(norm_biases.shape, jnp.float32)
    results = []
    grad_inputs = []
    for step in range(micro):
        live = positions < TRI + views[step, 0] * VIEW_TOK
        state = tokens[step, 0].astype(jnp.float32)
        index = 0
        weights = tuple((w[0] for w in fetch(tuple((w for w in stacked)))))
        layer_weights = [weights]
        state, saved = layer_forward(state, live, norm_gains[index], norm_biases[index], weights)
        saved_all = [saved]
        results.append(state.astype(jnp.bfloat16))
        grad_state = cotangent[step, 0].astype(jnp.float32)
        for index in reversed(range(layers)):
            grad_state, weight_grads, gain_grad, bias_grad = layer_backward(
                grad_state, live, norm_gains[index], layer_weights[index], saved_all[index]
            )
            gain_sums = gain_sums.at[index].add(gain_grad)
            bias_sums = bias_sums.at[index].add(bias_grad)
            shares = settle(tuple((grad[None] for grad in weight_grads)))
            shard_sums = tuple(
                (total.at[index].add(share[0]) for total, share in zip(shard_sums, shares))
            )
        grad_inputs.append(grad_state.astype(jnp.bfloat16))
    gain_out, bias_first, bias_second = (
        lax.psum_scatter(gain_sums, ("dp", "mp"), scatter_dimension=2, tiled=True),
        lax.psum_scatter(bias_sums[:, 0], ("dp", "mp"), scatter_dimension=1, tiled=True),
        lax.psum_scatter(bias_sums[:, 1], ("dp", "mp"), scatter_dimension=1, tiled=True),
    )
    output = jnp.stack(results)[:, None]
    grad_tokens = jnp.stack(grad_inputs)[:, None]
    return (
        output,
        grad_tokens,
        shard_sums[0],
        shard_sums[1],
        shard_sums[2],
        shard_sums[3],
        gain_out,
        bias_first,
        bias_second,
    )


def solution(mesh):
    placed = (
        P(None, "dp", "mp", None),
        P(None, "dp"),
        P(),
        P(),
        P(None, None, "dp", "mp"),
        P(None, "dp", "mp"),
        P(None, "dp", "mp"),
        P(None, "dp", "mp"),
        P(None, "dp", "mp", None),
    )
    return jax.shard_map(
        shards,
        mesh=mesh,
        in_specs=placed,
        out_specs=(
            P(None, "dp", "mp", None),
            P(None, "dp", "mp", None),
            P(None, None, "dp", "mp"),
            P(None, "dp", "mp"),
            P(None, "dp", "mp"),
            P(None, "dp", "mp"),
            P(None, None, ("dp", "mp")),
            P(None, ("dp", "mp")),
            P(None, ("dp", "mp")),
        ),
        check_vma=False,
    )
```

profile of v0, /device:TPU:0, one launch (start us, length us, event | category | flops | bytes accessed | tf_op | source)
XLA Modules:
  0.0 1956.9 jit_solution(11830977234847752476)
XLA Ops:
  17.7 12.8 all_gather.42
  39.8 65.7 %all-gather.14.cloned.1.call-done = bf16[1536,1024]{1,0:T(8,128)(2,1)} async-done(((bf16[384,1024]{1,0:T(8,128)(2,1)}), bf16[1536,1024]{1,0:T(8,128)(2,1)}) %all-gather.14.cloned.1.call-update) | async-done | bytes 3145744 | tf_op jit(solution)/shard_map/all_gather | solution.py:42
  118.3 30.2 %while.68 = (s32[]{:T(128)}, bf16[3,512,4,64]{1,3,2,0:T(8,128)(2,1)}, f32[3,4,512]{2,1,0:T(4,128)S(1)}, bf16[3,512,4,64]{1,3,2,0:T(8,128)(2,1)}, bf16[1536,4,64]...) while((s32[]{:T(128)}, bf16[3,512,4,64]{1,3,2,0:T(8,128)(2,1)}, ...), condition=%wide.region_5.6_spmd.clone, body=%wide.region_2.5_spmd.clone.sunk | while | flops 843054592 | bytes 40179820 | solution.py:70
  155.3 58.5 %reduce-scatter.34.cloned.1.call-done = bf16[384,1024]{1,0:T(8,128)(2,1)} async-done(((bf16[1536,1024]{1,0:T(8,128)(2,1)}), bf16[384,1024]{1,0:T(8,128)(2,1)}) %reduce-scatter.34.cloned.1.call-update) | async-done | bytes 786448 | tf_op jit(solution)/shard_map/reduce_scatter | solution.py:131
  217.5 63.0 %all-gather.24.cloned.1.call-done = bf16[1536,1024]{1,0:T(8,128)(2,1)} async-done(((bf16[384,1024]{1,0:T(8,128)(2,1)}), bf16[1536,1024]{1,0:T(8,128)(2,1)}) %all-gather.24.cloned.1.call-update) | async-done | bytes 3145744 | tf_op jit(solution)/shard_map/all_gather | solution.py:42
  293.1 30.2 %while.69 = (s32[]{:T(128)}, bf16[3,512,4,64]{1,3,2,0:T(8,128)(2,1)}, f32[3,4,512]{2,1,0:T(4,128)S(1)}, bf16[3,512,4,64]{1,3,2,0:T(8,128)(2,1)}, bf16[1536,4,64]...) while((s32[]{:T(128)}, ...), condition=%wide.region_15.16_spmd.clone, body=%wide.region_12.15_spmd.clone.sunk | while | flops 843054592 | bytes 40179820 | solution.py:70
  330.4 58.2 %reduce-scatter.38.cloned.1.call-done = bf16[384,1024]{1,0:T(8,128)(2,1)} async-done(((bf16[1536,1024]{1,0:T(8,128)(2,1)}), bf16[384,1024]{1,0:T(8,128)(2,1)}) %reduce-scatter.38.cloned.1.call-update) | async-done | bytes 786448 | tf_op jit(solution)/shard_map/reduce_scatter | solution.py:131
  397.7 20.6 %all-gather.20.cloned.1.call-done = bf16[1,1024,1024]{2,1,0:T(8,128)(2,1)} async-done(((bf16[1,128,1024]{2,1,0:T(8,128)(2,1)}), bf16[1,1024,1024]{2,1,0:T(8,128)(2,1)}) %all-gather.20.cloned.1.call-update) | async-done | bytes 2097168 | tf_op jit(solution)/shard_map/all_gather | solution.py:251
  418.3 65.7 %all-gather.26.cloned.1.call-done = bf16[1536,1024]{1,0:T(8,128)(2,1)} async-done(((bf16[384,1024]{1,0:T(8,128)(2,1)}), bf16[1536,1024]{1,0:T(8,128)(2,1)}) %all-gather.26.cloned.1.call-update) | async-done | bytes 3145744 | tf_op jit(solution)/shard_map/all_gather | solution.py:46
  484.0 20.1 %multiply_convert_fusion.2 = (bf16[1536,1024]{1,0:T(8,128)(2,1)}, f32[1536,1024]{1,0:T(8,128)}, f32[1536,1024]{1,0:T(8,128)}) fusion(bf16[1536,1024]{1,0:T(8,128)(2,1)} %all-gather.26.cloned.1.call-done, bf16[1,1024,1024]{2,1,0:T(8,128)(2,1)} %all-gather.20.cloned.1.call-done), kind=kOutput, calls=%fused_computation.100 | convolution fusion | flops 3323461632 | bytes 20971520 | tf_op jit(solution)/shard_map/dot_general | solution.py:142
  512.5 65.1 %all-gather.34.cloned.1.call-done = bf16[1,1,1536,1024]{3,2,1,0:T(8,128)(2,1)} async-done(((bf16[1,1,384,1024]{3,2,1,0:T(8,128)(2,1)}), bf16[1,1,1536,1024]{3,2,1,0:T(8,128)(2,1)}) %all-gather.34.cloned.1.call-update) | async-done | bytes 3145744 | tf_op jit(solution)/shard_map/all_gather | solution.py:192
  577.6 11.5 add_convert_fusion
  595.9 45.8 %all-gather.18.cloned.1.call-done = bf16[1536,1024]{1,0:T(8,128)(2,1)} async-done(((bf16[384,1024]{1,0:T(8,128)(2,1)}), bf16[1536,1024]{1,0:T(8,128)(2,1)}) %all-gather.18.cloned.1.call-update) | async-done | bytes 3145744 | tf_op jit(solution)/shard_map/all_gather | solution.py:46
  641.8 20.1 %multiply_convert_fusion.3 = (bf16[1536,1024]{1,0:T(8,128)(2,1)}, f32[1536,1024]{1,0:T(8,128)}, f32[1536,1024]{1,0:T(8,128)}) fusion(bf16[1536,1024]{1,0:T(8,128)(2,1)} %all-gather.18.cloned.1.call-done, bf16[1,1024,1024]{2,1,0:T(8,128)(2,1)} %all-gather.20.cloned.1.call-done), kind=kOutput, calls=%fused_computation.113 | convolution fusion | flops 3323461632 | bytes 20971520 | tf_op jit(solution)/shard_map/dot_general | solution.py:142
  661.8 43.7 %all-gather.32.cloned.1.call-done = bf16[1,1,1536,1024]{3,2,1,0:T(8,128)(2,1)} async-done(((bf16[1,1,384,1024]{3,2,1,0:T(8,128)(2,1)}), bf16[1,1,1536,1024]{3,2,1,0:T(8,128)(2,1)}) %all-gather.32.cloned.1.call-update) | async-done | bytes 3145744 | tf_op jit(solution)/shard_map/all_gather | solution.py:192
  705.5 11.5 add_convert_fusion.1
  731.9 34.8 %reduce-scatter.46.cloned.1.call-done = bf16[384,1024]{1,0:T(8,128)(2,1)} async-done(((bf16[1536,1024]{1,0:T(8,128)(2,1)}), bf16[384,1024]{1,0:T(8,128)(2,1)}) %reduce-scatter.46.cloned.1.call-update) | async-done | bytes 786448 | tf_op jit(solution)/shard_map/reduce_scatter | solution.py:203
  766.6 62.6 %reduce-scatter.42.cloned.1.call-done = bf16[384,1024]{1,0:T(8,128)(2,1)} async-done(((bf16[1536,1024]{1,0:T(8,128)(2,1)}), bf16[384,1024]{1,0:T(8,128)(2,1)}) %reduce-scatter.42.cloned.1.call-update) | async-done | bytes 786448 | tf_op jit(solution)/shard_map/reduce_scatter | solution.py:203
  832.9 58.8 %reduce-scatter.40.cloned.1.call-done = bf16[384,1024]{1,0:T(8,128)(2,1)} async-done(((bf16[1536,1024]{1,0:T(8,128)(2,1)}), bf16[384,1024]{1,0:T(8,128)(2,1)}) %reduce-scatter.40.cloned.1.call-update) | async-done | bytes 786448 | tf_op jit(solution)/shard_map/reduce_scatter | solution.py:145
  948.5 11.3 all-gather.30.cloned.1.call-done
  968.3 55.1 %all-gather.28.cloned.1.call-done = bf16[1536,1024]{1,0:T(8,128)(2,1)} async-done(((bf16[384,1024]{1,0:T(8,128)(2,1)}), bf16[1536,1024]{1,0:T(8,128)(2,1)}) %all-gather.28.cloned.1.call-update) | async-done | bytes 3145744 | tf_op jit(solution)/shard_map/all_gather | solution.py:215
  1028.5 63.1 %while.71 = (s32[]{:T(128)}, f32[1536,4,64]{0,2,1:T(8,128)S(1)}, f32[1536,4,64]{0,2,1:T(8,128)}, bf16[3,512,4,64]{1,3,2,0:T(8,128)(2,1)}, bf16[3,512,4,64]{1,3,2...) while((s32[]{:T(128)}, f32[1536,4,64]{0,2,1:T(8,128)S(1)}, ...), condition=%wide.region_34.35_spmd.clone, body=%wide.region_32.34_spmd.clone.sunk | while | flops 2043674112 | bytes 136097008 | solution.py:106
  1124.2 63.1 %while.70 = (s32[]{:T(128)}, f32[1536,4,64]{0,2,1:T(8,128)S(1)}, f32[1536,4,64]{0,2,1:T(8,128)}, bf16[3,512,4,64]{1,3,2,0:T(8,128)(2,1)}, bf16[3,512,4,64]{1,3,2...) while((s32[]{:T(128)}, f32[1536,4,64]{0,2,1:T(8,128)S(1)}, ...), condition=%wide.region_25.26_spmd.clone, body=%wide.region_23.25_spmd.clone.sunk | while | flops 2043674112 | bytes 136097008 | solution.py:106
  1237.7 37.6 %reduce-scatter.52.cloned.1.call-done = bf16[1,128,256]{2,1,0:T(8,128)(2,1)} async-done(((bf16[1,1024,256]{2,1,0:T(8,128)(2,1)}), bf16[1,128,256]{2,1,0:T(8,128)(2,1)}) %reduce-scatter.52.cloned.1.call-update) | async-done | bytes 65552 | tf_op jit(solution)/shard_map/reduce_scatter | solution.py:261
  1276.8 40.2 %reduce-scatter.60.cloned.1.call-done = bf16[128,768]{1,0:T(8,128)(2,1)} async-done(((bf16[1024,768]{1,0:T(8,128)(2,1)}), bf16[128,768]{1,0:T(8,128)(2,1)}) %reduce-scatter.60.cloned.1.call-update) | async-done | bytes 196624
  1318.3 41.0 %reduce-scatter.58.cloned.1.call-done = bf16[128,768]{1,0:T(8,128)(2,1)} async-done(((bf16[1024,768]{1,0:T(8,128)(2,1)}), bf16[128,768]{1,0:T(8,128)(2,1)}) %reduce-scatter.58.cloned.1.call-update) | async-done | bytes 196624
  1361.6 60.3 %reduce-scatter.48.cloned.1.call-done = bf16[384,1024]{1,0:T(8,128)(2,1)} async-done(((bf16[1536,1024]{1,0:T(8,128)(2,1)}), bf16[384,1024]{1,0:T(8,128)(2,1)}) %reduce-scatter.48.cloned.1.call-update) | async-done | bytes 786448 | tf_op jit(solution)/shard_map/reduce_scatter | solution.py:227
  1421.9 62.5 %reduce-scatter.44.cloned.1.call-done = bf16[384,1024]{1,0:T(8,128)(2,1)} async-done(((bf16[1536,1024]{1,0:T(8,128)(2,1)}), bf16[384,1024]{1,0:T(8,128)(2,1)}) %reduce-scatter.44.cloned.1.call-update) | async-done | bytes 786448 | tf_op jit(solution)/shard_map/reduce_scatter | solution.py:227
  1492.0 54.8 %reduce-scatter.36.cloned.1.call-done = bf16[384,1024]{1,0:T(8,128)(2,1)} async-done(((bf16[1536,1024]{1,0:T(8,128)(2,1)}), bf16[384,1024]{1,0:T(8,128)(2,1)}) %reduce-scatter.36.cloned.1.call-update) | async-done | bytes 786448 | tf_op jit(solution)/shard_map/reduce_scatter | solution.py:145
  1554.7 128.4 %reduce-scatter.70.cloned.1.call-done = f32[32,1]{1,0:T(8,128)} async-done(((f32[1024,1]{1,0:T(8,128)}), f32[32,1]{1,0:T(8,128)}) %reduce-scatter.70.cloned.1.call-update) | async-done | bytes 144
  1684.5 131.4 %reduce-scatter.68.cloned.1.call-done = f32[32,1]{1,0:T(8,128)} async-done(((f32[1024,1]{1,0:T(8,128)}), f32[32,1]{1,0:T(8,128)}) %reduce-scatter.68.cloned.1.call-update) | async-done | bytes 144
  1817.2 131.3 %reduce-scatter.66.cloned.1.call-done = f32[32,2]{1,0:T(8,128)} async-done(((f32[1024,2]{1,0:T(8,128)}), f32[32,2]{1,0:T(8,128)}) %reduce-scatter.66.cloned.1.call-update) | async-done | bytes 272
  (461 shorter events, 466.8 us)
Async XLA Ops:
  7.2 32.6 %all-gather.16.cloned.1.call-start = ((), (), s32[]{:S(2)}) async-start(), calls=%async_computation.20 | async-start | bytes 1769472 | tf_op jit(solution)/shard_map/all_gather | solution.py:249
  9.1 96.4 %all-gather.14.cloned.1.call-start = ((), (), s32[]{:S(2)}) async-start(), calls=%async_computation.19 | async-start | bytes 3932160 | tf_op jit(solution)/shard_map/all_gather | solution.py:42
  16.4 197.5 %reduce-scatter.34.cloned.1.call-start = ((), (), s32[]{:S(2)}) async-start(), calls=%async_computation.21 | async-start | bytes 3932160 | tf_op jit(solution)/shard_map/reduce_scatter | solution.py:131
  154.8 125.6 %all-gather.24.cloned.1.call-start = ((), (), s32[]{:S(2)}) async-start(), calls=%async_computation.26 | async-start | bytes 3932160 | tf_op jit(solution)/shard_map/all_gather | solution.py:42
  216.8 171.9 %reduce-scatter.38.cloned.1.call-start = ((), (), s32[]{:S(2)}) async-start(), calls=%async_computation.27 | async-start | bytes 3932160 | tf_op jit(solution)/shard_map/reduce_scatter | solution.py:131
  329.6 88.7 %all-gather.20.cloned.1.call-start = ((), (), s32[]{:S(2)}) async-start(), calls=%async_computation.23 | async-start | bytes 2359296 | tf_op jit(solution)/shard_map/all_gather | solution.py:251
  330.2 153.8 %all-gather.26.cloned.1.call-start = ((), (), s32[]{:S(2)}) async-start(), calls=%async_computation.28 | async-start | bytes 3932160 | tf_op jit(solution)/shard_map/all_gather | solution.py:46
  330.4 561.3 %copy-start.48 = (f32[384]{0:T(512)}, f32[384]{0:T(512)S(1)}, u32[]{:S(2)}) copy-start(f32[384]{0:T(512)S(1)} %broadcast_multiply_fusion.10) | copy-start | bytes 4612
  390.5 501.3 %copy-start.46 = (f32[384]{0:T(512)}, f32[384]{0:T(512)S(1)}, u32[]{:S(2)}) copy-start(f32[384]{0:T(512)S(1)} %get-tuple-element.714) | copy-start | bytes 4612
  392.9 119.6 %all-gather.22.cloned.1.call-start = ((), (), s32[]{:S(2)}) async-start(), calls=%async_computation.24 | async-start | bytes 2359296 | tf_op jit(solution)/shard_map/all_gather | solution.py:252
  393.6 184.0 %all-gather.34.cloned.1.call-start = ((), (), s32[]{:S(2)}) async-start(), calls=%async_computation.41 | async-start | bytes 3932160 | tf_op jit(solution)/shard_map/all_gather | solution.py:192
  396.3 245.4 %all-gather.18.cloned.1.call-start = ((), (), s32[]{:S(2)}) async-start(), calls=%async_computation.22 | async-start | bytes 3932160 | tf_op jit(solution)/shard_map/all_gather | solution.py:46
  396.9 308.6 %all-gather.32.cloned.1.call-start = ((), (), s32[]{:S(2)}) async-start(), calls=%async_computation.40 | async-start | bytes 3932160 | tf_op jit(solution)/shard_map/all_gather | solution.py:192
  397.7 369.0 %reduce-scatter.46.cloned.1.call-start = ((), (), s32[]{:S(2)}) async-start(), calls=%async_computation.33 | async-start | bytes 3932160 | tf_op jit(solution)/shard_map/reduce_scatter | solution.py:203
  595.7 233.6 %reduce-scatter.42.cloned.1.call-start = ((), (), s32[]{:S(2)}) async-start(), calls=%async_computation.30 | async-start | bytes 3932160 | tf_op jit(solution)/shard_map/reduce_scatter | solution.py:203
  723.7 168.0 %reduce-scatter.40.cloned.1.call-start = ((), (), s32[]{:S(2)}) async-start(), calls=%async_computation.29 | async-start | bytes 3932160 | tf_op jit(solution)/shard_map/reduce_scatter | solution.py:145
  731.8 227.9 %all-gather.30.cloned.1.call-start = ((), (), s32[]{:S(2)}) async-start(), calls=%async_computation.34 | async-start | bytes 3932160 | tf_op jit(solution)/shard_map/all_gather | solution.py:215
  896.1 127.3 %all-gather.28.cloned.1.call-start = ((), (), s32[]{:S(2)}) async-start(), calls=%async_computation.31 | async-start | bytes 3932160 | tf_op jit(solution)/shard_map/all_gather | solution.py:215
  896.6 330.4 %reduce-scatter.64.cloned.1.call-start = ((), (), s32[]{:S(2)}) async-start(), calls=%async_computation.45 | async-start | bytes 2359296
  915.1 313.6 %reduce-scatter.62.cloned.1.call-start = ((), (), s32[]{:S(2)}) async-start(), calls=%async_computation.44 | async-start | bytes 2359296
  934.0 297.5 %reduce-scatter.56.cloned.1.call-start = ((), (), s32[]{:S(2)}) async-start(), calls=%async_computation.39 | async-start | bytes 2359296 | tf_op jit(solution)/shard_map/reduce_scatter | solution.py:264
  940.7 290.9 %reduce-scatter.54.cloned.1.call-start = ((), (), s32[]{:S(2)}) async-start(), calls=%async_computation.38 | async-start | bytes 2359296 | tf_op jit(solution)/shard_map/reduce_scatter | solution.py:264
  948.4 289.3 %reduce-scatter.50.cloned.1.call-start = ((), (), s32[]{:S(2)}) async-start(), calls=%async_computation.36 | async-start | bytes 589824 | tf_op jit(solution)/shard_map/reduce_scatter | solution.py:261
  1027.3 248.0 %reduce-scatter.52.cloned.1.call-start = ((), (), s32[]{:S(2)}) async-start(), calls=%async_computation.37 | async-start | bytes 589824 | tf_op jit(solution)/shard_map/reduce_scatter | solution.py:261
  1102.5 214.6 %reduce-scatter.60.cloned.1.call-start = ((), (), s32[]{:S(2)}) async-start(), calls=%async_computation.43 | async-start | bytes 1769472
  1122.8 236.5 %reduce-scatter.58.cloned.1.call-start = ((), (), s32[]{:S(2)}) async-start(), calls=%async_computation.42 | async-start | bytes 1769472
  1205.2 216.7 %reduce-scatter.48.cloned.1.call-start = ((), (), s32[]{:S(2)}) async-start(), calls=%async_computation.35 | async-start | bytes 3932160 | tf_op jit(solution)/shard_map/reduce_scatter | solution.py:227
  1211.4 272.9 %reduce-scatter.44.cloned.1.call-start = ((), (), s32[]{:S(2)}) async-start(), calls=%async_computation.32 | async-start | bytes 3932160 | tf_op jit(solution)/shard_map/reduce_scatter | solution.py:227
  1218.5 328.3 %reduce-scatter.36.cloned.1.call-start = ((), (), s32[]{:S(2)}) async-start(), calls=%async_computation.25 | async-start | bytes 3932160 | tf_op jit(solution)/shard_map/reduce_scatter | solution.py:145
  1226.9 456.2 %reduce-scatter.70.cloned.1.call-start = ((), (), s32[]{:S(2)}) async-start(), calls=%async_computation.48 | async-start | bytes 540672
  1488.4 327.5 %reduce-scatter.68.cloned.1.call-start = ((), (), s32[]{:S(2)}) async-start(), calls=%async_computation.47 | async-start | bytes 540672
  1552.3 396.2 %reduce-scatter.66.cloned.1.call-start = ((), (), s32[]{:S(2)}) async-start(), calls=%async_computation.46 | async-start | bytes 540672
  (95 other events, 5456.5 us)
Sparse Core Ops, SparseCore 0:
  10.5 29.2 all-gather.15
  41.9 63.4 all-gather.13
  154.9 58.8 reduce-scatter.33
  216.9 63.5 all-gather.23
  329.7 58.8 reduce-scatter.37
  390.4 27.9 all-gather.19
  420.5 63.4 all-gather.25
  485.9 26.5 all-gather.21
  514.1 63.4 all-gather.33
  579.6 62.1 all-gather.17
  643.3 62.1 all-gather.31
  707.7 58.8 reduce-scatter.45
  768.9 60.2 reduce-scatter.41
  831.4 60.2 reduce-scatter.39
  896.2 63.5 all-gather.29
  961.2 62.1 all-gather.27
  1026.5 39.8 reduce-scatter.63
  1069.9 41.2 reduce-scatter.61
  1114.4 41.1 reduce-scatter.55
  1159.2 41.2 reduce-scatter.53
  1203.6 34.1 reduce-scatter.49
  1241.1 34.1 reduce-scatter.51
  1278.6 38.4 reduce-scatter.59
  1320.8 38.4 reduce-scatter.57
  1361.6 60.2 reduce-scatter.47
  1424.0 60.2 reduce-scatter.43
  1486.5 60.2 reduce-scatter.35
  1549.1 134.0 reduce-scatter.69
  1685.5 130.3 reduce-scatter.67
  1818.0 130.4 reduce-scatter.65
where the time goes:
time: 1970 us; the launch traced here: 1960 us
  waiting for transfers between devices  1420 us (72%)
  matrix products  311 us (16%)
  local copies, waits for them, and re-layouts  115 us (6%)
  other arithmetic  75.7 us (4%)
    unnamed x37, waiting for transfers between devices  476 us
    all_gather x2, waiting for transfers between devices, spread_attn(): return lax.all_gather(normed, 'mp', axis=0, tiled=True)  129 us
    reduce_scatter x2, waiting for transfers between devices, layer_backward(): lax.psum_scatter(jnp.einsum('ise,ide->sd', part, w_proj, preferred_elemen...  123 us
    reduce_scatter x2, waiting for transfers between devices, layer_forward(): lax.psum_scatter(lax.dot_general(part, w_out, (((1,), (1,)), ((), ())), p...  117 us
    reduce_scatter x2, waiting for transfers between devices, layer_forward(): lax.psum_scatter(lax.dot_general(part, w_down, (((1,), (1,)), ((), ())),...  114 us
    all_gather x2, waiting for transfers between devices, spread_mlp(): return lax.all_gather(normed, 'mp', axis=0, tiled=True)  112 us
    all_gather x2, waiting for transfers between devices, layer_backward(): lax.all_gather(grad_state.astype(jnp.bfloat16), 'mp', axis=0, tiled=True)  109 us
    reduce_scatter x2, waiting for transfers between devices, layer_backward(): lax.psum_scatter(lax.dot_general(part, w_up, (((1,), (1,)), ((), ())), pr...  97.4 us
  transfers between devices with their start and end apart: 30, of which 26 were waited for; matrix products, arithmetic and copies ran while one was open for 20% of the time, Pallas kernels for 0%

commit v1 on v0

v1 whole, which is shorter than its diff:
```python
import functools

import jax
import jax.numpy as jnp
from jax import lax
from jax.experimental import pallas as pl
from jax.experimental.pallas import tpu as pltpu
from jax.sharding import PartitionSpec as P

HDIM = 64
VIEW_TOK = 256
TRI = 768
EPSILON = 1e-05
MASKED = -1000000000.0
F32 = jnp.float32
BF16 = jnp.bfloat16
MIB = 1024 * 1024


def params(mib, *semantics):
    return pltpu.CompilerParams(
        vmem_limit_bytes=mib * MIB,
        dimension_semantics=semantics if semantics else None,
    )


def swap(value, bit, size):
    return lax.ppermute(value, "dp", [(i, i ^ bit) for i in range(size)])


def ring(value, step, size):
    return lax.ppermute(value, "mp", [(i, (i + step) % size) for i in range(size)])


def gather_pieces(shard, order, nd, nm):
    column, current = [shard], shard
    for _ in range(nm - 1):
        current = ring(current, 1, nm)
        column.append(current)
    pieces = {0: jnp.stack(column)}
    for bit in order:
        for j in list(pieces):
            pieces[j | bit] = swap(pieces[j], bit, nd)
    return [pieces[j] for j in range(nd)]


def scatter_pieces(pieces, order, nd, nm):
    pieces = dict(enumerate(pieces))
    for bit in order:
        for j in list(pieces):
            if j & bit:
                came = swap(pieces.pop(j), bit, nd)
                kept = pieces[j ^ bit]
                pieces[j ^ bit] = (kept.astype(F32) + came.astype(F32)).astype(BF16)
    own = pieces[0]
    current = own[nm - 1]
    for k in range(nm - 2, -1, -1):
        came = ring(current, -1, nm)
        total = own[k].astype(F32) + came.astype(F32)
        current = total.astype(BF16) if k else total
    return current


def assemble_kernel(nd, nm, place_ref, *refs):
    pieces, out_ref, sems = refs[:nd], refs[nd], refs[nd + 1]
    rows, cols = pieces[0].shape[-2:]
    copies = []
    for j in range(nd):
        row = place_ref[0] ^ j
        for k in range(nm):
            col = lax.rem(place_ref[1] + nm - k, nm)
            dst = out_ref.at[
                :,
                pl.ds(pl.multiple_of(row * rows, rows), rows),
                pl.ds(pl.multiple_of(col * cols, cols), cols),
            ]
            copies.append(pltpu.make_async_copy(pieces[j].at[k], dst, sems.at[j * nm + k]))
    for copy in copies:
        copy.start()
    for copy in copies:
        copy.wait()


def assemble(pieces, place, nd, nm):
    _, lead, rows, cols = pieces[0].shape
    return pl.pallas_call(
        functools.partial(assemble_kernel, nd, nm),
        out_shape=jax.ShapeDtypeStruct((lead, nd * rows, nm * cols), BF16),
        in_specs=[pl.BlockSpec(memory_space=pltpu.SMEM)]
        + [pl.BlockSpec(memory_space=pl.ANY)] * nd,
        out_specs=pl.BlockSpec(memory_space=pltpu.VMEM),
        compiler_params=params(32),
        scratch_shapes=[pltpu.SemaphoreType.DMA((nd * nm,))],
        name="assemble",
    )(place, *pieces)


def split_kernel(nd, nm, place_ref, in_ref, *refs):
    pieces, sems = refs[:nd], refs[nd]
    rows, cols = pieces[0].shape[-2:]
    copies = []
    for j in range(nd):
        row = place_ref[0] ^ j
        for k in range(nm):
            col = lax.rem(place_ref[1] + nm - k, nm)
            src = in_ref.at[
                :,
                pl.ds(pl.multiple_of(row * rows, rows), rows),
                pl.ds(pl.multiple_of(col * cols, cols), cols),
            ]
            copies.append(pltpu.make_async_copy(src, pieces[j].at[k], sems.at[j * nm + k]))
    for copy in copies:
        copy.start()
    for copy in copies:
        copy.wait()


def split(full, place, nd, nm):
    lead, rows, cols = full.shape
    piece = jax.ShapeDtypeStruct((nm, lead, rows // nd, cols // nm), BF16)
    return pl.pallas_call(
        functools.partial(split_kernel, nd, nm),
        out_shape=[piece] * nd,
        in_specs=[pl.BlockSpec(memory_space=pltpu.SMEM), pl.BlockSpec(memory_space=pltpu.VMEM)],
        compiler_params=params(32),
        out_specs=[pl.BlockSpec(memory_space=pl.ANY)] * nd,
        scratch_shapes=[pltpu.SemaphoreType.DMA((nd * nm,))],
        name="split",
    )(place, full)


def dot_nt(a, b):
    return lax.dot_general(a, b, (((1,), (1,)), ((), ())), preferred_element_type=F32)


def dot_nn(a, b):
    return lax.dot_general(a, b, (((1,), (0,)), ((), ())), preferred_element_type=F32)


def dot_tn(a, b):
    return lax.dot_general(a, b, (((0,), (0,)), ((), ())), preferred_element_type=F32)


def attend_kernel(q_ref, k_ref, v_ref, bias_ref, out_ref, lse_ref):
    rows = q_ref.shape[1]
    low = lax.broadcasted_iota(jnp.int32, (1, 2 * HDIM), 1) < HDIM
    query = q_ref[0] * jnp.asarray(HDIM ** (-0.5), BF16)
    keys, values = k_ref[0], v_ref[0]
    bias = bias_ref[...]
    mixed = None
    for head in range(2):
        mine = low if head == 0 else jnp.logical_not(low)
        scores = dot_nt(jnp.where(mine, query, jnp.zeros_like(query)), keys)
        scores = jnp.where(bias < 0.0, MASKED, scores)
        top = jnp.max(scores, axis=1, keepdims=True)
        expo = jnp.exp(scores - top)
        total = jnp.sum(expo, axis=1, keepdims=True)
        part = dot_nn(expo.astype(BF16), values) / total
        mixed = part if head == 0 else jnp.where(low, mixed, part)
        lse = top + jnp.log(total)
        lse_ref[0, head : head + 1, :] = jnp.transpose(jnp.broadcast_to(lse, (rows, 128)))[0:1, :]
    out_ref[...] = mixed.astype(BF16)


def attend(qkv, keys_values, bias, block=256):
    _, rows, width = qkv.shape
    keys = keys_values.shape[1]
    pairs = width // (2 * HDIM)
    return pl.pallas_call(
        attend_kernel,
        grid=(pairs, rows // block),
        in_specs=[
            pl.BlockSpec((1, block, 2 * HDIM), lambda h, i: (0, i, h)),
            pl.BlockSpec((1, keys, 2 * HDIM), lambda h, i: (0, 0, h)),
            pl.BlockSpec((1, keys, 2 * HDIM), lambda h, i: (1, 0, h)),
            pl.BlockSpec((1, keys), lambda h, i: (0, 0)),
        ],
        out_specs=[
            pl.BlockSpec((block, 2 * HDIM), lambda h, i: (i, h)),
            pl.BlockSpec((1, 2, block), lambda h, i: (h, 0, i)),
        ],
        out_shape=[
            jax.ShapeDtypeStruct((rows, width), BF16),
            jax.ShapeDtypeStruct((pairs, 2, rows), F32),
        ],
        compiler_params=params(48),
        cost_estimate=pl.CostEstimate(
            flops=16 * rows * keys * width, bytes_accessed=8 * keys * width, transcendentals=0
        ),
        name="attend",
    )(qkv, keys_values, keys_values, bias)


def attend_back_kernel(
    q_ref, k_ref, v_ref, bias_ref, lse_ref, mixed_ref, grad_ref, dq_ref, dkv_ref, dk_acc, dv_acc
):
    step = pl.program_id(1)
    low = lax.broadcasted_iota(jnp.int32, (1, 2 * HDIM), 1) < HDIM
    scale = jnp.asarray(HDIM ** (-0.5), BF16)
    query = q_ref[0] * scale
    grad = grad_ref[...]
    keys, values = k_ref[0], v_ref[0]
    bias = bias_ref[...]
    product = mixed_ref[...].astype(F32) * grad.astype(F32)
    grad_query = None
    new_key, new_value = None, None
    for head in range(2):
        mine = low if head == 0 else jnp.logical_not(low)
        q_mine = jnp.where(mine, query, jnp.zeros_like(query))
        g_mine = jnp.where(mine, grad, jnp.zeros_like(grad))
        delta = jnp.sum(jnp.where(mine, product, 0.0), axis=1, keepdims=True)
        delta = jnp.transpose(jnp.broadcast_to(delta, (delta.shape[0], 128)))[0:1, :]
        scores = dot_nt(keys, q_mine)
        scores = jnp.where(bias < 0.0, MASKED, scores)
        probs = jnp.exp(scores - lse_ref[0, head : head + 1, :])
        upstream = dot_nt(values, g_mine)
        grad_scores = (probs * (upstream - delta)).astype(BF16)
        value_part = dot_nn(probs.astype(BF16), g_mine)
        key_part = dot_nn(grad_scores, q_mine)
        query_part = dot_tn(grad_scores, keys)
        if head == 0:
            new_key, new_value, grad_query = key_part, value_part, query_part
        else:
            new_key, new_value = new_key + key_part, new_value + value_part
            grad_query = jnp.where(low, grad_query, query_part)
    dq_ref[...] = (grad_query * HDIM ** (-0.5)).astype(BF16)

    @pl.when(step == 0)
    def _():
        dk_acc[...] = new_key
        dv_acc[...] = new_value

    @pl.when(step > 0)
    def _():
        dk_acc[...] += new_key
        dv_acc[...] += new_value

    @pl.when(step == pl.num_programs(1) - 1)
    def _():
        dkv_ref[0] = dk_acc[...].astype(BF16)
        dkv_ref[1] = dv_acc[...].astype(BF16)


def attend_back(qkv, keys_values, bias, lse, mixed, grad_mixed, block=256):
    _, rows, width = qkv.shape
    keys = keys_values.shape[1]
    pairs = width // (2 * HDIM)
    return pl.pallas_call(
        attend_back_kernel,
        grid=(pairs, rows // block),
        in_specs=[
            pl.BlockSpec((1, block, 2 * HDIM), lambda h, i: (0, i, h)),
            pl.BlockSpec((1, keys, 2 * HDIM), lambda h, i: (0, 0, h)),
            pl.BlockSpec((1, keys, 2 * HDIM), lambda h, i: (1, 0, h)),
            pl.BlockSpec((keys, 1), lambda h, i: (0, 0)),
            pl.BlockSpec((1, 2, block), lambda h, i: (h, 0, i)),
            pl.BlockSpec((block, 2 * HDIM), lambda h, i: (i, h)),
            pl.BlockSpec((block, 2 * HDIM), lambda h, i: (i, h)),
        ],
        out_specs=[
            pl.BlockSpec((block, 2 * HDIM), lambda h, i: (i, h)),
            pl.BlockSpec((2, keys, 2 * HDIM), lambda h, i: (0, 0, h)),
        ],
        out_shape=[
            jax.ShapeDtypeStruct((rows, width), BF16),
            jax.ShapeDtypeStruct((2, keys, width), BF16),
        ],
        scratch_shapes=[pltpu.VMEM((keys, 2 * HDIM), F32), pltpu.VMEM((keys, 2 * HDIM), F32)],
        compiler_params=params(48),
        cost_estimate=pl.CostEstimate(
            flops=40 * rows * keys * width, bytes_accessed=16 * keys * width, transcendentals=0
        ),
        name="attend_back",
    )(qkv, keys_values, keys_values, bias, lse, mixed, grad_mixed)


def normalize(state, gain, bias):
    centre = jnp.mean(state, axis=-1, keepdims=True)
    centred = state - centre
    spread = jnp.mean(centred * centred, axis=-1, keepdims=True)
    inverse = lax.rsqrt(spread + EPSILON)
    scaled = centred * inverse
    return (scaled * gain + bias, scaled, inverse)


def normalize_back(grad, scaled, inverse, gain):
    weighted = grad * gain
    first = jnp.mean(weighted, axis=-1, keepdims=True)
    second = jnp.mean(weighted * scaled, axis=-1, keepdims=True)
    return (
        inverse * (weighted - first - scaled * second),
        jnp.sum(grad * scaled, axis=0),
        jnp.sum(grad, axis=0),
    )


def gelu_exact(values):
    return jax.nn.gelu(values, approximate=False)


def shards(nd, nm, tokens, views, norm_gains, norm_biases, w_proj, w_out, w_up, w_down, cotangent):
    micro, _, chunk, width = tokens.shape
    ranks = nm // micro
    half = max(ranks // 2, 1)
    rows = micro * chunk
    dp, mp = lax.axis_index("dp"), lax.axis_index("mp")
    core = dp & 1
    place = jnp.stack([dp, mp]).astype(jnp.int32)
    gains, biases = norm_gains[0], norm_biases[0]
    orders = [[1 << b for b in range(1, nd.bit_length() - 1)]]
    orders.append(orders[0][::-1])
    orders = [order + [1] for order in orders]
    group = mp // half
    step_here = group // 2
    rank = core + 2 * (mp % half)

    def routes(k):
        pairs = []
        for d in range(nd):
            for z in range(nm):
                m = (k + z) % micro
                r = z // micro
                to_d = (d & ~1) | (r & 1)
                to_z = (2 * m + (d & 1)) * half + r // 2
                pairs.append((d * nm + z, to_d * nm + to_z))
        return pairs

    def bring(value):
        came = [
            lax.ppermute(
                lax.dynamic_index_in_dim(value, (k + mp) % micro, 0, keepdims=False),
                ("dp", "mp"),
                routes(k),
            )
            for k in range(micro)
        ]
        came = jnp.stack(came)
        slots = [
            lax.dynamic_index_in_dim(came, (step_here - s) % micro, 0, keepdims=False)
            for s in range(micro)
        ]
        return jnp.concatenate(slots, axis=0)

    def send_back(value):
        slots = value.reshape((micro, chunk) + value.shape[1:])
        back = jnp.stack(
            [
                lax.ppermute(
                    lax.dynamic_index_in_dim(slots, (step_here - k) % micro, 0, keepdims=False),
                    ("dp", "mp"),
                    [(b, a) for a, b in routes(k)],
                )
                for k in range(micro)
            ]
        )
        return jnp.stack(
            [
                lax.dynamic_index_in_dim(back, (m - mp) % micro, 0, keepdims=False)
                for m in range(micro)
            ]
        )

    state = bring(tokens[:, 0]).astype(F32)
    count = lax.ppermute(
        lax.dynamic_index_in_dim(views[:, 0], mp % micro, 0, keepdims=True), ("dp", "mp"), routes(0)
    )[0]

    gather = functools.partial(gather_pieces, nd=nd, nm=nm)
    wq_out = gather(jnp.stack([w_proj[0, 0], w_out[0]]), orders[0])
    wk_v = gather(w_proj[0, 1:], orders[1])
    up_pieces = gather(w_up, orders[0])
    down_pieces = gather(w_down, orders[1])
    full_a = assemble(wq_out, place, nd, nm)
    full_b = assemble(wk_v, place, nd, nm)
    wq, wo = full_a[0], full_a[1]
    upw = assemble(up_pieces, place, nd, nm)[0]
    dnw = assemble(down_pieces, place, nd, nm)[0]
    grad_state = bring(cotangent[:, 0])

    normed, scaled_one, inverse_one = normalize(state, gains[0], biases[0])
    normed = normed.astype(BF16)
    query = jnp.dot(normed, wq, preferred_element_type=F32).astype(BF16)
    kv = jnp.einsum("sd,ide->ise", normed, full_b, preferred_element_type=F32).astype(BF16)
    qkv = query[None]
    pieces = {0: kv}
    bits = [1 << b for b in range(ranks.bit_length() - 1)]

    def swap_rank(value, bit):
        if bit == 1:
            return swap(value, 1, nd)
        return lax.ppermute(value, "mp", [(i, i ^ (bit >> 1)) for i in range(nm)])

    for bit in bits:
        for j in list(pieces):
            pieces[j | bit] = swap_rank(pieces[j], bit)
    all_kv = jnp.concatenate([pieces[j] for j in range(ranks)], axis=1)
    position = jnp.concatenate(
        [(rank ^ j) * rows + jnp.arange(rows, dtype=jnp.int32) for j in range(ranks)]
    )
    bias = jnp.where(position < TRI + count * VIEW_TOK, 0.0, -1.0).astype(F32)
    mixed, lse = attend(qkv, all_kv, bias[None, :])
    middle = state + dot_nt(mixed, wo)

    normed_two, scaled_two, inverse_two = normalize(middle, gains[1], biases[1])
    normed_two = normed_two.astype(BF16)
    hidden_pre = jnp.dot(normed_two, upw, preferred_element_type=F32)
    activation, pull = jax.vjp(gelu_exact, hidden_pre)
    activation = activation.astype(BF16)
    result = middle + dot_nt(activation, dnw)
    output = send_back(result.astype(BF16))

    give = functools.partial(scatter_pieces, nd=nd, nm=nm)
    back_orders = [[1] + order[:-1][::-1] for order in orders]
    grad_down = dot_tn(grad_state, activation).astype(BF16)
    g_down = give(split(grad_down[None], place, nd, nm), back_orders[1])
    grad_hidden = pull(jnp.dot(grad_state, dnw, preferred_element_type=F32))[0].astype(BF16)
    grad_up = dot_tn(normed_two, grad_hidden).astype(BF16)
    g_up = give(split(grad_up[None], place, nd, nm), back_orders[0])
    grad_normed_two = dot_nt(grad_hidden, upw)
    grad_norm_two, gain_two, bias_two = normalize_back(
        grad_normed_two, scaled_two, inverse_two, gains[1]
    )
    grad_middle = grad_state.astype(F32) + grad_norm_two
    grad_attn = grad_middle.astype(BF16)

    grad_out = dot_tn(grad_attn, mixed).astype(BF16)
    grad_mixed = jnp.dot(grad_attn, wo, preferred_element_type=F32).astype(BF16)
    grad_query, grad_kv = attend_back(qkv, all_kv, bias[:, None], lse, mixed, grad_mixed)
    parts = {j: grad_kv[:, j * rows : (j + 1) * rows] for j in range(ranks)}
    for bit in bits[::-1]:
        for j in list(parts):
            if j & bit:
                came = swap_rank(parts.pop(j), bit)
                parts[j ^ bit] = (parts[j ^ bit].astype(F32) + came.astype(F32)).astype(BF16)
    grad_kv = parts[0]
    grad_q_w = dot_tn(normed, grad_query).astype(BF16)
    grad_kv_w = jnp.einsum("sd,ise->ide", normed, grad_kv, preferred_element_type=F32).astype(BF16)
    g_qo = give(split(jnp.stack([grad_q_w, grad_out]), place, nd, nm), back_orders[0])
    g_kv = give(split(grad_kv_w, place, nd, nm), back_orders[1])
    grad_normed = (
        dot_nt(grad_query, wq) + dot_nt(grad_kv[0], full_b[0]) + dot_nt(grad_kv[1], full_b[1])
    )
    grad_norm_one, gain_one, bias_one = normalize_back(
        grad_normed, scaled_one, inverse_one, gains[0]
    )
    grad_tokens = send_back((grad_middle + grad_norm_one).astype(BF16))

    def everywhere(value):
        bit = 1
        while bit < nd:
            value = value + swap(value, bit, nd)
            bit *= 2
        bit = 1
        while bit < nm:
            value = value + lax.ppermute(value, "mp", [(i, i ^ bit) for i in range(nm)])
            bit *= 2
        share = width // (nd * nm)
        return lax.dynamic_slice_in_dim(value, (dp * nm + mp) * share, share, 1)

    second = everywhere(jnp.stack([gain_two, bias_two]))
    first = everywhere(jnp.stack([gain_one, bias_one]))
    return (
        output[:, None],
        grad_tokens[:, None],
        jnp.concatenate([g_qo[:1], g_kv])[None],
        g_qo[1][None],
        g_up,
        g_down,
        jnp.stack([first[0], second[0]])[None],
        first[1][None],
        second[1][None],
    )


def solution(mesh):
    placed = (
        P(None, "dp", "mp", None),
        P(None, "dp"),
        P(),
        P(),
        P(None, None, "dp", "mp"),
        P(None, "dp", "mp"),
        P(None, "dp", "mp"),
        P(None, "dp", "mp"),
        P(None, "dp", "mp", None),
    )
    return jax.shard_map(
        functools.partial(shards, mesh.shape["dp"], mesh.shape["mp"]),
        mesh=mesh,
        in_specs=placed,
        out_specs=(
            P(None, "dp", "mp", None),
            P(None, "dp", "mp", None),
            P(None, None, "dp", "mp"),
            P(None, "dp", "mp"),
            P(None, "dp", "mp"),
            P(None, "dp", "mp"),
            P(None, None, ("dp", "mp")),
            P(None, ("dp", "mp")),
            P(None, ("dp", "mp")),
        ),
        check_vma=False,
    )
```

time: 1970 us -> 774 us (0.39)
  waiting for transfers between devices: 1420 us -> 285 us
  matrix products: 311 us -> 136 us
  starting transfers between devices: 3.45 us -> 140 us
  Pallas kernels: 0 us -> 129 us
  local copies, waits for them, and re-layouts: 115 us -> 26.2 us
  other arithmetic: 75.7 us -> 47.8 us
    reduce_scatter x12 -> x0, waiting for transfers between devices: 492 us -> none  [the longest x2 123 us: layer_backward(): lax.psum_scatter(jnp.einsum('ise,ide->sd', part, w_proj, preferred_elemen...]
    unnamed x37 -> x0, waiting for transfers between devices: 476 us -> none
    all_gather x11 -> x0, waiting for transfers between devices: 454 us -> none  [the longest x2 129 us: spread_attn(): return lax.all_gather(normed, 'mp', axis=0, tiled=True)]
    ppermute x0 -> x101, waiting for transfers between devices: none -> 285 us  [the longest x64 114 us: swap(): return lax.ppermute(value, 'dp', [(i, i ^ bit) for i in range(size)])]
    dot_general x66 -> x16, matrix products: 311 us -> 136 us  [the longest x1 37.4 us: shards(): hidden_pre = jnp.dot(normed_two, upw, preferred_element_type=F32)]
    ppermute x0 -> x101, starting transfers between devices: none -> 140 us  [the longest x64 62.9 us: swap(): return lax.ppermute(value, 'dp', [(i, i ^ bit) for i in range(size)])]
    pallas_call x0 -> x10, Pallas kernels: none -> 129 us  [the longest x1 68.5 us: attend_back(): pl.pallas_call(attend_back_kernel, grid=(pairs, rows // block), in_specs=...]
    unnamed x189 -> x194, local copies, waits for them, and re-layouts: 70.4 us -> 16.5 us
  transfers between devices with their start and end apart: 30 -> 101, of which waited for: 26 -> 36; matrix products, arithmetic and copies ran while one was open for 20% -> 12% of each run, Pallas kernels for 0% -> 2%
where the time goes in v1:
time: 774 us; the launch traced here: 766 us
  waiting for transfers between devices  285 us (37%)
  starting transfers between devices  140 us (18%)
  matrix products  136 us (18%)
  Pallas kernels  129 us (17%)
  other arithmetic  47.8 us (6%)
  local copies, waits for them, and re-layouts  26.2 us (3%)
    ppermute x64, waiting for transfers between devices, swap(): return lax.ppermute(value, 'dp', [(i, i ^ bit) for i in range(size)])  114 us
    ppermute x24, waiting for transfers between devices, ring(): lax.ppermute(value, 'mp', [(i, (i + step) % size) for i in range(size)])  111 us
    pallas_call x1, Pallas kernels, attend_back(): pl.pallas_call(attend_back_kernel, grid=(pairs, rows // block), in_specs=...  68.5 us
    ppermute x64, starting transfers between devices, swap(): return lax.ppermute(value, 'dp', [(i, i ^ bit) for i in range(size)])  62.9 us
    ppermute x4, waiting for transfers between devices, send_back(): lax.ppermute(lax.dynamic_index_in_dim(slots, (step_here - k) % micro, 0,...  55.6 us
    ppermute x24, starting transfers between devices, ring(): lax.ppermute(value, 'mp', [(i, (i + step) % size) for i in range(size)])  48.2 us
    pallas_call x1, Pallas kernels, attend(): pl.pallas_call(attend_kernel, grid=(pairs, rows // block), in_specs=[pl.B...  39.5 us
    dot_general x1, matrix products, shards(): hidden_pre = jnp.dot(normed_two, upw, preferred_element_type=F32)  37.4 us
  transfers between devices with their start and end apart: 101, of which 36 were waited for; matrix products, arithmetic and copies ran while one was open for 12% of the time, Pallas kernels for 2%

profile of v1, /device:TPU:0, one launch (start us, length us, event | category | flops | bytes accessed | tf_op | source)
XLA Modules:
  0.0 766.2 jit_solution(11594958228070038528)
XLA Ops:
  8.7 4.5 collective-permute-done.24
  21.6 8.5 %collective-permute-done.12 = bf16[2,128,256]{2,1,0:T(8,128)(2,1)} collective-permute-done((bf16[2,128,256]{2,1,0:T(8,128)(2,1)S(1)}, bf16[2,128,256]{2,1,0:T(8,128)(2,1)}, u32[]{:S(2)}, u32[]{:S(2)}) %collective-permute-start.12) | collective-permute-done | bytes 131104 | tf_op jit(solution)/shard_map/ppermute | solution.py:32
  39.4 13.3 %collective-permute-done.4 = bf16[2,128,256]{2,1,0:T(8,128)(2,1)S(1)} collective-permute-done((bf16[2,128,256]{2,1,0:T(8,128)(2,1)S(1)}, bf16[2,128,256]{2,1,0:T(8,128)(2,1)S(1)}, u32[]{:S(2)}, u32[]{:S(2)}) %collective-permute-start.4) | collective-permute-done | bytes 131104 | tf_op jit(solution)/shard_map/ppermute | solution.py:32
  61.1 48.0 %collective-permute-done.36 = bf16[1,128,1024]{2,1,0:T(8,128)(2,1)S(1)} collective-permute-done((bf16[1,128,1024]{2,1,0:T(8,128)(2,1)S(1)}, bf16[1,128,1024]{2,1,0:T(8,128)(2,1)S(1)}, u32[]{:S(2)}, u32[]{:S(2)}) %collective-permute-start.36) | collective-permute-done | bytes 262176 | tf_op jit(solution)/shard_map/ppermute | solution.py:32
  113.8 5.4 collective-permute-done.18.refs_4_
  121.6 8.1 %collective-permute-start.15 = (bf16[4,2,128,256]{3,2,1,0:T(8,128)(2,1)S(1)}, bf16[4,2,128,256]{3,2,1,0:T(8,128)(2,1)}, u32[]{:S(2)}, u32[]{:S(2)}) collective-permute-start(bf16[4,2,128,256]{3,2,1,0:T(8,128)(2,1)S(1)} %pad_maximum_fusion.7.refs_0_), channel_id=1, source_target_pairs={{0,4},{4,0},{8,12},{12,8},{16,20},{20,16},{24,28},{28,24},{1,5},{5... | collective-permute-start | bytes 1572872 | tf_op jit(solution)/shard_map/ppermute | solution.py:28
  132.9 6.9 collective-permute-start.17
  144.1 6.2 collective-permute-start.21
  162.2 6.7 collective-permute-done.10.refs_6_
  170.9 5.9 convert_bitcast_fusion.3
  179.7 11.8 %collective-permute-done.30.refs_4_ = bf16[4,1,128,1024]{3,2,1,0:T(8,128)(2,1)} collective-permute-done((bf16[4,1,128,1024]{3,2,1,0:T(8,128)(2,1)S(1)}, bf16[4,1,128,1024]{3,2,1,0:T(8,128)(2,1)}, u32[]{:S(2)}, u32[]{:S(2)}) %collective-permute-start.30) | collective-permute-done | bytes 1048608 | tf_op jit(solution)/shard_map/ppermute | solution.py:28
  192.5 21.3 %collective-permute-done.40.refs_4_ = bf16[4,1,128,1024]{3,2,1,0:T(8,128)(2,1)} collective-permute-done((bf16[4,1,128,1024]{3,2,1,0:T(8,128)(2,1)S(1)}, bf16[4,1,128,1024]{3,2,1,0:T(8,128)(2,1)}, u32[]{:S(2)}, u32[]{:S(2)}) %collective-permute-start.40) | collective-permute-done | bytes 1048608 | tf_op jit(solution)/shard_map/ppermute | solution.py:28
  216.4 19.5 %collective-permute-done.32.refs_6_ = bf16[4,1,128,1024]{3,2,1,0:T(8,128)(2,1)} collective-permute-done((bf16[4,1,128,1024]{3,2,1,0:T(8,128)(2,1)}, bf16[4,1,128,1024]{3,2,1,0:T(8,128)(2,1)}, u32[]{:S(2)}, u32[]{:S(2)}) %collective-permute-start.32) | collective-permute-done | bytes 1048608 | tf_op jit(solution)/shard_map/ppermute | solution.py:28
  255.5 5.0 assemble.7
  263.9 6.2 pad_maximum_fusion.k_ref.v_ref
  271.5 39.5 %attend.1 = (bf16[768,1024]{1,0:T(8,128)(2,1)S(1)}, f32[8,2,768]{2,1,0:T(2,128)S(1)}) custom-call(bf16[1,768,1024]{2,1,0:T(8,128)(2,1)S(1)} %copy-done.42, bf16[2,1536,1024]{2,1,0:T(8,128)(2,1)} %pad_maximum_fusion.k_ref.v_ref, bf16[2,1536,1024]{2,1,0:T(8,128)(2,1)} %pad_maximum_fusion.k_ref.v_ref, f32[1,1536]{1,0:T(1,128)S(1)} %compare_select_fusion.bias_ref), custom_call_target="tpu_custom_call" | custom-call | flops 19327352832 | bytes 12582912 | tf_op jit(solution)/shard_map/attend/pallas_call | solution.py:169
  315.4 37.4 %multiply_convert_fusion = (bf16[768,4096]{1,0:T(8,128)(2,1)}, f32[768,4096]{1,0:T(8,128)}, f32[768,4096]{1,0:T(8,128)}) fusion(bf16[1,1024,4096]{2,1,0:T(8,128)(2,1)S(1)} %assemble.6, f32[768,1024]{1,0:T(8,128)S(1)} %get-tuple-element.122, f32[1024]{0:T(1024)S(1)} %bitcast.282, f32[1024]{0:T(1024)S(1)} %bitcast.268, f32[768]{0:T(1024)S(1)} %add_rsqrt_fusion, ...), kind=kOutput, calls=%fused_computation.3 | convolution fusion | flops 6650855424 | bytes 43005952 | tf_op jit(solution)/shard_map/dot_general | solution.py:406
  352.8 17.8 %add_convert_fusion = bf16[768,4096]{1,0:T(8,128)(2,1)} fusion(f32[768,4096]{1,0:T(8,128)} %get-tuple-element.90, f32[768,4096]{1,0:T(8,128)} %get-tuple-element.123, bf16[1,1024,4096]{2,1,0:T(8,128)(2,1)} %copy-done.3, bf16[384,1024]{1,0:T(8,128)(2,1)} %get-tuple-element.96, bf16[384,1024]{1,0:T(8,128)(2,1)} %get-tuple-element.95), kind=kOutput, calls=%fused_computation.2 | convolution fusion | flops 6489636864 | bytes 41418752 | tf_op jit(solution)/shard_map/dot_general | solution.py:416
  370.5 12.9 %multiply_reduce_fusion = (f32[1024]{0:T(1024)S(1)}, f32[768]{0:T(1024)S(1)}, f32[768]{0:T(1024)S(1)}, f32[1024]{0:T(1024)S(1)}, f32[768,1024]{1,0:T(8,128)S(1)}) fusion(f32[768,1024]{1,0:T(8,128)} %copy-done.52, f32[768]{0:T(1024)S(1)} %add_rsqrt_fusion, f32[768]{0:T(1024)S(1)} %broadcast_multiply_fusion.4, f32[1024]{0:T(1024)S(1)} %bitcast.269, ...), kind=kOutput, calls=%fused_computation.49 | convolution fusion | flops 6449524736 | bytes 20996096 | tf_op jit(solution)/shard_map/dot_general | solution.py:133
  391.4 10.4 %add_convert_fusion.2 = bf16[768,1024]{1,0:T(8,128)(2,1)} fusion(f32[768,1024]{1,0:T(8,128)} %copy-done.52, bf16[768,4096]{1,0:T(8,128)(2,1)} %get-tuple-element.89, bf16[1,1024,4096]{2,1,0:T(8,128)(2,1)S(1)} %bitcast.228), kind=kOutput, calls=%fused_computation.53 | convolution fusion | flops 6444023808 | bytes 19398656 | tf_op jit(solution)/shard_map/dot_general | solution.py:133
  401.9 68.5 %attend_back.1 = (bf16[768,1024]{1,0:T(8,128)(2,1)S(1)}, bf16[2,1536,1024]{2,1,0:T(8,128)(2,1)}) custom-call(bf16[1,768,1024]{2,1,0:T(8,128)(2,1)S(1)} %copy-done.43, bf16[2,1536,1024]{2,1,0:T(8,128)(2,1)} %pad_maximum_fusion.k_ref.v_ref, bf16[2,1536,1024]{2,1,0:T(8,128)(2,1)} %pad_maximum_fusion.k_ref.v_ref, f32[1536,1]{1,0:T(8,128)S(1)} %copy-done.13, ...), custom_call_target="tpu_custom_call" | custom-call | flops 48318382080 | bytes 25165824 | tf_op jit(solution)/shard_map/attend_back/pallas_call | solution.py:248
  476.3 12.3 %convert_bitcast_fusion.1.in_ref = bf16[1,1024,4096]{2,1,0:T(8,128)(2,1)} fusion(bf16[768,4096]{1,0:T(8,128)(2,1)} %add_convert_fusion, f32[768,1024]{1,0:T(8,128)S(1)} %copy-done.54, f32[1024]{0:T(1024)S(1)} %bitcast.283, f32[1024]{0:T(1024)S(1)} %bitcast.271, f32[768]{0:T(1024)S(1)} %add_rsqrt_fusion, f32[768]{0:T(1024)S(1)} %broadcast_multiply_fusion.4), kind=kOutput, calls=%fused_computation.26 | convolution fusion | flops 6450577408 | bytes 17840128 | tf_op jit(solution)/shard_map/dot_general | solution.py:141
  491.9 10.0 %convert_bitcast_fusion.in_ref = bf16[1,1024,4096]{2,1,0:T(8,128)(2,1)S(1)} fusion(bf16[768,4096]{1,0:T(8,128)(2,1)} %get-tuple-element.89, bf16[384,1024]{1,0:T(8,128)(2,1)S(1)} %copy-done.60, bf16[384,1024]{1,0:T(8,128)(2,1)S(1)} %copy-done.58), kind=kOutput, calls=%fused_computation.25 | convolution fusion | flops 6449790976 | bytes 16252928 | tf_op jit(solution)/shard_map/dot_general | solution.py:141
  518.6 12.8 %collective-permute-start.99 = (f32[2,1024]{1,0:T(2,128)S(1)}, f32[2,1024]{1,0:T(2,128)S(1)}, u32[]{:S(2)}, u32[]{:S(2)}) collective-permute-start(f32[2,1024]{1,0:T(2,128)S(1)} %add.410), channel_id=1, source_target_pairs={{0,1},{1,0},{2,3},{3,2},{4,5},{5,4},{6,7},{7,6},{8,9},{9,8},{10,11... | collective-permute-start | bytes 24584 | tf_op jit(solution)/shard_map/ppermute | solution.py:455
  564.8 13.9 %collective-permute-done.76 = bf16[4,1,128,1024]{3,2,1,0:T(8,128)(2,1)S(1)} collective-permute-done((bf16[4,1,128,1024]{3,2,1,0:T(8,128)(2,1)S(1)}, bf16[4,1,128,1024]{3,2,1,0:T(8,128)(2,1)S(1)}, u32[]{:S(2)}, u32[]{:S(2)}) %collective-permute-start.76) | collective-permute-done | bytes 1048608 | tf_op jit(solution)/shard_map/ppermute | solution.py:28
  594.3 4.4 fusion.29
  609.1 21.3 %collective-permute-done.77 = bf16[4,1,128,1024]{3,2,1,0:T(8,128)(2,1)} collective-permute-done((bf16[4,1,128,1024]{3,2,1,0:T(8,128)(2,1)}, bf16[4,1,128,1024]{3,2,1,0:T(8,128)(2,1)}, u32[]{:S(2)}, u32[]{:S(2)}) %collective-permute-start.77) | collective-permute-done | bytes 1048608 | tf_op jit(solution)/shard_map/ppermute | solution.py:28
  665.4 4.5 collective-permute-done.79
  683.8 4.9 collective-permute-done.90
  692.4 5.5 collective-permute-start.68
  698.0 7.6 collective-permute-done.45
  705.5 48.0 %collective-permute-done.50 = bf16[384,1024]{1,0:T(8,128)(2,1)S(1)} collective-permute-done((bf16[384,1024]{1,0:T(8,128)(2,1)S(1)}, bf16[384,1024]{1,0:T(8,128)(2,1)S(1)}, u32[]{:S(2)}, u32[]{:S(2)}) %collective-permute-start.50) | collective-permute-done | bytes 786464 | tf_op jit(solution)/shard_map/ppermute | solution.py:348
  (488 shorter events, 254.3 us)
Async XLA Ops:
  30.1 26.1 %collective-permute-start.35 = (bf16[1,128,1024]{2,1,0:T(8,128)(2,1)S(1)}, bf16[1,128,1024]{2,1,0:T(8,128)(2,1)S(1)}, u32[]{:S(2)}, u32[]{:S(2)}) collective-permute-start(bf16[1,128,1024]{2,1,0:T(8,128)(2,1)S(1)} %collective-permute-done.34), channel_id=1, source_target_pairs={{0,1},{1,2},{2,3},{3,0},{4,5},{5,6},{6,7},{7,4},{8,9},{9,10},{10,1... | collective-permute-start | bytes 786440 | tf_op jit(solution)/shard_map/ppermute | solution.py:32
  31.7 27.7 %collective-permute-start.26 = (bf16[1,128,1024]{2,1,0:T(8,128)(2,1)S(1)}, bf16[1,128,1024]{2,1,0:T(8,128)(2,1)S(1)}, u32[]{:S(2)}, u32[]{:S(2)}) collective-permute-start(bf16[1,128,1024]{2,1,0:T(8,128)(2,1)S(1)} %collective-permute-done.25), channel_id=1, source_target_pairs={{0,1},{1,2},{2,3},{3,0},{4,5},{5,6},{6,7},{7,4},{8,9},{9,10},{10,1... | collective-permute-start | bytes 786440 | tf_op jit(solution)/shard_map/ppermute | solution.py:32
  38.7 71.8 %collective-permute-start = (bf16[384,1024]{1,0:T(8,128)(2,1)S(1)}, bf16[384,1024]{1,0:T(8,128)(2,1)S(1)}, u32[]{:S(2)}, u32[]{:S(2)}) collective-permute-start(bf16[384,1024]{1,0:T(8,128)(2,1)S(1)} %get-tuple-element.106), channel_id=1, source_target_pairs={{0,0},{1,2},{2,4},{3,6},{4,1},{5,3},{6,5},{7,7},{8,8},{9,10},{10,1... | collective-permute-start | bytes 2359304 | tf_op jit(solution)/shard_map/ppermute | solution.py:330
  52.7 57.9 %collective-permute-start.1 = (bf16[384,1024]{1,0:T(8,128)(2,1)S(1)}, bf16[384,1024]{1,0:T(8,128)(2,1)S(1)}, u32[]{:S(2)}, u32[]{:S(2)}) collective-permute-start(bf16[384,1024]{1,0:T(8,128)(2,1)S(1)} %get-tuple-element.105), channel_id=1, source_target_pairs={{0,2},{1,0},{2,6},{3,4},{4,3},{5,1},{6,7},{7,5},{8,10},{9,8},{10,1... | collective-permute-start | bytes 2359304 | tf_op jit(solution)/shard_map/ppermute | solution.py:330
  55.5 56.7 %collective-permute-start.46 = (bf16[384,1024]{1,0:T(8,128)(2,1)S(1)}, bf16[384,1024]{1,0:T(8,128)(2,1)S(1)}, u32[]{:S(2)}, u32[]{:S(2)}) collective-permute-start(bf16[384,1024]{1,0:T(8,128)(2,1)S(1)} %get-tuple-element.98), channel_id=1, source_target_pairs={{0,0},{1,2},{2,4},{3,6},{4,1},{5,3},{6,5},{7,7},{8,8},{9,10},{10,1... | collective-permute-start | bytes 2359304 | tf_op jit(solution)/shard_map/ppermute | solution.py:330
  56.2 56.9 %collective-permute-start.47 = (bf16[384,1024]{1,0:T(8,128)(2,1)S(1)}, bf16[384,1024]{1,0:T(8,128)(2,1)S(1)}, u32[]{:S(2)}, u32[]{:S(2)}) collective-permute-start(bf16[384,1024]{1,0:T(8,128)(2,1)S(1)} %get-tuple-element.97), channel_id=1, source_target_pairs={{0,2},{1,0},{2,6},{3,4},{4,3},{5,1},{6,7},{7,5},{8,10},{9,8},{10,1... | collective-permute-start | bytes 2359304 | tf_op jit(solution)/shard_map/ppermute | solution.py:330
  59.4 49.7 %collective-permute-start.36 = (bf16[1,128,1024]{2,1,0:T(8,128)(2,1)S(1)}, bf16[1,128,1024]{2,1,0:T(8,128)(2,1)S(1)}, u32[]{:S(2)}, u32[]{:S(2)}) collective-permute-start(bf16[1,128,1024]{2,1,0:T(8,128)(2,1)S(1)} %collective-permute-done.35), channel_id=1, source_target_pairs={{0,1},{1,2},{2,3},{3,0},{4,5},{5,6},{6,7},{7,4},{8,9},{9,10},{10,1... | collective-permute-start | bytes 786440 | tf_op jit(solution)/shard_map/ppermute | solution.py:32
  113.1 27.9 %collective-permute-start.8 = (bf16[4,2,128,256]{3,2,1,0:T(8,128)(2,1)S(1)}, bf16[4,2,128,256]{3,2,1,0:T(8,128)(2,1)S(1)}, u32[]{:S(2)}, u32[]{:S(2)}) collective-permute-start(bf16[4,2,128,256]{3,2,1,0:T(8,128)(2,1)S(1)} %pad_maximum_fusion.6.refs_0_), channel_id=1, source_target_pairs={{0,16},{4,20},{8,24},{12,28},{16,0},{20,4},{24,8},{28,12},{1,17},{... | collective-permute-start | bytes 1572872 | tf_op jit(solution)/shard_map/ppermute | solution.py:28
  121.6 32.4 %collective-permute-start.15 = (bf16[4,2,128,256]{3,2,1,0:T(8,128)(2,1)S(1)}, bf16[4,2,128,256]{3,2,1,0:T(8,128)(2,1)}, u32[]{:S(2)}, u32[]{:S(2)}) collective-permute-start(bf16[4,2,128,256]{3,2,1,0:T(8,128)(2,1)S(1)} %pad_maximum_fusion.7.refs_0_), channel_id=1, source_target_pairs={{0,4},{4,0},{8,12},{12,8},{16,20},{20,16},{24,28},{28,24},{1,5},{5... | collective-permute-start | bytes 1572872 | tf_op jit(solution)/shard_map/ppermute | solution.py:28
  141.0 28.0 %collective-permute-start.28 = (bf16[4,1,128,1024]{3,2,1,0:T(8,128)(2,1)S(1)}, bf16[4,1,128,1024]{3,2,1,0:T(8,128)(2,1)}, u32[]{:S(2)}, u32[]{:S(2)}) collective-permute-start(bf16[4,1,128,1024]{3,2,1,0:T(8,128)(2,1)S(1)} %pad_maximum_fusion.4.refs_0_), channel_id=1, source_target_pairs={{0,8},{4,12},{8,0},{12,4},{16,24},{20,28},{24,16},{28,20},{1,9},{5... | collective-permute-start | bytes 3145736 | tf_op jit(solution)/shard_map/ppermute | solution.py:28
  158.5 32.9 %collective-permute-start.30 = (bf16[4,1,128,1024]{3,2,1,0:T(8,128)(2,1)S(1)}, bf16[4,1,128,1024]{3,2,1,0:T(8,128)(2,1)}, u32[]{:S(2)}, u32[]{:S(2)}) collective-permute-start(bf16[4,1,128,1024]{3,2,1,0:T(8,128)(2,1)S(1)} %pad_maximum_fusion.4.refs_0_), channel_id=1, source_target_pairs={{0,16},{4,20},{8,24},{12,28},{16,0},{20,4},{24,8},{28,12},{1,17},{... | collective-permute-start | bytes 3145736 | tf_op jit(solution)/shard_map/ppermute | solution.py:28
  160.4 31.0 %collective-permute-start.38 = (bf16[4,1,128,1024]{3,2,1,0:T(8,128)(2,1)S(1)}, bf16[4,1,128,1024]{3,2,1,0:T(8,128)(2,1)}, u32[]{:S(2)}, u32[]{:S(2)}) collective-permute-start(bf16[4,1,128,1024]{3,2,1,0:T(8,128)(2,1)S(1)} %pad_maximum_fusion.5.refs_0_), channel_id=1, source_target_pairs={{0,8},{4,12},{8,0},{12,4},{16,24},{20,28},{24,16},{28,20},{1,9},{5... | collective-permute-start | bytes 3145736 | tf_op jit(solution)/shard_map/ppermute | solution.py:28
  168.8 45.0 %collective-permute-start.40 = (bf16[4,1,128,1024]{3,2,1,0:T(8,128)(2,1)S(1)}, bf16[4,1,128,1024]{3,2,1,0:T(8,128)(2,1)}, u32[]{:S(2)}, u32[]{:S(2)}) collective-permute-start(bf16[4,1,128,1024]{3,2,1,0:T(8,128)(2,1)S(1)} %pad_maximum_fusion.5.refs_0_), channel_id=1, source_target_pairs={{0,16},{4,20},{8,24},{12,28},{16,0},{20,4},{24,8},{28,12},{1,17},{... | collective-permute-start | bytes 3145736 | tf_op jit(solution)/shard_map/ppermute | solution.py:28
  169.0 66.8 %collective-permute-start.32 = (bf16[4,1,128,1024]{3,2,1,0:T(8,128)(2,1)}, bf16[4,1,128,1024]{3,2,1,0:T(8,128)(2,1)}, u32[]{:S(2)}, u32[]{:S(2)}) collective-permute-start(bf16[4,1,128,1024]{3,2,1,0:T(8,128)(2,1)} %collective-permute-done.28.refs_2_), channel_id=1, source_target_pairs={{0,16},{4,20},{8,24},{12,28},{16,0},{20,4},{24,8},{28,12},{1,17},{... | collective-permute-start | bytes 3145736 | tf_op jit(solution)/shard_map/ppermute | solution.py:28
  177.8 86.1 %collective-permute-start.22 = (bf16[2,768,1024]{2,1,0:T(8,128)(2,1)}, bf16[2,768,1024]{2,1,0:T(8,128)(2,1)}, u32[]{:S(2)}, u32[]{:S(2)}) collective-permute-start(bf16[2,768,1024]{2,1,0:T(8,128)(2,1)} %convert_bitcast_fusion.3), channel_id=1, source_target_pairs={{0,4},{4,0},{8,12},{12,8},{16,20},{20,16},{24,28},{28,24},{1,5},{5... | collective-permute-start | bytes 9437192 | tf_op jit(solution)/shard_map/ppermute | solution.py:28
  191.4 45.6 %collective-permute-start.29 = (bf16[4,1,128,1024]{3,2,1,0:T(8,128)(2,1)}, bf16[4,1,128,1024]{3,2,1,0:T(8,128)(2,1)}, u32[]{:S(2)}, u32[]{:S(2)}) collective-permute-start(bf16[4,1,128,1024]{3,2,1,0:T(8,128)(2,1)} %collective-permute-done.28.refs_2_), channel_id=1, source_target_pairs={{0,4},{4,0},{8,12},{12,8},{16,20},{20,16},{24,28},{28,24},{1,5},{5... | collective-permute-start | bytes 3145736 | tf_op jit(solution)/shard_map/ppermute | solution.py:28
  502.0 34.5 %collective-permute-start.51 = (bf16[4,2,128,256]{3,2,1,0:T(8,128)(2,1)}, bf16[4,2,128,256]{3,2,1,0:T(8,128)(2,1)}, u32[]{:S(2)}, u32[]{:S(2)}) collective-permute-start(bf16[4,2,128,256]{3,2,1,0:T(8,128)(2,1)} %get-tuple-element.50), channel_id=1, source_target_pairs={{0,4},{4,0},{8,12},{12,8},{16,20},{20,16},{24,28},{28,24},{1,5},{5... | collective-permute-start | bytes 1572872 | tf_op jit(solution)/shard_map/ppermute | solution.py:28
  508.0 30.9 %collective-permute-start.75 = (bf16[4,1,128,1024]{3,2,1,0:T(8,128)(2,1)}, bf16[4,1,128,1024]{3,2,1,0:T(8,128)(2,1)S(1)}, u32[]{:S(2)}, u32[]{:S(2)}) collective-permute-start(bf16[4,1,128,1024]{3,2,1,0:T(8,128)(2,1)} %get-tuple-element.72), channel_id=1, source_target_pairs={{0,4},{4,0},{8,12},{12,8},{16,20},{20,16},{24,28},{28,24},{1,5},{5... | collective-permute-start | bytes 3145736 | tf_op jit(solution)/shard_map/ppermute | solution.py:28
  536.4 51.6 %collective-permute-start.48 = (bf16[2,768,1024]{2,1,0:T(8,128)(2,1)}, bf16[2,768,1024]{2,1,0:T(8,128)(2,1)S(1)}, u32[]{:S(2)}, u32[]{:S(2)}) collective-permute-start(bf16[2,768,1024]{2,1,0:T(8,128)(2,1)} %slice.123), channel_id=1, source_target_pairs={{0,4},{4,0},{8,12},{12,8},{16,20},{20,16},{24,28},{28,24},{1,5},{5... | collective-permute-start | bytes 9437192 | tf_op jit(solution)/shard_map/ppermute | solution.py:28
  536.5 28.3 %collective-permute-start.74 = (bf16[4,1,128,1024]{3,2,1,0:T(8,128)(2,1)S(1)}, bf16[4,1,128,1024]{3,2,1,0:T(8,128)(2,1)S(1)}, u32[]{:S(2)}, u32[]{:S(2)}) collective-permute-start(bf16[4,1,128,1024]{3,2,1,0:T(8,128)(2,1)S(1)} %copy-done.35), channel_id=1, source_target_pairs={{0,4},{4,0},{8,12},{12,8},{16,20},{20,16},{24,28},{28,24},{1,5},{5... | collective-permute-start | bytes 3145736 | tf_op jit(solution)/shard_map/ppermute | solution.py:28
  564.8 40.1 %collective-permute-start.71 = (bf16[4,1,128,1024]{3,2,1,0:T(8,128)(2,1)S(1)}, bf16[4,1,128,1024]{3,2,1,0:T(8,128)(2,1)}, u32[]{:S(2)}, u32[]{:S(2)}) collective-permute-start(bf16[4,1,128,1024]{3,2,1,0:T(8,128)(2,1)S(1)} %copy-done.33), channel_id=1, source_target_pairs={{0,4},{4,0},{8,12},{12,8},{16,20},{20,16},{24,28},{28,24},{1,5},{5... | collective-permute-start | bytes 3145736 | tf_op jit(solution)/shard_map/ppermute | solution.py:28
  578.7 58.2 %collective-permute-start.81 = (bf16[4,1,128,1024]{3,2,1,0:T(8,128)(2,1)S(1)}, bf16[4,1,128,1024]{3,2,1,0:T(8,128)(2,1)S(1)}, u32[]{:S(2)}, u32[]{:S(2)}) collective-permute-start(bf16[4,1,128,1024]{3,2,1,0:T(8,128)(2,1)S(1)} %get-tuple-element.74), channel_id=1, source_target_pairs={{0,4},{4,0},{8,12},{12,8},{16,20},{20,16},{24,28},{28,24},{1,5},{5... | collective-permute-start | bytes 3145736 | tf_op jit(solution)/shard_map/ppermute | solution.py:28
  580.3 26.1 %collective-permute-start.73 = (bf16[4,1,128,1024]{3,2,1,0:T(8,128)(2,1)S(1)}, bf16[4,1,128,1024]{3,2,1,0:T(8,128)(2,1)}, u32[]{:S(2)}, u32[]{:S(2)}) collective-permute-start(bf16[4,1,128,1024]{3,2,1,0:T(8,128)(2,1)S(1)} %add_convert_fusion.16), channel_id=1, source_target_pairs={{0,16},{4,20},{8,24},{12,28},{16,0},{20,4},{24,8},{28,12},{1,17},{... | collective-permute-start | bytes 3145736 | tf_op jit(solution)/shard_map/ppermute | solution.py:28
  584.9 52.6 %collective-permute-start.83 = (bf16[4,1,128,1024]{3,2,1,0:T(8,128)(2,1)}, bf16[4,1,128,1024]{3,2,1,0:T(8,128)(2,1)}, u32[]{:S(2)}, u32[]{:S(2)}) collective-permute-start(bf16[4,1,128,1024]{3,2,1,0:T(8,128)(2,1)} %add_convert_fusion.9), channel_id=1, source_target_pairs={{0,8},{4,12},{8,0},{12,4},{16,24},{20,28},{24,16},{28,20},{1,9},{5... | collective-permute-start | bytes 3145736 | tf_op jit(solution)/shard_map/ppermute | solution.py:28
  588.0 42.4 %collective-permute-start.77 = (bf16[4,1,128,1024]{3,2,1,0:T(8,128)(2,1)}, bf16[4,1,128,1024]{3,2,1,0:T(8,128)(2,1)}, u32[]{:S(2)}, u32[]{:S(2)}) collective-permute-start(bf16[4,1,128,1024]{3,2,1,0:T(8,128)(2,1)} %add_convert_fusion.12), channel_id=1, source_target_pairs={{0,8},{4,12},{8,0},{12,4},{16,24},{20,28},{24,16},{28,20},{1,9},{5... | collective-permute-start | bytes 3145736 | tf_op jit(solution)/shard_map/ppermute | solution.py:28
  604.9 32.6 %collective-permute-start.87 = (bf16[4,1,128,1024]{3,2,1,0:T(8,128)(2,1)S(1)}, bf16[4,1,128,1024]{3,2,1,0:T(8,128)(2,1)S(1)}, u32[]{:S(2)}, u32[]{:S(2)}) collective-permute-start(bf16[4,1,128,1024]{3,2,1,0:T(8,128)(2,1)S(1)} %copy-done.66), channel_id=1, source_target_pairs={{0,16},{4,20},{8,24},{12,28},{16,0},{20,4},{24,8},{28,12},{1,17},{... | collective-permute-start | bytes 3145736 | tf_op jit(solution)/shard_map/ppermute | solution.py:28
  606.4 40.7 %collective-permute-start.100 = (f32[2,1024]{1,0:T(2,128)S(1)}, f32[2,1024]{1,0:T(2,128)S(1)}, u32[]{:S(2)}, u32[]{:S(2)}) collective-permute-start(f32[2,1024]{1,0:T(2,128)S(1)} %add.411), channel_id=1, source_target_pairs={{0,2},{1,3},{2,0},{3,1},{4,6},{5,7},{6,4},{7,5},{8,10},{9,11},{10,... | collective-permute-start | bytes 24584 | tf_op jit(solution)/shard_map/ppermute | solution.py:455
  636.9 26.5 %collective-permute-start.65 = (bf16[4,2,128,256]{3,2,1,0:T(8,128)(2,1)S(1)}, bf16[4,2,128,256]{3,2,1,0:T(8,128)(2,1)S(1)}, u32[]{:S(2)}, u32[]{:S(2)}) collective-permute-start(bf16[4,2,128,256]{3,2,1,0:T(8,128)(2,1)S(1)} %get-tuple-element.64), channel_id=1, source_target_pairs={{0,4},{4,0},{8,12},{12,8},{16,20},{20,16},{24,28},{28,24},{1,5},{5... | collective-permute-start | bytes 1572872 | tf_op jit(solution)/shard_map/ppermute | solution.py:28
  636.9 40.1 %collective-permute-start.64 = (bf16[4,2,128,256]{3,2,1,0:T(8,128)(2,1)S(1)}, bf16[4,2,128,256]{3,2,1,0:T(8,128)(2,1)S(1)}, u32[]{:S(2)}, u32[]{:S(2)}) collective-permute-start(bf16[4,2,128,256]{3,2,1,0:T(8,128)(2,1)S(1)} %get-tuple-element.62), channel_id=1, source_target_pairs={{0,4},{4,0},{8,12},{12,8},{16,20},{20,16},{24,28},{28,24},{1,5},{5... | collective-permute-start | bytes 1572872 | tf_op jit(solution)/shard_map/ppermute | solution.py:28
  637.5 26.2 %collective-permute-start.62 = (bf16[4,2,128,256]{3,2,1,0:T(8,128)(2,1)S(1)}, bf16[4,2,128,256]{3,2,1,0:T(8,128)(2,1)S(1)}, u32[]{:S(2)}, u32[]{:S(2)}) collective-permute-start(bf16[4,2,128,256]{3,2,1,0:T(8,128)(2,1)S(1)} %get-tuple-element.60), channel_id=1, source_target_pairs={{0,4},{4,0},{8,12},{12,8},{16,20},{20,16},{24,28},{28,24},{1,5},{5... | collective-permute-start | bytes 1572872 | tf_op jit(solution)/shard_map/ppermute | solution.py:28
  689.4 64.1 %collective-permute-start.50 = (bf16[384,1024]{1,0:T(8,128)(2,1)S(1)}, bf16[384,1024]{1,0:T(8,128)(2,1)S(1)}, u32[]{:S(2)}, u32[]{:S(2)}) collective-permute-start(bf16[384,1024]{1,0:T(8,128)(2,1)S(1)} %get-tuple-element.93), channel_id=1, source_target_pairs={{2,0},{0,1},{6,2},{4,3},{3,4},{1,5},{7,6},{5,7},{10,8},{8,9},{14,1... | collective-permute-start | bytes 2359304 | tf_op jit(solution)/shard_map/ppermute | solution.py:348
  692.4 62.2 %collective-permute-start.68 = (bf16[2,128,256]{2,1,0:T(8,128)(2,1)S(1)}, bf16[2,128,256]{2,1,0:T(8,128)(2,1)S(1)}, u32[]{:S(2)}, u32[]{:S(2)}) collective-permute-start(bf16[2,128,256]{2,1,0:T(8,128)(2,1)S(1)} %slice_bitcast_fusion.34), channel_id=1, source_target_pairs={{0,3},{1,0},{2,1},{3,2},{4,7},{5,4},{6,5},{7,6},{8,11},{9,8},{10,9... | collective-permute-start | bytes 393224 | tf_op jit(solution)/shard_map/ppermute | solution.py:32
  (166 other events, 3134.7 us)

commit v2 on v1

v2 whole, which is shorter than its diff:
```python
import functools

import jax
import jax.numpy as jnp
from jax import lax
from jax.experimental import pallas as pl
from jax.experimental.pallas import tpu as pltpu
from jax.sharding import PartitionSpec as P

HDIM = 64
PAIR = 2 * HDIM
VIEW_TOK = 256
TRI = 768
EPSILON = 1e-05
MASKED = -1000000000.0
F32 = jnp.float32
BF16 = jnp.bfloat16
MIB = 1024 * 1024
ANY = pl.BlockSpec(memory_space=pl.ANY)
WHOLE = pl.BlockSpec(memory_space=pltpu.VMEM)
SHAPE = jax.ShapeDtypeStruct


def params(mib=56):
    return pltpu.CompilerParams(vmem_limit_bytes=mib * MIB)


def cost(flops, nbytes):
    return pl.CostEstimate(flops=int(flops), bytes_accessed=int(nbytes), transcendentals=0)


def dot_nt(a, b):
    return lax.dot_general(a, b, (((1,), (1,)), ((), ())), preferred_element_type=F32)


def dot_nn(a, b):
    return lax.dot_general(a, b, (((1,), (0,)), ((), ())), preferred_element_type=F32)


def dot_tn(a, b):
    return lax.dot_general(a, b, (((0,), (0,)), ((), ())), preferred_element_type=F32)


def row_block(rows):
    return 256 if rows % 256 == 0 else 128


def swap(value, bit, nd):
    return lax.ppermute(value, "dp", [(i, i ^ bit) for i in range(nd)])


def ring(value, step, nm):
    return lax.ppermute(value, "mp", [(i, (i + step) % nm) for i in range(nm)])


class Flow:
    def __init__(self, nd, nm):
        self.nd, self.nm = nd, nm
        self.bits = [1 << b for b in range(1, nd.bit_length() - 1)]
        self.queue = {bit: [] for bit in self.bits}
        self.order, self.pieces, self.flying, self.kept = {}, {}, {}, {}

    def add(self, name, value, order):
        self.order[name] = list(order)
        self.pieces[name] = [(0, value)]
        self.next(name)

    def next(self, name):
        if self.order[name]:
            self.queue[self.order[name][0]].append(name)

    def launch(self, chip=1):
        for bit, tasks in self.queue.items():
            for _ in range(chip):
                if tasks:
                    name = tasks.pop(0)
                    values = [value for _, value in self.pieces[name]]
                    value = values[0][None] if len(values) == 1 else jnp.stack(values)
                    self.flying["chip", name] = swap(value, bit, self.nd)

    def fly(self, name, value):
        self.flying["kept", name] = value

    def land(self, *extra):
        names, flying, kept = list(self.pieces), list(self.flying), list(self.kept)
        values = lax.optimization_barrier(
            (
                [self.pieces[name] for name in names],
                [self.flying[key] for key in flying],
                [self.kept[key] for key in kept],
                extra,
            )
        )
        for name, pieces in zip(names, values[0]):
            self.pieces[name] = [(j, v) for (j, _), (_, v) in zip(self.pieces[name], pieces)]
        self.kept = dict(zip(kept, values[2]))
        self.flying = {}
        for (kind, name), value in zip(flying, values[1]):
            if kind == "kept":
                self.kept[name] = value
                continue
            bit = self.order[name].pop(0)
            held = self.pieces[name]
            self.pieces[name] = held + [(j | bit, value[n]) for n, (j, _) in enumerate(held)]
            self.next(name)
        extra = values[3]
        return extra[0] if len(extra) == 1 else extra

    def whole(self, name):
        return name in self.pieces and not self.order[name]

    def take_half(self, name):
        pieces = dict(self.pieces.pop(name))
        return jnp.stack([pieces[2 * i] for i in range(self.nd // 2)])


def pack_kernel(index_ref, in_ref, out_ref):
    nd = index_ref.shape[0] - 1
    wide = in_ref.shape[2] // nd
    for p in range(nd):
        there = pl.ds(pl.multiple_of(index_ref[p] * wide, wide), wide)
        out_ref[:, p * wide : (p + 1) * wide] = in_ref[index_ref[nd], :, there]


def pack_features(value, index, which):
    micro, rows, width = value.shape
    nd = index.shape[0]
    if width // nd % 128:
        chunk = lax.dynamic_index_in_dim(value, which, 0, keepdims=False)
        return jnp.take(chunk.reshape(rows, nd, -1), index, axis=1).reshape(rows, width)
    return pl.pallas_call(
        pack_kernel,
        in_specs=[pl.BlockSpec(memory_space=pltpu.SMEM), WHOLE],
        out_specs=WHOLE,
        out_shape=SHAPE((rows, width), value.dtype),
        compiler_params=params(),
        cost_estimate=cost(0, 6 * rows * width),
        name="pack_features",
    )(jnp.append(index, which.astype(jnp.int32)), value)


def unpack_kernel(index_ref, *refs):
    ins, out_ref = refs[:-1], refs[-1]
    nd = index_ref.shape[0] - len(ins)
    wide = out_ref.shape[2] // nd
    for k, in_ref in enumerate(ins):
        for p in range(nd):
            there = pl.ds(pl.multiple_of(index_ref[p] * wide, wide), wide)
            out_ref[index_ref[nd + k], :, there] = in_ref[:, p * wide : (p + 1) * wide]


def unpack_features(chunks, index, places):
    rows, width = chunks[0].shape
    micro, nd = len(chunks), index.shape[0]
    places = [place.astype(jnp.int32) for place in places]
    if width // nd % 128:
        back = jnp.argsort(index)
        stacked = jnp.stack(chunks).reshape(micro, rows, nd, -1)
        stacked = jnp.take(stacked, back, axis=2).reshape(micro, rows, width)
        return jnp.take(stacked, jnp.argsort(jnp.stack(places)), axis=0)
    return pl.pallas_call(
        unpack_kernel,
        in_specs=[pl.BlockSpec(memory_space=pltpu.SMEM)] + [WHOLE] * micro,
        out_specs=WHOLE,
        out_shape=SHAPE((micro, rows, width), chunks[0].dtype),
        compiler_params=params(),
        cost_estimate=cost(0, 4 * micro * rows * width),
        name="unpack_features",
    )(jnp.concatenate([index, jnp.stack(places)]), *chunks)


def standardize(state):
    centre = jnp.mean(state, axis=-1, keepdims=True)
    centred = state - centre
    spread = jnp.mean(centred * centred, axis=-1, keepdims=True)
    inverse = lax.rsqrt(spread + EPSILON)
    return centred * inverse, inverse


def norm_back(grad, state, gain):
    scaled, inverse = standardize(state)
    weighted = grad * gain
    first = jnp.mean(weighted, axis=-1, keepdims=True)
    second = jnp.mean(weighted * scaled, axis=-1, keepdims=True)
    sums = jnp.concatenate(
        [jnp.sum(grad * scaled, axis=0, keepdims=True), jnp.sum(grad, axis=0, keepdims=True)], 0
    )
    return inverse * (weighted - first - scaled * second), sums


def first_norm_kernel(micro, *refs):
    chunks = refs[:micro]
    gain_ref, bias_ref, x_ref, out_ref, flip_ref = refs[micro:]
    rows = chunks[0].shape[0]
    for k, ref in enumerate(chunks):
        here = slice(k * rows, (k + 1) * rows)
        x_ref[here] = ref[...]
        scaled, _ = standardize(ref[...].astype(F32))
        normed = (scaled * gain_ref[...] + bias_ref[...]).astype(BF16)
        out_ref[here] = normed
        flip_ref[:, here] = normed.T


def first_norm(chunks, gain, bias):
    rows, width = chunks[0].shape
    rows = rows * len(chunks)
    return pl.pallas_call(
        functools.partial(first_norm_kernel, len(chunks)),
        in_specs=[WHOLE] * (len(chunks) + 2),
        out_specs=[WHOLE] * 3,
        out_shape=[SHAPE((rows, width), BF16)] * 2 + [SHAPE((width, rows), BF16)],
        compiler_params=params(),
        cost_estimate=cost(0, 10 * rows * width),
        name="first_norm",
    )(*chunks, gain, bias)


def flip_kernel(*refs):
    chunks, out_ref, flip_ref = refs[:-2], refs[-2], refs[-1]
    rows = chunks[0].shape[0]
    for k, ref in enumerate(chunks):
        here = slice(k * rows, (k + 1) * rows)
        out_ref[here] = ref[...]
        flip_ref[:, here] = ref[...].T


def flip(chunks):
    rows, width = chunks[0].shape
    rows = rows * len(chunks)
    return pl.pallas_call(
        flip_kernel,
        in_specs=[WHOLE] * len(chunks),
        out_specs=[WHOLE] * 2,
        out_shape=[SHAPE((rows, width), BF16), SHAPE((width, rows), BF16)],
        compiler_params=params(),
        cost_estimate=cost(0, 6 * rows * width),
        name="flip",
    )(*chunks)


def proj_kernel(in_ref, own_ref, other_ref, out_ref):
    value = in_ref[...]
    half = value.shape[1] // 2
    wide = own_ref.shape[-1]
    for k in range(own_ref.shape[1]):
        first = own_ref[:, k, 0].reshape(half, wide)
        second = other_ref[:, k, 0].reshape(half, wide)
        total = dot_nn(value[:, :half], first) + dot_nn(value[:, half:], second)
        out_ref[0, :, k * wide : (k + 1) * wide] = total.astype(BF16)


def project(value, own, other, start, count):
    rows, width = value.shape
    chips, nm, _, deep, wide = own.shape
    spec = pl.BlockSpec((chips, nm, 1, deep, wide), lambda i: (0, 0, start + i, 0, 0))
    return pl.pallas_call(
        proj_kernel,
        grid=(count,),
        in_specs=[pl.BlockSpec((rows, width), lambda i: (0, 0)), spec, spec],
        out_specs=pl.BlockSpec((1, rows, nm * wide), lambda i: (i, 0, 0)),
        out_shape=SHAPE((count, rows, nm * wide), BF16),
        compiler_params=params(),
        cost_estimate=cost(2 * count * rows * width * nm * wide, 2 * count * rows * width),
        name="project",
    )(value, own, other)


def attend_kernel(parts, q_ref, *refs):
    k_refs, v_refs = refs[:parts], refs[parts : 2 * parts]
    bias_ref, out_ref, lse_ref = refs[2 * parts :]
    rows = q_ref.shape[1]
    low = lax.broadcasted_iota(jnp.int32, (1, PAIR), 1) < HDIM
    query = q_ref[0] * jnp.asarray(HDIM ** (-0.5), BF16)
    mixed = None
    for head in range(2):
        mine = low if head == 0 else jnp.logical_not(low)
        q_mine = jnp.where(mine, query, jnp.zeros_like(query))
        scores = [
            jnp.where(bias_ref[p : p + 1, :] < 0.0, MASKED, dot_nt(q_mine, k_refs[p][0]))
            for p in range(parts)
        ]
        top = functools.reduce(
            jnp.maximum, [jnp.max(part, axis=1, keepdims=True) for part in scores]
        )
        total, part = 0.0, 0.0
        for p in range(parts):
            expo = jnp.exp(scores[p] - top)
            total = total + jnp.sum(expo, axis=1, keepdims=True)
            part = part + dot_nn(expo.astype(BF16), v_refs[p][0])
        part = part / total
        mixed = part if head == 0 else jnp.where(low, mixed, part)
        lse = top + jnp.log(total)
        lse_ref[0, head : head + 1, :] = jnp.transpose(jnp.broadcast_to(lse, (rows, 128)))[0:1, :]
    out_ref[...] = mixed.astype(BF16)


def attend(query, kvs, bias, start, count):
    _, rows, width = query.shape
    parts = len(kvs)
    block = row_block(rows)
    keys = rows * parts
    key_spec = pl.BlockSpec((1, rows, PAIR), lambda h, i: (0, 0, start + h))
    value_spec = pl.BlockSpec((1, rows, PAIR), lambda h, i: (1, 0, start + h))
    return pl.pallas_call(
        functools.partial(attend_kernel, parts),
        grid=(count, rows // block),
        in_specs=[pl.BlockSpec((1, block, PAIR), lambda h, i: (0, i, start + h))]
        + [key_spec] * parts
        + [value_spec] * parts
        + [pl.BlockSpec((parts, rows), lambda h, i: (0, 0))],
        out_specs=[
            pl.BlockSpec((block, PAIR), lambda h, i: (i, h)),
            pl.BlockSpec((1, 2, block), lambda h, i: (h, 0, i)),
        ],
        out_shape=[SHAPE((rows, count * PAIR), BF16), SHAPE((count, 2, rows), F32)],
        compiler_params=params(),
        cost_estimate=cost(16 * rows * keys * count * PAIR, 8 * keys * count * PAIR),
        name="attend",
    )(query, *kvs, *kvs, bias)


def attend_back_kernel(parts, q_ref, *refs):
    k_refs, v_refs = refs[:parts], refs[parts : 2 * parts]
    bias_ref, lse_ref, mixed_ref, grad_ref, dq_ref = refs[2 * parts : 2 * parts + 5]
    dkv_refs = refs[2 * parts + 5 : 3 * parts + 5]
    dk_acc, dv_acc = refs[3 * parts + 5 :]
    step = pl.program_id(1)
    low = lax.broadcasted_iota(jnp.int32, (1, PAIR), 1) < HDIM
    query = q_ref[0] * jnp.asarray(HDIM ** (-0.5), BF16)
    grad = grad_ref[0]
    product = mixed_ref[...].astype(F32) * grad.astype(F32)

    @pl.when(step == 0)
    def _():
        dk_acc[...] = jnp.zeros_like(dk_acc)
        dv_acc[...] = jnp.zeros_like(dv_acc)

    grad_query = None
    for head in range(2):
        mine = low if head == 0 else jnp.logical_not(low)
        q_mine = jnp.where(mine, query, jnp.zeros_like(query))
        g_mine = jnp.where(mine, grad, jnp.zeros_like(grad))
        delta = jnp.sum(jnp.where(mine, product, 0.0), axis=1, keepdims=True)
        delta = jnp.transpose(jnp.broadcast_to(delta, (delta.shape[0], 128)))[0:1, :]
        query_part = 0.0
        for p in range(parts):
            keys, values = k_refs[p][0], v_refs[p][0]
            scores = jnp.where(bias_ref[p] < 0.0, MASKED, dot_nt(keys, q_mine))
            probs = jnp.exp(scores - lse_ref[0, head : head + 1, :])
            upstream = dot_nt(values, g_mine)
            grad_scores = (probs * (upstream - delta)).astype(BF16)
            dv_acc[p] += dot_nn(probs.astype(BF16), g_mine)
            dk_acc[p] += dot_nn(grad_scores, q_mine)
            query_part = query_part + dot_tn(grad_scores, keys)
        grad_query = query_part if head == 0 else jnp.where(low, grad_query, query_part)
    dq_ref[...] = (grad_query * HDIM ** (-0.5)).astype(BF16)

    @pl.when(step == pl.num_programs(1) - 1)
    def _():
        for p in range(parts):
            dkv_refs[p][0] = dk_acc[p].astype(BF16)
            dkv_refs[p][1] = dv_acc[p].astype(BF16)


def attend_back(query, kvs, bias, lse, mixed, grad, start, count):
    _, rows, width = query.shape
    parts = len(kvs)
    block = row_block(rows)
    keys = rows * parts
    key_spec = pl.BlockSpec((1, rows, PAIR), lambda h, i: (0, 0, start + h))
    value_spec = pl.BlockSpec((1, rows, PAIR), lambda h, i: (1, 0, start + h))
    return pl.pallas_call(
        functools.partial(attend_back_kernel, parts),
        grid=(count, rows // block),
        in_specs=[pl.BlockSpec((1, block, PAIR), lambda h, i: (0, i, start + h))]
        + [key_spec] * parts
        + [value_spec] * parts
        + [
            pl.BlockSpec((parts, rows, 1), lambda h, i: (0, 0, 0)),
            pl.BlockSpec((1, 2, block), lambda h, i: (h, 0, i)),
            pl.BlockSpec((block, PAIR), lambda h, i: (i, h)),
            pl.BlockSpec((1, block, PAIR), lambda h, i: (0, i, start + h)),
        ],
        out_specs=[pl.BlockSpec((block, PAIR), lambda h, i: (i, h))]
        + [pl.BlockSpec((2, rows, PAIR), lambda h, i: (0, 0, h))] * parts,
        out_shape=[SHAPE((rows, count * PAIR), BF16)]
        + [SHAPE((2, rows, count * PAIR), BF16)] * parts,
        scratch_shapes=[pltpu.VMEM((parts, rows, PAIR), F32)] * 2,
        compiler_params=params(),
        cost_estimate=cost(40 * rows * keys * count * PAIR, 16 * keys * count * PAIR),
        name="attend_back",
    )(query, *kvs, *kvs, bias, lse, mixed, grad)


def middle_kernel(nm, x_ref, *refs):
    mixed_refs = refs[:nm]
    own_ref, other_ref, gain_ref, bias_ref, mid_ref, out_ref, flip_ref = refs[nm:]
    half = x_ref.shape[1] // 2
    wide = own_ref.shape[-1]
    sides = []
    for ref in (own_ref, other_ref):
        total = 0.0
        for k in range(nm):
            total = total + dot_nt(mixed_refs[k][...], ref[:, k, 0].reshape(half, wide))
        sides.append(total)
    middle = x_ref[...].astype(F32) + jnp.concatenate(sides, axis=1)
    mid_ref[...] = middle
    scaled, _ = standardize(middle)
    normed = (scaled * gain_ref[...] + bias_ref[...]).astype(BF16)
    out_ref[...] = normed
    flip_ref[...] = normed.T


def middle_norm(x, mixed, own, other, which, gain, bias):
    rows, width = x.shape
    chips, nm, _, deep, wide = own.shape
    block = row_block(rows)
    vector = pl.BlockSpec((1, width), lambda i: (0, 0))
    spec = pl.BlockSpec((chips, nm, 1, deep, wide), lambda i: (0, 0, which, 0, 0))
    line = pl.BlockSpec((block, width), lambda i: (i, 0))
    return pl.pallas_call(
        functools.partial(middle_kernel, nm),
        grid=(rows // block,),
        in_specs=[line]
        + [pl.BlockSpec((block, wide), lambda i: (i, 0))] * nm
        + [spec, spec, vector, vector],
        out_specs=[line, line, pl.BlockSpec((width, block), lambda i: (0, i))],
        out_shape=[
            SHAPE((rows, width), F32),
            SHAPE((rows, width), BF16),
            SHAPE((width, rows), BF16),
        ],
        compiler_params=params(),
        cost_estimate=cost(2 * rows * width * nm * wide, 14 * x.size),
        name="middle_norm",
    )(x, *mixed, own, other, gain, bias)


def load_weights(sizes, refs, held, sems):
    step = pl.program_id(0)
    nm = sum(sizes)
    copies, k, refs = {}, 0, list(refs)
    for size in sizes:
        sides = [refs.pop(0) for _ in range(4)]
        for i in range(size):
            for n, ref in enumerate(sides):
                w, side = n // 2, n % 2
                copies[w, 2 * k + side] = pltpu.make_async_copy(
                    ref.at[:, i], held.at[w, 2 * k + side], sems.at[w, 2 * k + side]
                )
            k += 1

    @pl.when(step == 0)
    def _():
        for copy in copies.values():
            copy.start()

    for k in range(nm):

        @pl.when(step == k)
        def _():
            for w in range(2):
                for side in range(2):
                    copies[w, 2 * k + side].wait()


def feed_kernel(sizes, *refs):
    nm, count = sum(sizes), 4 * len(sizes)
    in_ref, mid_ref, out_ref, act_ref, slope_ref, held, acc, sems = refs[count:]
    step = pl.program_id(0)
    load_weights(sizes, refs[:count], held, sems)
    half = in_ref.shape[1] // 2
    up = [held[0, 2 * step + side].reshape(half, -1) for side in range(2)]
    down = [held[1, 2 * step + side].reshape(half, -1) for side in range(2)]

    @pl.when(step == 0)
    def _():
        acc[...] = mid_ref[...]

    hidden = dot_nn(in_ref[:, :half], up[0]) + dot_nn(in_ref[:, half:], up[1])
    below = 0.5 + 0.5 * lax.erf(hidden * (0.5**0.5))
    density = jnp.exp(-0.5 * hidden * hidden) * 0.3989422804014327
    active = (hidden * below).astype(BF16)
    act_ref[0] = active
    slope_ref[0] = (below + hidden * density).astype(BF16)
    acc[:, :half] += dot_nt(active, down[0])
    acc[:, half:] += dot_nt(active, down[1])

    @pl.when(step == nm - 1)
    def _():
        out_ref[...] = acc[...].astype(BF16)


def feed(normed, middle, sizes, weights):
    rows, width = normed.shape
    nm = sum(sizes)
    chips, _, deep, hidden = weights[0].shape
    line = pl.BlockSpec((rows, width), lambda k: (0, 0))
    wide = pl.BlockSpec((1, rows, hidden), lambda k: (k, 0, 0))
    return pl.pallas_call(
        functools.partial(feed_kernel, sizes),
        grid=(nm,),
        in_specs=[ANY] * len(weights) + [line, line],
        out_specs=[line, wide, wide],
        out_shape=[SHAPE((rows, width), BF16)] + [SHAPE((nm, rows, hidden), BF16)] * 2,
        scratch_shapes=[
            pltpu.VMEM((2, 2 * nm, chips, deep, hidden), BF16),
            pltpu.VMEM((rows, width), F32),
            pltpu.SemaphoreType.DMA((2, 2 * nm)),
        ],
        compiler_params=params(60),
        cost_estimate=cost(4 * rows * width * nm * hidden, 4 * nm * width * hidden),
        name="feed",
    )(*weights, normed, middle)


def feed_back_kernel(sizes, *refs):
    nm, count = sum(sizes), 4 * len(sizes)
    g_ref, slope_ref, mid_ref, gain_ref = refs[count : count + 4]
    hid_ref, gmid_ref, attn_ref, flip_ref, sums_ref, held, acc, sems = refs[count + 4 :]
    step = pl.program_id(0)
    load_weights(sizes, refs[:count], held, sems)
    half = g_ref.shape[1] // 2
    up = [held[0, 2 * step + side].reshape(half, -1) for side in range(2)]
    down = [held[1, 2 * step + side].reshape(half, -1) for side in range(2)]
    active = dot_nn(g_ref[:, :half], down[0]) + dot_nn(g_ref[:, half:], down[1])
    hidden = (active * slope_ref[0].astype(F32)).astype(BF16)
    hid_ref[0] = hidden
    first, second = dot_nt(hidden, up[0]), dot_nt(hidden, up[1])

    @pl.when(step == 0)
    def _():
        acc[:, :half] = first
        acc[:, half:] = second

    @pl.when(step > 0)
    def _():
        acc[:, :half] += first
        acc[:, half:] += second

    @pl.when(step == nm - 1)
    def _():
        into, sums = norm_back(acc[...], mid_ref[...], gain_ref[...])
        result = g_ref[...].astype(F32) + into
        gmid_ref[...] = result
        attn = result.astype(BF16)
        attn_ref[...] = attn
        flip_ref[...] = attn.T
        sums_ref[...] = sums


def feed_back(grad, slope, middle, gain, sizes, weights):
    rows, width = grad.shape
    nm = sum(sizes)
    chips, _, deep, hidden = weights[0].shape
    line = pl.BlockSpec((rows, width), lambda k: (0, 0))
    wide = pl.BlockSpec((1, rows, hidden), lambda k: (k, 0, 0))
    return pl.pallas_call(
        functools.partial(feed_back_kernel, sizes),
        grid=(nm,),
        in_specs=[ANY] * len(weights)
        + [line, wide, line, pl.BlockSpec((1, width), lambda k: (0, 0))],
        out_specs=[
            wide,
            line,
            line,
            pl.BlockSpec((width, rows), lambda k: (0, 0)),
            pl.BlockSpec((2, width), lambda k: (0, 0)),
        ],
        out_shape=[
            SHAPE((nm, rows, hidden), BF16),
            SHAPE((rows, width), F32),
            SHAPE((rows, width), BF16),
            SHAPE((width, rows), BF16),
            SHAPE((2, width), F32),
        ],
        scratch_shapes=[
            pltpu.VMEM((2, 2 * nm, chips, deep, hidden), BF16),
            pltpu.VMEM((rows, width), F32),
            pltpu.SemaphoreType.DMA((2, 2 * nm)),
        ],
        compiler_params=params(60),
        cost_estimate=cost(4 * rows * width * nm * hidden, 4 * nm * width * hidden),
        name="feed_back",
    )(*weights, grad, slope, middle, gain)


def wide_grad_kernel(a_ref, b_ref, keep_ref, give_ref):
    half = a_ref.shape[0] // 2
    value = b_ref[0]
    keep_ref[0] = dot_nn(a_ref[:half], value).astype(BF16)
    give_ref[0] = dot_nn(a_ref[half:], value).astype(BF16)


def wide_grad(flipped, values, first, count, chips):
    width, rows = flipped.shape
    hidden = values.shape[2]
    block = min(512, hidden)
    piece = SHAPE((count, width // 2, hidden), BF16)
    out = pl.BlockSpec((1, width // 2, block), lambda k, i: (k, 0, i))
    keep, give = pl.pallas_call(
        wide_grad_kernel,
        grid=(count, hidden // block),
        in_specs=[
            pl.BlockSpec((width, rows), lambda k, i: (0, 0)),
            pl.BlockSpec((1, rows, block), lambda k, i: (first + k, 0, i)),
        ],
        out_specs=[out, out],
        out_shape=[piece, piece],
        compiler_params=params(),
        cost_estimate=cost(2 * count * width * rows * hidden, 4 * count * width * hidden),
        name="wide_grad",
    )(flipped, values)
    shape = (count, chips, width // 2 // chips, hidden)
    return keep.reshape(shape), give.reshape(shape)


def head_grad_kernel(count, *refs):
    n_ref, g_ref = refs[:2]
    mixeds, dqs, dkvs, cames = (refs[2 + i * count : 2 + (i + 1) * count] for i in range(4))
    sums = refs[2 + 4 * count : 2 + 5 * count]
    ka_ref, ga_ref, kb_ref, gb_ref = refs[2 + 5 * count :]
    half = n_ref.shape[0] // 2
    for n in range(count):
        total = (dkvs[n][...].astype(F32) + cames[n][...].astype(F32)).astype(BF16)
        sums[n][...] = total
        pairs = (
            (n_ref, dqs[n][...], ka_ref, ga_ref, 0),
            (g_ref, mixeds[n][...], ka_ref, ga_ref, 1),
            (n_ref, total[0], kb_ref, gb_ref, 0),
            (n_ref, total[1], kb_ref, gb_ref, 1),
        )
        for left, right, keep, give, i in pairs:
            shape = (keep.shape[1],) + keep.shape[3:]
            keep[n, :, i] = dot_nn(left[:half], right).astype(BF16).reshape(shape)
            give[n, :, i] = dot_nn(left[half:], right).astype(BF16).reshape(shape)


def head_grad(n_flip, g_flip, mixeds, dqs, dkvs, cames, chips):
    width, rows = n_flip.shape
    count, wide = len(dqs), dqs[0].shape[1]
    piece = SHAPE((count, chips, 2, width // 2 // chips, wide), BF16)
    return pl.pallas_call(
        functools.partial(head_grad_kernel, count),
        in_specs=[WHOLE] * (2 + 4 * count),
        out_specs=[WHOLE] * (count + 4),
        out_shape=[SHAPE(dkvs[0].shape, BF16)] * count + [piece] * 4,
        compiler_params=params(),
        cost_estimate=cost(8 * count * width * rows * wide, 8 * count * width * wide),
        name="head_grad",
    )(n_flip, g_flip, *mixeds, *dqs, *dkvs, *cames)


def first_back_kernel(nm, x_ref, gmid_ref, gain_ref, *refs):
    dqs, dkvs = refs[:nm], refs[nm : 2 * nm]
    qo_refs, kv_refs, out_ref, sums_ref = refs[2 * nm : 2 * nm + 2], refs[2 * nm + 2 : 2 * nm + 4], *refs[2 * nm + 4 :]
    step = pl.program_id(0)
    half = x_ref.shape[1] // 2
    wide = dqs[0].shape[1]
    sides = []
    for side in range(2):
        total = 0.0
        for k in range(nm):
            total = total + dot_nt(dqs[k][...], qo_refs[side][:, k, 0].reshape(half, wide))
            for i in range(2):
                total = total + dot_nt(dkvs[k][i], kv_refs[side][:, k, i].reshape(half, wide))
        sides.append(total)
    into, sums = norm_back(
        jnp.concatenate(sides, axis=1), x_ref[...].astype(F32), gain_ref[...]
    )
    out_ref[...] = (gmid_ref[...] + into).astype(BF16)

    @pl.when(step == 0)
    def _():
        sums_ref[...] = sums

    @pl.when(step > 0)
    def _():
        sums_ref[...] += sums


def first_back(x, gmid, gain, dqs, dkvs, qo, kv):
    rows, width = x.shape
    chips, nm, _, deep, wide = qo[0].shape
    block = row_block(rows)
    line = pl.BlockSpec((block, width), lambda i: (i, 0))
    q_spec = pl.BlockSpec((chips, nm, 1, deep, wide), lambda i: (0, 0, 0, 0, 0))
    kv_spec = pl.BlockSpec((chips, nm, 2, deep, wide), lambda i: (0, 0, 0, 0, 0))
    return pl.pallas_call(
        functools.partial(first_back_kernel, nm),
        grid=(rows // block,),
        in_specs=[line, line, pl.BlockSpec((1, width), lambda i: (0, 0))]
        + [pl.BlockSpec((block, wide), lambda i: (i, 0))] * nm
        + [pl.BlockSpec((2, block, wide), lambda i: (0, i, 0))] * nm
        + [q_spec, q_spec, kv_spec, kv_spec],
        out_specs=[line, pl.BlockSpec((2, width), lambda i: (0, 0))],
        out_shape=[SHAPE((rows, width), BF16), SHAPE((2, width), F32)],
        compiler_params=params(),
        cost_estimate=cost(6 * rows * width * nm * wide, 12 * x.size),
        name="first_back",
    )(x, gmid, gain, *dqs, *dkvs, *qo, *kv)


def add_low(a, b):
    return (a.astype(F32) + b.astype(F32)).astype(BF16)


class Scatter:
    def __init__(self, nd, nm, bits):
        self.nd, self.nm = nd, nm
        self.queue = {1: [], **{bit: [] for bit in bits}, "z": []}
        self.order, self.kept, self.waits, self.flying = {}, {}, {}, {}
        self.ends, self.came, self.done = {}, {}, {}

    def add(self, name, ks, keep, give, order):
        self.order[name] = order
        self.push(1, (name, tuple(ks), -1), list(range(0, self.nd, 2)), keep, give)

    def push(self, link, key, places, keep, give):
        self.kept[key], self.waits[key] = (places, keep), give
        self.queue[link].append(key)

    def launch(self, core=1, chip=1, z=1):
        for link, tasks in self.queue.items():
            for _ in range({1: core, "z": z}.get(link, chip)):
                if not tasks:
                    break
                key = tasks.pop(0)
                value = self.waits.pop(key)
                if link == "z":
                    self.flying[key] = ring(value, -1, self.nm)
                else:
                    self.flying[key] = swap(value, link, self.nd)

    def busy(self):
        return bool(self.flying) or any(self.queue.values())

    def land(self, *extra):
        waits, flying = list(self.waits), list(self.flying)
        values = lax.optimization_barrier(
            ([self.waits[key] for key in waits], [self.flying[key] for key in flying], extra)
        )
        self.waits = dict(zip(waits, values[0]))
        came = dict(zip(flying, values[1]))
        self.flying = {}
        for key, value in came.items():
            self.arrive(key, value)
        extra = values[2]
        return extra[0] if len(extra) == 1 else extra

    def arrive(self, key, value):
        name, ks, stage = key
        if stage == "z":
            self.came[name, ks - 1] = value
            self.advance(name, ks - 1)
            return
        order = self.order[name]
        places, keep = self.kept.pop(key)
        if stage + 1 == len(order):
            for n, k in enumerate(ks):
                self.ends[name, k] = (keep[n, 0], value[n, 0])
            for k in reversed(ks):
                self.advance(name, k)
            return
        bit = order[stage + 1]
        stays = [n for n, j in enumerate(places) if not j & bit]
        goes = [n for n, j in enumerate(places) if j & bit]

        def take(array, which):
            return jnp.stack([array[:, n] for n in which], axis=1)

        self.push(
            bit,
            (name, ks, stage + 1),
            [places[n] for n in stays],
            add_low(take(keep, stays), take(value, stays)),
            add_low(take(keep, goes), take(value, goes)),
        )

    def advance(self, name, k):
        if (name, k) not in self.ends or (k < self.nm - 1 and (name, k) not in self.came):
            return
        total = sum(part.astype(F32) for part in self.ends.pop((name, k)))
        if k < self.nm - 1:
            total = total + self.came.pop((name, k)).astype(F32)
        if k:
            key = (name, k, "z")
            self.waits[key] = total.astype(BF16)
            self.queue["z"].append(key)
        else:
            self.done[name] = total


def shards(nd, nm, tokens, views, norm_gains, norm_biases, w_proj, w_out, w_up, w_down, cotangent):
    micro, _, chunk, width = tokens.shape
    ranks = nm // micro
    half = max(ranks // 2, 1)
    rows = micro * chunk
    chips = nd // 2
    wide = w_out.shape[2]
    per_k = wide // PAIR
    hidden = w_up.shape[2]
    dp, mp = lax.axis_index("dp"), lax.axis_index("mp")
    group = mp // half
    step_here = group // 2
    rank = (dp & 1) + 2 * (mp % half)
    order_of = [2 * (p % chips) + p // chips for p in range(nd)]
    offsets = jnp.asarray(order_of, jnp.int32)
    index = dp.astype(jnp.int32) ^ offsets

    def routes(k):
        pairs = []
        for d in range(nd):
            for z in range(nm):
                m = (k + z) % micro
                r = z // micro
                to_d = (d & ~1) | (r & 1)
                to_z = (2 * m + (d & 1)) * half + r // 2
                pairs.append((d * nm + z, to_d * nm + to_z))
        return pairs

    there = ((dp & ~1) | ((mp // micro) & 1)).astype(jnp.int32) ^ offsets

    def pack(value):
        return [pack_features(value, there, (k + mp) % micro) for k in range(micro)]

    def send(packed, k):
        return lax.ppermute(packed[k], ("dp", "mp"), routes(k))

    def send_chunk(chunks, k):
        return lax.ppermute(chunks[k], ("dp", "mp"), [(b, a) for a, b in routes(k)])

    def unpack(came):
        return unpack_features(came, there, [(k + mp) % micro for k in range(micro)])

    def by_place(vector):
        return jnp.take(vector.reshape(-1, nd, width // nd), index, axis=1).reshape(-1, width)

    gains, biases = by_place(norm_gains[0]), by_place(norm_biases[0])

    flow = Flow(nd, nm)
    forth, back = flow.bits, flow.bits[::-1]
    groups = [[0], [1]] if nm > 1 else [[0]]
    groups += [list(range(k, min(k + 2, nm))) for k in range(2, nm, 2)]
    sizes = tuple(len(group) for group in groups)
    head = [jnp.concatenate([w_proj[0, :1], w_out, w_proj[0, 1:]])]
    up, down = [w_up[0]], [w_down[0]]
    flow.add("up0", w_up, forth)
    flow.add("down0", w_down, back)
    for step in range(nm - 1):
        head.append(ring(head[-1], 1, nm))
        flow.launch(chip=1 if step == 0 else 0)
        head = flow.land(head)
    token_parts = pack(tokens[:, 0])
    view = lax.dynamic_index_in_dim(views[:, 0], mp % micro, 0, keepdims=True)
    view = lax.ppermute(view, ("dp", "mp"), routes(0))
    flow.add("qo", jnp.stack([h[:2] for h in head]), forth)
    flow.add("kv", jnp.stack([h[2:] for h in head]), back)
    came = []
    while not (flow.whole("qo") and flow.whole("kv") and len(came) == micro):
        flow.launch(chip=2)
        if len(came) < micro:
            came.append(send(token_parts, len(came)))
        came, token_parts = flow.land(came, token_parts)
    qo_own, kv_own = flow.take_half("qo"), flow.take_half("kv")

    def turn():
        if len(up) < nm:
            up.append(ring(up[-1], 1, nm))
            down.append(ring(down[-1], 1, nm))

    def turned():
        for n, group in enumerate(groups):
            if f"up{n}" not in flow.order and group[-1] < len(up):
                flow.add(f"up{n}", jnp.stack([up[k] for k in group]), forth)
                flow.add(f"down{n}", jnp.stack([down[k] for k in group]), back)

    halves = {}

    def core_halves(most):
        for n in range(len(groups)):
            for name in (f"up{n}", f"down{n}"):
                if most and flow.whole(name):
                    halves[name] = flow.take_half(name)
                    flow.fly(name, swap(halves[name], 1, nd))
                    most -= 1

    flow.fly("kv", swap(kv_own, 1, nd))
    turn()
    x, normed, n_flip = first_norm(came, gains[:1], biases[:1])
    x, normed, n_flip, view, qo_own, kv_own, up, down = flow.land(
        x, normed, n_flip, view, qo_own, kv_own, up, down
    )
    turned()
    kv = [kv_own, flow.kept.pop("kv")]

    flow.fly("qo", swap(qo_own, 1, nd))
    turn()
    flow.launch()
    own_kv = project(normed, kv[0], kv[1], 0, 2)
    own_kv, normed, qo_own, up, down = flow.land(own_kv, normed, qo_own, up, down)
    turned()
    qo = [qo_own, flow.kept.pop("qo")]

    def swap_rank(value, bit):
        if bit == 1:
            return swap(value, 1, nd)
        return lax.ppermute(value, "mp", [(i, i ^ (bit >> 1)) for i in range(nm)])

    rank_bits = [1 << b for b in range(ranks.bit_length() - 1)]
    kvs = {0: own_kv}
    for bit in rank_bits:
        for j in list(kvs):
            kvs[j | bit] = swap_rank(kvs[j], bit)
    kvs = [kvs[j] for j in range(ranks)]
    turn()
    flow.launch(chip=1)
    query = project(normed, qo[0], qo[1], 0, 1)
    slot = jnp.stack([(step_here - t) % micro for t in range(micro)])
    within = (slot[:, None] * chunk + jnp.arange(chunk)[None]).reshape(-1)
    position = jnp.stack([(rank ^ j) * rows + within for j in range(ranks)])
    bias = jnp.where(position < TRI + view[0] * VIEW_TOK, 0.0, -1.0).astype(F32)
    grad_parts = pack(cotangent[:, 0])
    kvs, query, up, down, bias, grad_parts = flow.land(kvs, query, up, down, bias, grad_parts)
    turned()

    grad_came, mixed, lses = [], [], []
    last = [f"{name}{n}" for n in range(len(groups)) for name in ("up", "down")]
    at_once = max(nm // 2, 1)
    while len(mixed) < nm or len(grad_came) < micro or not all(
        name in halves or flow.whole(name) for name in last
    ):
        core_halves(2)
        turn()
        flow.launch(chip=1)
        if len(grad_came) < micro:
            grad_came.append(send(grad_parts, len(grad_came)))
        for k in range(len(mixed), min(len(mixed) + at_once, nm)):
            part, lse = attend(query, kvs, bias, k * per_k, per_k)
            mixed.append(part)
            lses.append(lse)
        mixed, query, halves, grad_parts, grad_came, up, down = flow.land(
            mixed, query, halves, grad_parts, grad_came, up, down
        )
        turned()
    core_halves(len(last))
    middle, normed_two, flip_two = middle_norm(x, mixed, *qo, 1, gains[1:], biases[1:])
    grad, grad_flip = flip(grad_came)
    middle, normed_two, flip_two, halves, grad, grad_flip = flow.land(
        middle, normed_two, flip_two, halves, grad, grad_flip
    )
    weights = []
    for name in last:
        weights += [halves[name], flow.kept.pop(name)]

    result, active, slope = feed(normed_two, middle, sizes, weights)
    out_chunks = result.reshape((micro, chunk, width))
    output = []

    sums = Scatter(nd, nm, flow.bits)
    pairs = [list(range(k, min(k + 2, nm))) for k in range(0, nm, 2)][::-1]

    def wide_grads(flipped, values):
        return [wide_grad(flipped, values, ks[0], len(ks), chips) for ks in pairs]

    for ks in pairs:
        sums.launch(chip=0)
        pieces = wide_grad(grad_flip, active, ks[0], len(ks), chips)
        pieces, active, grad_flip, out_chunks, grad = sums.land(
            pieces, active, grad_flip, out_chunks, grad
        )
        sums.add("down", ks, *pieces, back[::-1])
    sums.launch(core=2)
    output.append(send_chunk(out_chunks, 0))
    hid, gmid, attn, attn_flip, sums_two = feed_back(
        grad, slope, middle, gains[1:], sizes, weights
    )
    hid, gmid, attn, attn_flip, sums_two, flip_two, out_chunks, output = sums.land(
        hid, gmid, attn, attn_flip, sums_two, flip_two, out_chunks, output
    )
    sums.launch(core=0)
    pieces = wide_grads(flip_two, hid)
    pieces, attn = sums.land(pieces, attn)
    for ks, piece in zip(pairs, pieces):
        sums.add("up", ks, *piece, forth[::-1])

    sums.launch(core=2, chip=0)
    grad_mixed = project(attn, *qo, 1, 1)
    grad_mixed, query, out_chunks = sums.land(grad_mixed, query, out_chunks)
    dqs, dkvs, pending = {}, {}, []
    bias_tall = bias[:, :, None]
    closing = [[k] for k in range(min(2, nm))] + [
        list(range(k, min(k + 2, nm))) for k in range(2, nm, 2)
    ]

    def head_grads(dkv_part, dkv_came):
        if not closing or any(k not in dkv_came for k in closing[-1]):
            return None
        ks = closing.pop()
        outs = head_grad(
            n_flip,
            attn_flip,
            [mixed[k] for k in ks],
            [dqs[k] for k in ks],
            [dkv_part[k] for k in ks],
            [dkv_came[k] for k in ks],
            chips,
        )
        for n, k in enumerate(ks):
            dkvs[k] = outs[n]
        return ks, outs[len(ks) :]

    dkv_part, dkv_came = {}, {}

    def exchange(parts):
        parts = dict(enumerate(parts))
        came = None
        for bit in rank_bits[::-1]:
            if came is not None:
                parts = {j: add_low(part, came[j]) for j, part in parts.items()}
            came = {j ^ bit: swap_rank(parts.pop(j), bit) for j in list(parts) if j & bit}
        return parts[0], came[0]

    parts = None
    for k in list(reversed(range(nm))) + [-1, -2]:
        sums.launch(core=2, chip=1 if k >= 0 else 2, z=2 if k >= 0 else 3)
        if k >= 0 and len(output) < micro:
            output.append(send_chunk(out_chunks, len(output)))
        ready = head_grads(dkv_part, dkv_came)
        if parts is not None:
            dkv_part[k + 1], dkv_came[k + 1] = exchange(parts)
            parts = None
        if k >= 0:
            dqs[k], *parts = attend_back(
                query, kvs, bias_tall, lses[k], mixed[k], grad_mixed, k * per_k, per_k
            )
        live = (ready and ready[1], dqs, parts, query, dkv_part, dkv_came, dkvs, output, gmid)
        live = sums.land(*live)
        outs, dqs, parts, query, dkv_part, dkv_came, dkvs, output, gmid = live
        if ready:
            sums.add("qo", ready[0], outs[0], outs[1], forth[::-1])
            sums.add("kv", ready[0], outs[2], outs[3], back[::-1])
    sums.launch(core=2, chip=2, z=3)
    first, sums_one = first_back(
        x, gmid, gains[:1], [dqs[k] for k in range(nm)], [dkvs[k] for k in range(nm)], qo, kv
    )
    first, sums_one = sums.land(first, sums_one)
    first = first.reshape((micro, chunk, width))
    grad_tokens = [send_chunk(first, k) for k in range(micro)]
    while sums.busy():
        sums.launch(core=2, chip=2, z=3)
        sums.land()
    g_qo, g_kv, g_up, g_down = (sums.done[name] for name in ("qo", "kv", "up", "down"))

    def everywhere(value):
        count = value.shape[0]
        value = jnp.take(
            value.reshape(count, nd, width // nd), jnp.argsort(index), axis=1
        ).reshape(count, width)
        bit = 1
        while bit < nd:
            value = value + swap(value, bit, nd)
            bit *= 2
        bit = 1
        while bit < nm:
            value = value + lax.ppermute(value, "mp", [(i, i ^ bit) for i in range(nm)])
            bit *= 2
        share = width // (nd * nm)
        return lax.dynamic_slice_in_dim(value, (dp * nm + mp) * share, share, 1)

    vectors = everywhere(jnp.concatenate([sums_one, sums_two]))
    return (
        unpack(output)[:, None],
        unpack(grad_tokens)[:, None],
        jnp.concatenate([g_qo[:1], g_kv])[None],
        g_qo[1][None],
        g_up[None],
        g_down[None],
        jnp.stack([vectors[0], vectors[2]])[None],
        vectors[1][None],
        vectors[3][None],
    )


def solution(mesh):
    placed = (
        P(None, "dp", "mp", None),
        P(None, "dp"),
        P(),
        P(),
        P(None, None, "dp", "mp"),
        P(None, "dp", "mp"),
        P(None, "dp", "mp"),
        P(None, "dp", "mp"),
        P(None, "dp", "mp", None),
    )
    return jax.shard_map(
        functools.partial(shards, mesh.shape["dp"], mesh.shape["mp"]),
        mesh=mesh,
        in_specs=placed,
        out_specs=(
            P(None, "dp", "mp", None),
            P(None, "dp", "mp", None),
            P(None, None, "dp", "mp"),
            P(None, "dp", "mp"),
            P(None, "dp", "mp"),
            P(None, "dp", "mp"),
            P(None, None, ("dp", "mp")),
            P(None, ("dp", "mp")),
            P(None, ("dp", "mp")),
        ),
        check_vma=False,
    )
```

time: 774 us -> 605 us (0.78)
  the two profiles are of different devices: /device:TPU:0 before, /device:TPU:8 now
where the time goes in v2:
time: 605 us; the launch traced here: 596 us
  Pallas kernels  271 us (45%)
  waiting for transfers between devices  140 us (23%)
  starting transfers between devices  101 us (17%)
  other arithmetic  51.4 us (8%)
  local copies, waits for them, and re-layouts  29.5 us (5%)
    pallas_call x4, Pallas kernels, attend_back(): pl.pallas_call(functools.partial(attend_back_kernel, parts), grid=(count,...  69.7 us
    ppermute x21, waiting for transfers between devices, ring(): return lax.ppermute(value, 'mp', [(i, (i + step) % nm) for i in range(nm)])  58.6 us
    ppermute x62, waiting for transfers between devices, swap(): return lax.ppermute(value, 'dp', [(i, i ^ bit) for i in range(nd)])  52 us
    pallas_call x4, Pallas kernels, attend(): pl.pallas_call(functools.partial(attend_kernel, parts), grid=(count, rows...  46.1 us
    ppermute x62, starting transfers between devices, swap(): return lax.ppermute(value, 'dp', [(i, i ^ bit) for i in range(nd)])  44.5 us
    ppermute x21, starting transfers between devices, ring(): return lax.ppermute(value, 'mp', [(i, (i + step) % nm) for i in range(nm)])  35.5 us
    pallas_call x4, Pallas kernels, wide_grad(): pl.pallas_call(wide_grad_kernel, grid=(count, hidden // block), in_specs=...  27.5 us
    pallas_call x1, Pallas kernels, feed_back(): pl.pallas_call(functools.partial(feed_back_kernel, sizes), grid=(nm,), in...  26.1 us
  transfers between devices with their start and end apart: 94, of which 30 were waited for; matrix products, arithmetic and copies ran while one was open for 11% of the time, Pallas kernels for 40%

profile of v2, /device:TPU:8, one launch (start us, length us, event | category | flops | bytes accessed | tf_op | source)
XLA Modules:
  0.0 595.6 jit_solution(4804995103622122744)
XLA Ops:
  15.5 5.6 collective-permute-done.3
  37.5 7.2 %collective-permute-done.9.refs_0_ = bf16[384,1024]{1,0:T(8,128)(2,1)S(1)} collective-permute-done((bf16[384,1024]{1,0:T(8,128)(2,1)}, bf16[384,1024]{1,0:T(8,128)(2,1)S(1)}, u32[]{:S(2)}, u32[]{:S(2)}) %collective-permute-start.9) | collective-permute-done | bytes 786464 | tf_op jit(solution)/shard_map/ppermute | solution.py:828
  44.6 9.2 %collective-permute-done.6 = bf16[1,4,2,128,256]{4,3,2,1,0:T(8,128)(2,1)S(1)} collective-permute-done((bf16[1,4,2,128,256]{4,3,2,1,0:T(8,128)(2,1)S(1)}, bf16[1,4,2,128,256]{4,3,2,1,0:T(8,128)(2,1)S(1)}, u32[]{:S(2)}, u32[]{:S(2)}) %collective-permute-start.6) | collective-permute-done | bytes 524320 | tf_op jit(solution)/shard_map/ppermute | solution.py:49
  62.0 15.7 %collective-permute-done.12.refs_1_ = bf16[384,1024]{1,0:T(8,128)(2,1)S(1)} collective-permute-done((bf16[384,1024]{1,0:T(8,128)(2,1)S(1)}, bf16[384,1024]{1,0:T(8,128)(2,1)S(1)}, u32[]{:S(2)}, u32[]{:S(2)}) %collective-permute-start.12) | collective-permute-done | bytes 786464 | tf_op jit(solution)/shard_map/ppermute | solution.py:828
  91.5 4.8 first_norm.1
  104.9 6.8 %project.3.refs_0_.refs_2_ = bf16[2,768,1024]{2,1,0:T(8,128)(2,1)} custom-call(bf16[768,1024]{1,0:T(8,128)(2,1)} %get-tuple-element.471.in_ref, bf16[4,4,2,128,256]{4,3,2,1,0:T(8,128)(2,1)} %pad_maximum_fusion.own_ref.refs_10_, bf16[4,4,2,128,256]{4,3,2,1,0:T(8,128)(2,1)} %collective-permute-done.13.other_ref.refs_11_), custom_call_target="tpu_custom_call" | custom-call | flops 3221225472 | bytes 3145728 | tf_op jit(solution)/shard_map/project/pallas_call | solution.py:256
  129.4 5.0 project.4.q_ref
  152.4 11.5 %attend.4 = (bf16[768,256]{1,0:T(8,128)(2,1)}, f32[2,2,768]{2,1,0:T(2,128)}) custom-call(bf16[1,768,1024]{2,1,0:T(8,128)(2,1)} %project.4.q_ref, bf16[2,768,1024]{2,1,0:T(8,128)(2,1)} %project.3.refs_0_.refs_2_, bf16[2,768,1024]{2,1,0:T(8,128)(2,1)} %collective-permute-done.24.refs_1_.refs_3_, bf16[2,768,1024]{2,1,0:T(8,128)(2,1)} %project.3.refs_0_.refs_2_, ...), custom_call_target="tpu_custom_call" | custom-call | flops 4831838208 | bytes 3145728 | tf_op jit(solution)/shard_map/attend/pallas_call | solution.py:304
  164.0 11.6 %attend.5 = (bf16[768,256]{1,0:T(8,128)(2,1)}, f32[2,2,768]{2,1,0:T(2,128)}) custom-call(bf16[1,768,1024]{2,1,0:T(8,128)(2,1)} %project.4.q_ref, bf16[2,768,1024]{2,1,0:T(8,128)(2,1)} %project.3.refs_0_.refs_2_, bf16[2,768,1024]{2,1,0:T(8,128)(2,1)} %collective-permute-done.24.refs_1_.refs_3_, bf16[2,768,1024]{2,1,0:T(8,128)(2,1)} %project.3.refs_0_.refs_2_, ...), custom_call_target="tpu_custom_call" | custom-call | flops 4831838208 | bytes 3145728 | tf_op jit(solution)/shard_map/attend/pallas_call | solution.py:304
  184.5 11.5 %attend.6 = (bf16[768,256]{1,0:T(8,128)(2,1)}, f32[2,2,768]{2,1,0:T(2,128)}) custom-call(bf16[1,768,1024]{2,1,0:T(8,128)(2,1)} %project.4.q_ref, bf16[2,768,1024]{2,1,0:T(8,128)(2,1)} %project.3.refs_0_.refs_2_, bf16[2,768,1024]{2,1,0:T(8,128)(2,1)} %collective-permute-done.24.refs_1_.refs_3_, bf16[2,768,1024]{2,1,0:T(8,128)(2,1)} %project.3.refs_0_.refs_2_, ...), custom_call_target="tpu_custom_call" | custom-call | flops 4831838208 | bytes 3145728 | tf_op jit(solution)/shard_map/attend/pallas_call | solution.py:304
  196.0 11.5 %attend.7 = (bf16[768,256]{1,0:T(8,128)(2,1)}, f32[2,2,768]{2,1,0:T(2,128)}) custom-call(bf16[1,768,1024]{2,1,0:T(8,128)(2,1)} %project.4.q_ref, bf16[2,768,1024]{2,1,0:T(8,128)(2,1)} %project.3.refs_0_.refs_2_, bf16[2,768,1024]{2,1,0:T(8,128)(2,1)} %collective-permute-done.24.refs_1_.refs_3_, bf16[2,768,1024]{2,1,0:T(8,128)(2,1)} %project.3.refs_0_.refs_2_, ...), custom_call_target="tpu_custom_call" | custom-call | flops 4831838208 | bytes 3145728 | tf_op jit(solution)/shard_map/attend/pallas_call | solution.py:304
  215.7 6.8 %middle_norm.1 = (f32[768,1024]{1,0:T(8,128)}, bf16[768,1024]{1,0:T(8,128)(2,1)}, bf16[1024,768]{1,0:T(8,128)(2,1)}) custom-call(bf16[768,1024]{1,0:T(8,128)(2,1)} %get-tuple-element.536.x_ref, bf16[768,256]{1,0:T(8,128)(2,1)} %get-tuple-element.537.refs_0_.refs_6_.refs_2_, bf16[768,256]{1,0:T(8,128)(2,1)} %get-tuple-element.538.refs_1_.refs_6_.refs_2_, ...), custom_call_target="tpu_custom_call" | custom-call | flops 1610612736 | bytes 11010048 | tf_op jit(solution)/shard_map/middle_norm/pallas_call | solution.py:421
  222.5 22.9 %feed.1 = (bf16[768,1024]{1,0:T(8,128)(2,1)}, bf16[4,768,1024]{2,1,0:T(8,128)(2,1)}, bf16[4,768,1024]{2,1,0:T(8,128)(2,1)}) custom-call(bf16[4,1,128,1024]{3,2,1,0:T(8,128)(2,1)} %copy-done.19, bf16[4,1,128,1024]{3,2,1,0:T(8,128)(2,1)} %collective-permute-done.27.refs_1_, bf16[4,1,128,1024]{3,2,1,0:T(8,128)(2,1)} %copy-done.20, ...), custom_call_target="tpu_custom_call" | custom-call | flops 12884901888 | bytes 16777216 | tf_op jit(solution)/shard_map/feed/pallas_call | solution.py:500
  245.4 6.9 %wide_grad.4 = (bf16[2,512,1024]{2,1,0:T(8,128)(2,1)}, bf16[2,512,1024]{2,1,0:T(8,128)(2,1)}) custom-call(bf16[1024,768]{1,0:T(8,128)(2,1)} %get-tuple-element.573.a_ref, bf16[4,768,1024]{2,1,0:T(8,128)(2,1)} %get-tuple-element.574.b_ref), custom_call_target="tpu_custom_call" | custom-call | flops 3221225472 | bytes 8388608 | tf_op jit(solution)/shard_map/wide_grad/pallas_call | solution.py:601
  254.0 6.9 %wide_grad.5 = (bf16[2,512,1024]{2,1,0:T(8,128)(2,1)}, bf16[2,512,1024]{2,1,0:T(8,128)(2,1)}) custom-call(bf16[1024,768]{1,0:T(8,128)(2,1)} %get-tuple-element.573.a_ref, bf16[4,768,1024]{2,1,0:T(8,128)(2,1)} %get-tuple-element.574.b_ref), custom_call_target="tpu_custom_call" | custom-call | flops 3221225472 | bytes 8388608 | tf_op jit(solution)/shard_map/wide_grad/pallas_call | solution.py:601
  270.9 26.1 %feed_back.1 = (bf16[4,768,1024]{2,1,0:T(8,128)(2,1)}, f32[768,1024]{1,0:T(8,128)}, bf16[768,1024]{1,0:T(8,128)(2,1)}, bf16[1024,768]{1,0:T(8,128)(2,1)}, f32[2,1024]{1,0:T(2,128)}) custom-call(bf16[4,1,128,1024]{3,2,1,0:T(8,128)(2,1)} %copy-done.19, bf16[4,1,128,1024]{3,2,1,0:T(8,128)(2,1)} %collective-permute-done.27.refs_1_, ...), custom_call_target="tpu_custom_call" | custom-call | flops 12884901888 | bytes 16777216 | tf_op jit(solution)/shard_map/feed_back/pallas_call | solution.py:558
  304.0 6.9 %wide_grad.6 = (bf16[2,512,1024]{2,1,0:T(8,128)(2,1)}, bf16[2,512,1024]{2,1,0:T(8,128)(2,1)}) custom-call(bf16[1024,768]{1,0:T(8,128)(2,1)} %get-tuple-element.594.a_ref, bf16[4,768,1024]{2,1,0:T(8,128)(2,1)} %get-tuple-element.595.b_ref), custom_call_target="tpu_custom_call" | custom-call | flops 3221225472 | bytes 8388608 | tf_op jit(solution)/shard_map/wide_grad/pallas_call | solution.py:601
  310.9 6.9 %wide_grad.7 = (bf16[2,512,1024]{2,1,0:T(8,128)(2,1)}, bf16[2,512,1024]{2,1,0:T(8,128)(2,1)}) custom-call(bf16[1024,768]{1,0:T(8,128)(2,1)} %get-tuple-element.594.a_ref, bf16[4,768,1024]{2,1,0:T(8,128)(2,1)} %get-tuple-element.595.b_ref), custom_call_target="tpu_custom_call" | custom-call | flops 3221225472 | bytes 8388608 | tf_op jit(solution)/shard_map/wide_grad/pallas_call | solution.py:601
  317.8 5.7 collective-permute-done.43
  330.8 4.9 project.5.refs_7_
  341.0 17.5 %attend_back.4 = (bf16[768,256]{1,0:T(8,128)(2,1)}, bf16[2,768,256]{2,1,0:T(8,128)(2,1)}, bf16[2,768,256]{2,1,0:T(8,128)(2,1)}) custom-call(bf16[1,768,1024]{2,1,0:T(8,128)(2,1)} %project.4.q_ref, bf16[2,768,1024]{2,1,0:T(8,128)(2,1)} %project.3.refs_0_.refs_2_, bf16[2,768,1024]{2,1,0:T(8,128)(2,1)} %collective-permute-done.24.refs_1_.refs_3_, ...), custom_call_target="tpu_custom_call" | custom-call | flops 12079595520 | bytes 6291456 | tf_op jit(solution)/shard_map/attend_back/pallas_call | solution.py:372
  368.5 17.4 %attend_back.5 = (bf16[768,256]{1,0:T(8,128)(2,1)}, bf16[2,768,256]{2,1,0:T(8,128)(2,1)}, bf16[2,768,256]{2,1,0:T(8,128)(2,1)}) custom-call(bf16[1,768,1024]{2,1,0:T(8,128)(2,1)} %project.4.q_ref, bf16[2,768,1024]{2,1,0:T(8,128)(2,1)} %project.3.refs_0_.refs_2_, bf16[2,768,1024]{2,1,0:T(8,128)(2,1)} %collective-permute-done.24.refs_1_.refs_3_, ...), custom_call_target="tpu_custom_call" | custom-call | flops 12079595520 | bytes 6291456 | tf_op jit(solution)/shard_map/attend_back/pallas_call | solution.py:372
  392.5 17.4 %attend_back.6 = (bf16[768,256]{1,0:T(8,128)(2,1)}, bf16[2,768,256]{2,1,0:T(8,128)(2,1)}, bf16[2,768,256]{2,1,0:T(8,128)(2,1)}) custom-call(bf16[1,768,1024]{2,1,0:T(8,128)(2,1)} %project.4.q_ref, bf16[2,768,1024]{2,1,0:T(8,128)(2,1)} %project.3.refs_0_.refs_2_, bf16[2,768,1024]{2,1,0:T(8,128)(2,1)} %collective-permute-done.24.refs_1_.refs_3_, ...), custom_call_target="tpu_custom_call" | custom-call | flops 12079595520 | bytes 6291456 | tf_op jit(solution)/shard_map/attend_back/pallas_call | solution.py:372
  415.2 4.9 collective-permute-start.58
  420.1 17.4 %attend_back.7 = (bf16[768,256]{1,0:T(8,128)(2,1)}, bf16[2,768,256]{2,1,0:T(8,128)(2,1)}, bf16[2,768,256]{2,1,0:T(8,128)(2,1)}) custom-call(bf16[1,768,1024]{2,1,0:T(8,128)(2,1)} %project.4.q_ref, bf16[2,768,1024]{2,1,0:T(8,128)(2,1)} %project.3.refs_0_.refs_2_, bf16[2,768,1024]{2,1,0:T(8,128)(2,1)} %collective-permute-done.24.refs_1_.refs_3_, ...), custom_call_target="tpu_custom_call" | custom-call | flops 12079595520 | bytes 6291456 | tf_op jit(solution)/shard_map/attend_back/pallas_call | solution.py:372
  437.5 8.3 %head_grad.3 = (bf16[2,768,256]{2,1,0:T(8,128)(2,1)}, bf16[2,768,256]{2,1,0:T(8,128)(2,1)}, bf16[2,4,2,128,256]{4,3,2,1,0:T(8,128)(2,1)}, bf16[2,4,2,128,256]{4,...) custom-call(bf16[1024,768]{1,0:T(8,128)(2,1)} %get-tuple-element.656.refs_0_, ...), custom_call_target="tpu_custom_call" | custom-call | flops 3221225472 | bytes 4194304 | tf_op jit(solution)/shard_map/head_grad/pallas_call | solution.py:643
  454.7 5.4 head_grad.4
  469.3 5.3 head_grad.5
  485.7 11.4 %first_back.1 = (bf16[768,1024]{1,0:T(8,128)(2,1)}, f32[2,1024]{1,0:T(2,128)}) custom-call(bf16[768,1024]{1,0:T(8,128)(2,1)} %get-tuple-element.536.x_ref, f32[768,1024]{1,0:T(8,128)} %get-tuple-element.737.gmid_ref, f32[1,1024]{1,0:T(1,128)} %get-tuple-element.891.refs_2_.gain_ref, bf16[768,256]{1,0:T(8,128)(2,1)} %get-tuple-element.738.refs_3_.refs_0_, ...), custom_call_target="tpu_custom_call" | custom-call | flops 4831838208 | bytes 9437184 | tf_op jit(solution)/shard_map/first_back/pallas_call | solution.py:689
  499.1 5.7 collective-permute-done.74
  519.7 4.8 collective-permute-done.91
  556.7 30.1 %collective-permute-done.87 = bf16[2,128,256]{2,1,0:T(8,128)(2,1)S(1)} collective-permute-done((bf16[2,128,256]{2,1,0:T(8,128)(2,1)S(1)}, bf16[2,128,256]{2,1,0:T(8,128)(2,1)S(1)}, u32[]{:S(2)}, u32[]{:S(2)}) %collective-permute-start.87) | collective-permute-done | bytes 131104 | tf_op jit(solution)/shard_map/ppermute | solution.py:53
  (471 shorter events, 252.7 us)
Async XLA Ops:
  33.4 23.4 %collective-permute-start.8 = (bf16[1,4,2,128,256]{4,3,2,1,0:T(8,128)(2,1)S(1)}, bf16[1,4,2,128,256]{4,3,2,1,0:T(8,128)(2,1)S(1)}, u32[]{:S(2)}, u32[]{:S(2)}) collective-permute-start(bf16[1,4,2,128,256]{4,3,2,1,0:T(8,128)(2,1)S(1)} %get-tuple-element.874), channel_id=1, source_target_pairs={{0,16},{4,20},{8,24},{12,28},{16,0},{20,4},{24,8},{28,12},{1,17},{... | collective-permute-start | bytes 1572872 | tf_op jit(solution)/shard_map/ppermute | solution.py:49
  56.9 25.2 %collective-permute-start.10 = (bf16[2,4,2,128,256]{4,3,2,1,0:T(8,128)(2,1)S(1)}, bf16[2,4,2,128,256]{4,3,2,1,0:T(8,128)(2,1)S(1)}, u32[]{:S(2)}, u32[]{:S(2)}) collective-permute-start(bf16[2,4,2,128,256]{4,3,2,1,0:T(8,128)(2,1)S(1)} %pad_maximum_fusion.4), channel_id=1, source_target_pairs={{0,8},{4,12},{8,0},{12,4},{16,24},{20,28},{24,16},{28,20},{1,9},{5... | collective-permute-start | bytes 3145736 | tf_op jit(solution)/shard_map/ppermute | solution.py:49
  57.6 25.7 %collective-permute-start.11 = (bf16[2,4,2,128,256]{4,3,2,1,0:T(8,128)(2,1)S(1)}, bf16[2,4,2,128,256]{4,3,2,1,0:T(8,128)(2,1)}, u32[]{:S(2)}, u32[]{:S(2)}) collective-permute-start(bf16[2,4,2,128,256]{4,3,2,1,0:T(8,128)(2,1)S(1)} %pad_maximum_fusion.5), channel_id=1, source_target_pairs={{0,16},{4,20},{8,24},{12,28},{16,0},{20,4},{24,8},{28,12},{1,17},{... | collective-permute-start | bytes 3145736 | tf_op jit(solution)/shard_map/ppermute | solution.py:49
  118.4 24.0 %collective-permute-start.24 = (bf16[2,768,1024]{2,1,0:T(8,128)(2,1)}, bf16[2,768,1024]{2,1,0:T(8,128)(2,1)}, u32[]{:S(2)}, u32[]{:S(2)}) collective-permute-start(bf16[2,768,1024]{2,1,0:T(8,128)(2,1)} %project.3.refs_0_.refs_2_), channel_id=1, source_target_pairs={{0,4},{4,0},{8,12},{12,8},{16,20},{20,16},{24,28},{28,24},{1,5},{5... | collective-permute-start | bytes 9437192 | tf_op jit(solution)/shard_map/ppermute | solution.py:49
  142.6 33.0 %collective-permute-start.27 = (bf16[4,1,128,1024]{3,2,1,0:T(8,128)(2,1)S(1)}, bf16[4,1,128,1024]{3,2,1,0:T(8,128)(2,1)}, u32[]{:S(2)}, u32[]{:S(2)}) collective-permute-start(bf16[4,1,128,1024]{3,2,1,0:T(8,128)(2,1)S(1)} %pad_maximum_fusion.6.refs_0_), channel_id=1, source_target_pairs={{0,4},{4,0},{8,12},{12,8},{16,20},{20,16},{24,28},{28,24},{1,5},{5... | collective-permute-start | bytes 3145736 | tf_op jit(solution)/shard_map/ppermute | solution.py:49
  144.3 31.4 %collective-permute-start.28 = (bf16[4,1,128,1024]{3,2,1,0:T(8,128)(2,1)S(1)}, bf16[4,1,128,1024]{3,2,1,0:T(8,128)(2,1)}, u32[]{:S(2)}, u32[]{:S(2)}) collective-permute-start(bf16[4,1,128,1024]{3,2,1,0:T(8,128)(2,1)S(1)} %pad_maximum_fusion.7.refs_2_), channel_id=1, source_target_pairs={{0,4},{4,0},{8,12},{12,8},{16,20},{20,16},{24,28},{28,24},{1,5},{5... | collective-permute-start | bytes 3145736 | tf_op jit(solution)/shard_map/ppermute | solution.py:49
  145.8 29.8 %collective-permute-start.29 = (bf16[1,2,128,1024]{3,2,1,0:T(8,128)(2,1)S(1)}, bf16[1,2,128,1024]{3,2,1,0:T(8,128)(2,1)S(1)}, u32[]{:S(2)}, u32[]{:S(2)}) collective-permute-start(bf16[1,2,128,1024]{3,2,1,0:T(8,128)(2,1)S(1)} %get-tuple-element.864), channel_id=1, source_target_pairs={{0,8},{4,12},{8,0},{12,4},{16,24},{20,28},{24,16},{28,20},{1,9},{5... | collective-permute-start | bytes 1572872 | tf_op jit(solution)/shard_map/ppermute | solution.py:49
  148.1 27.6 %collective-permute-start.30 = (bf16[1,2,128,1024]{3,2,1,0:T(8,128)(2,1)}, bf16[1,2,128,1024]{3,2,1,0:T(8,128)(2,1)S(1)}, u32[]{:S(2)}, u32[]{:S(2)}) collective-permute-start(bf16[1,2,128,1024]{3,2,1,0:T(8,128)(2,1)} %get-tuple-element.862), channel_id=1, source_target_pairs={{0,16},{4,20},{8,24},{12,28},{16,0},{20,4},{24,8},{28,12},{1,17},{... | collective-permute-start | bytes 1572872 | tf_op jit(solution)/shard_map/ppermute | solution.py:49
  149.8 25.8 %collective-permute-start.31 = (bf16[384,1024]{1,0:T(8,128)(2,1)S(1)}, bf16[384,1024]{1,0:T(8,128)(2,1)S(1)}, u32[]{:S(2)}, u32[]{:S(2)}) collective-permute-start(bf16[384,1024]{1,0:T(8,128)(2,1)S(1)} %copy-done.40), channel_id=1, source_target_pairs={{0,0},{1,2},{2,4},{3,6},{4,1},{5,3},{6,5},{7,7},{8,8},{9,10},{10,1... | collective-permute-start | bytes 2359304 | tf_op jit(solution)/shard_map/ppermute | solution.py:828
  177.0 30.5 %collective-permute-start.32 = (bf16[4,1,128,1024]{3,2,1,0:T(8,128)(2,1)S(1)}, bf16[4,1,128,1024]{3,2,1,0:T(8,128)(2,1)}, u32[]{:S(2)}, u32[]{:S(2)}) collective-permute-start(bf16[4,1,128,1024]{3,2,1,0:T(8,128)(2,1)S(1)} %pad_maximum_fusion.8.refs_4_), channel_id=1, source_target_pairs={{0,4},{4,0},{8,12},{12,8},{16,20},{20,16},{24,28},{28,24},{1,5},{5... | collective-permute-start | bytes 3145736 | tf_op jit(solution)/shard_map/ppermute | solution.py:49
  179.7 27.8 %collective-permute-start.33 = (bf16[4,1,128,1024]{3,2,1,0:T(8,128)(2,1)S(1)}, bf16[4,1,128,1024]{3,2,1,0:T(8,128)(2,1)}, u32[]{:S(2)}, u32[]{:S(2)}) collective-permute-start(bf16[4,1,128,1024]{3,2,1,0:T(8,128)(2,1)S(1)} %pad_maximum_fusion.9.refs_6_), channel_id=1, source_target_pairs={{0,4},{4,0},{8,12},{12,8},{16,20},{20,16},{24,28},{28,24},{1,5},{5... | collective-permute-start | bytes 3145736 | tf_op jit(solution)/shard_map/ppermute | solution.py:49
  180.1 27.4 %collective-permute-start.34 = (bf16[2,2,128,1024]{3,2,1,0:T(8,128)(2,1)S(1)}, bf16[2,2,128,1024]{3,2,1,0:T(8,128)(2,1)S(1)}, u32[]{:S(2)}, u32[]{:S(2)}) collective-permute-start(bf16[2,2,128,1024]{3,2,1,0:T(8,128)(2,1)S(1)} %pad_maximum_fusion.10), channel_id=1, source_target_pairs={{0,8},{4,12},{8,0},{12,4},{16,24},{20,28},{24,16},{28,20},{1,9},{5... | collective-permute-start | bytes 3145736 | tf_op jit(solution)/shard_map/ppermute | solution.py:49
  182.7 25.4 %collective-permute-start.35 = (bf16[2,2,128,1024]{3,2,1,0:T(8,128)(2,1)}, bf16[2,2,128,1024]{3,2,1,0:T(8,128)(2,1)}, u32[]{:S(2)}, u32[]{:S(2)}) collective-permute-start(bf16[2,2,128,1024]{3,2,1,0:T(8,128)(2,1)} %pad_maximum_fusion.11), channel_id=1, source_target_pairs={{0,16},{4,20},{8,24},{12,28},{16,0},{20,4},{24,8},{28,12},{1,17},{... | collective-permute-start | bytes 3145736 | tf_op jit(solution)/shard_map/ppermute | solution.py:49
  183.2 24.3 %collective-permute-start.36 = (bf16[384,1024]{1,0:T(8,128)(2,1)S(1)}, bf16[384,1024]{1,0:T(8,128)(2,1)}, u32[]{:S(2)}, u32[]{:S(2)}) collective-permute-start(bf16[384,1024]{1,0:T(8,128)(2,1)S(1)} %copy-done.39), channel_id=1, source_target_pairs={{0,2},{1,0},{2,6},{3,4},{4,3},{5,1},{6,7},{7,5},{8,10},{9,8},{10,1... | collective-permute-start | bytes 2359304 | tf_op jit(solution)/shard_map/ppermute | solution.py:828
  260.9 36.1 %collective-permute-start.40 = (bf16[2,4,128,1024]{3,2,1,0:T(8,128)(2,1)}, bf16[2,4,128,1024]{3,2,1,0:T(8,128)(2,1)S(1)}, u32[]{:S(2)}, u32[]{:S(2)}) collective-permute-start(bf16[2,4,128,1024]{3,2,1,0:T(8,128)(2,1)} %bitcast.257), channel_id=1, source_target_pairs={{0,4},{4,0},{8,12},{12,8},{16,20},{20,16},{24,28},{28,24},{1,5},{5... | collective-permute-start | bytes 6291464 | tf_op jit(solution)/shard_map/ppermute | solution.py:49
  264.0 33.0 %collective-permute-start.41 = (bf16[2,2,128,1024]{3,2,1,0:T(8,128)(2,1)}, bf16[2,2,128,1024]{3,2,1,0:T(8,128)(2,1)}, u32[]{:S(2)}, u32[]{:S(2)}) collective-permute-start(bf16[2,2,128,1024]{3,2,1,0:T(8,128)(2,1)} %add_convert_fusion.7), channel_id=1, source_target_pairs={{0,8},{4,12},{8,0},{12,4},{16,24},{20,28},{24,16},{28,20},{1,9},{5... | collective-permute-start | bytes 3145736 | tf_op jit(solution)/shard_map/ppermute | solution.py:49
  265.4 31.5 %collective-permute-start.42 = (bf16[384,1024]{1,0:T(8,128)(2,1)}, bf16[384,1024]{1,0:T(8,128)(2,1)}, u32[]{:S(2)}, u32[]{:S(2)}) collective-permute-start(bf16[384,1024]{1,0:T(8,128)(2,1)} %slice_bitcast_fusion.1), channel_id=1, source_target_pairs={{0,0},{2,1},{4,2},{6,3},{1,4},{3,5},{5,6},{7,7},{8,8},{10,9},{12,1... | collective-permute-start | bytes 2359304 | tf_op jit(solution)/shard_map/ppermute | solution.py:831
  298.8 24.6 %collective-permute-start.43 = (bf16[2,2,128,1024]{3,2,1,0:T(8,128)(2,1)S(1)}, bf16[2,2,128,1024]{3,2,1,0:T(8,128)(2,1)S(1)}, u32[]{:S(2)}, u32[]{:S(2)}) collective-permute-start(bf16[2,2,128,1024]{3,2,1,0:T(8,128)(2,1)S(1)} %add_convert_fusion.6), channel_id=1, source_target_pairs={{0,8},{4,12},{8,0},{12,4},{16,24},{20,28},{24,16},{28,20},{1,9},{5... | collective-permute-start | bytes 3145736 | tf_op jit(solution)/shard_map/ppermute | solution.py:49
  337.0 25.2 %collective-permute-start.48 = (bf16[2,1,128,1024]{3,2,1,0:T(8,128)(2,1)}, bf16[2,1,128,1024]{3,2,1,0:T(8,128)(2,1)S(1)}, u32[]{:S(2)}, u32[]{:S(2)}) collective-permute-start(bf16[2,1,128,1024]{3,2,1,0:T(8,128)(2,1)} %get-tuple-element.612), channel_id=1, source_target_pairs={{0,16},{4,20},{8,24},{12,28},{16,0},{20,4},{24,8},{28,12},{1,17},{... | collective-permute-start | bytes 1572872 | tf_op jit(solution)/shard_map/ppermute | solution.py:49
  338.6 23.6 %collective-permute-start.49 = (bf16[128,1024]{1,0:T(8,128)(2,1)}, bf16[128,1024]{1,0:T(8,128)(2,1)}, u32[]{:S(2)}, u32[]{:S(2)}) collective-permute-start(bf16[128,1024]{1,0:T(8,128)(2,1)} %fusion.5), channel_id=1, source_target_pairs={{0,3},{1,0},{2,1},{3,2},{4,7},{5,4},{6,5},{7,6},{8,11},{9,8},{10,9... | collective-permute-start | bytes 786440 | tf_op jit(solution)/shard_map/ppermute | solution.py:53
  340.7 26.2 %collective-permute-start.50 = (bf16[384,1024]{1,0:T(8,128)(2,1)S(1)}, bf16[384,1024]{1,0:T(8,128)(2,1)}, u32[]{:S(2)}, u32[]{:S(2)}) collective-permute-start(bf16[384,1024]{1,0:T(8,128)(2,1)S(1)} %slice_bitcast_fusion), channel_id=1, source_target_pairs={{2,0},{0,1},{6,2},{4,3},{3,4},{1,5},{7,6},{5,7},{10,8},{8,9},{14,1... | collective-permute-start | bytes 2359304 | tf_op jit(solution)/shard_map/ppermute | solution.py:831
  414.6 31.2 %collective-permute-start.57 = (bf16[2,1,128,1024]{3,2,1,0:T(8,128)(2,1)S(1)}, bf16[2,1,128,1024]{3,2,1,0:T(8,128)(2,1)S(1)}, u32[]{:S(2)}, u32[]{:S(2)}) collective-permute-start(bf16[2,1,128,1024]{3,2,1,0:T(8,128)(2,1)S(1)} %get-tuple-element.801), channel_id=1, source_target_pairs={{0,8},{4,12},{8,0},{12,4},{16,24},{20,28},{24,16},{28,20},{1,9},{5... | collective-permute-start | bytes 1572872 | tf_op jit(solution)/shard_map/ppermute | solution.py:49
  415.2 30.6 %collective-permute-start.58 = (bf16[128,1024]{1,0:T(8,128)(2,1)S(1)}, bf16[128,1024]{1,0:T(8,128)(2,1)S(1)}, u32[]{:S(2)}, u32[]{:S(2)}) collective-permute-start(bf16[128,1024]{1,0:T(8,128)(2,1)S(1)} %fusion.7), channel_id=1, source_target_pairs={{0,3},{1,0},{2,1},{3,2},{4,7},{5,4},{6,5},{7,6},{8,11},{9,8},{10,9... | collective-permute-start | bytes 786440 | tf_op jit(solution)/shard_map/ppermute | solution.py:53
  420.1 25.7 %collective-permute-start.59 = (bf16[2,768,256]{2,1,0:T(8,128)(2,1)S(1)}, bf16[2,768,256]{2,1,0:T(8,128)(2,1)S(1)}, u32[]{:S(2)}, u32[]{:S(2)}) collective-permute-start(bf16[2,768,256]{2,1,0:T(8,128)(2,1)S(1)} %copy-done.80), channel_id=1, source_target_pairs={{0,4},{4,0},{8,12},{12,8},{16,20},{20,16},{24,28},{28,24},{1,5},{5... | collective-permute-start | bytes 2359304 | tf_op jit(solution)/shard_map/ppermute | solution.py:49
  479.7 25.0 %collective-permute-start.69 = (bf16[1,4,2,128,256]{4,3,2,1,0:T(8,128)(2,1)}, bf16[1,4,2,128,256]{4,3,2,1,0:T(8,128)(2,1)S(1)}, u32[]{:S(2)}, u32[]{:S(2)}) collective-permute-start(bf16[1,4,2,128,256]{4,3,2,1,0:T(8,128)(2,1)} %get-tuple-element.729), channel_id=1, source_target_pairs={{0,4},{4,0},{8,12},{12,8},{16,20},{20,16},{24,28},{28,24},{1,5},{5... | collective-permute-start | bytes 1572872 | tf_op jit(solution)/shard_map/ppermute | solution.py:49
  479.7 25.0 %collective-permute-start.70 = (bf16[1,4,2,128,256]{4,3,2,1,0:T(8,128)(2,1)}, bf16[1,4,2,128,256]{4,3,2,1,0:T(8,128)(2,1)S(1)}, u32[]{:S(2)}, u32[]{:S(2)}) collective-permute-start(bf16[1,4,2,128,256]{4,3,2,1,0:T(8,128)(2,1)} %get-tuple-element.730), channel_id=1, source_target_pairs={{0,4},{4,0},{8,12},{12,8},{16,20},{20,16},{24,28},{28,24},{1,5},{5... | collective-permute-start | bytes 1572872 | tf_op jit(solution)/shard_map/ppermute | solution.py:49
  506.9 30.0 %collective-permute-start.77 = (bf16[1,2,2,128,256]{4,3,2,1,0:T(8,128)(2,1)}, bf16[1,2,2,128,256]{4,3,2,1,0:T(8,128)(2,1)}, u32[]{:S(2)}, u32[]{:S(2)}) collective-permute-start(bf16[1,2,2,128,256]{4,3,2,1,0:T(8,128)(2,1)} %add_convert_fusion.26), channel_id=1, source_target_pairs={{0,8},{4,12},{8,0},{12,4},{16,24},{20,28},{24,16},{28,20},{1,9},{5... | collective-permute-start | bytes 786440 | tf_op jit(solution)/shard_map/ppermute | solution.py:49
  512.6 24.3 %collective-permute-start.79 = (bf16[1,2,2,128,256]{4,3,2,1,0:T(8,128)(2,1)S(1)}, bf16[1,2,2,128,256]{4,3,2,1,0:T(8,128)(2,1)S(1)}, u32[]{:S(2)}, u32[]{:S(2)}) collective-permute-start(bf16[1,2,2,128,256]{4,3,2,1,0:T(8,128)(2,1)S(1)} %get-tuple-element.830), channel_id=1, source_target_pairs={{0,16},{4,20},{8,24},{12,28},{16,0},{20,4},{24,8},{28,12},{1,17},{... | collective-permute-start | bytes 786440 | tf_op jit(solution)/shard_map/ppermute | solution.py:49
  545.2 45.5 %collective-permute-start.75 = (bf16[384,1024]{1,0:T(8,128)(2,1)S(1)}, bf16[384,1024]{1,0:T(8,128)(2,1)S(1)}, u32[]{:S(2)}, u32[]{:S(2)}) collective-permute-start(bf16[384,1024]{1,0:T(8,128)(2,1)S(1)} %get-tuple-element.825), channel_id=1, source_target_pairs={{0,0},{2,1},{4,2},{6,3},{1,4},{3,5},{5,6},{7,7},{8,8},{10,9},{12,1... | collective-permute-start | bytes 2359304 | tf_op jit(solution)/shard_map/ppermute | solution.py:831
  547.2 43.5 %collective-permute-start.76 = (bf16[384,1024]{1,0:T(8,128)(2,1)S(1)}, bf16[384,1024]{1,0:T(8,128)(2,1)S(1)}, u32[]{:S(2)}, u32[]{:S(2)}) collective-permute-start(bf16[384,1024]{1,0:T(8,128)(2,1)S(1)} %get-tuple-element.824), channel_id=1, source_target_pairs={{2,0},{0,1},{6,2},{4,3},{3,4},{1,5},{7,6},{5,7},{10,8},{8,9},{14,1... | collective-permute-start | bytes 2359304 | tf_op jit(solution)/shard_map/ppermute | solution.py:831
  548.6 38.2 %collective-permute-start.87 = (bf16[2,128,256]{2,1,0:T(8,128)(2,1)S(1)}, bf16[2,128,256]{2,1,0:T(8,128)(2,1)S(1)}, u32[]{:S(2)}, u32[]{:S(2)}) collective-permute-start(bf16[2,128,256]{2,1,0:T(8,128)(2,1)S(1)} %fusion.9), channel_id=1, source_target_pairs={{0,3},{1,0},{2,1},{3,2},{4,7},{5,4},{6,5},{7,6},{8,11},{9,8},{10,9... | collective-permute-start | bytes 393224 | tf_op jit(solution)/shard_map/ppermute | solution.py:53
  551.2 37.0 %collective-permute-start.88 = (bf16[2,128,256]{2,1,0:T(8,128)(2,1)S(1)}, bf16[2,128,256]{2,1,0:T(8,128)(2,1)S(1)}, u32[]{:S(2)}, u32[]{:S(2)}) collective-permute-start(bf16[2,128,256]{2,1,0:T(8,128)(2,1)S(1)} %fusion.8), channel_id=1, source_target_pairs={{0,3},{1,0},{2,1},{3,2},{4,7},{5,4},{6,5},{7,6},{8,11},{9,8},{10,9... | collective-permute-start | bytes 393224 | tf_op jit(solution)/shard_map/ppermute | solution.py:53
  (145 other events, 1545.8 us)

commit v3 on v2

--- a/solution.py
+++ b/solution.py
@@ -119,7 +119,7 @@
     wide = in_ref.shape[2] // nd
     for p in range(nd):
         there = pl.ds(pl.multiple_of(index_ref[p] * wide, wide), wide)
-        out_ref[:, p * wide : (p + 1) * wide] = in_ref[index_ref[nd], :, there]
+        out_ref[:, p * wide : (p + 1) * wide] = in_ref[0, :, there]
 
 
 def pack_features(value, index, which):
@@ -130,8 +130,12 @@
         return jnp.take(chunk.reshape(rows, nd, -1), index, axis=1).reshape(rows, width)
     return pl.pallas_call(
         pack_kernel,
-        in_specs=[pl.BlockSpec(memory_space=pltpu.SMEM), WHOLE],
-        out_specs=WHOLE,
+        grid_spec=pltpu.PrefetchScalarGridSpec(
+            num_scalar_prefetch=1,
+            grid=(1,),
+            in_specs=[pl.BlockSpec((1, rows, width), lambda i, index_ref: (index_ref[nd], 0, 0))],
+            out_specs=pl.BlockSpec((rows, width), lambda i, index_ref: (0, 0)),
+        ),
         out_shape=SHAPE((rows, width), value.dtype),
         compiler_params=params(),
         cost_estimate=cost(0, 6 * rows * width),
@@ -615,45 +619,40 @@
     return keep.reshape(shape), give.reshape(shape)
 
 
-def head_grad_kernel(count, *refs):
-    n_ref, g_ref = refs[:2]
-    mixeds, dqs, dkvs, cames = (refs[2 + i * count : 2 + (i + 1) * count] for i in range(4))
-    sums = refs[2 + 4 * count : 2 + 5 * count]
-    ka_ref, ga_ref, kb_ref, gb_ref = refs[2 + 5 * count :]
+def head_grad_kernel(
+    n_ref, g_ref, mixed_ref, dq_ref, dkv_ref, came_ref, sum_ref, keep_ref, give_ref
+):
     half = n_ref.shape[0] // 2
-    for n in range(count):
-        total = (dkvs[n][...].astype(F32) + cames[n][...].astype(F32)).astype(BF16)
-        sums[n][...] = total
-        pairs = (
-            (n_ref, dqs[n][...], ka_ref, ga_ref, 0),
-            (g_ref, mixeds[n][...], ka_ref, ga_ref, 1),
-            (n_ref, total[0], kb_ref, gb_ref, 0),
-            (n_ref, total[1], kb_ref, gb_ref, 1),
-        )
-        for left, right, keep, give, i in pairs:
-            shape = (keep.shape[1],) + keep.shape[3:]
-            keep[n, :, i] = dot_nn(left[:half], right).astype(BF16).reshape(shape)
-            give[n, :, i] = dot_nn(left[half:], right).astype(BF16).reshape(shape)
-
-
-def head_grad(n_flip, g_flip, mixeds, dqs, dkvs, cames, chips):
+    chips, _, deep, wide = keep_ref.shape
+    total = (dkv_ref[...].astype(F32) + came_ref[...].astype(F32)).astype(BF16)
+    sum_ref[...] = total
+    pairs = ((n_ref, dq_ref[...]), (g_ref, mixed_ref[...]), (n_ref, total[0]), (n_ref, total[1]))
+    for i, (left, right) in enumerate(pairs):
+        for out, side in ((keep_ref, left[:half]), (give_ref, left[half:])):
+            out[:, i] = dot_nn(side, right).astype(BF16).reshape(chips, deep, wide)
+
+
+def head_grad(n_flip, g_flip, mixed, dq, dkv, came, chips):
     width, rows = n_flip.shape
-    count, wide = len(dqs), dqs[0].shape[1]
-    piece = SHAPE((count, chips, 2, width // 2 // chips, wide), BF16)
-    return pl.pallas_call(
-        functools.partial(head_grad_kernel, count),
-        in_specs=[WHOLE] * (2 + 4 * count),
-        out_specs=[WHOLE] * (count + 4),
-        out_shape=[SHAPE(dkvs[0].shape, BF16)] * count + [piece] * 4,
+    wide = dq.shape[1]
+    piece = SHAPE((chips, 4, width // 2 // chips, wide), BF16)
+    total, keep, give = pl.pallas_call(
+        head_grad_kernel,
+        in_specs=[WHOLE] * 6,
+        out_specs=[WHOLE] * 3,
+        out_shape=[SHAPE(dkv.shape, BF16), piece, piece],
         compiler_params=params(),
-        cost_estimate=cost(8 * count * width * rows * wide, 8 * count * width * wide),
+        cost_estimate=cost(8 * width * rows * wide, 8 * width * wide),
         name="head_grad",
-    )(n_flip, g_flip, *mixeds, *dqs, *dkvs, *cames)
+    )(n_flip, g_flip, mixed, dq, dkv, came)
+    return total, keep[None], give[None]
 
 
 def first_back_kernel(nm, x_ref, gmid_ref, gain_ref, *refs):
-    dqs, dkvs = refs[:nm], refs[nm : 2 * nm]
-    qo_refs, kv_refs, out_ref, sums_ref = refs[2 * nm : 2 * nm + 2], refs[2 * nm + 2 : 2 * nm + 4], *refs[2 * nm + 4 :]
+    dqs, dkvs, came_ref = refs[:nm], refs[nm : 2 * nm], refs[2 * nm]
+    qo_refs, kv_refs = refs[2 * nm + 1 : 2 * nm + 3], refs[2 * nm + 3 : 2 * nm + 5]
+    out_ref, sums_ref = refs[2 * nm + 5 :]
+    last = (dkvs[0][...].astype(F32) + came_ref[...].astype(F32)).astype(BF16)
     step = pl.program_id(0)
     half = x_ref.shape[1] // 2
     wide = dqs[0].shape[1]
@@ -663,7 +662,8 @@
         for k in range(nm):
             total = total + dot_nt(dqs[k][...], qo_refs[side][:, k, 0].reshape(half, wide))
             for i in range(2):
-                total = total + dot_nt(dkvs[k][i], kv_refs[side][:, k, i].reshape(half, wide))
+                dkv = dkvs[k][i] if k else last[i]
+                total = total + dot_nt(dkv, kv_refs[side][:, k, i].reshape(half, wide))
         sides.append(total)
     into, sums = norm_back(
         jnp.concatenate(sides, axis=1), x_ref[...].astype(F32), gain_ref[...]
@@ -679,7 +679,7 @@
         sums_ref[...] += sums
 
 
-def first_back(x, gmid, gain, dqs, dkvs, qo, kv):
+def first_back(x, gmid, gain, dqs, dkvs, came, qo, kv):
     rows, width = x.shape
     chips, nm, _, deep, wide = qo[0].shape
     block = row_block(rows)
@@ -691,14 +691,14 @@
         grid=(rows // block,),
         in_specs=[line, line, pl.BlockSpec((1, width), lambda i: (0, 0))]
         + [pl.BlockSpec((block, wide), lambda i: (i, 0))] * nm
-        + [pl.BlockSpec((2, block, wide), lambda i: (0, i, 0))] * nm
+        + [pl.BlockSpec((2, block, wide), lambda i: (0, i, 0))] * (nm + 1)
         + [q_spec, q_spec, kv_spec, kv_spec],
         out_specs=[line, pl.BlockSpec((2, width), lambda i: (0, 0))],
         out_shape=[SHAPE((rows, width), BF16), SHAPE((2, width), F32)],
         compiler_params=params(),
         cost_estimate=cost(6 * rows * width * nm * wide, 12 * x.size),
         name="first_back",
-    )(x, gmid, gain, *dqs, *dkvs, *qo, *kv)
+    )(x, gmid, gain, *dqs, *dkvs, came, *qo, *kv)
 
 
 def add_low(a, b):
@@ -708,29 +708,34 @@
 class Scatter:
     def __init__(self, nd, nm, bits):
         self.nd, self.nm = nd, nm
-        self.queue = {1: [], **{bit: [] for bit in bits}, "z": []}
+        self.queue = {1: [], **{bit: [] for bit in bits}, "direct": [], "z": []}
         self.order, self.kept, self.waits, self.flying = {}, {}, {}, {}
-        self.ends, self.came, self.done = {}, {}, {}
-
-    def add(self, name, ks, keep, give, order):
-        self.order[name] = order
+        self.ends, self.came, self.done, self.rings = {}, {}, {}, {}
+
+    def add(self, name, ks, keep, give, order, rings=True):
+        self.order[name, tuple(ks)], self.rings[name] = order, rings
         self.push(1, (name, tuple(ks), -1), list(range(0, self.nd, 2)), keep, give)
 
     def push(self, link, key, places, keep, give):
         self.kept[key], self.waits[key] = (places, keep), give
         self.queue[link].append(key)
 
-    def launch(self, core=1, chip=1, z=1):
+    def launch(self, core=1, chip=1, direct=1, z=1):
         for link, tasks in self.queue.items():
-            for _ in range({1: core, "z": z}.get(link, chip)):
+            for _ in range({1: core, "direct": direct, "z": z}.get(link, chip)):
                 if not tasks:
                     break
                 key = tasks.pop(0)
                 value = self.waits.pop(key)
-                if link == "z":
-                    self.flying[key] = ring(value, -1, self.nm)
+                if link == "z" and isinstance(value, list):
+                    value = [ring(part, -n - 1, self.nm) for n, part in enumerate(value)]
+                elif link == "z":
+                    value = ring(value, -1, self.nm)
+                elif link == "direct":
+                    value = [swap(part, 2 * n + 2, self.nd) for n, part in enumerate(value)]
                 else:
-                    self.flying[key] = swap(value, link, self.nd)
+                    value = swap(value, link, self.nd)
+                self.flying[key] = value
 
     def busy(self):
         return bool(self.flying) or any(self.queue.values())
@@ -750,12 +755,26 @@
 
     def arrive(self, key, value):
         name, ks, stage = key
+        if stage == "z" and not self.rings[name]:
+            parts = [*self.ends.pop((name, 0)), *value]
+            self.done[name] = sum(part.astype(F32) for part in parts)
+            return
         if stage == "z":
             self.came[name, ks - 1] = value
             self.advance(name, ks - 1)
             return
-        order = self.order[name]
+        order = self.order[name, ks]
         places, keep = self.kept.pop(key)
+        if order is None and stage == -1:
+            parts = [add_low(keep[:, n], value[:, n]) for n in range(1, len(places))]
+            own = (keep[:, 0], value[:, 0])
+            self.push("direct", (name, ks, 0), own, None, parts)
+            return
+        if order is None:
+            for n, k in enumerate(ks):
+                self.ends[name, k] = tuple(part[n] for part in [*places, *value])
+                self.advance(name, k)
+            return
         if stage + 1 == len(order):
             for n, k in enumerate(ks):
                 self.ends[name, k] = (keep[n, 0], value[n, 0])
@@ -778,6 +797,15 @@
         )
 
     def advance(self, name, k):
+        if not self.rings[name]:
+            if all((name, k) in self.ends for k in range(self.nm)):
+                key = (name, 0, "z")
+                self.waits[key] = [
+                    sum(part.astype(F32) for part in self.ends.pop((name, k))).astype(BF16)
+                    for k in range(1, self.nm)
+                ]
+                self.queue["z"].append(key)
+            return
         if (name, k) not in self.ends or (k < self.nm - 1 and (name, k) not in self.came):
             return
         total = sum(part.astype(F32) for part in self.ends.pop((name, k)))
@@ -821,8 +849,8 @@
 
     there = ((dp & ~1) | ((mp // micro) & 1)).astype(jnp.int32) ^ offsets
 
-    def pack(value):
-        return [pack_features(value, there, (k + mp) % micro) for k in range(micro)]
+    def pack(value, k):
+        return pack_features(value, there, (k + mp) % micro)
 
     def send(packed, k):
         return lax.ppermute(packed[k], ("dp", "mp"), routes(k))
@@ -835,8 +863,6 @@
 
     def by_place(vector):
         return jnp.take(vector.reshape(-1, nd, width // nd), index, axis=1).reshape(-1, width)
-
-    gains, biases = by_place(norm_gains[0]), by_place(norm_biases[0])
 
     flow = Flow(nd, nm)
     forth, back = flow.bits, flow.bits[::-1]
@@ -844,52 +870,64 @@
     groups += [list(range(k, min(k + 2, nm))) for k in range(2, nm, 2)]
     sizes = tuple(len(group) for group in groups)
     head = [jnp.concatenate([w_proj[0, :1], w_out, w_proj[0, 1:]])]
-    up, down = [w_up[0]], [w_down[0]]
+    feeds = [jnp.concatenate([w_up, w_down])]
     flow.add("up0", w_up, forth)
     flow.add("down0", w_down, back)
     for step in range(nm - 1):
         head.append(ring(head[-1], 1, nm))
-        flow.launch(chip=1 if step == 0 else 0)
-        head = flow.land(head)
-    token_parts = pack(tokens[:, 0])
-    view = lax.dynamic_index_in_dim(views[:, 0], mp % micro, 0, keepdims=True)
-    view = lax.ppermute(view, ("dp", "mp"), routes(0))
+        if step == 0:
+            flow.launch()
+            head, tokens, views, index, there = flow.land(head, tokens, views, index, there)
+        elif step == 1:
+            token_parts = [pack(tokens[:, 0], k) for k in range(micro)]
+            head, token_parts, index = flow.land(head, token_parts, index)
+        else:
+            view = lax.dynamic_index_in_dim(views[:, 0], mp % micro, 0, keepdims=True)
+            gains, biases = by_place(norm_gains[0]), by_place(norm_biases[0])
+            head, view, gains, biases = flow.land(head, view, gains, biases)
     flow.add("qo", jnp.stack([h[:2] for h in head]), forth)
     flow.add("kv", jnp.stack([h[2:] for h in head]), back)
+    flow.fly("view", lax.ppermute(view, ("dp", "mp"), routes(0)))
     came = []
     while not (flow.whole("qo") and flow.whole("kv") and len(came) == micro):
         flow.launch(chip=2)
         if len(came) < micro:
             came.append(send(token_parts, len(came)))
-        came, token_parts = flow.land(came, token_parts)
-    qo_own, kv_own = flow.take_half("qo"), flow.take_half("kv")
+        if len(came) == 1:
+            grad_parts = [pack(cotangent[:, 0], k) for k in range(micro)]
+        came, token_parts, grad_parts, feeds = flow.land(came, token_parts, grad_parts, feeds)
+    view = flow.kept.pop("view")
 
     def turn():
-        if len(up) < nm:
-            up.append(ring(up[-1], 1, nm))
-            down.append(ring(down[-1], 1, nm))
+        if len(feeds) < nm:
+            feeds.append(ring(feeds[-1], 1, nm))
 
     def turned():
         for n, group in enumerate(groups):
-            if f"up{n}" not in flow.order and group[-1] < len(up):
-                flow.add(f"up{n}", jnp.stack([up[k] for k in group]), forth)
-                flow.add(f"down{n}", jnp.stack([down[k] for k in group]), back)
-
+            if f"up{n}" not in flow.order and group[-1] < len(feeds):
+                flow.add(f"up{n}", jnp.stack([feeds[k][0] for k in group]), forth)
+                flow.add(f"down{n}", jnp.stack([feeds[k][1] for k in group]), back)
+
+    last = [f"{name}{n}" for n in range(len(groups)) for name in ("up", "down")]
     halves = {}
 
     def core_halves(most):
-        for n in range(len(groups)):
-            for name in (f"up{n}", f"down{n}"):
-                if most and flow.whole(name):
-                    halves[name] = flow.take_half(name)
-                    flow.fly(name, swap(halves[name], 1, nd))
-                    most -= 1
-
+        for name in last:
+            if most and flow.whole(name):
+                halves[name] = flow.take_half(name)
+                flow.fly(name, swap(halves[name], 1, nd))
+                most -= 1
+
+    kv_own, qo_own = flow.take_half("kv"), flow.take_half("qo")
+    slot = jnp.stack([(step_here - t) % micro for t in range(micro)])
+    within = (slot[:, None] * chunk + jnp.arange(chunk)[None]).reshape(-1)
+    position = jnp.stack([(rank ^ j) * rows + within for j in range(ranks)])
+    bias = jnp.where(position < TRI + view[0] * VIEW_TOK, 0.0, -1.0).astype(F32)
     flow.fly("kv", swap(kv_own, 1, nd))
     turn()
     x, normed, n_flip = first_norm(came, gains[:1], biases[:1])
-    x, normed, n_flip, view, qo_own, kv_own, up, down = flow.land(
-        x, normed, n_flip, view, qo_own, kv_own, up, down
+    x, normed, n_flip, bias, qo_own, kv_own, feeds = flow.land(
+        x, normed, n_flip, bias, qo_own, kv_own, feeds
     )
     turned()
     kv = [kv_own, flow.kept.pop("kv")]
@@ -898,7 +936,7 @@
     turn()
     flow.launch()
     own_kv = project(normed, kv[0], kv[1], 0, 2)
-    own_kv, normed, qo_own, up, down = flow.land(own_kv, normed, qo_own, up, down)
+    own_kv, normed, qo_own, feeds = flow.land(own_kv, normed, qo_own, feeds)
     turned()
     qo = [qo_own, flow.kept.pop("qo")]
 
@@ -914,33 +952,27 @@
             kvs[j | bit] = swap_rank(kvs[j], bit)
     kvs = [kvs[j] for j in range(ranks)]
     turn()
-    flow.launch(chip=1)
+    flow.launch()
     query = project(normed, qo[0], qo[1], 0, 1)
-    slot = jnp.stack([(step_here - t) % micro for t in range(micro)])
-    within = (slot[:, None] * chunk + jnp.arange(chunk)[None]).reshape(-1)
-    position = jnp.stack([(rank ^ j) * rows + within for j in range(ranks)])
-    bias = jnp.where(position < TRI + view[0] * VIEW_TOK, 0.0, -1.0).astype(F32)
-    grad_parts = pack(cotangent[:, 0])
-    kvs, query, up, down, bias, grad_parts = flow.land(kvs, query, up, down, bias, grad_parts)
+    kvs, query, bias, grad_parts, feeds = flow.land(kvs, query, bias, grad_parts, feeds)
     turned()
 
     grad_came, mixed, lses = [], [], []
-    last = [f"{name}{n}" for n in range(len(groups)) for name in ("up", "down")]
     at_once = max(nm // 2, 1)
     while len(mixed) < nm or len(grad_came) < micro or not all(
         name in halves or flow.whole(name) for name in last
     ):
-        core_halves(2)
         turn()
-        flow.launch(chip=1)
+        flow.launch()
         if len(grad_came) < micro:
             grad_came.append(send(grad_parts, len(grad_came)))
+        core_halves(2)
         for k in range(len(mixed), min(len(mixed) + at_once, nm)):
             part, lse = attend(query, kvs, bias, k * per_k, per_k)
             mixed.append(part)
             lses.append(lse)
-        mixed, query, halves, grad_parts, grad_came, up, down = flow.land(
-            mixed, query, halves, grad_parts, grad_came, up, down
+        mixed, query, halves, grad_parts, grad_came, feeds = flow.land(
+            mixed, query, halves, grad_parts, grad_came, feeds
         )
         turned()
     core_halves(len(last))
@@ -959,17 +991,14 @@
 
     sums = Scatter(nd, nm, flow.bits)
     pairs = [list(range(k, min(k + 2, nm))) for k in range(0, nm, 2)][::-1]
-
-    def wide_grads(flipped, values):
-        return [wide_grad(flipped, values, ks[0], len(ks), chips) for ks in pairs]
-
+    ways = [back[::-1], forth[::-1]]
     for ks in pairs:
         sums.launch(chip=0)
         pieces = wide_grad(grad_flip, active, ks[0], len(ks), chips)
         pieces, active, grad_flip, out_chunks, grad = sums.land(
             pieces, active, grad_flip, out_chunks, grad
         )
-        sums.add("down", ks, *pieces, back[::-1])
+        sums.add("down", ks, *pieces, ways[0])
     sums.launch(core=2)
     output.append(send_chunk(out_chunks, 0))
     hid, gmid, attn, attn_flip, sums_two = feed_back(
@@ -978,39 +1007,29 @@
     hid, gmid, attn, attn_flip, sums_two, flip_two, out_chunks, output = sums.land(
         hid, gmid, attn, attn_flip, sums_two, flip_two, out_chunks, output
     )
-    sums.launch(core=0)
-    pieces = wide_grads(flip_two, hid)
-    pieces, attn = sums.land(pieces, attn)
-    for ks, piece in zip(pairs, pieces):
-        sums.add("up", ks, *piece, forth[::-1])
-
-    sums.launch(core=2, chip=0)
+    sums.launch(core=0, direct=0, z=0)
+    pieces = [wide_grad(flip_two, hid, ks[0], len(ks), chips) for ks in pairs]
     grad_mixed = project(attn, *qo, 1, 1)
-    grad_mixed, query, out_chunks = sums.land(grad_mixed, query, out_chunks)
-    dqs, dkvs, pending = {}, {}, []
+    pieces, grad_mixed, query, out_chunks = sums.land(pieces, grad_mixed, query, out_chunks)
+    for n, (ks, piece) in enumerate(zip(pairs, pieces)):
+        sums.add("up", ks, *piece, ways[n % 2], rings=False)
+
+    dqs, dkvs = {}, {}
     bias_tall = bias[:, :, None]
-    closing = [[k] for k in range(min(2, nm))] + [
-        list(range(k, min(k + 2, nm))) for k in range(2, nm, 2)
-    ]
-
-    def head_grads(dkv_part, dkv_came):
-        if not closing or any(k not in dkv_came for k in closing[-1]):
+    closing = list(range(nm))
+    dkv_part, dkv_came = {}, {}
+
+    def head_grads():
+        if not closing or closing[-1] not in dkv_came:
             return None
-        ks = closing.pop()
-        outs = head_grad(
-            n_flip,
-            attn_flip,
-            [mixed[k] for k in ks],
-            [dqs[k] for k in ks],
-            [dkv_part[k] for k in ks],
-            [dkv_came[k] for k in ks],
-            chips,
+        k = closing.pop()
+        dkvs[k], keep, give = head_grad(
+            n_flip, attn_flip, mixed[k], dqs[k], dkv_part[k], dkv_came[k], chips
         )
-        for n, k in enumerate(ks):
-            dkvs[k] = outs[n]
-        return ks, outs[len(ks) :]
-
-    dkv_part, dkv_came = {}, {}
+        return k, (keep, give)
+
+    def add_heads(ready, outs):
+        sums.add("head", [ready[0]], outs[0], outs[1], None)
 
     def exchange(parts):
         parts = dict(enumerate(parts))
@@ -1022,11 +1041,18 @@
         return parts[0], came[0]
 
     parts = None
-    for k in list(reversed(range(nm))) + [-1, -2]:
-        sums.launch(core=2, chip=1 if k >= 0 else 2, z=2 if k >= 0 else 3)
+    for k in list(reversed(range(nm))) + [-1]:
+        if k == nm - 1:
+            sums.launch(core=2)
+        elif k >= 1:
+            sums.launch(core=nm - 4, chip=1)
+        elif k == 0:
+            sums.launch()
+        else:
+            sums.launch(direct=0, z=0)
         if k >= 0 and len(output) < micro:
             output.append(send_chunk(out_chunks, len(output)))
-        ready = head_grads(dkv_part, dkv_came)
+        ready = head_grads()
         if parts is not None:
             dkv_part[k + 1], dkv_came[k + 1] = exchange(parts)
             parts = None
@@ -1038,42 +1064,53 @@
         live = sums.land(*live)
         outs, dqs, parts, query, dkv_part, dkv_came, dkvs, output, gmid = live
         if ready:
-            sums.add("qo", ready[0], outs[0], outs[1], forth[::-1])
-            sums.add("kv", ready[0], outs[2], outs[3], back[::-1])
-    sums.launch(core=2, chip=2, z=3)
+            add_heads(ready, outs)
+
+    sums.launch()
     first, sums_one = first_back(
-        x, gmid, gains[:1], [dqs[k] for k in range(nm)], [dkvs[k] for k in range(nm)], qo, kv
+        x,
+        gmid,
+        gains[:1],
+        [dqs[k] for k in range(nm)],
+        [dkvs.get(k, dkv_part[k]) for k in range(nm)],
+        dkv_came[0],
+        qo,
+        kv,
     )
-    first, sums_one = sums.land(first, sums_one)
+    first, sums_one, dkv_part, dkv_came = sums.land(first, sums_one, dkv_part, dkv_came)
     first = first.reshape((micro, chunk, width))
-    grad_tokens = [send_chunk(first, k) for k in range(micro)]
-    while sums.busy():
-        sums.launch(core=2, chip=2, z=3)
-        sums.land()
-    g_qo, g_kv, g_up, g_down = (sums.done[name] for name in ("qo", "kv", "up", "down"))
-
-    def everywhere(value):
-        count = value.shape[0]
-        value = jnp.take(
-            value.reshape(count, nd, width // nd), jnp.argsort(index), axis=1
-        ).reshape(count, width)
-        bit = 1
-        while bit < nd:
-            value = value + swap(value, bit, nd)
-            bit *= 2
-        bit = 1
-        while bit < nm:
-            value = value + lax.ppermute(value, "mp", [(i, i ^ bit) for i in range(nm)])
-            bit *= 2
-        share = width // (nd * nm)
-        return lax.dynamic_slice_in_dim(value, (dp * nm + mp) * share, share, 1)
-
-    vectors = everywhere(jnp.concatenate([sums_one, sums_two]))
+    vectors = jnp.take(
+        jnp.concatenate([sums_one, sums_two]).reshape(4, nd, width // nd),
+        jnp.argsort(index),
+        axis=1,
+    ).reshape(4, width)
+    hops = [lambda value, bit=1 << b: swap(value, bit, nd) for b in range(nd.bit_length() - 1)]
+    hops += [
+        lambda value, bit=1 << b: lax.ppermute(value, "mp", [(i, i ^ bit) for i in range(nm)])
+        for b in range(nm.bit_length() - 1)
+    ]
+    grad_tokens = []
+    while sums.busy() or hops or len(grad_tokens) < micro:
+        if len(grad_tokens) < micro:
+            grad_tokens.append(send_chunk(first, len(grad_tokens)))
+        sums.launch(direct=2)
+        if len(grad_tokens) == micro:
+            for _ in range(min(3, len(hops))):
+                vectors = vectors + hops.pop(0)(vectors)
+        ready = head_grads()
+        grad_tokens, first, outs, vectors = sums.land(
+            grad_tokens, first, ready and ready[1], vectors
+        )
+        if ready:
+            add_heads(ready, outs)
+    g_head, g_up, g_down = (sums.done[name] for name in ("head", "up", "down"))
+    share = width // (nd * nm)
+    vectors = lax.dynamic_slice_in_dim(vectors, (dp * nm + mp) * share, share, 1)
     return (
         unpack(output)[:, None],
         unpack(grad_tokens)[:, None],
-        jnp.concatenate([g_qo[:1], g_kv])[None],
-        g_qo[1][None],
+        jnp.concatenate([g_head[:1], g_head[2:]])[None],
+        g_head[1][None],
         g_up[None],
         g_down[None],
         jnp.stack([vectors[0], vectors[2]])[None],

time: 605 us -> 557 us (0.921)
  the two profiles are of different devices: /device:TPU:8 before, /device:TPU:0 now
where the time goes in v3:
time: 557 us; the launch traced here: 548 us
  Pallas kernels  277 us (50%)
  waiting for transfers between devices  102 us (18%)
  starting transfers between devices  94.4 us (17%)
  other arithmetic  43.1 us (8%)
  local copies, waits for them, and re-layouts  28.1 us (5%)
    pallas_call x4, Pallas kernels, attend_back(): pl.pallas_call(functools.partial(attend_back_kernel, parts), grid=(count,...  69.6 us
    ppermute x60, starting transfers between devices, swap(): return lax.ppermute(value, 'dp', [(i, i ^ bit) for i in range(nd)])  48.6 us
    pallas_call x4, Pallas kernels, attend(): pl.pallas_call(functools.partial(attend_kernel, parts), grid=(count, rows...  46.1 us
    ppermute x15, waiting for transfers between devices, ring(): return lax.ppermute(value, 'mp', [(i, (i + step) % nm) for i in range(nm)])  42.6 us
    ppermute x60, waiting for transfers between devices, swap(): return lax.ppermute(value, 'dp', [(i, i ^ bit) for i in range(nd)])  40.5 us
    pallas_call x4, Pallas kernels, wide_grad(): pl.pallas_call(wide_grad_kernel, grid=(count, hidden // block), in_specs=...  27.5 us
    pallas_call x1, Pallas kernels, feed_back(): pl.pallas_call(functools.partial(feed_back_kernel, sizes), grid=(nm,), in...  26.3 us
    pallas_call x1, Pallas kernels, feed(): pl.pallas_call(functools.partial(feed_kernel, sizes), grid=(nm,), in_spec...  23 us
  transfers between devices with their start and end apart: 86, of which 26 were waited for; matrix products, arithmetic and copies ran while one was open for 9% of the time, Pallas kernels for 45%

profile of v3, /device:TPU:0, one launch (start us, length us, event | category | flops | bytes accessed | tf_op | source)
XLA Modules:
  0.0 547.6 jit_solution(6258903931179800823)
XLA Ops:
  11.6 5.6 %collective-permute-done.2 = bf16[4,128,256]{2,1,0:T(8,128)(2,1)S(1)} collective-permute-done((bf16[4,128,256]{2,1,0:T(8,128)(2,1)S(1)}, bf16[4,128,256]{2,1,0:T(8,128)(2,1)S(1)}, u32[]{:S(2)}, u32[]{:S(2)}) %collective-permute-start.2) | collective-permute-done | bytes 262176 | tf_op jit(solution)/shard_map/ppermute | solution.py:53
  27.8 6.2 %collective-permute-done.4 = bf16[4,128,256]{2,1,0:T(8,128)(2,1)S(1)} collective-permute-done((bf16[4,128,256]{2,1,0:T(8,128)(2,1)S(1)}, bf16[4,128,256]{2,1,0:T(8,128)(2,1)S(1)}, u32[]{:S(2)}, u32[]{:S(2)}) %collective-permute-start.4) | collective-permute-done | bytes 262176 | tf_op jit(solution)/shard_map/ppermute | solution.py:53
  50.9 9.0 %collective-permute-done.7 = bf16[1,4,2,128,256]{4,3,2,1,0:T(8,128)(2,1)S(1)} collective-permute-done((bf16[1,4,2,128,256]{4,3,2,1,0:T(8,128)(2,1)S(1)}, bf16[1,4,2,128,256]{4,3,2,1,0:T(8,128)(2,1)S(1)}, u32[]{:S(2)}, u32[]{:S(2)}) %collective-permute-start.7) | collective-permute-done | bytes 524320 | tf_op jit(solution)/shard_map/ppermute | solution.py:49
  68.4 17.3 %collective-permute-done.13.refs_1_ = bf16[384,1024]{1,0:T(8,128)(2,1)S(1)} collective-permute-done((bf16[384,1024]{1,0:T(8,128)(2,1)S(1)}, bf16[384,1024]{1,0:T(8,128)(2,1)S(1)}, u32[]{:S(2)}, u32[]{:S(2)}) %collective-permute-start.13) | collective-permute-done | bytes 786464 | tf_op jit(solution)/shard_map/ppermute | solution.py:856
  100.5 6.5 %collective-permute-done.15 = bf16[2,128,1024]{2,1,0:T(8,128)(2,1)} collective-permute-done((bf16[2,128,1024]{2,1,0:T(8,128)(2,1)}, bf16[2,128,1024]{2,1,0:T(8,128)(2,1)}, u32[]{:S(2)}, u32[]{:S(2)}) %collective-permute-start.15) | collective-permute-done | bytes 524320 | tf_op jit(solution)/shard_map/ppermute | solution.py:53
  111.4 6.8 %project.3.refs_0_.refs_2_ = bf16[2,768,1024]{2,1,0:T(8,128)(2,1)} custom-call(bf16[768,1024]{1,0:T(8,128)(2,1)} %get-tuple-element.486.in_ref, bf16[4,4,2,128,256]{4,3,2,1,0:T(8,128)(2,1)} %pad_maximum_fusion.own_ref.refs_11_, bf16[4,4,2,128,256]{4,3,2,1,0:T(8,128)(2,1)} %collective-permute-done.14.other_ref.refs_12_), custom_call_target="tpu_custom_call" | custom-call | flops 3221225472 | bytes 3145728 | tf_op jit(solution)/shard_map/project/pallas_call | solution.py:260
  125.6 5.0 project.4.q_ref
  130.5 7.2 %collective-permute-done.20 = bf16[2,1,128,1024]{3,2,1,0:T(8,128)(2,1)S(1)} collective-permute-done((bf16[2,1,128,1024]{3,2,1,0:T(8,128)(2,1)S(1)}, bf16[2,1,128,1024]{3,2,1,0:T(8,128)(2,1)S(1)}, u32[]{:S(2)}, u32[]{:S(2)}) %collective-permute-start.20) | collective-permute-done | bytes 524320 | tf_op jit(solution)/shard_map/ppermute | solution.py:49
  148.4 11.5 %attend.4 = (bf16[768,256]{1,0:T(8,128)(2,1)}, f32[2,2,768]{2,1,0:T(2,128)}) custom-call(bf16[1,768,1024]{2,1,0:T(8,128)(2,1)} %project.4.q_ref, bf16[2,768,1024]{2,1,0:T(8,128)(2,1)} %project.3.refs_0_.refs_2_, bf16[2,768,1024]{2,1,0:T(8,128)(2,1)} %collective-permute-done.22.refs_1_.refs_3_, bf16[2,768,1024]{2,1,0:T(8,128)(2,1)} %project.3.refs_0_.refs_2_, ...), custom_call_target="tpu_custom_call" | custom-call | flops 4831838208 | bytes 3145728 | tf_op jit(solution)/shard_map/attend/pallas_call | solution.py:308
  160.0 11.5 %attend.5 = (bf16[768,256]{1,0:T(8,128)(2,1)}, f32[2,2,768]{2,1,0:T(2,128)}) custom-call(bf16[1,768,1024]{2,1,0:T(8,128)(2,1)} %project.4.q_ref, bf16[2,768,1024]{2,1,0:T(8,128)(2,1)} %project.3.refs_0_.refs_2_, bf16[2,768,1024]{2,1,0:T(8,128)(2,1)} %collective-permute-done.22.refs_1_.refs_3_, bf16[2,768,1024]{2,1,0:T(8,128)(2,1)} %project.3.refs_0_.refs_2_, ...), custom_call_target="tpu_custom_call" | custom-call | flops 4831838208 | bytes 3145728 | tf_op jit(solution)/shard_map/attend/pallas_call | solution.py:308
  180.2 11.5 %attend.6 = (bf16[768,256]{1,0:T(8,128)(2,1)}, f32[2,2,768]{2,1,0:T(2,128)}) custom-call(bf16[1,768,1024]{2,1,0:T(8,128)(2,1)} %project.4.q_ref, bf16[2,768,1024]{2,1,0:T(8,128)(2,1)} %project.3.refs_0_.refs_2_, bf16[2,768,1024]{2,1,0:T(8,128)(2,1)} %collective-permute-done.22.refs_1_.refs_3_, bf16[2,768,1024]{2,1,0:T(8,128)(2,1)} %project.3.refs_0_.refs_2_, ...), custom_call_target="tpu_custom_call" | custom-call | flops 4831838208 | bytes 3145728 | tf_op jit(solution)/shard_map/attend/pallas_call | solution.py:308
  191.7 11.5 %attend.7 = (bf16[768,256]{1,0:T(8,128)(2,1)}, f32[2,2,768]{2,1,0:T(2,128)}) custom-call(bf16[1,768,1024]{2,1,0:T(8,128)(2,1)} %project.4.q_ref, bf16[2,768,1024]{2,1,0:T(8,128)(2,1)} %project.3.refs_0_.refs_2_, bf16[2,768,1024]{2,1,0:T(8,128)(2,1)} %collective-permute-done.22.refs_1_.refs_3_, bf16[2,768,1024]{2,1,0:T(8,128)(2,1)} %project.3.refs_0_.refs_2_, ...), custom_call_target="tpu_custom_call" | custom-call | flops 4831838208 | bytes 3145728 | tf_op jit(solution)/shard_map/attend/pallas_call | solution.py:308
  211.6 6.8 %middle_norm.1 = (f32[768,1024]{1,0:T(8,128)}, bf16[768,1024]{1,0:T(8,128)(2,1)}, bf16[1024,768]{1,0:T(8,128)(2,1)}) custom-call(bf16[768,1024]{1,0:T(8,128)(2,1)} %get-tuple-element.550.x_ref, bf16[768,256]{1,0:T(8,128)(2,1)} %get-tuple-element.551.refs_0_.refs_6_.mixed_ref, bf16[768,256]{1,0:T(8,128)(2,1)} %get-tuple-element.552.refs_1_.refs_6_.mixed_ref, ...), custom_call_target="tpu_custom_call" | custom-call | flops 1610612736 | bytes 11010048 | tf_op jit(solution)/shard_map/middle_norm/pallas_call | solution.py:425
  218.4 23.0 %feed.1 = (bf16[768,1024]{1,0:T(8,128)(2,1)}, bf16[4,768,1024]{2,1,0:T(8,128)(2,1)}, bf16[4,768,1024]{2,1,0:T(8,128)(2,1)}) custom-call(bf16[4,1,128,1024]{3,2,1,0:T(8,128)(2,1)} %copy-done.22, bf16[4,1,128,1024]{3,2,1,0:T(8,128)(2,1)} %collective-permute-done.26.refs_1_, bf16[4,1,128,1024]{3,2,1,0:T(8,128)(2,1)} %copy-done.24, ...), custom_call_target="tpu_custom_call" | custom-call | flops 12884901888 | bytes 16777216 | tf_op jit(solution)/shard_map/feed/pallas_call | solution.py:504
  241.4 6.9 %wide_grad.4 = (bf16[2,512,1024]{2,1,0:T(8,128)(2,1)}, bf16[2,512,1024]{2,1,0:T(8,128)(2,1)}) custom-call(bf16[1024,768]{1,0:T(8,128)(2,1)} %get-tuple-element.587.a_ref, bf16[4,768,1024]{2,1,0:T(8,128)(2,1)} %get-tuple-element.588.b_ref), custom_call_target="tpu_custom_call" | custom-call | flops 3221225472 | bytes 8388608 | tf_op jit(solution)/shard_map/wide_grad/pallas_call | solution.py:605
  251.2 6.8 %wide_grad.5 = (bf16[2,512,1024]{2,1,0:T(8,128)(2,1)}, bf16[2,512,1024]{2,1,0:T(8,128)(2,1)}) custom-call(bf16[1024,768]{1,0:T(8,128)(2,1)} %get-tuple-element.587.a_ref, bf16[4,768,1024]{2,1,0:T(8,128)(2,1)} %get-tuple-element.588.b_ref), custom_call_target="tpu_custom_call" | custom-call | flops 3221225472 | bytes 8388608 | tf_op jit(solution)/shard_map/wide_grad/pallas_call | solution.py:605
  264.4 7.6 %collective-permute-start.39 = (bf16[384,1024]{1,0:T(8,128)(2,1)}, bf16[384,1024]{1,0:T(8,128)(2,1)}, u32[]{:S(2)}, u32[]{:S(2)}) collective-permute-start(bf16[384,1024]{1,0:T(8,128)(2,1)} %slice_bitcast_fusion.2), channel_id=1, source_target_pairs={{0,0},{2,1},{4,2},{6,3},{1,4},{3,5},{5,6},{7,7},{8,8},{10,9},{12,1... | collective-permute-start | bytes 2359304 | tf_op jit(solution)/shard_map/ppermute | solution.py:859
  273.6 26.3 %feed_back.1 = (bf16[4,768,1024]{2,1,0:T(8,128)(2,1)}, f32[768,1024]{1,0:T(8,128)}, bf16[768,1024]{1,0:T(8,128)(2,1)}, bf16[1024,768]{1,0:T(8,128)(2,1)}, f32[2,1024]{1,0:T(2,128)}) custom-call(bf16[4,1,128,1024]{3,2,1,0:T(8,128)(2,1)} %copy-done.22, bf16[4,1,128,1024]{3,2,1,0:T(8,128)(2,1)} %collective-permute-done.26.refs_1_, ...), custom_call_target="tpu_custom_call" | custom-call | flops 12884901888 | bytes 16777216 | tf_op jit(solution)/shard_map/feed_back/pallas_call | solution.py:562
  306.3 6.9 %wide_grad.6 = (bf16[2,512,1024]{2,1,0:T(8,128)(2,1)}, bf16[2,512,1024]{2,1,0:T(8,128)(2,1)}) custom-call(bf16[1024,768]{1,0:T(8,128)(2,1)} %get-tuple-element.608.a_ref, bf16[4,768,1024]{2,1,0:T(8,128)(2,1)} %get-tuple-element.609.b_ref), custom_call_target="tpu_custom_call" | custom-call | flops 3221225472 | bytes 8388608 | tf_op jit(solution)/shard_map/wide_grad/pallas_call | solution.py:605
  313.7 5.0 project.5.refs_7_
  318.7 6.9 %wide_grad.7 = (bf16[2,512,1024]{2,1,0:T(8,128)(2,1)}, bf16[2,512,1024]{2,1,0:T(8,128)(2,1)}) custom-call(bf16[1024,768]{1,0:T(8,128)(2,1)} %get-tuple-element.608.a_ref, bf16[4,768,1024]{2,1,0:T(8,128)(2,1)} %get-tuple-element.609.b_ref), custom_call_target="tpu_custom_call" | custom-call | flops 3221225472 | bytes 8388608 | tf_op jit(solution)/shard_map/wide_grad/pallas_call | solution.py:605
  332.4 17.5 %attend_back.4 = (bf16[768,256]{1,0:T(8,128)(2,1)}, bf16[2,768,256]{2,1,0:T(8,128)(2,1)}, bf16[2,768,256]{2,1,0:T(8,128)(2,1)}) custom-call(bf16[1,768,1024]{2,1,0:T(8,128)(2,1)} %project.4.q_ref, bf16[2,768,1024]{2,1,0:T(8,128)(2,1)} %project.3.refs_0_.refs_2_, bf16[2,768,1024]{2,1,0:T(8,128)(2,1)} %collective-permute-done.22.refs_1_.refs_3_, ...), custom_call_target="tpu_custom_call" | custom-call | flops 12079595520 | bytes 6291456 | tf_op jit(solution)/shard_map/attend_back/pallas_call | solution.py:376
  361.4 17.4 %attend_back.5 = (bf16[768,256]{1,0:T(8,128)(2,1)}, bf16[2,768,256]{2,1,0:T(8,128)(2,1)}, bf16[2,768,256]{2,1,0:T(8,128)(2,1)}) custom-call(bf16[1,768,1024]{2,1,0:T(8,128)(2,1)} %project.4.q_ref, bf16[2,768,1024]{2,1,0:T(8,128)(2,1)} %project.3.refs_0_.refs_2_, bf16[2,768,1024]{2,1,0:T(8,128)(2,1)} %collective-permute-done.22.refs_1_.refs_3_, ...), custom_call_target="tpu_custom_call" | custom-call | flops 12079595520 | bytes 6291456 | tf_op jit(solution)/shard_map/attend_back/pallas_call | solution.py:376
  389.2 17.4 %attend_back.6 = (bf16[768,256]{1,0:T(8,128)(2,1)}, bf16[2,768,256]{2,1,0:T(8,128)(2,1)}, bf16[2,768,256]{2,1,0:T(8,128)(2,1)}) custom-call(bf16[1,768,1024]{2,1,0:T(8,128)(2,1)} %project.4.q_ref, bf16[2,768,1024]{2,1,0:T(8,128)(2,1)} %project.3.refs_0_.refs_2_, bf16[2,768,1024]{2,1,0:T(8,128)(2,1)} %collective-permute-done.22.refs_1_.refs_3_, ...), custom_call_target="tpu_custom_call" | custom-call | flops 12079595520 | bytes 6291456 | tf_op jit(solution)/shard_map/attend_back/pallas_call | solution.py:376
  406.5 5.6 %head_grad.4 = (bf16[2,768,256]{2,1,0:T(8,128)(2,1)}, bf16[4,4,128,256]{3,2,1,0:T(8,128)(2,1)}, bf16[4,4,128,256]{3,2,1,0:T(8,128)(2,1)}) custom-call(bf16[1024,768]{1,0:T(8,128)(2,1)} %get-tuple-element.650.n_ref, bf16[1024,768]{1,0:T(8,128)(2,1)} %get-tuple-element.651.g_ref, bf16[768,256]{1,0:T(8,128)(2,1)} %get-tuple-element.554.refs_3_.refs_6_.mixed_ref, ...), custom_call_target="tpu_custom_call" | custom-call | flops 1610612736 | bytes 2097152 | tf_op jit(solution)/shard_map/head_grad/pallas_call | solution.py:639
  415.7 17.3 %attend_back.7 = (bf16[768,256]{1,0:T(8,128)(2,1)}, bf16[2,768,256]{2,1,0:T(8,128)(2,1)}, bf16[2,768,256]{2,1,0:T(8,128)(2,1)}) custom-call(bf16[1,768,1024]{2,1,0:T(8,128)(2,1)} %project.4.q_ref, bf16[2,768,1024]{2,1,0:T(8,128)(2,1)} %project.3.refs_0_.refs_2_, bf16[2,768,1024]{2,1,0:T(8,128)(2,1)} %collective-permute-done.22.refs_1_.refs_3_, ...), custom_call_target="tpu_custom_call" | custom-call | flops 12079595520 | bytes 6291456 | tf_op jit(solution)/shard_map/attend_back/pallas_call | solution.py:376
  433.0 5.7 %head_grad.5 = (bf16[2,768,256]{2,1,0:T(8,128)(2,1)}, bf16[4,4,128,256]{3,2,1,0:T(8,128)(2,1)}, bf16[4,4,128,256]{3,2,1,0:T(8,128)(2,1)}) custom-call(bf16[1024,768]{1,0:T(8,128)(2,1)} %get-tuple-element.650.n_ref, bf16[1024,768]{1,0:T(8,128)(2,1)} %get-tuple-element.651.g_ref, bf16[768,256]{1,0:T(8,128)(2,1)} %get-tuple-element.553.refs_2_.refs_6_.mixed_ref, ...), custom_call_target="tpu_custom_call" | custom-call | flops 1610612736 | bytes 2097152 | tf_op jit(solution)/shard_map/head_grad/pallas_call | solution.py:639
  441.5 5.8 %head_grad.6 = (bf16[2,768,256]{2,1,0:T(8,128)(2,1)}, bf16[4,4,128,256]{3,2,1,0:T(8,128)(2,1)}, bf16[4,4,128,256]{3,2,1,0:T(8,128)(2,1)}) custom-call(bf16[1024,768]{1,0:T(8,128)(2,1)} %get-tuple-element.650.n_ref, bf16[1024,768]{1,0:T(8,128)(2,1)} %get-tuple-element.651.g_ref, bf16[768,256]{1,0:T(8,128)(2,1)} %get-tuple-element.552.refs_1_.refs_6_.mixed_ref, ...), custom_call_target="tpu_custom_call" | custom-call | flops 1610612736 | bytes 2097152 | tf_op jit(solution)/shard_map/head_grad/pallas_call | solution.py:639
  452.4 11.5 %first_back.1 = (bf16[768,1024]{1,0:T(8,128)(2,1)}, f32[2,1024]{1,0:T(2,128)}) custom-call(bf16[768,1024]{1,0:T(8,128)(2,1)} %get-tuple-element.550.x_ref, f32[768,1024]{1,0:T(8,128)} %get-tuple-element.718.gmid_ref, f32[1,1024]{1,0:T(1,128)} %get-tuple-element.898.refs_2_.gain_ref, bf16[768,256]{1,0:T(8,128)(2,1)} %get-tuple-element.719.refs_0_.dq_ref, ...), custom_call_target="tpu_custom_call" | custom-call | flops 4831838208 | bytes 9437184 | tf_op jit(solution)/shard_map/first_back/pallas_call | solution.py:689
  473.3 5.7 %head_grad.7 = (bf16[2,768,256]{2,1,0:T(8,128)(2,1)}, bf16[4,4,128,256]{3,2,1,0:T(8,128)(2,1)}, bf16[4,4,128,256]{3,2,1,0:T(8,128)(2,1)}) custom-call(bf16[1024,768]{1,0:T(8,128)(2,1)} %get-tuple-element.650.n_ref, bf16[1024,768]{1,0:T(8,128)(2,1)} %get-tuple-element.651.g_ref, bf16[768,256]{1,0:T(8,128)(2,1)} %get-tuple-element.551.refs_0_.refs_6_.mixed_ref, ...), custom_call_target="tpu_custom_call" | custom-call | flops 1610612736 | bytes 2097152 | tf_op jit(solution)/shard_map/head_grad/pallas_call | solution.py:639
  487.0 7.6 %collective-permute-done.70 = bf16[1,4,128,256]{3,2,1,0:T(8,128)(2,1)} collective-permute-done((bf16[1,4,128,256]{3,2,1,0:T(8,128)(2,1)}, bf16[1,4,128,256]{3,2,1,0:T(8,128)(2,1)}, u32[]{:S(2)}, u32[]{:S(2)}) %collective-permute-start.70) | collective-permute-done | bytes 262176 | tf_op jit(solution)/shard_map/ppermute | solution.py:49
  510.6 13.6 %collective-permute-done.75 = bf16[4,128,256]{2,1,0:T(8,128)(2,1)S(1)} collective-permute-done((bf16[4,128,256]{2,1,0:T(8,128)(2,1)S(1)}, bf16[4,128,256]{2,1,0:T(8,128)(2,1)S(1)}, u32[]{:S(2)}, u32[]{:S(2)}) %collective-permute-start.75) | collective-permute-done | bytes 262176 | tf_op jit(solution)/shard_map/ppermute | solution.py:53
  (425 shorter events, 214.1 us)
Async XLA Ops:
  27.0 34.1 %collective-permute-start.10 = (bf16[384,1024]{1,0:T(8,128)(2,1)S(1)}, bf16[384,1024]{1,0:T(8,128)(2,1)S(1)}, u32[]{:S(2)}, u32[]{:S(2)}) collective-permute-start(bf16[384,1024]{1,0:T(8,128)(2,1)S(1)} %copy-done.44), channel_id=1, source_target_pairs={{0,0},{1,2},{2,4},{3,6},{4,1},{5,3},{6,5},{7,7},{8,8},{9,10},{10,1... | collective-permute-start | bytes 2359304 | tf_op jit(solution)/shard_map/ppermute | solution.py:856
  62.1 25.7 %collective-permute-start.11 = (bf16[2,4,2,128,256]{4,3,2,1,0:T(8,128)(2,1)S(1)}, bf16[2,4,2,128,256]{4,3,2,1,0:T(8,128)(2,1)S(1)}, u32[]{:S(2)}, u32[]{:S(2)}) collective-permute-start(bf16[2,4,2,128,256]{4,3,2,1,0:T(8,128)(2,1)S(1)} %pad_maximum_fusion.4), channel_id=1, source_target_pairs={{0,8},{4,12},{8,0},{12,4},{16,24},{20,28},{24,16},{28,20},{1,9},{5... | collective-permute-start | bytes 3145736 | tf_op jit(solution)/shard_map/ppermute | solution.py:49
  62.8 25.9 %collective-permute-start.12 = (bf16[2,4,2,128,256]{4,3,2,1,0:T(8,128)(2,1)S(1)}, bf16[2,4,2,128,256]{4,3,2,1,0:T(8,128)(2,1)S(1)}, u32[]{:S(2)}, u32[]{:S(2)}) collective-permute-start(bf16[2,4,2,128,256]{4,3,2,1,0:T(8,128)(2,1)S(1)} %pad_maximum_fusion.5), channel_id=1, source_target_pairs={{0,16},{4,20},{8,24},{12,28},{16,0},{20,4},{24,8},{28,12},{1,17},{... | collective-permute-start | bytes 3145736 | tf_op jit(solution)/shard_map/ppermute | solution.py:49
  143.0 28.6 %collective-permute-start.24 = (bf16[1,2,128,1024]{3,2,1,0:T(8,128)(2,1)}, bf16[1,2,128,1024]{3,2,1,0:T(8,128)(2,1)S(1)}, u32[]{:S(2)}, u32[]{:S(2)}) collective-permute-start(bf16[1,2,128,1024]{3,2,1,0:T(8,128)(2,1)} %get-tuple-element.848), channel_id=1, source_target_pairs={{0,8},{4,12},{8,0},{12,4},{16,24},{20,28},{24,16},{28,20},{1,9},{5... | collective-permute-start | bytes 1572872 | tf_op jit(solution)/shard_map/ppermute | solution.py:49
  144.2 27.3 %collective-permute-start.25 = (bf16[1,2,128,1024]{3,2,1,0:T(8,128)(2,1)}, bf16[1,2,128,1024]{3,2,1,0:T(8,128)(2,1)S(1)}, u32[]{:S(2)}, u32[]{:S(2)}) collective-permute-start(bf16[1,2,128,1024]{3,2,1,0:T(8,128)(2,1)} %get-tuple-element.846), channel_id=1, source_target_pairs={{0,16},{4,20},{8,24},{12,28},{16,0},{20,4},{24,8},{28,12},{1,17},{... | collective-permute-start | bytes 1572872 | tf_op jit(solution)/shard_map/ppermute | solution.py:49
  146.1 25.5 %collective-permute-start.26 = (bf16[4,1,128,1024]{3,2,1,0:T(8,128)(2,1)S(1)}, bf16[4,1,128,1024]{3,2,1,0:T(8,128)(2,1)}, u32[]{:S(2)}, u32[]{:S(2)}) collective-permute-start(bf16[4,1,128,1024]{3,2,1,0:T(8,128)(2,1)S(1)} %pad_maximum_fusion.6.refs_0_), channel_id=1, source_target_pairs={{0,4},{4,0},{8,12},{12,8},{16,20},{20,16},{24,28},{28,24},{1,5},{5... | collective-permute-start | bytes 3145736 | tf_op jit(solution)/shard_map/ppermute | solution.py:49
  146.3 25.3 %collective-permute-start.27 = (bf16[4,1,128,1024]{3,2,1,0:T(8,128)(2,1)S(1)}, bf16[4,1,128,1024]{3,2,1,0:T(8,128)(2,1)}, u32[]{:S(2)}, u32[]{:S(2)}) collective-permute-start(bf16[4,1,128,1024]{3,2,1,0:T(8,128)(2,1)S(1)} %pad_maximum_fusion.7.refs_2_), channel_id=1, source_target_pairs={{0,4},{4,0},{8,12},{12,8},{16,20},{20,16},{24,28},{28,24},{1,5},{5... | collective-permute-start | bytes 3145736 | tf_op jit(solution)/shard_map/ppermute | solution.py:49
  147.3 24.3 %collective-permute-start.28 = (bf16[384,1024]{1,0:T(8,128)(2,1)S(1)}, bf16[384,1024]{1,0:T(8,128)(2,1)S(1)}, u32[]{:S(2)}, u32[]{:S(2)}) collective-permute-start(bf16[384,1024]{1,0:T(8,128)(2,1)S(1)} %copy-done.42), channel_id=1, source_target_pairs={{0,0},{1,2},{2,4},{3,6},{4,1},{5,3},{6,5},{7,7},{8,8},{9,10},{10,1... | collective-permute-start | bytes 2359304 | tf_op jit(solution)/shard_map/ppermute | solution.py:856
  172.6 30.7 %collective-permute-start.29 = (bf16[2,2,128,1024]{3,2,1,0:T(8,128)(2,1)S(1)}, bf16[2,2,128,1024]{3,2,1,0:T(8,128)(2,1)S(1)}, u32[]{:S(2)}, u32[]{:S(2)}) collective-permute-start(bf16[2,2,128,1024]{3,2,1,0:T(8,128)(2,1)S(1)} %pad_maximum_fusion.8), channel_id=1, source_target_pairs={{0,8},{4,12},{8,0},{12,4},{16,24},{20,28},{24,16},{28,20},{1,9},{5... | collective-permute-start | bytes 3145736 | tf_op jit(solution)/shard_map/ppermute | solution.py:49
  175.3 28.0 %collective-permute-start.30 = (bf16[2,2,128,1024]{3,2,1,0:T(8,128)(2,1)}, bf16[2,2,128,1024]{3,2,1,0:T(8,128)(2,1)}, u32[]{:S(2)}, u32[]{:S(2)}) collective-permute-start(bf16[2,2,128,1024]{3,2,1,0:T(8,128)(2,1)} %pad_maximum_fusion.9), channel_id=1, source_target_pairs={{0,16},{4,20},{8,24},{12,28},{16,0},{20,4},{24,8},{28,12},{1,17},{... | collective-permute-start | bytes 3145736 | tf_op jit(solution)/shard_map/ppermute | solution.py:49
  175.9 27.4 %collective-permute-start.31 = (bf16[4,1,128,1024]{3,2,1,0:T(8,128)(2,1)S(1)}, bf16[4,1,128,1024]{3,2,1,0:T(8,128)(2,1)}, u32[]{:S(2)}, u32[]{:S(2)}) collective-permute-start(bf16[4,1,128,1024]{3,2,1,0:T(8,128)(2,1)S(1)} %pad_maximum_fusion.10.refs_4_), channel_id=1, source_target_pairs={{0,4},{4,0},{8,12},{12,8},{16,20},{20,16},{24,28},{28,24},{1,5},{5... | collective-permute-start | bytes 3145736 | tf_op jit(solution)/shard_map/ppermute | solution.py:49
  176.6 26.8 %collective-permute-start.32 = (bf16[4,1,128,1024]{3,2,1,0:T(8,128)(2,1)S(1)}, bf16[4,1,128,1024]{3,2,1,0:T(8,128)(2,1)}, u32[]{:S(2)}, u32[]{:S(2)}) collective-permute-start(bf16[4,1,128,1024]{3,2,1,0:T(8,128)(2,1)S(1)} %pad_maximum_fusion.11.refs_6_), channel_id=1, source_target_pairs={{0,4},{4,0},{8,12},{12,8},{16,20},{20,16},{24,28},{28,24},{1,5},{5... | collective-permute-start | bytes 3145736 | tf_op jit(solution)/shard_map/ppermute | solution.py:49
  176.7 26.6 %collective-permute-start.33 = (bf16[384,1024]{1,0:T(8,128)(2,1)}, bf16[384,1024]{1,0:T(8,128)(2,1)S(1)}, u32[]{:S(2)}, u32[]{:S(2)}) collective-permute-start(bf16[384,1024]{1,0:T(8,128)(2,1)} %pack_features.7), channel_id=1, source_target_pairs={{0,2},{1,0},{2,6},{3,4},{4,3},{5,1},{6,7},{7,5},{8,10},{9,8},{10,1... | collective-permute-start | bytes 2359304 | tf_op jit(solution)/shard_map/ppermute | solution.py:856
  259.5 40.4 %collective-permute-start.37 = (bf16[2,4,128,1024]{3,2,1,0:T(8,128)(2,1)}, bf16[2,4,128,1024]{3,2,1,0:T(8,128)(2,1)S(1)}, u32[]{:S(2)}, u32[]{:S(2)}) collective-permute-start(bf16[2,4,128,1024]{3,2,1,0:T(8,128)(2,1)} %bitcast.314), channel_id=1, source_target_pairs={{0,4},{4,0},{8,12},{12,8},{16,20},{20,16},{24,28},{28,24},{1,5},{5... | collective-permute-start | bytes 6291464 | tf_op jit(solution)/shard_map/ppermute | solution.py:49
  263.1 36.8 %collective-permute-start.38 = (bf16[2,2,128,1024]{3,2,1,0:T(8,128)(2,1)}, bf16[2,2,128,1024]{3,2,1,0:T(8,128)(2,1)}, u32[]{:S(2)}, u32[]{:S(2)}) collective-permute-start(bf16[2,2,128,1024]{3,2,1,0:T(8,128)(2,1)} %add_convert_fusion.7), channel_id=1, source_target_pairs={{0,8},{4,12},{8,0},{12,4},{16,24},{20,28},{24,16},{28,20},{1,9},{5... | collective-permute-start | bytes 3145736 | tf_op jit(solution)/shard_map/ppermute | solution.py:49
  264.4 35.4 %collective-permute-start.39 = (bf16[384,1024]{1,0:T(8,128)(2,1)}, bf16[384,1024]{1,0:T(8,128)(2,1)}, u32[]{:S(2)}, u32[]{:S(2)}) collective-permute-start(bf16[384,1024]{1,0:T(8,128)(2,1)} %slice_bitcast_fusion.2), channel_id=1, source_target_pairs={{0,0},{2,1},{4,2},{6,3},{1,4},{3,5},{5,6},{7,7},{8,8},{10,9},{12,1... | collective-permute-start | bytes 2359304 | tf_op jit(solution)/shard_map/ppermute | solution.py:859
  301.4 24.2 %collective-permute-start.40 = (bf16[2,2,128,1024]{3,2,1,0:T(8,128)(2,1)S(1)}, bf16[2,2,128,1024]{3,2,1,0:T(8,128)(2,1)}, u32[]{:S(2)}, u32[]{:S(2)}) collective-permute-start(bf16[2,2,128,1024]{3,2,1,0:T(8,128)(2,1)S(1)} %add_convert_fusion.6), channel_id=1, source_target_pairs={{0,8},{4,12},{8,0},{12,4},{16,24},{20,28},{24,16},{28,20},{1,9},{5... | collective-permute-start | bytes 3145736 | tf_op jit(solution)/shard_map/ppermute | solution.py:49
  325.6 28.6 %collective-permute-start.42 = (bf16[2,4,128,1024]{3,2,1,0:T(8,128)(2,1)}, bf16[2,4,128,1024]{3,2,1,0:T(8,128)(2,1)S(1)}, u32[]{:S(2)}, u32[]{:S(2)}) collective-permute-start(bf16[2,4,128,1024]{3,2,1,0:T(8,128)(2,1)} %bitcast.313), channel_id=1, source_target_pairs={{0,4},{4,0},{8,12},{12,8},{16,20},{20,16},{24,28},{28,24},{1,5},{5... | collective-permute-start | bytes 6291464 | tf_op jit(solution)/shard_map/ppermute | solution.py:49
  325.7 28.5 %collective-permute-start.43 = (bf16[2,4,128,1024]{3,2,1,0:T(8,128)(2,1)}, bf16[2,4,128,1024]{3,2,1,0:T(8,128)(2,1)S(1)}, u32[]{:S(2)}, u32[]{:S(2)}) collective-permute-start(bf16[2,4,128,1024]{3,2,1,0:T(8,128)(2,1)} %bitcast.315), channel_id=1, source_target_pairs={{0,4},{4,0},{8,12},{12,8},{16,20},{20,16},{24,28},{28,24},{1,5},{5... | collective-permute-start | bytes 6291464 | tf_op jit(solution)/shard_map/ppermute | solution.py:49
  328.6 25.5 %collective-permute-start.44 = (bf16[2,1,128,1024]{3,2,1,0:T(8,128)(2,1)}, bf16[2,1,128,1024]{3,2,1,0:T(8,128)(2,1)}, u32[]{:S(2)}, u32[]{:S(2)}) collective-permute-start(bf16[2,1,128,1024]{3,2,1,0:T(8,128)(2,1)} %get-tuple-element.811), channel_id=1, source_target_pairs={{0,16},{4,20},{8,24},{12,28},{16,0},{20,4},{24,8},{28,12},{1,17},{... | collective-permute-start | bytes 1572872 | tf_op jit(solution)/shard_map/ppermute | solution.py:49
  329.2 25.0 %collective-permute-start.45 = (bf16[128,1024]{1,0:T(8,128)(2,1)S(1)}, bf16[128,1024]{1,0:T(8,128)(2,1)}, u32[]{:S(2)}, u32[]{:S(2)}) collective-permute-start(bf16[128,1024]{1,0:T(8,128)(2,1)S(1)} %fusion.12), channel_id=1, source_target_pairs={{0,3},{1,0},{2,1},{3,2},{4,7},{5,4},{6,5},{7,6},{8,11},{9,8},{10,9... | collective-permute-start | bytes 786440 | tf_op jit(solution)/shard_map/ppermute | solution.py:53
  355.8 24.1 %collective-permute-start.47 = (bf16[2,2,128,1024]{3,2,1,0:T(8,128)(2,1)}, bf16[2,2,128,1024]{3,2,1,0:T(8,128)(2,1)S(1)}, u32[]{:S(2)}, u32[]{:S(2)}) collective-permute-start(bf16[2,2,128,1024]{3,2,1,0:T(8,128)(2,1)} %add_convert_fusion.2), channel_id=1, source_target_pairs={{0,8},{4,12},{8,0},{12,4},{16,24},{20,28},{24,16},{28,20},{1,9},{5... | collective-permute-start | bytes 3145736 | tf_op jit(solution)/shard_map/ppermute | solution.py:49
  381.7 30.4 %collective-permute-start.51 = (bf16[2,1,128,1024]{3,2,1,0:T(8,128)(2,1)S(1)}, bf16[2,1,128,1024]{3,2,1,0:T(8,128)(2,1)S(1)}, u32[]{:S(2)}, u32[]{:S(2)}) collective-permute-start(bf16[2,1,128,1024]{3,2,1,0:T(8,128)(2,1)S(1)} %get-tuple-element.809), channel_id=1, source_target_pairs={{0,8},{4,12},{8,0},{12,4},{16,24},{20,28},{24,16},{28,20},{1,9},{5... | collective-permute-start | bytes 1572872 | tf_op jit(solution)/shard_map/ppermute | solution.py:49
  383.4 28.8 %collective-permute-start.52 = (bf16[2,1,128,1024]{3,2,1,0:T(8,128)(2,1)S(1)}, bf16[2,1,128,1024]{3,2,1,0:T(8,128)(2,1)S(1)}, u32[]{:S(2)}, u32[]{:S(2)}) collective-permute-start(bf16[2,1,128,1024]{3,2,1,0:T(8,128)(2,1)S(1)} %get-tuple-element.807), channel_id=1, source_target_pairs={{0,16},{4,20},{8,24},{12,28},{16,0},{20,4},{24,8},{28,12},{1,17},{... | collective-permute-start | bytes 1572872 | tf_op jit(solution)/shard_map/ppermute | solution.py:49
  386.1 26.1 %collective-permute-start.53 = (bf16[128,1024]{1,0:T(8,128)(2,1)S(1)}, bf16[128,1024]{1,0:T(8,128)(2,1)S(1)}, u32[]{:S(2)}, u32[]{:S(2)}) collective-permute-start(bf16[128,1024]{1,0:T(8,128)(2,1)S(1)} %fusion.10), channel_id=1, source_target_pairs={{0,3},{1,0},{2,1},{3,2},{4,7},{5,4},{6,5},{7,6},{8,11},{9,8},{10,9... | collective-permute-start | bytes 786440 | tf_op jit(solution)/shard_map/ppermute | solution.py:53
  412.2 26.5 %collective-permute-start.55 = (bf16[1,4,4,128,256]{4,3,2,1,0:T(8,128)(2,1)}, bf16[1,4,4,128,256]{4,3,2,1,0:T(8,128)(2,1)S(1)}, u32[]{:S(2)}, u32[]{:S(2)}) collective-permute-start(bf16[1,4,4,128,256]{4,3,2,1,0:T(8,128)(2,1)} %bitcast.318), channel_id=1, source_target_pairs={{0,4},{4,0},{8,12},{12,8},{16,20},{20,16},{24,28},{28,24},{1,5},{5... | collective-permute-start | bytes 3145736 | tf_op jit(solution)/shard_map/ppermute | solution.py:49
  412.9 25.8 %collective-permute-start.56 = (bf16[128,1024]{1,0:T(8,128)(2,1)S(1)}, bf16[128,1024]{1,0:T(8,128)(2,1)S(1)}, u32[]{:S(2)}, u32[]{:S(2)}) collective-permute-start(bf16[128,1024]{1,0:T(8,128)(2,1)S(1)} %fusion.13), channel_id=1, source_target_pairs={{0,3},{1,0},{2,1},{3,2},{4,7},{5,4},{6,5},{7,6},{8,11},{9,8},{10,9... | collective-permute-start | bytes 786440 | tf_op jit(solution)/shard_map/ppermute | solution.py:53
  413.2 25.5 %collective-permute-start.57 = (bf16[128,1024]{1,0:T(8,128)(2,1)S(1)}, bf16[128,1024]{1,0:T(8,128)(2,1)S(1)}, u32[]{:S(2)}, u32[]{:S(2)}) collective-permute-start(bf16[128,1024]{1,0:T(8,128)(2,1)S(1)} %get-tuple-element.839), channel_id=1, source_target_pairs={{0,2},{1,3},{2,0},{3,1},{4,6},{5,7},{6,4},{7,5},{8,10},{9,11},{10,... | collective-permute-start | bytes 786440 | tf_op jit(solution)/shard_map/ppermute | solution.py:53
  413.7 25.1 %collective-permute-start.58 = (bf16[128,1024]{1,0:T(8,128)(2,1)S(1)}, bf16[128,1024]{1,0:T(8,128)(2,1)S(1)}, u32[]{:S(2)}, u32[]{:S(2)}) collective-permute-start(bf16[128,1024]{1,0:T(8,128)(2,1)S(1)} %get-tuple-element.838), channel_id=1, source_target_pairs={{0,1},{1,2},{2,3},{3,0},{4,5},{5,6},{6,7},{7,4},{8,9},{9,10},{10,1... | collective-permute-start | bytes 786440 | tf_op jit(solution)/shard_map/ppermute | solution.py:53
  469.8 24.8 %collective-permute-start.73 = (bf16[384,1024]{1,0:T(8,128)(2,1)S(1)}, bf16[384,1024]{1,0:T(8,128)(2,1)}, u32[]{:S(2)}, u32[]{:S(2)}) collective-permute-start(bf16[384,1024]{1,0:T(8,128)(2,1)S(1)} %slice.520), channel_id=1, source_target_pairs={{0,0},{2,1},{4,2},{6,3},{1,4},{3,5},{5,6},{7,7},{8,8},{10,9},{12,1... | collective-permute-start | bytes 2359304 | tf_op jit(solution)/shard_map/ppermute | solution.py:859
  494.6 29.6 %collective-permute-start.74 = (bf16[1,4,4,128,256]{4,3,2,1,0:T(8,128)(2,1)}, bf16[1,4,4,128,256]{4,3,2,1,0:T(8,128)(2,1)}, u32[]{:S(2)}, u32[]{:S(2)}) collective-permute-start(bf16[1,4,4,128,256]{4,3,2,1,0:T(8,128)(2,1)} %bitcast.317), channel_id=1, source_target_pairs={{0,4},{4,0},{8,12},{12,8},{16,20},{20,16},{24,28},{28,24},{1,5},{5... | collective-permute-start | bytes 3145736 | tf_op jit(solution)/shard_map/ppermute | solution.py:49
  497.2 27.0 %collective-permute-start.76 = (bf16[384,1024]{1,0:T(8,128)(2,1)S(1)}, bf16[384,1024]{1,0:T(8,128)(2,1)}, u32[]{:S(2)}, u32[]{:S(2)}) collective-permute-start(bf16[384,1024]{1,0:T(8,128)(2,1)S(1)} %slice_bitcast_fusion), channel_id=1, source_target_pairs={{2,0},{0,1},{6,2},{4,3},{3,4},{1,5},{7,6},{5,7},{10,8},{8,9},{14,1... | collective-permute-start | bytes 2359304 | tf_op jit(solution)/shard_map/ppermute | solution.py:859
  (127 other events, 1406.5 us)

commit v4 on v3

--- a/solution.py
+++ b/solution.py
@@ -69,14 +69,13 @@
         if self.order[name]:
             self.queue[self.order[name][0]].append(name)
 
-    def launch(self, chip=1):
+    def launch(self, chip=1, names=("",)):
         for bit, tasks in self.queue.items():
-            for _ in range(chip):
-                if tasks:
-                    name = tasks.pop(0)
-                    values = [value for _, value in self.pieces[name]]
-                    value = values[0][None] if len(values) == 1 else jnp.stack(values)
-                    self.flying["chip", name] = swap(value, bit, self.nd)
+            for name in [name for name in tasks if name.startswith(names)][:chip]:
+                tasks.remove(name)
+                values = [value for _, value in self.pieces[name]]
+                value = values[0][None] if len(values) == 1 else jnp.stack(values)
+                self.flying["chip", name] = swap(value, bit, self.nd)
 
     def fly(self, name, value):
         self.flying["kept", name] = value
@@ -242,31 +241,43 @@
     )(*chunks)
 
 
-def proj_kernel(in_ref, own_ref, other_ref, out_ref):
+def each_k(refs):
+    return [(ref, n) for ref in refs for n in range(ref.shape[1])]
+
+
+def proj_kernel(parts, in_ref, *refs):
+    owns, others, out_ref = refs[:parts], refs[parts : 2 * parts], refs[-1]
     value = in_ref[...]
     half = value.shape[1] // 2
-    wide = own_ref.shape[-1]
-    for k in range(own_ref.shape[1]):
-        first = own_ref[:, k, 0].reshape(half, wide)
-        second = other_ref[:, k, 0].reshape(half, wide)
+    wide = owns[0].shape[-1]
+    for k, ((own, n), (other, _)) in enumerate(zip(each_k(owns), each_k(others))):
+        first = own[:, n, 0].reshape(half, wide)
+        second = other[:, n, 0].reshape(half, wide)
         total = dot_nn(value[:, :half], first) + dot_nn(value[:, half:], second)
         out_ref[0, :, k * wide : (k + 1) * wide] = total.astype(BF16)
 
 
-def project(value, own, other, start, count):
+def head_spec(array, count, index_map):
+    chips, ks, _, deep, wide = array.shape
+    return pl.BlockSpec((chips, ks, count, deep, wide), index_map)
+
+
+def project(value, weights, start, count):
     rows, width = value.shape
-    chips, nm, _, deep, wide = own.shape
-    spec = pl.BlockSpec((chips, nm, 1, deep, wide), lambda i: (0, 0, start + i, 0, 0))
+    wide = weights[0][0].shape[-1]
+    nm = sum(array.shape[1] for array in weights[0])
+    arrays = [*weights[0], *weights[1]]
     return pl.pallas_call(
-        proj_kernel,
+        functools.partial(proj_kernel, len(weights[0])),
         grid=(count,),
-        in_specs=[pl.BlockSpec((rows, width), lambda i: (0, 0)), spec, spec],
+        in_specs=[pl.BlockSpec((rows, width), lambda i: (0, 0))]
+        + [head_spec(array, 1, lambda i: (0, 0, start + i, 0, 0)) for array in arrays],
         out_specs=pl.BlockSpec((1, rows, nm * wide), lambda i: (i, 0, 0)),
         out_shape=SHAPE((count, rows, nm * wide), BF16),
         compiler_params=params(),
         cost_estimate=cost(2 * count * rows * width * nm * wide, 2 * count * rows * width),
         name="project",
-    )(value, own, other)
+    )(value, *arrays)
 
 
 def attend_kernel(parts, q_ref, *refs):
@@ -396,16 +407,16 @@
     )(query, *kvs, *kvs, bias, lse, mixed, grad)
 
 
-def middle_kernel(nm, x_ref, *refs):
-    mixed_refs = refs[:nm]
-    own_ref, other_ref, gain_ref, bias_ref, mid_ref, out_ref, flip_ref = refs[nm:]
+def middle_kernel(nm, parts, x_ref, *refs):
+    mixed_refs, refs = refs[:nm], refs[nm:]
+    weights = refs[:parts], refs[parts : 2 * parts]
+    gain_ref, bias_ref, mid_ref, out_ref, flip_ref = refs[2 * parts :]
     half = x_ref.shape[1] // 2
-    wide = own_ref.shape[-1]
     sides = []
-    for ref in (own_ref, other_ref):
+    for side in weights:
         total = 0.0
-        for k in range(nm):
-            total = total + dot_nt(mixed_refs[k][...], ref[:, k, 0].reshape(half, wide))
+        for k, (ref, n) in enumerate(each_k(side)):
+            total = total + dot_nt(mixed_refs[k][...], ref[:, n, 0].reshape(half, -1))
         sides.append(total)
     middle = x_ref[...].astype(F32) + jnp.concatenate(sides, axis=1)
     mid_ref[...] = middle
@@ -415,19 +426,20 @@
     flip_ref[...] = normed.T
 
 
-def middle_norm(x, mixed, own, other, which, gain, bias):
+def middle_norm(x, mixed, weights, which, gain, bias):
     rows, width = x.shape
-    chips, nm, _, deep, wide = own.shape
+    nm, wide = len(mixed), mixed[0].shape[1]
     block = row_block(rows)
     vector = pl.BlockSpec((1, width), lambda i: (0, 0))
-    spec = pl.BlockSpec((chips, nm, 1, deep, wide), lambda i: (0, 0, which, 0, 0))
     line = pl.BlockSpec((block, width), lambda i: (i, 0))
+    arrays = [*weights[0], *weights[1]]
     return pl.pallas_call(
-        functools.partial(middle_kernel, nm),
+        functools.partial(middle_kernel, nm, len(weights[0])),
         grid=(rows // block,),
         in_specs=[line]
         + [pl.BlockSpec((block, wide), lambda i: (i, 0))] * nm
-        + [spec, spec, vector, vector],
+        + [head_spec(array, 1, lambda i: (0, 0, which, 0, 0)) for array in arrays]
+        + [vector, vector],
         out_specs=[line, line, pl.BlockSpec((width, block), lambda i: (0, i))],
         out_shape=[
             SHAPE((rows, width), F32),
@@ -437,42 +449,53 @@
         compiler_params=params(),
         cost_estimate=cost(2 * rows * width * nm * wide, 14 * x.size),
         name="middle_norm",
-    )(x, *mixed, own, other, gain, bias)
-
-
-def load_weights(sizes, refs, held, sems):
+    )(x, *mixed, *arrays, gain, bias)
+
+
+def load_weights(firsts, sizes, index_ref, refs, held, sems):
     step = pl.program_id(0)
-    nm = sum(sizes)
-    copies, k, refs = {}, 0, list(refs)
+    nm = firsts + sum(sizes)
+    chips = held.shape[2]
+    copies, refs = {k: [] for k in range(nm)}, list(refs)
+
+    def add(k, source, w, side, n, sem):
+        copies[k].append(
+            pltpu.make_async_copy(source, held.at[w, 2 * k + side, n], sems.at[w, 2 * k + side, sem])
+        )
+
+    for k in range(firsts):
+        ref = refs.pop(0)
+        for w in range(2):
+            for side in range(2):
+                for n in range(chips):
+                    add(k, ref.at[index_ref[side * chips + n], w], w, side, n, n)
+    k = firsts
     for size in sizes:
         sides = [refs.pop(0) for _ in range(4)]
         for i in range(size):
             for n, ref in enumerate(sides):
-                w, side = n // 2, n % 2
-                copies[w, 2 * k + side] = pltpu.make_async_copy(
-                    ref.at[:, i], held.at[w, 2 * k + side], sems.at[w, 2 * k + side]
-                )
+                add(k, ref.at[:, i], n // 2, n % 2, slice(None), 0)
             k += 1
 
     @pl.when(step == 0)
     def _():
-        for copy in copies.values():
-            copy.start()
+        for k in range(nm):
+            for copy in copies[k]:
+                copy.start()
 
     for k in range(nm):
 
         @pl.when(step == k)
         def _():
-            for w in range(2):
-                for side in range(2):
-                    copies[w, 2 * k + side].wait()
-
-
-def feed_kernel(sizes, *refs):
-    nm, count = sum(sizes), 4 * len(sizes)
+            for copy in copies[k]:
+                copy.wait()
+
+
+def feed_kernel(firsts, sizes, index_ref, *refs):
+    nm, count = firsts + sum(sizes), firsts + 4 * len(sizes)
     in_ref, mid_ref, out_ref, act_ref, slope_ref, held, acc, sems = refs[count:]
     step = pl.program_id(0)
-    load_weights(sizes, refs[:count], held, sems)
+    load_weights(firsts, sizes, index_ref, refs[:count], held, sems)
     half = in_ref.shape[1] // 2
     up = [held[0, 2 * step + side].reshape(half, -1) for side in range(2)]
     down = [held[1, 2 * step + side].reshape(half, -1) for side in range(2)]
@@ -495,35 +518,38 @@
         out_ref[...] = acc[...].astype(BF16)
 
 
-def feed(normed, middle, sizes, weights):
+def feed(normed, middle, index, firsts, sizes, weights):
     rows, width = normed.shape
-    nm = sum(sizes)
-    chips, _, deep, hidden = weights[0].shape
+    nm = firsts + sum(sizes)
+    nd, (deep, hidden) = index.shape[0], weights[0].shape[2:]
+    chips = nd // 2
     line = pl.BlockSpec((rows, width), lambda k: (0, 0))
     wide = pl.BlockSpec((1, rows, hidden), lambda k: (k, 0, 0))
     return pl.pallas_call(
-        functools.partial(feed_kernel, sizes),
+        functools.partial(feed_kernel, firsts, sizes),
         grid=(nm,),
-        in_specs=[ANY] * len(weights) + [line, line],
+        in_specs=[pl.BlockSpec(memory_space=pltpu.SMEM)]
+        + [ANY] * len(weights)
+        + [line, line],
         out_specs=[line, wide, wide],
         out_shape=[SHAPE((rows, width), BF16)] + [SHAPE((nm, rows, hidden), BF16)] * 2,
         scratch_shapes=[
             pltpu.VMEM((2, 2 * nm, chips, deep, hidden), BF16),
             pltpu.VMEM((rows, width), F32),
-            pltpu.SemaphoreType.DMA((2, 2 * nm)),
+            pltpu.SemaphoreType.DMA((2, 2 * nm, chips)),
         ],
         compiler_params=params(60),
         cost_estimate=cost(4 * rows * width * nm * hidden, 4 * nm * width * hidden),
         name="feed",
-    )(*weights, normed, middle)
-
-
-def feed_back_kernel(sizes, *refs):
-    nm, count = sum(sizes), 4 * len(sizes)
+    )(index, *weights, normed, middle)
+
+
+def feed_back_kernel(firsts, sizes, index_ref, *refs):
+    nm, count = firsts + sum(sizes), firsts + 4 * len(sizes)
     g_ref, slope_ref, mid_ref, gain_ref = refs[count : count + 4]
     hid_ref, gmid_ref, attn_ref, flip_ref, sums_ref, held, acc, sems = refs[count + 4 :]
     step = pl.program_id(0)
-    load_weights(sizes, refs[:count], held, sems)
+    load_weights(firsts, sizes, index_ref, refs[:count], held, sems)
     half = g_ref.shape[1] // 2
     up = [held[0, 2 * step + side].reshape(half, -1) for side in range(2)]
     down = [held[1, 2 * step + side].reshape(half, -1) for side in range(2)]
@@ -553,16 +579,18 @@
         sums_ref[...] = sums
 
 
-def feed_back(grad, slope, middle, gain, sizes, weights):
+def feed_back(grad, slope, middle, gain, index, firsts, sizes, weights):
     rows, width = grad.shape
-    nm = sum(sizes)
-    chips, _, deep, hidden = weights[0].shape
+    nm = firsts + sum(sizes)
+    nd, (deep, hidden) = index.shape[0], weights[0].shape[2:]
+    chips = nd // 2
     line = pl.BlockSpec((rows, width), lambda k: (0, 0))
     wide = pl.BlockSpec((1, rows, hidden), lambda k: (k, 0, 0))
     return pl.pallas_call(
-        functools.partial(feed_back_kernel, sizes),
+        functools.partial(feed_back_kernel, firsts, sizes),
         grid=(nm,),
-        in_specs=[ANY] * len(weights)
+        in_specs=[pl.BlockSpec(memory_space=pltpu.SMEM)]
+        + [ANY] * len(weights)
         + [line, wide, line, pl.BlockSpec((1, width), lambda k: (0, 0))],
         out_specs=[
             wide,
@@ -581,42 +609,40 @@
         scratch_shapes=[
             pltpu.VMEM((2, 2 * nm, chips, deep, hidden), BF16),
             pltpu.VMEM((rows, width), F32),
-            pltpu.SemaphoreType.DMA((2, 2 * nm)),
+            pltpu.SemaphoreType.DMA((2, 2 * nm, chips)),
         ],
         compiler_params=params(60),
         cost_estimate=cost(4 * rows * width * nm * hidden, 4 * nm * width * hidden),
         name="feed_back",
-    )(*weights, grad, slope, middle, gain)
-
-
-def wide_grad_kernel(a_ref, b_ref, keep_ref, give_ref):
-    half = a_ref.shape[0] // 2
-    value = b_ref[0]
-    keep_ref[0] = dot_nn(a_ref[:half], value).astype(BF16)
-    give_ref[0] = dot_nn(a_ref[half:], value).astype(BF16)
-
-
-def wide_grad(flipped, values, first, count, chips):
+    )(index, *weights, grad, slope, middle, gain)
+
+
+def wide_grad_kernel(index_ref, a_ref, b_ref, out_ref):
+    part = dot_nn(a_ref[...], b_ref[0]).astype(BF16)
+    nd, deep = out_ref.shape[0], out_ref.shape[2]
+    for p in range(nd):
+        out_ref[index_ref[p], 0] = part[p * deep : (p + 1) * deep]
+
+
+def wide_grad(flipped, values, index):
     width, rows = flipped.shape
-    hidden = values.shape[2]
+    nm, _, hidden = values.shape
+    nd = index.shape[0]
     block = min(512, hidden)
-    piece = SHAPE((count, width // 2, hidden), BF16)
-    out = pl.BlockSpec((1, width // 2, block), lambda k, i: (k, 0, i))
-    keep, give = pl.pallas_call(
+    return pl.pallas_call(
         wide_grad_kernel,
-        grid=(count, hidden // block),
+        grid=(nm, hidden // block),
         in_specs=[
+            pl.BlockSpec(memory_space=pltpu.SMEM),
             pl.BlockSpec((width, rows), lambda k, i: (0, 0)),
-            pl.BlockSpec((1, rows, block), lambda k, i: (first + k, 0, i)),
+            pl.BlockSpec((1, rows, block), lambda k, i: (k, 0, i)),
         ],
-        out_specs=[out, out],
-        out_shape=[piece, piece],
+        out_specs=pl.BlockSpec((nd, 1, width // nd, block), lambda k, i: (0, k, 0, i)),
+        out_shape=SHAPE((nd, nm, width // nd, hidden), BF16),
         compiler_params=params(),
-        cost_estimate=cost(2 * count * width * rows * hidden, 4 * count * width * hidden),
+        cost_estimate=cost(2 * nm * width * rows * hidden, 4 * nm * width * hidden),
         name="wide_grad",
-    )(flipped, values)
-    shape = (count, chips, width // 2 // chips, hidden)
-    return keep.reshape(shape), give.reshape(shape)
+    )(index, flipped, values)
 
 
 def head_grad_kernel(
@@ -648,26 +674,24 @@
     return total, keep[None], give[None]
 
 
-def first_back_kernel(nm, x_ref, gmid_ref, gain_ref, *refs):
-    dqs, dkvs, came_ref = refs[:nm], refs[nm : 2 * nm], refs[2 * nm]
-    qo_refs, kv_refs = refs[2 * nm + 1 : 2 * nm + 3], refs[2 * nm + 3 : 2 * nm + 5]
-    out_ref, sums_ref = refs[2 * nm + 5 :]
+def first_back_kernel(nm, parts, x_ref, gmid_ref, gain_ref, *refs):
+    dqs, dkvs, came_ref, refs = refs[:nm], refs[nm : 2 * nm], refs[2 * nm], refs[2 * nm + 1 :]
+    qo = refs[:parts], refs[parts : 2 * parts]
+    kv = refs[2 * parts : 3 * parts], refs[3 * parts : 4 * parts]
+    out_ref, sums_ref = refs[4 * parts :]
     last = (dkvs[0][...].astype(F32) + came_ref[...].astype(F32)).astype(BF16)
     step = pl.program_id(0)
     half = x_ref.shape[1] // 2
-    wide = dqs[0].shape[1]
     sides = []
     for side in range(2):
         total = 0.0
-        for k in range(nm):
-            total = total + dot_nt(dqs[k][...], qo_refs[side][:, k, 0].reshape(half, wide))
+        for k, ((qo_ref, n), (kv_ref, _)) in enumerate(zip(each_k(qo[side]), each_k(kv[side]))):
+            total = total + dot_nt(dqs[k][...], qo_ref[:, n, 0].reshape(half, -1))
             for i in range(2):
                 dkv = dkvs[k][i] if k else last[i]
-                total = total + dot_nt(dkv, kv_refs[side][:, k, i].reshape(half, wide))
+                total = total + dot_nt(dkv, kv_ref[:, n, i].reshape(half, -1))
         sides.append(total)
-    into, sums = norm_back(
-        jnp.concatenate(sides, axis=1), x_ref[...].astype(F32), gain_ref[...]
-    )
+    into, sums = norm_back(jnp.concatenate(sides, axis=1), x_ref[...].astype(F32), gain_ref[...])
     out_ref[...] = (gmid_ref[...] + into).astype(BF16)
 
     @pl.when(step == 0)
@@ -681,28 +705,48 @@
 
 def first_back(x, gmid, gain, dqs, dkvs, came, qo, kv):
     rows, width = x.shape
-    chips, nm, _, deep, wide = qo[0].shape
+    nm, wide = len(dqs), dqs[0].shape[1]
     block = row_block(rows)
     line = pl.BlockSpec((block, width), lambda i: (i, 0))
-    q_spec = pl.BlockSpec((chips, nm, 1, deep, wide), lambda i: (0, 0, 0, 0, 0))
-    kv_spec = pl.BlockSpec((chips, nm, 2, deep, wide), lambda i: (0, 0, 0, 0, 0))
+    still = lambda i: (0, 0, 0, 0, 0)
+    qo_arrays, kv_arrays = [*qo[0], *qo[1]], [*kv[0], *kv[1]]
     return pl.pallas_call(
-        functools.partial(first_back_kernel, nm),
+        functools.partial(first_back_kernel, nm, len(qo[0])),
         grid=(rows // block,),
         in_specs=[line, line, pl.BlockSpec((1, width), lambda i: (0, 0))]
         + [pl.BlockSpec((block, wide), lambda i: (i, 0))] * nm
         + [pl.BlockSpec((2, block, wide), lambda i: (0, i, 0))] * (nm + 1)
-        + [q_spec, q_spec, kv_spec, kv_spec],
+        + [head_spec(array, 1, still) for array in qo_arrays]
+        + [head_spec(array, 2, still) for array in kv_arrays],
         out_specs=[line, pl.BlockSpec((2, width), lambda i: (0, 0))],
         out_shape=[SHAPE((rows, width), BF16), SHAPE((2, width), F32)],
         compiler_params=params(),
         cost_estimate=cost(6 * rows * width * nm * wide, 12 * x.size),
         name="first_back",
-    )(x, gmid, gain, *dqs, *dkvs, came, *qo, *kv)
+    )(x, gmid, gain, *dqs, *dkvs, came, *qo_arrays, *kv_arrays)
 
 
 def add_low(a, b):
     return (a.astype(F32) + b.astype(F32)).astype(BF16)
+
+
+def add_parts_kernel(keep_ref, came_ref, *outs):
+    for n, out in enumerate(outs):
+        out[...] = add_low(keep_ref[:, n + 1], came_ref[:, n + 1])
+
+
+def add_parts(keep, came):
+    count = keep.shape[1] - 1
+    piece = SHAPE(keep.shape[:1] + keep.shape[2:], keep.dtype)
+    return pl.pallas_call(
+        add_parts_kernel,
+        in_specs=[WHOLE] * 2,
+        out_specs=[WHOLE] * count,
+        out_shape=[piece] * count,
+        compiler_params=params(),
+        cost_estimate=cost(0, 6 * keep.size),
+        name="add_parts",
+    )(keep, came)
 
 
 class Scatter:
@@ -710,11 +754,17 @@
         self.nd, self.nm = nd, nm
         self.queue = {1: [], **{bit: [] for bit in bits}, "direct": [], "z": []}
         self.order, self.kept, self.waits, self.flying = {}, {}, {}, {}
-        self.ends, self.came, self.done, self.rings = {}, {}, {}, {}
+        self.ends, self.came, self.done, self.rings, self.joined = {}, {}, {}, {}, {}
 
     def add(self, name, ks, keep, give, order, rings=True):
         self.order[name, tuple(ks)], self.rings[name] = order, rings
         self.push(1, (name, tuple(ks), -1), list(range(0, self.nd, 2)), keep, give)
+
+    def add_line(self, name, value, rings):
+        self.rings[name] = rings
+        for k in range(self.nm):
+            self.ends[name, k] = (value[k],)
+        self.advance(name, self.nm - 1)
 
     def push(self, link, key, places, keep, give):
         self.kept[key], self.waits[key] = (places, keep), give
@@ -732,7 +782,13 @@
                 elif link == "z":
                     value = ring(value, -1, self.nm)
                 elif link == "direct":
+                    more = [tasks.pop(0) for _ in range(min(direct - 1, len(tasks)))]
+                    self.joined[key] = more
+                    values = [value] + [self.waits.pop(other) for other in more]
+                    value = [jnp.concatenate(parts) for parts in zip(*values)]
                     value = [swap(part, 2 * n + 2, self.nd) for n, part in enumerate(value)]
+                    self.flying[key] = value
+                    break
                 else:
                     value = swap(value, link, self.nd)
                 self.flying[key] = value
@@ -749,7 +805,10 @@
         came = dict(zip(flying, values[1]))
         self.flying = {}
         for key, value in came.items():
-            self.arrive(key, value)
+            for other in [key] + self.joined.pop(key, []):
+                mine = len(other[1]) if isinstance(value, list) and other[2] != "z" else None
+                self.arrive(other, value if mine is None else [part[:mine] for part in value])
+                value = value if mine is None else [part[mine:] for part in value]
         extra = values[2]
         return extra[0] if len(extra) == 1 else extra
 
@@ -766,7 +825,7 @@
         order = self.order[name, ks]
         places, keep = self.kept.pop(key)
         if order is None and stage == -1:
-            parts = [add_low(keep[:, n], value[:, n]) for n in range(1, len(places))]
+            parts = list(add_parts(keep, value))
             own = (keep[:, 0], value[:, 0])
             self.push("direct", (name, ks, 0), own, None, parts)
             return
@@ -866,79 +925,99 @@
 
     flow = Flow(nd, nm)
     forth, back = flow.bits, flow.bits[::-1]
-    groups = [[0], [1]] if nm > 1 else [[0]]
-    groups += [list(range(k, min(k + 2, nm))) for k in range(2, nm, 2)]
+    firsts = min(2, nm)
+    groups = [list(range(k, min(k + 2, nm))) for k in range(firsts, nm, 2)]
     sizes = tuple(len(group) for group in groups)
     head = [jnp.concatenate([w_proj[0, :1], w_out, w_proj[0, 1:]])]
     feeds = [jnp.concatenate([w_up, w_down])]
-    flow.add("up0", w_up, forth)
-    flow.add("down0", w_down, back)
+    gather = functools.partial(lax.all_gather, axis_name="dp")
+    cut = max(nm // 2, 1)
+    head_groups = [list(range(0, cut)), list(range(cut, nm))] if nm > 1 else [[0]]
+
+    def headed():
+        for n, group in enumerate(head_groups):
+            if f"qo{n}" not in flow.order and group[-1] < len(head):
+                flow.add(f"qo{n}", jnp.stack([head[k][:2] for k in group]), forth)
+                flow.add(f"kv{n}", jnp.stack([head[k][2:] for k in group]), back)
+
+    halves = {}
+
+    def core_halves(most, names):
+        for name in names:
+            if most and flow.whole(name):
+                halves[name] = flow.take_half(name)
+                flow.fly(name, swap(halves[name], 1, nd))
+                most -= 1
+
     for step in range(nm - 1):
         head.append(ring(head[-1], 1, nm))
+        flow.launch()
         if step == 0:
-            flow.launch()
-            head, tokens, views, index, there = flow.land(head, tokens, views, index, there)
-        elif step == 1:
-            token_parts = [pack(tokens[:, 0], k) for k in range(micro)]
-            head, token_parts, index = flow.land(head, token_parts, index)
+            view = lax.dynamic_index_in_dim(views[:, 0], mp % micro, 0, keepdims=True)
+            view = lax.ppermute(view, ("dp", "mp"), routes(0))
+            gains, biases = by_place(norm_gains[0]), by_place(norm_biases[0])
+            head, tokens, view, gains, biases, there = flow.land(
+                head, tokens, view, gains, biases, there
+            )
+            token_parts = []
+        elif len(token_parts) < micro:
+            token_parts.append(pack(tokens[:, 0], len(token_parts)))
+            head, tokens, token_parts, cotangent, there = flow.land(
+                head, tokens, token_parts, cotangent, there
+            )
         else:
-            view = lax.dynamic_index_in_dim(views[:, 0], mp % micro, 0, keepdims=True)
-            gains, biases = by_place(norm_gains[0]), by_place(norm_biases[0])
-            head, view, gains, biases = flow.land(head, view, gains, biases)
-    flow.add("qo", jnp.stack([h[:2] for h in head]), forth)
-    flow.add("kv", jnp.stack([h[2:] for h in head]), back)
-    flow.fly("view", lax.ppermute(view, ("dp", "mp"), routes(0)))
+            head = flow.land(head)
+        headed()
+    head, feeds = flow.land(head, feeds)
+    weights = [gather(feeds[0])]
     came = []
-    while not (flow.whole("qo") and flow.whole("kv") and len(came) == micro):
-        flow.launch(chip=2)
+    head_names = [f"{name}{n}" for n in range(len(head_groups)) for name in ("kv", "qo")]
+    while len(came) < micro or not all(n in halves or flow.whole(n) for n in head_names):
         if len(came) < micro:
             came.append(send(token_parts, len(came)))
+        flow.launch(chip=2)
+        if len(came) == micro:
+            core_halves(2, head_names)
         if len(came) == 1:
             grad_parts = [pack(cotangent[:, 0], k) for k in range(micro)]
-        came, token_parts, grad_parts, feeds = flow.land(came, token_parts, grad_parts, feeds)
-    view = flow.kept.pop("view")
+        came, token_parts, grad_parts, feeds, halves = flow.land(
+            came, token_parts, grad_parts, feeds, halves
+        )
 
     def turn():
         if len(feeds) < nm:
             feeds.append(ring(feeds[-1], 1, nm))
 
     def turned():
+        if len(weights) < firsts and len(weights) < len(feeds):
+            weights.append(gather(feeds[len(weights)]))
         for n, group in enumerate(groups):
             if f"up{n}" not in flow.order and group[-1] < len(feeds):
                 flow.add(f"up{n}", jnp.stack([feeds[k][0] for k in group]), forth)
                 flow.add(f"down{n}", jnp.stack([feeds[k][1] for k in group]), back)
 
     last = [f"{name}{n}" for n in range(len(groups)) for name in ("up", "down")]
-    halves = {}
-
-    def core_halves(most):
-        for name in last:
-            if most and flow.whole(name):
-                halves[name] = flow.take_half(name)
-                flow.fly(name, swap(halves[name], 1, nd))
-                most -= 1
-
-    kv_own, qo_own = flow.take_half("kv"), flow.take_half("qo")
     slot = jnp.stack([(step_here - t) % micro for t in range(micro)])
     within = (slot[:, None] * chunk + jnp.arange(chunk)[None]).reshape(-1)
     position = jnp.stack([(rank ^ j) * rows + within for j in range(ranks)])
     bias = jnp.where(position < TRI + view[0] * VIEW_TOK, 0.0, -1.0).astype(F32)
-    flow.fly("kv", swap(kv_own, 1, nd))
+    core_halves(len(head_names), head_names)
     turn()
     x, normed, n_flip = first_norm(came, gains[:1], biases[:1])
-    x, normed, n_flip, bias, qo_own, kv_own, feeds = flow.land(
-        x, normed, n_flip, bias, qo_own, kv_own, feeds
-    )
+    x, normed, n_flip, bias, halves, feeds = flow.land(x, normed, n_flip, bias, halves, feeds)
     turned()
-    kv = [kv_own, flow.kept.pop("kv")]
-
-    flow.fly("qo", swap(qo_own, 1, nd))
+
+    def both(name):
+        names = [f"{name}{n}" for n in range(len(head_groups))]
+        return [halves.pop(n) for n in names], [flow.kept.pop(n) for n in names]
+
+    qo, kv = both("qo"), both("kv")
+
     turn()
     flow.launch()
-    own_kv = project(normed, kv[0], kv[1], 0, 2)
-    own_kv, normed, qo_own, feeds = flow.land(own_kv, normed, qo_own, feeds)
+    own_kv = project(normed, kv, 0, 2)
+    own_kv, normed, qo, feeds = flow.land(own_kv, normed, qo, feeds)
     turned()
-    qo = [qo_own, flow.kept.pop("qo")]
 
     def swap_rank(value, bit):
         if bit == 1:
@@ -953,7 +1032,7 @@
     kvs = [kvs[j] for j in range(ranks)]
     turn()
     flow.launch()
-    query = project(normed, qo[0], qo[1], 0, 1)
+    query = project(normed, qo, 0, 1)
     kvs, query, bias, grad_parts, feeds = flow.land(kvs, query, bias, grad_parts, feeds)
     turned()
 
@@ -966,7 +1045,7 @@
         flow.launch()
         if len(grad_came) < micro:
             grad_came.append(send(grad_parts, len(grad_came)))
-        core_halves(2)
+        core_halves(2, last)
         for k in range(len(mixed), min(len(mixed) + at_once, nm)):
             part, lse = attend(query, kvs, bias, k * per_k, per_k)
             mixed.append(part)
@@ -975,44 +1054,31 @@
             mixed, query, halves, grad_parts, grad_came, feeds
         )
         turned()
-    core_halves(len(last))
-    middle, normed_two, flip_two = middle_norm(x, mixed, *qo, 1, gains[1:], biases[1:])
+    core_halves(len(last), last)
+    middle, normed_two, flip_two = middle_norm(x, mixed, qo, 1, gains[1:], biases[1:])
     grad, grad_flip = flip(grad_came)
     middle, normed_two, flip_two, halves, grad, grad_flip = flow.land(
         middle, normed_two, flip_two, halves, grad, grad_flip
     )
-    weights = []
     for name in last:
         weights += [halves[name], flow.kept.pop(name)]
 
-    result, active, slope = feed(normed_two, middle, sizes, weights)
+    result, active, slope = feed(normed_two, middle, index, firsts, sizes, weights)
     out_chunks = result.reshape((micro, chunk, width))
     output = []
 
     sums = Scatter(nd, nm, flow.bits)
-    pairs = [list(range(k, min(k + 2, nm))) for k in range(0, nm, 2)][::-1]
-    ways = [back[::-1], forth[::-1]]
-    for ks in pairs:
-        sums.launch(chip=0)
-        pieces = wide_grad(grad_flip, active, ks[0], len(ks), chips)
-        pieces, active, grad_flip, out_chunks, grad = sums.land(
-            pieces, active, grad_flip, out_chunks, grad
-        )
-        sums.add("down", ks, *pieces, ways[0])
-    sums.launch(core=2)
-    output.append(send_chunk(out_chunks, 0))
+    output = [send_chunk(out_chunks, 0)]
+    over_dp = functools.partial(lax.psum_scatter, axis_name="dp", scatter_dimension=0, tiled=True)
+    grads_down = over_dp(wide_grad(grad_flip, active, index))
     hid, gmid, attn, attn_flip, sums_two = feed_back(
-        grad, slope, middle, gains[1:], sizes, weights
+        grad, slope, middle, gains[1:], index, firsts, sizes, weights
     )
-    hid, gmid, attn, attn_flip, sums_two, flip_two, out_chunks, output = sums.land(
-        hid, gmid, attn, attn_flip, sums_two, flip_two, out_chunks, output
+    hid, gmid, attn, attn_flip, sums_two, flip_two, output, out_chunks = sums.land(
+        hid, gmid, attn, attn_flip, sums_two, flip_two, output, out_chunks
     )
-    sums.launch(core=0, direct=0, z=0)
-    pieces = [wide_grad(flip_two, hid, ks[0], len(ks), chips) for ks in pairs]
-    grad_mixed = project(attn, *qo, 1, 1)
-    pieces, grad_mixed, query, out_chunks = sums.land(pieces, grad_mixed, query, out_chunks)
-    for n, (ks, piece) in enumerate(zip(pairs, pieces)):
-        sums.add("up", ks, *piece, ways[n % 2], rings=False)
+    grads_up = over_dp(wide_grad(flip_two, hid, index))
+    grad_mixed = project(attn, qo, 1, 1)
 
     dqs, dkvs = {}, {}
     bias_tall = bias[:, :, None]
@@ -1042,15 +1108,12 @@
 
     parts = None
     for k in list(reversed(range(nm))) + [-1]:
-        if k == nm - 1:
-            sums.launch(core=2)
-        elif k >= 1:
-            sums.launch(core=nm - 4, chip=1)
-        elif k == 0:
-            sums.launch()
-        else:
-            sums.launch(direct=0, z=0)
-        if k >= 0 and len(output) < micro:
+        if k == 0:
+            sums.add_line("down", grads_down[0], rings=False)
+        if k < 0:
+            sums.add_line("up", grads_up[0], rings=True)
+        sums.launch(direct=1 if k >= 0 else 0)
+        while k >= 0 and len(output) < min(micro, nm - k + 1):
             output.append(send_chunk(out_chunks, len(output)))
         ready = head_grads()
         if parts is not None:
@@ -1060,9 +1123,9 @@
             dqs[k], *parts = attend_back(
                 query, kvs, bias_tall, lses[k], mixed[k], grad_mixed, k * per_k, per_k
             )
-        live = (ready and ready[1], dqs, parts, query, dkv_part, dkv_came, dkvs, output, gmid)
-        live = sums.land(*live)
-        outs, dqs, parts, query, dkv_part, dkv_came, dkvs, output, gmid = live
+        live = (ready and ready[1], dqs, parts, query, dkv_part, dkv_came, dkvs, gmid)
+        live = sums.land(*live, output)
+        outs, dqs, parts, query, dkv_part, dkv_came, dkvs, gmid, output = live
         if ready:
             add_heads(ready, outs)
 
@@ -1077,7 +1140,9 @@
         qo,
         kv,
     )
-    first, sums_one, dkv_part, dkv_came = sums.land(first, sums_one, dkv_part, dkv_came)
+    first, sums_one, dkv_part, dkv_came, output = sums.land(
+        first, sums_one, dkv_part, dkv_came, output
+    )
     first = first.reshape((micro, chunk, width))
     vectors = jnp.take(
         jnp.concatenate([sums_one, sums_two]).reshape(4, nd, width // nd),
@@ -1091,15 +1156,16 @@
     ]
     grad_tokens = []
     while sums.busy() or hops or len(grad_tokens) < micro:
+        z = 1 if not grad_tokens else 2
         if len(grad_tokens) < micro:
             grad_tokens.append(send_chunk(first, len(grad_tokens)))
-        sums.launch(direct=2)
+        sums.launch(direct=2, z=z)
         if len(grad_tokens) == micro:
             for _ in range(min(3, len(hops))):
                 vectors = vectors + hops.pop(0)(vectors)
         ready = head_grads()
-        grad_tokens, first, outs, vectors = sums.land(
-            grad_tokens, first, ready and ready[1], vectors
+        grad_tokens, first, outs, vectors, output = sums.land(
+            grad_tokens, first, ready and ready[1], vectors, output
         )
         if ready:
             add_heads(ready, outs)

time: 557 us -> 541 us (0.971)
  other arithmetic: 43.1 us -> 27.7 us
  waiting for transfers between devices: 102 us -> 88.1 us
  between operations: 2.65 us -> 15.6 us
  Pallas kernels: 277 us -> 288 us
  starting transfers between devices: 94.4 us -> 88.4 us
    ppermute x4, waiting for transfers between devices: 17.3 us -> 0.01 us  [send(): return lax.ppermute(packed[k], ('dp', 'mp'), routes(k))]
    convert_element_type x17 -> x0, other arithmetic: 16.5 us -> none  [the longest x15 16.2 us: add_low(): return (a.astype(F32) + b.astype(F32)).astype(BF16)]
    pallas_call x11 -> x13, Pallas kernels: 112 us -> 122 us  [the longest x1 28 us: feed_back(): pl.pallas_call(functools.partial(feed_back_kernel, firsts, sizes), grid=(...]
    ppermute x60 -> x39, starting transfers between devices: 48.6 us -> 41.1 us  [swap(): return lax.ppermute(value, 'dp', [(i, i ^ bit) for i in range(nd)])]
    ppermute x15, waiting for transfers between devices: 42.6 us -> 48.5 us  [ring(): return lax.ppermute(value, 'mp', [(i, (i + step) % nm) for i in range(nm)])]
    ppermute x60 -> x39, waiting for transfers between devices: 40.5 us -> 35.4 us  [swap(): return lax.ppermute(value, 'dp', [(i, i ^ bit) for i in range(nd)])]
    unnamed x148 -> x120, local copies, waits for them, and re-layouts: 7.92 us -> 11.3 us
  transfers between devices with their start and end apart: 86 -> 69, of which waited for: 26 -> 23; matrix products, arithmetic and copies ran while one was open for 9% -> 6% of each run, Pallas kernels for 45% -> 45%
where the time goes in v4:
time: 541 us; the launch traced here: 532 us
  Pallas kernels  288 us (53%)
  starting transfers between devices  88.4 us (16%)
  waiting for transfers between devices  88.1 us (16%)
  other arithmetic  27.7 us (5%)
  local copies, waits for them, and re-layouts  24.2 us (4%)
  between operations  15.6 us (3%)
    pallas_call x4, Pallas kernels, attend_back(): pl.pallas_call(functools.partial(attend_back_kernel, parts), grid=(count,...  69.8 us
    ppermute x15, waiting for transfers between devices, ring(): return lax.ppermute(value, 'mp', [(i, (i + step) % nm) for i in range(nm)])  48.5 us
    pallas_call x4, Pallas kernels, attend(): pl.pallas_call(functools.partial(attend_kernel, parts), grid=(count, rows...  46.1 us
    ppermute x39, starting transfers between devices, swap(): return lax.ppermute(value, 'dp', [(i, i ^ bit) for i in range(nd)])  41.1 us
    ppermute x39, waiting for transfers between devices, swap(): return lax.ppermute(value, 'dp', [(i, i ^ bit) for i in range(nd)])  35.4 us
    pallas_call x1, Pallas kernels, feed_back(): pl.pallas_call(functools.partial(feed_back_kernel, firsts, sizes), grid=(...  28 us
    pallas_call x2, Pallas kernels, wide_grad(): pl.pallas_call(wide_grad_kernel, grid=(nm, hidden // block), in_specs=[pl...  25.4 us
    pallas_call x1, Pallas kernels, feed(): pl.pallas_call(functools.partial(feed_kernel, firsts, sizes), grid=(nm,),...  23.6 us
  transfers between devices with their start and end apart: 69, of which 23 were waited for; matrix products, arithmetic and copies ran while one was open for 6% of the time, Pallas kernels for 45%

profile of v4, /device:TPU:0, one launch (start us, length us, event | category | flops | bytes accessed | tf_op | source)
XLA Modules:
  0.0 531.9 jit_solution(13623856626840186888)
XLA Ops:
  67.2 5.0 collective-permute-start.15
  74.4 18.8 %collective-permute-done.11 = bf16[2,2,2,128,256]{4,3,2,1,0:T(8,128)(2,1)S(1)} collective-permute-done((bf16[2,2,2,128,256]{4,3,2,1,0:T(8,128)(2,1)S(1)}, bf16[2,2,2,128,256]{4,3,2,1,0:T(8,128)(2,1)S(1)}, u32[]{:S(2)}, u32[]{:S(2)}) %collective-permute-start.11) | collective-permute-done | bytes 524320 | tf_op jit(solution)/shard_map/ppermute | solution.py:49
  100.4 4.8 first_norm.1
  105.2 7.5 %collective-permute-done.18 = bf16[2,128,1024]{2,1,0:T(8,128)(2,1)S(1)} collective-permute-done((bf16[2,128,1024]{2,1,0:T(8,128)(2,1)S(1)}, bf16[2,128,1024]{2,1,0:T(8,128)(2,1)S(1)}, u32[]{:S(2)}, u32[]{:S(2)}) %collective-permute-start.18) | collective-permute-done | bytes 524320 | tf_op jit(solution)/shard_map/ppermute | solution.py:53
  112.7 7.3 %project.3.refs_0_.refs_2_ = bf16[2,768,1024]{2,1,0:T(8,128)(2,1)} custom-call(bf16[768,1024]{1,0:T(8,128)(2,1)} %get-tuple-element.405.in_ref, bf16[4,2,2,128,256]{4,3,2,1,0:T(8,128)(2,1)} %copy-done.6, bf16[4,2,2,128,256]{4,3,2,1,0:T(8,128)(2,1)} %pad_maximum_fusion.4.refs_1_.refs_14_, bf16[4,2,2,128,256]{4,3,2,1,0:T(8,128)(2,1)} %copy-done.16, ...), custom_call_target="tpu_custom_call" | custom-call | flops 3221225472 | bytes 3145728 | tf_op jit(solution)/shard_map/project/pallas_call | solution.py:270
  120.0 7.6 %collective-permute-done.19 = bf16[2,128,1024]{2,1,0:T(8,128)(2,1)S(1)} collective-permute-done((bf16[2,128,1024]{2,1,0:T(8,128)(2,1)S(1)}, bf16[2,128,1024]{2,1,0:T(8,128)(2,1)S(1)}, u32[]{:S(2)}, u32[]{:S(2)}) %collective-permute-start.19) | collective-permute-done | bytes 524320 | tf_op jit(solution)/shard_map/ppermute | solution.py:53
  127.8 5.0 project.4.q_ref
  132.7 11.2 %collective-permute-done.21 = bf16[2,128,1024]{2,1,0:T(8,128)(2,1)S(1)} collective-permute-done((bf16[2,128,1024]{2,1,0:T(8,128)(2,1)S(1)}, bf16[2,128,1024]{2,1,0:T(8,128)(2,1)S(1)}, u32[]{:S(2)}, u32[]{:S(2)}) %collective-permute-start.21) | collective-permute-done | bytes 524320 | tf_op jit(solution)/shard_map/ppermute | solution.py:53
  147.2 11.5 %attend.4 = (bf16[768,256]{1,0:T(8,128)(2,1)}, f32[2,2,768]{2,1,0:T(2,128)}) custom-call(bf16[1,768,1024]{2,1,0:T(8,128)(2,1)} %project.4.q_ref, bf16[2,768,1024]{2,1,0:T(8,128)(2,1)} %project.3.refs_0_.refs_2_, bf16[2,768,1024]{2,1,0:T(8,128)(2,1)} %collective-permute-done.20.refs_1_.refs_3_, bf16[2,768,1024]{2,1,0:T(8,128)(2,1)} %project.3.refs_0_.refs_2_, ...), custom_call_target="tpu_custom_call" | custom-call | flops 4831838208 | bytes 3145728 | tf_op jit(solution)/shard_map/attend/pallas_call | solution.py:319
  158.7 11.5 %attend.5 = (bf16[768,256]{1,0:T(8,128)(2,1)}, f32[2,2,768]{2,1,0:T(2,128)}) custom-call(bf16[1,768,1024]{2,1,0:T(8,128)(2,1)} %project.4.q_ref, bf16[2,768,1024]{2,1,0:T(8,128)(2,1)} %project.3.refs_0_.refs_2_, bf16[2,768,1024]{2,1,0:T(8,128)(2,1)} %collective-permute-done.20.refs_1_.refs_3_, bf16[2,768,1024]{2,1,0:T(8,128)(2,1)} %project.3.refs_0_.refs_2_, ...), custom_call_target="tpu_custom_call" | custom-call | flops 4831838208 | bytes 3145728 | tf_op jit(solution)/shard_map/attend/pallas_call | solution.py:319
  175.9 11.5 %attend.6 = (bf16[768,256]{1,0:T(8,128)(2,1)}, f32[2,2,768]{2,1,0:T(2,128)}) custom-call(bf16[1,768,1024]{2,1,0:T(8,128)(2,1)} %project.4.q_ref, bf16[2,768,1024]{2,1,0:T(8,128)(2,1)} %project.3.refs_0_.refs_2_, bf16[2,768,1024]{2,1,0:T(8,128)(2,1)} %collective-permute-done.20.refs_1_.refs_3_, bf16[2,768,1024]{2,1,0:T(8,128)(2,1)} %project.3.refs_0_.refs_2_, ...), custom_call_target="tpu_custom_call" | custom-call | flops 4831838208 | bytes 3145728 | tf_op jit(solution)/shard_map/attend/pallas_call | solution.py:319
  187.4 11.5 %attend.7 = (bf16[768,256]{1,0:T(8,128)(2,1)}, f32[2,2,768]{2,1,0:T(2,128)}) custom-call(bf16[1,768,1024]{2,1,0:T(8,128)(2,1)} %project.4.q_ref, bf16[2,768,1024]{2,1,0:T(8,128)(2,1)} %project.3.refs_0_.refs_2_, bf16[2,768,1024]{2,1,0:T(8,128)(2,1)} %collective-permute-done.20.refs_1_.refs_3_, bf16[2,768,1024]{2,1,0:T(8,128)(2,1)} %project.3.refs_0_.refs_2_, ...), custom_call_target="tpu_custom_call" | custom-call | flops 4831838208 | bytes 3145728 | tf_op jit(solution)/shard_map/attend/pallas_call | solution.py:319
  201.2 4.3 flip.1
  205.6 6.7 %middle_norm.1 = (f32[768,1024]{1,0:T(8,128)}, bf16[768,1024]{1,0:T(8,128)(2,1)}, bf16[1024,768]{1,0:T(8,128)(2,1)}) custom-call(bf16[768,1024]{1,0:T(8,128)(2,1)} %get-tuple-element.441.x_ref, bf16[768,256]{1,0:T(8,128)(2,1)} %get-tuple-element.442.refs_0_.refs_6_.mixed_ref, bf16[768,256]{1,0:T(8,128)(2,1)} %get-tuple-element.443.refs_1_.refs_6_.mixed_ref, ...), custom_call_target="tpu_custom_call" | custom-call | flops 1610612736 | bytes 11010048 | tf_op jit(solution)/shard_map/middle_norm/pallas_call | solution.py:436
  213.6 23.6 %feed.1 = (bf16[768,1024]{1,0:T(8,128)(2,1)}, bf16[4,768,1024]{2,1,0:T(8,128)(2,1)}, bf16[4,768,1024]{2,1,0:T(8,128)(2,1)}) custom-call(s32[8]{0:T(128)} %copy-done.50, bf16[8,2,128,1024]{3,2,1,0:T(8,128)(2,1)} %bitcast.243, bf16[8,2,128,1024]{3,2,1,0:T(8,128)(2,1)} %bitcast.245, bf16[4,2,128,1024]{3,2,1,0:T(8,128)(2,1)} %copy-done.7, ...), custom_call_target="tpu_custom_call" | custom-call | flops 12884901888 | bytes 16777216 | tf_op jit(solution)/shard_map/feed/pallas_call | solution.py:528
  237.3 12.4 %wide_grad.3 = bf16[8,4,128,1024]{3,2,1,0:T(8,128)(2,1)} custom-call(s32[8]{0:T(128)} %copy-done.50, bf16[1024,768]{1,0:T(8,128)(2,1)} %get-tuple-element.510.a_ref, bf16[4,768,1024]{2,1,0:T(8,128)(2,1)} %get-tuple-element.511.b_ref), custom_call_target="tpu_custom_call" | custom-call | flops 6442450944 | bytes 16777216 | tf_op jit(solution)/shard_map/wide_grad/pallas_call | solution.py:632
  252.0 28.0 %feed_back.1 = (bf16[4,768,1024]{2,1,0:T(8,128)(2,1)}, f32[768,1024]{1,0:T(8,128)}, bf16[768,1024]{1,0:T(8,128)(2,1)}, bf16[1024,768]{1,0:T(8,128)(2,1)}, f32[2,1024]{1,0:T(2,128)}) custom-call(s32[8]{0:T(128)} %copy-done.50, bf16[8,2,128,1024]{3,2,1,0:T(8,128)(2,1)} %bitcast.244, bf16[8,2,128,1024]{3,2,1,0:T(8,128)(2,1)} %bitcast.246, ...), custom_call_target="tpu_custom_call" | custom-call | flops 12884901888 | bytes 16777216 | tf_op jit(solution)/shard_map/feed_back/pallas_call | solution.py:589
  280.1 13.0 %wide_grad.2 = bf16[8,4,128,1024]{3,2,1,0:T(8,128)(2,1)} custom-call(s32[8]{0:T(128)} %copy-done.50, bf16[1024,768]{1,0:T(8,128)(2,1)} %get-tuple-element.468.a_ref, bf16[4,768,1024]{2,1,0:T(8,128)(2,1)} %get-tuple-element.469.b_ref), custom_call_target="tpu_custom_call" | custom-call | flops 6442450944 | bytes 16777216 | tf_op jit(solution)/shard_map/wide_grad/pallas_call | solution.py:632
  298.5 4.9 project.5.refs_7_
  303.4 17.4 %attend_back.4 = (bf16[768,256]{1,0:T(8,128)(2,1)}, bf16[2,768,256]{2,1,0:T(8,128)(2,1)}, bf16[2,768,256]{2,1,0:T(8,128)(2,1)}) custom-call(bf16[1,768,1024]{2,1,0:T(8,128)(2,1)} %project.4.q_ref, bf16[2,768,1024]{2,1,0:T(8,128)(2,1)} %project.3.refs_0_.refs_2_, bf16[2,768,1024]{2,1,0:T(8,128)(2,1)} %collective-permute-done.20.refs_1_.refs_3_, ...), custom_call_target="tpu_custom_call" | custom-call | flops 12079595520 | bytes 6291456 | tf_op jit(solution)/shard_map/attend_back/pallas_call | solution.py:387
  320.9 17.6 %attend_back.5 = (bf16[768,256]{1,0:T(8,128)(2,1)}, bf16[2,768,256]{2,1,0:T(8,128)(2,1)}, bf16[2,768,256]{2,1,0:T(8,128)(2,1)}) custom-call(bf16[1,768,1024]{2,1,0:T(8,128)(2,1)} %project.4.q_ref, bf16[2,768,1024]{2,1,0:T(8,128)(2,1)} %project.3.refs_0_.refs_2_, bf16[2,768,1024]{2,1,0:T(8,128)(2,1)} %collective-permute-done.20.refs_1_.refs_3_, ...), custom_call_target="tpu_custom_call" | custom-call | flops 12079595520 | bytes 6291456 | tf_op jit(solution)/shard_map/attend_back/pallas_call | solution.py:387
  339.3 5.7 %head_grad.4 = (bf16[2,768,256]{2,1,0:T(8,128)(2,1)}, bf16[4,4,128,256]{3,2,1,0:T(8,128)(2,1)}, bf16[4,4,128,256]{3,2,1,0:T(8,128)(2,1)}) custom-call(bf16[1024,768]{1,0:T(8,128)(2,1)} %get-tuple-element.470.n_ref, bf16[1024,768]{1,0:T(8,128)(2,1)} %get-tuple-element.471.g_ref, bf16[768,256]{1,0:T(8,128)(2,1)} %get-tuple-element.445.refs_3_.refs_6_.mixed_ref, ...), custom_call_target="tpu_custom_call" | custom-call | flops 1610612736 | bytes 2097152 | tf_op jit(solution)/shard_map/head_grad/pallas_call | solution.py:665
  345.0 17.5 %attend_back.6 = (bf16[768,256]{1,0:T(8,128)(2,1)}, bf16[2,768,256]{2,1,0:T(8,128)(2,1)}, bf16[2,768,256]{2,1,0:T(8,128)(2,1)}) custom-call(bf16[1,768,1024]{2,1,0:T(8,128)(2,1)} %project.4.q_ref, bf16[2,768,1024]{2,1,0:T(8,128)(2,1)} %project.3.refs_0_.refs_2_, bf16[2,768,1024]{2,1,0:T(8,128)(2,1)} %collective-permute-done.20.refs_1_.refs_3_, ...), custom_call_target="tpu_custom_call" | custom-call | flops 12079595520 | bytes 6291456 | tf_op jit(solution)/shard_map/attend_back/pallas_call | solution.py:387
  368.8 17.3 %attend_back.7 = (bf16[768,256]{1,0:T(8,128)(2,1)}, bf16[2,768,256]{2,1,0:T(8,128)(2,1)}, bf16[2,768,256]{2,1,0:T(8,128)(2,1)}) custom-call(bf16[1,768,1024]{2,1,0:T(8,128)(2,1)} %project.4.q_ref, bf16[2,768,1024]{2,1,0:T(8,128)(2,1)} %project.3.refs_0_.refs_2_, bf16[2,768,1024]{2,1,0:T(8,128)(2,1)} %collective-permute-done.20.refs_1_.refs_3_, ...), custom_call_target="tpu_custom_call" | custom-call | flops 12079595520 | bytes 6291456 | tf_op jit(solution)/shard_map/attend_back/pallas_call | solution.py:387
  386.2 5.8 %head_grad.5 = (bf16[2,768,256]{2,1,0:T(8,128)(2,1)}, bf16[4,4,128,256]{3,2,1,0:T(8,128)(2,1)}, bf16[4,4,128,256]{3,2,1,0:T(8,128)(2,1)}) custom-call(bf16[1024,768]{1,0:T(8,128)(2,1)} %get-tuple-element.470.n_ref, bf16[1024,768]{1,0:T(8,128)(2,1)} %get-tuple-element.471.g_ref, bf16[768,256]{1,0:T(8,128)(2,1)} %get-tuple-element.444.refs_2_.refs_6_.mixed_ref, ...), custom_call_target="tpu_custom_call" | custom-call | flops 1610612736 | bytes 2097152 | tf_op jit(solution)/shard_map/head_grad/pallas_call | solution.py:665
  400.3 5.9 %head_grad.6 = (bf16[2,768,256]{2,1,0:T(8,128)(2,1)}, bf16[4,4,128,256]{3,2,1,0:T(8,128)(2,1)}, bf16[4,4,128,256]{3,2,1,0:T(8,128)(2,1)}) custom-call(bf16[1024,768]{1,0:T(8,128)(2,1)} %get-tuple-element.470.n_ref, bf16[1024,768]{1,0:T(8,128)(2,1)} %get-tuple-element.471.g_ref, bf16[768,256]{1,0:T(8,128)(2,1)} %get-tuple-element.443.refs_1_.refs_6_.mixed_ref, ...), custom_call_target="tpu_custom_call" | custom-call | flops 1610612736 | bytes 2097152 | tf_op jit(solution)/shard_map/head_grad/pallas_call | solution.py:665
  414.3 11.5 %first_back.1 = (bf16[768,1024]{1,0:T(8,128)(2,1)}, f32[2,1024]{1,0:T(2,128)}) custom-call(bf16[768,1024]{1,0:T(8,128)(2,1)} %get-tuple-element.441.x_ref, f32[768,1024]{1,0:T(8,128)} %get-tuple-element.563.gmid_ref, f32[1,1024]{1,0:T(1,128)} %get-tuple-element.699.refs_2_.gain_ref, bf16[768,256]{1,0:T(8,128)(2,1)} %get-tuple-element.564.refs_0_.dq_ref, ...), custom_call_target="tpu_custom_call" | custom-call | flops 4831838208 | bytes 9437184 | tf_op jit(solution)/shard_map/first_back/pallas_call | solution.py:713
  442.9 5.7 %head_grad.7 = (bf16[2,768,256]{2,1,0:T(8,128)(2,1)}, bf16[4,4,128,256]{3,2,1,0:T(8,128)(2,1)}, bf16[4,4,128,256]{3,2,1,0:T(8,128)(2,1)}) custom-call(bf16[1024,768]{1,0:T(8,128)(2,1)} %get-tuple-element.470.n_ref, bf16[1024,768]{1,0:T(8,128)(2,1)} %get-tuple-element.471.g_ref, bf16[768,256]{1,0:T(8,128)(2,1)} %get-tuple-element.442.refs_0_.refs_6_.mixed_ref, ...), custom_call_target="tpu_custom_call" | custom-call | flops 1610612736 | bytes 2097152 | tf_op jit(solution)/shard_map/head_grad/pallas_call | solution.py:665
  449.4 6.1 %collective-permute-done.50 = bf16[4,128,256]{2,1,0:T(8,128)(2,1)} collective-permute-done((bf16[4,128,256]{2,1,0:T(8,128)(2,1)}, bf16[4,128,256]{2,1,0:T(8,128)(2,1)}, u32[]{:S(2)}, u32[]{:S(2)}) %collective-permute-start.50) | collective-permute-done | bytes 262176 | tf_op jit(solution)/shard_map/ppermute | solution.py:53
  458.8 6.5 %collective-permute-start.55 = (bf16[384,1024]{1,0:T(8,128)(2,1)S(1)}, bf16[384,1024]{1,0:T(8,128)(2,1)S(1)}, u32[]{:S(2)}, u32[]{:S(2)}) collective-permute-start(bf16[384,1024]{1,0:T(8,128)(2,1)S(1)} %slice_bitcast_fusion), channel_id=1, source_target_pairs={{2,0},{0,1},{6,2},{4,3},{3,4},{1,5},{7,6},{5,7},{10,8},{8,9},{14,1... | collective-permute-start | bytes 2359304 | tf_op jit(solution)/shard_map/ppermute | solution.py:918
  468.9 9.5 %collective-permute-start.57 = (f32[4,1024]{1,0:T(4,128)S(1)}, f32[4,1024]{1,0:T(4,128)S(1)}, u32[]{:S(2)}, u32[]{:S(2)}) collective-permute-start(f32[4,1024]{1,0:T(4,128)S(1)} %add.250), channel_id=1, source_target_pairs={{0,8},{4,12},{8,0},{12,4},{16,24},{20,28},{24,16},{28,20},{1,9},{5... | collective-permute-start | bytes 49160 | tf_op jit(solution)/shard_map/ppermute | solution.py:49
  487.1 5.3 collective-permute-done.54
  (348 shorter events, 178.4 us)
Async XLA Ops:
  7.2 206.4 %all-gather.5.cloned.1.call-start = ((), (), s32[]{:S(2)}) async-start(), calls=%async_computation.4 | async-start | bytes 4718592 | tf_op jit(solution)/shard_map/all_gather | solution.py:972
  49.8 163.8 %all-gather.7.cloned.1.call-start = ((), (), s32[]{:S(2)}) async-start(), calls=%async_computation.5 | async-start | bytes 4718592 | tf_op jit(solution)/shard_map/all_gather | solution.py:993
  64.3 29.0 %collective-permute-start.13 = (bf16[4,2,2,128,256]{4,3,2,1,0:T(8,128)(2,1)S(1)}, bf16[4,2,2,128,256]{4,3,2,1,0:T(8,128)(2,1)S(1)}, u32[]{:S(2)}, u32[]{:S(2)}) collective-permute-start(bf16[4,2,2,128,256]{4,3,2,1,0:T(8,128)(2,1)S(1)} %pad_maximum_fusion.2.refs_0_.refs_13_), channel_id=1, source_target_pairs={{0,4},{4,0},{8,12},{12,8},{16,20},{20,16},{24,28},{28,24},{1,5},{5... | collective-permute-start | bytes 3145736 | tf_op jit(solution)/shard_map/ppermute | solution.py:49
  67.1 26.2 %collective-permute-start.14 = (bf16[4,2,2,128,256]{4,3,2,1,0:T(8,128)(2,1)S(1)}, bf16[4,2,2,128,256]{4,3,2,1,0:T(8,128)(2,1)S(1)}, u32[]{:S(2)}, u32[]{:S(2)}) collective-permute-start(bf16[4,2,2,128,256]{4,3,2,1,0:T(8,128)(2,1)S(1)} %pad_maximum_fusion.3.refs_0_.refs_4_.refs_9_), channel_id=1, source_target_pairs={{0,4},{4,0},{8,12},{12,8},{16,20},{20,16},{24,28},{28,24},{1,5},{5... | collective-permute-start | bytes 3145736 | tf_op jit(solution)/shard_map/ppermute | solution.py:49
  67.2 26.1 %collective-permute-start.15 = (bf16[384,1024]{1,0:T(8,128)(2,1)S(1)}, bf16[384,1024]{1,0:T(8,128)(2,1)S(1)}, u32[]{:S(2)}, u32[]{:S(2)}) collective-permute-start(bf16[384,1024]{1,0:T(8,128)(2,1)S(1)} %copy-done.22), channel_id=1, source_target_pairs={{0,2},{1,0},{2,6},{3,4},{4,3},{5,1},{6,7},{7,5},{8,10},{9,8},{10,1... | collective-permute-start | bytes 2359304 | tf_op jit(solution)/shard_map/ppermute | solution.py:915
  72.3 20.9 %collective-permute-start.11 = (bf16[2,2,2,128,256]{4,3,2,1,0:T(8,128)(2,1)S(1)}, bf16[2,2,2,128,256]{4,3,2,1,0:T(8,128)(2,1)S(1)}, u32[]{:S(2)}, u32[]{:S(2)}) collective-permute-start(bf16[2,2,2,128,256]{4,3,2,1,0:T(8,128)(2,1)S(1)} %pad_maximum_fusion.11), channel_id=1, source_target_pairs={{0,8},{4,12},{8,0},{12,4},{16,24},{20,28},{24,16},{28,20},{1,9},{5... | collective-permute-start | bytes 1572872 | tf_op jit(solution)/shard_map/ppermute | solution.py:49
  127.7 236.2 %reduce-scatter.5.cloned.1.call-start = ((), (), s32[]{:S(2)}) async-start(), calls=%async_computation.3 | async-start | bytes 9437184 | tf_op jit(solution)/shard_map/reduce_scatter | solution.py:1073
  144.1 26.2 %collective-permute-start.22 = (bf16[1,2,128,1024]{3,2,1,0:T(8,128)(2,1)S(1)}, bf16[1,2,128,1024]{3,2,1,0:T(8,128)(2,1)S(1)}, u32[]{:S(2)}, u32[]{:S(2)}) collective-permute-start(bf16[1,2,128,1024]{3,2,1,0:T(8,128)(2,1)S(1)} %get-tuple-element.672), channel_id=1, source_target_pairs={{0,8},{4,12},{8,0},{12,4},{16,24},{20,28},{24,16},{28,20},{1,9},{5... | collective-permute-start | bytes 1572872 | tf_op jit(solution)/shard_map/ppermute | solution.py:49
  145.7 24.6 %collective-permute-start.23 = (bf16[1,2,128,1024]{3,2,1,0:T(8,128)(2,1)S(1)}, bf16[1,2,128,1024]{3,2,1,0:T(8,128)(2,1)S(1)}, u32[]{:S(2)}, u32[]{:S(2)}) collective-permute-start(bf16[1,2,128,1024]{3,2,1,0:T(8,128)(2,1)S(1)} %get-tuple-element.670), channel_id=1, source_target_pairs={{0,16},{4,20},{8,24},{12,28},{16,0},{20,4},{24,8},{28,12},{1,17},{... | collective-permute-start | bytes 1572872 | tf_op jit(solution)/shard_map/ppermute | solution.py:49
  146.3 24.0 %collective-permute-start.24 = (bf16[384,1024]{1,0:T(8,128)(2,1)S(1)}, bf16[384,1024]{1,0:T(8,128)(2,1)S(1)}, u32[]{:S(2)}, u32[]{:S(2)}) collective-permute-start(bf16[384,1024]{1,0:T(8,128)(2,1)S(1)} %copy-done.20), channel_id=1, source_target_pairs={{0,0},{1,2},{2,4},{3,6},{4,1},{5,3},{6,5},{7,7},{8,8},{9,10},{10,1... | collective-permute-start | bytes 2359304 | tf_op jit(solution)/shard_map/ppermute | solution.py:915
  170.4 28.6 %collective-permute-start.25 = (bf16[2,2,128,1024]{3,2,1,0:T(8,128)(2,1)S(1)}, bf16[2,2,128,1024]{3,2,1,0:T(8,128)(2,1)S(1)}, u32[]{:S(2)}, u32[]{:S(2)}) collective-permute-start(bf16[2,2,128,1024]{3,2,1,0:T(8,128)(2,1)S(1)} %pad_maximum_fusion.6), channel_id=1, source_target_pairs={{0,8},{4,12},{8,0},{12,4},{16,24},{20,28},{24,16},{28,20},{1,9},{5... | collective-permute-start | bytes 3145736 | tf_op jit(solution)/shard_map/ppermute | solution.py:49
  172.0 27.0 %collective-permute-start.26 = (bf16[2,2,128,1024]{3,2,1,0:T(8,128)(2,1)S(1)}, bf16[2,2,128,1024]{3,2,1,0:T(8,128)(2,1)S(1)}, u32[]{:S(2)}, u32[]{:S(2)}) collective-permute-start(bf16[2,2,128,1024]{3,2,1,0:T(8,128)(2,1)S(1)} %pad_maximum_fusion.7), channel_id=1, source_target_pairs={{0,16},{4,20},{8,24},{12,28},{16,0},{20,4},{24,8},{28,12},{1,17},{... | collective-permute-start | bytes 3145736 | tf_op jit(solution)/shard_map/ppermute | solution.py:49
  172.9 26.1 %collective-permute-start.27 = (bf16[384,1024]{1,0:T(8,128)(2,1)S(1)}, bf16[384,1024]{1,0:T(8,128)(2,1)S(1)}, u32[]{:S(2)}, u32[]{:S(2)}) collective-permute-start(bf16[384,1024]{1,0:T(8,128)(2,1)S(1)} %copy-done.19), channel_id=1, source_target_pairs={{0,2},{1,0},{2,6},{3,4},{4,3},{5,1},{6,7},{7,5},{8,10},{9,8},{10,1... | collective-permute-start | bytes 2359304 | tf_op jit(solution)/shard_map/ppermute | solution.py:915
  249.7 144.0 %reduce-scatter.3.cloned.1.call-start = ((), (), s32[]{:S(2)}) async-start(), calls=%async_computation.2 | async-start | bytes 9437184 | tf_op jit(solution)/shard_map/reduce_scatter | solution.py:1080
  251.1 29.0 %collective-permute-start.30 = (bf16[384,1024]{1,0:T(8,128)(2,1)S(1)}, bf16[384,1024]{1,0:T(8,128)(2,1)S(1)}, u32[]{:S(2)}, u32[]{:S(2)}) collective-permute-start(bf16[384,1024]{1,0:T(8,128)(2,1)S(1)} %slice.221), channel_id=1, source_target_pairs={{0,0},{2,1},{4,2},{6,3},{1,4},{3,5},{5,6},{7,7},{8,8},{10,9},{12,1... | collective-permute-start | bytes 2359304 | tf_op jit(solution)/shard_map/ppermute | solution.py:918
  295.1 25.7 %collective-permute-start.31 = (bf16[384,1024]{1,0:T(8,128)(2,1)S(1)}, bf16[384,1024]{1,0:T(8,128)(2,1)S(1)}, u32[]{:S(2)}, u32[]{:S(2)}) collective-permute-start(bf16[384,1024]{1,0:T(8,128)(2,1)S(1)} %slice_bitcast_fusion.1), channel_id=1, source_target_pairs={{2,0},{0,1},{6,2},{4,3},{3,4},{1,5},{7,6},{5,7},{10,8},{8,9},{14,1... | collective-permute-start | bytes 2359304 | tf_op jit(solution)/shard_map/ppermute | solution.py:918
  338.4 24.1 %collective-permute-start.33 = (bf16[2,768,256]{2,1,0:T(8,128)(2,1)}, bf16[2,768,256]{2,1,0:T(8,128)(2,1)S(1)}, u32[]{:S(2)}, u32[]{:S(2)}) collective-permute-start(bf16[2,768,256]{2,1,0:T(8,128)(2,1)} %get-tuple-element.504), channel_id=1, source_target_pairs={{0,4},{4,0},{8,12},{12,8},{16,20},{20,16},{24,28},{28,24},{1,5},{5... | collective-permute-start | bytes 2359304 | tf_op jit(solution)/shard_map/ppermute | solution.py:49
  363.4 28.6 %collective-permute-start.34 = (bf16[1,4,4,128,256]{4,3,2,1,0:T(8,128)(2,1)S(1)}, bf16[1,4,4,128,256]{4,3,2,1,0:T(8,128)(2,1)S(1)}, u32[]{:S(2)}, u32[]{:S(2)}) collective-permute-start(bf16[1,4,4,128,256]{4,3,2,1,0:T(8,128)(2,1)S(1)} %bitcast.249), channel_id=1, source_target_pairs={{0,4},{4,0},{8,12},{12,8},{16,20},{20,16},{24,28},{28,24},{1,5},{5... | collective-permute-start | bytes 3145736 | tf_op jit(solution)/shard_map/ppermute | solution.py:49
  363.7 28.2 %collective-permute-start.38 = (bf16[2,768,256]{2,1,0:T(8,128)(2,1)}, bf16[2,768,256]{2,1,0:T(8,128)(2,1)S(1)}, u32[]{:S(2)}, u32[]{:S(2)}) collective-permute-start(bf16[2,768,256]{2,1,0:T(8,128)(2,1)} %get-tuple-element.525), channel_id=1, source_target_pairs={{0,4},{4,0},{8,12},{12,8},{16,20},{20,16},{24,28},{28,24},{1,5},{5... | collective-permute-start | bytes 2359304 | tf_op jit(solution)/shard_map/ppermute | solution.py:49
  365.1 26.9 %collective-permute-start.35 = (bf16[128,1024]{1,0:T(8,128)(2,1)S(1)}, bf16[128,1024]{1,0:T(8,128)(2,1)S(1)}, u32[]{:S(2)}, u32[]{:S(2)}) collective-permute-start(bf16[128,1024]{1,0:T(8,128)(2,1)S(1)} %get-tuple-element.665), channel_id=1, source_target_pairs={{0,3},{1,0},{2,1},{3,2},{4,7},{5,4},{6,5},{7,6},{8,11},{9,8},{10,9... | collective-permute-start | bytes 786440 | tf_op jit(solution)/shard_map/ppermute | solution.py:53
  368.1 23.9 %collective-permute-start.36 = (bf16[128,1024]{1,0:T(8,128)(2,1)S(1)}, bf16[128,1024]{1,0:T(8,128)(2,1)S(1)}, u32[]{:S(2)}, u32[]{:S(2)}) collective-permute-start(bf16[128,1024]{1,0:T(8,128)(2,1)S(1)} %get-tuple-element.664), channel_id=1, source_target_pairs={{0,2},{1,3},{2,0},{3,1},{4,6},{5,7},{6,4},{7,5},{8,10},{9,11},{10,... | collective-permute-start | bytes 786440 | tf_op jit(solution)/shard_map/ppermute | solution.py:53
  368.1 24.0 %collective-permute-start.37 = (bf16[128,1024]{1,0:T(8,128)(2,1)S(1)}, bf16[128,1024]{1,0:T(8,128)(2,1)S(1)}, u32[]{:S(2)}, u32[]{:S(2)}) collective-permute-start(bf16[128,1024]{1,0:T(8,128)(2,1)S(1)} %get-tuple-element.663), channel_id=1, source_target_pairs={{0,1},{1,2},{2,3},{3,0},{4,5},{5,6},{6,7},{7,4},{8,9},{9,10},{10,1... | collective-permute-start | bytes 786440 | tf_op jit(solution)/shard_map/ppermute | solution.py:53
  406.2 19.6 %collective-permute-start.42 = (bf16[1,4,4,128,256]{4,3,2,1,0:T(8,128)(2,1)}, bf16[1,4,4,128,256]{4,3,2,1,0:T(8,128)(2,1)S(1)}, u32[]{:S(2)}, u32[]{:S(2)}) collective-permute-start(bf16[1,4,4,128,256]{4,3,2,1,0:T(8,128)(2,1)} %bitcast.248), channel_id=1, source_target_pairs={{0,4},{4,0},{8,12},{12,8},{16,20},{20,16},{24,28},{28,24},{1,5},{5... | collective-permute-start | bytes 3145736 | tf_op jit(solution)/shard_map/ppermute | solution.py:49
  431.4 24.1 %collective-permute-start.47 = (bf16[2,4,128,256]{3,2,1,0:T(8,128)(2,1)}, bf16[2,4,128,256]{3,2,1,0:T(8,128)(2,1)}, u32[]{:S(2)}, u32[]{:S(2)}) collective-permute-start(bf16[2,4,128,256]{3,2,1,0:T(8,128)(2,1)} %pad_maximum_fusion.15), channel_id=1, source_target_pairs={{0,8},{4,12},{8,0},{12,4},{16,24},{20,28},{24,16},{28,20},{1,9},{5... | collective-permute-start | bytes 1572872 | tf_op jit(solution)/shard_map/ppermute | solution.py:49
  434.2 24.5 %collective-permute-start.48 = (bf16[2,4,128,256]{3,2,1,0:T(8,128)(2,1)}, bf16[2,4,128,256]{3,2,1,0:T(8,128)(2,1)}, u32[]{:S(2)}, u32[]{:S(2)}) collective-permute-start(bf16[2,4,128,256]{3,2,1,0:T(8,128)(2,1)} %pad_maximum_fusion.16), channel_id=1, source_target_pairs={{0,16},{4,20},{8,24},{12,28},{16,0},{20,4},{24,8},{28,12},{1,17},{... | collective-permute-start | bytes 1572872 | tf_op jit(solution)/shard_map/ppermute | solution.py:49
  435.8 23.0 %collective-permute-start.49 = (bf16[2,4,128,256]{3,2,1,0:T(8,128)(2,1)}, bf16[2,4,128,256]{3,2,1,0:T(8,128)(2,1)}, u32[]{:S(2)}, u32[]{:S(2)}) collective-permute-start(bf16[2,4,128,256]{3,2,1,0:T(8,128)(2,1)} %pad_maximum_fusion.17), channel_id=1, source_target_pairs={{0,24},{4,28},{8,16},{12,20},{16,8},{20,12},{24,0},{28,4},{1,25},{... | collective-permute-start | bytes 1572872 | tf_op jit(solution)/shard_map/ppermute | solution.py:49
  437.6 21.1 %collective-permute-start.51 = (bf16[384,1024]{1,0:T(8,128)(2,1)S(1)}, bf16[384,1024]{1,0:T(8,128)(2,1)}, u32[]{:S(2)}, u32[]{:S(2)}) collective-permute-start(bf16[384,1024]{1,0:T(8,128)(2,1)S(1)} %slice.231), channel_id=1, source_target_pairs={{0,0},{2,1},{4,2},{6,3},{1,4},{3,5},{5,6},{7,7},{8,8},{10,9},{12,1... | collective-permute-start | bytes 2359304 | tf_op jit(solution)/shard_map/ppermute | solution.py:918
  458.7 33.7 %collective-permute-start.52 = (bf16[1,4,4,128,256]{4,3,2,1,0:T(8,128)(2,1)}, bf16[1,4,4,128,256]{4,3,2,1,0:T(8,128)(2,1)S(1)}, u32[]{:S(2)}, u32[]{:S(2)}) collective-permute-start(bf16[1,4,4,128,256]{4,3,2,1,0:T(8,128)(2,1)} %bitcast.247), channel_id=1, source_target_pairs={{0,4},{4,0},{8,12},{12,8},{16,20},{20,16},{24,28},{28,24},{1,5},{5... | collective-permute-start | bytes 3145736 | tf_op jit(solution)/shard_map/ppermute | solution.py:49
  458.8 33.7 %collective-permute-start.55 = (bf16[384,1024]{1,0:T(8,128)(2,1)S(1)}, bf16[384,1024]{1,0:T(8,128)(2,1)S(1)}, u32[]{:S(2)}, u32[]{:S(2)}) collective-permute-start(bf16[384,1024]{1,0:T(8,128)(2,1)S(1)} %slice_bitcast_fusion), channel_id=1, source_target_pairs={{2,0},{0,1},{6,2},{4,3},{3,4},{1,5},{7,6},{5,7},{10,8},{8,9},{14,1... | collective-permute-start | bytes 2359304 | tf_op jit(solution)/shard_map/ppermute | solution.py:918
  465.3 21.9 %collective-permute-start.53 = (bf16[128,1024]{1,0:T(8,128)(2,1)}, bf16[128,1024]{1,0:T(8,128)(2,1)}, u32[]{:S(2)}, u32[]{:S(2)}) collective-permute-start(bf16[128,1024]{1,0:T(8,128)(2,1)} %fusion.11), channel_id=1, source_target_pairs={{0,3},{1,0},{2,1},{3,2},{4,7},{5,4},{6,5},{7,6},{8,11},{9,8},{10,9... | collective-permute-start | bytes 786440 | tf_op jit(solution)/shard_map/ppermute | solution.py:53
  466.8 25.6 %collective-permute-start.54 = (bf16[4,128,256]{2,1,0:T(8,128)(2,1)S(1)}, bf16[4,128,256]{2,1,0:T(8,128)(2,1)S(1)}, u32[]{:S(2)}, u32[]{:S(2)}) collective-permute-start(bf16[4,128,256]{2,1,0:T(8,128)(2,1)S(1)} %fusion.8), channel_id=1, source_target_pairs={{0,3},{1,0},{2,1},{3,2},{4,7},{5,4},{6,5},{7,6},{8,11},{9,8},{10,9... | collective-permute-start | bytes 786440 | tf_op jit(solution)/shard_map/ppermute | solution.py:53
  495.9 19.4 %collective-permute-start.59 = (bf16[1,4,128,256]{3,2,1,0:T(8,128)(2,1)}, bf16[1,4,128,256]{3,2,1,0:T(8,128)(2,1)S(1)}, u32[]{:S(2)}, u32[]{:S(2)}) collective-permute-start(bf16[1,4,128,256]{3,2,1,0:T(8,128)(2,1)} %get-tuple-element.612), channel_id=1, source_target_pairs={{0,8},{4,12},{8,0},{12,4},{16,24},{20,28},{24,16},{28,20},{1,9},{5... | collective-permute-start | bytes 786440 | tf_op jit(solution)/shard_map/ppermute | solution.py:49
  (96 other events, 979.4 us)
Sparse Core Ops, SparseCore 0:
  49.9 40.1 all-gather.4
  127.8 44.2 all-gather.6
  249.8 68.1 reduce-scatter.4
  321.7 71.6 reduce-scatter.2

commit v5 on v4

--- a/solution.py
+++ b/solution.py
@@ -463,12 +463,12 @@
             pltpu.make_async_copy(source, held.at[w, 2 * k + side, n], sems.at[w, 2 * k + side, sem])
         )
 
+    ref = refs.pop(0)
     for k in range(firsts):
-        ref = refs.pop(0)
         for w in range(2):
             for side in range(2):
                 for n in range(chips):
-                    add(k, ref.at[index_ref[side * chips + n], w], w, side, n, n)
+                    add(k, ref.at[index_ref[side * chips + n], k, w], w, side, n, n)
     k = firsts
     for size in sizes:
         sides = [refs.pop(0) for _ in range(4)]
@@ -492,7 +492,7 @@
 
 
 def feed_kernel(firsts, sizes, index_ref, *refs):
-    nm, count = firsts + sum(sizes), firsts + 4 * len(sizes)
+    nm, count = firsts + sum(sizes), 1 + 4 * len(sizes)
     in_ref, mid_ref, out_ref, act_ref, slope_ref, held, acc, sems = refs[count:]
     step = pl.program_id(0)
     load_weights(firsts, sizes, index_ref, refs[:count], held, sems)
@@ -521,7 +521,7 @@
 def feed(normed, middle, index, firsts, sizes, weights):
     rows, width = normed.shape
     nm = firsts + sum(sizes)
-    nd, (deep, hidden) = index.shape[0], weights[0].shape[2:]
+    nd, (deep, hidden) = index.shape[0], weights[0].shape[3:]
     chips = nd // 2
     line = pl.BlockSpec((rows, width), lambda k: (0, 0))
     wide = pl.BlockSpec((1, rows, hidden), lambda k: (k, 0, 0))
@@ -545,7 +545,7 @@
 
 
 def feed_back_kernel(firsts, sizes, index_ref, *refs):
-    nm, count = firsts + sum(sizes), firsts + 4 * len(sizes)
+    nm, count = firsts + sum(sizes), 1 + 4 * len(sizes)
     g_ref, slope_ref, mid_ref, gain_ref = refs[count : count + 4]
     hid_ref, gmid_ref, attn_ref, flip_ref, sums_ref, held, acc, sems = refs[count + 4 :]
     step = pl.program_id(0)
@@ -582,7 +582,7 @@
 def feed_back(grad, slope, middle, gain, index, firsts, sizes, weights):
     rows, width = grad.shape
     nm = firsts + sum(sizes)
-    nd, (deep, hidden) = index.shape[0], weights[0].shape[2:]
+    nd, (deep, hidden) = index.shape[0], weights[0].shape[3:]
     chips = nd // 2
     line = pl.BlockSpec((rows, width), lambda k: (0, 0))
     wide = pl.BlockSpec((1, rows, hidden), lambda k: (k, 0, 0))
@@ -754,7 +754,7 @@
         self.nd, self.nm = nd, nm
         self.queue = {1: [], **{bit: [] for bit in bits}, "direct": [], "z": []}
         self.order, self.kept, self.waits, self.flying = {}, {}, {}, {}
-        self.ends, self.came, self.done, self.rings, self.joined = {}, {}, {}, {}, {}
+        self.ends, self.came, self.done, self.rings = {}, {}, {}, {}
 
     def add(self, name, ks, keep, give, order, rings=True):
         self.order[name, tuple(ks)], self.rings[name] = order, rings
@@ -762,9 +762,15 @@
 
     def add_line(self, name, value, rings):
         self.rings[name] = rings
-        for k in range(self.nm):
-            self.ends[name, k] = (value[k],)
-        self.advance(name, self.nm - 1)
+        if rings:
+            for k in range(self.nm):
+                self.ends[name, k] = (value[k],)
+            self.advance(name, self.nm - 1)
+            return
+        self.ends[name] = [value[0]]
+        for k in sorted(range(1, self.nm), key=lambda k: min(k, self.nm - k)):
+            self.waits[name, k, "z"] = value[k]
+            self.queue["z"].append((name, k, "z"))
 
     def push(self, link, key, places, keep, give):
         self.kept[key], self.waits[key] = (places, keep), give
@@ -777,18 +783,14 @@
                     break
                 key = tasks.pop(0)
                 value = self.waits.pop(key)
-                if link == "z" and isinstance(value, list):
-                    value = [ring(part, -n - 1, self.nm) for n, part in enumerate(value)]
+                if link == "z" and not self.rings[key[0]]:
+                    value = ring(value, -key[1], self.nm)
                 elif link == "z":
                     value = ring(value, -1, self.nm)
                 elif link == "direct":
-                    more = [tasks.pop(0) for _ in range(min(direct - 1, len(tasks)))]
-                    self.joined[key] = more
-                    values = [value] + [self.waits.pop(other) for other in more]
-                    value = [jnp.concatenate(parts) for parts in zip(*values)]
-                    value = [swap(part, 2 * n + 2, self.nd) for n, part in enumerate(value)]
-                    self.flying[key] = value
-                    break
+                    value = [
+                        swap(part, 2 * n + 2, self.nd) for n, part in enumerate(add_parts(*value))
+                    ]
                 else:
                     value = swap(value, link, self.nd)
                 self.flying[key] = value
@@ -805,18 +807,16 @@
         came = dict(zip(flying, values[1]))
         self.flying = {}
         for key, value in came.items():
-            for other in [key] + self.joined.pop(key, []):
-                mine = len(other[1]) if isinstance(value, list) and other[2] != "z" else None
-                self.arrive(other, value if mine is None else [part[:mine] for part in value])
-                value = value if mine is None else [part[mine:] for part in value]
+            self.arrive(key, value)
         extra = values[2]
         return extra[0] if len(extra) == 1 else extra
 
     def arrive(self, key, value):
         name, ks, stage = key
         if stage == "z" and not self.rings[name]:
-            parts = [*self.ends.pop((name, 0)), *value]
-            self.done[name] = sum(part.astype(F32) for part in parts)
+            self.ends[name].append(value)
+            if len(self.ends[name]) == self.nm:
+                self.done[name] = sum(part.astype(F32) for part in self.ends.pop(name))
             return
         if stage == "z":
             self.came[name, ks - 1] = value
@@ -825,9 +825,8 @@
         order = self.order[name, ks]
         places, keep = self.kept.pop(key)
         if order is None and stage == -1:
-            parts = list(add_parts(keep, value))
             own = (keep[:, 0], value[:, 0])
-            self.push("direct", (name, ks, 0), own, None, parts)
+            self.push("direct", (name, ks, 0), own, None, (keep, value))
             return
         if order is None:
             for n, k in enumerate(ks):
@@ -856,15 +855,6 @@
         )
 
     def advance(self, name, k):
-        if not self.rings[name]:
-            if all((name, k) in self.ends for k in range(self.nm)):
-                key = (name, 0, "z")
-                self.waits[key] = [
-                    sum(part.astype(F32) for part in self.ends.pop((name, k))).astype(BF16)
-                    for k in range(1, self.nm)
-                ]
-                self.queue["z"].append(key)
-            return
         if (name, k) not in self.ends or (k < self.nm - 1 and (name, k) not in self.came):
             return
         total = sum(part.astype(F32) for part in self.ends.pop((name, k)))
@@ -931,14 +921,11 @@
     head = [jnp.concatenate([w_proj[0, :1], w_out, w_proj[0, 1:]])]
     feeds = [jnp.concatenate([w_up, w_down])]
     gather = functools.partial(lax.all_gather, axis_name="dp")
-    cut = max(nm // 2, 1)
-    head_groups = [list(range(0, cut)), list(range(cut, nm))] if nm > 1 else [[0]]
-
-    def headed():
-        for n, group in enumerate(head_groups):
-            if f"qo{n}" not in flow.order and group[-1] < len(head):
-                flow.add(f"qo{n}", jnp.stack([head[k][:2] for k in group]), forth)
-                flow.add(f"kv{n}", jnp.stack([head[k][2:] for k in group]), back)
+    head_groups = [[0], list(range(1, nm))]
+
+    def headed(n):
+        flow.add(f"qo{n}", jnp.stack([head[k][:2] for k in head_groups[n]]), forth)
+        flow.add(f"kv{n}", jnp.stack([head[k][2:] for k in head_groups[n]]), back)
 
     halves = {}
 
@@ -949,27 +936,18 @@
                 flow.fly(name, swap(halves[name], 1, nd))
                 most -= 1
 
-    for step in range(nm - 1):
-        head.append(ring(head[-1], 1, nm))
-        flow.launch()
-        if step == 0:
-            view = lax.dynamic_index_in_dim(views[:, 0], mp % micro, 0, keepdims=True)
-            view = lax.ppermute(view, ("dp", "mp"), routes(0))
-            gains, biases = by_place(norm_gains[0]), by_place(norm_biases[0])
-            head, tokens, view, gains, biases, there = flow.land(
-                head, tokens, view, gains, biases, there
-            )
-            token_parts = []
-        elif len(token_parts) < micro:
-            token_parts.append(pack(tokens[:, 0], len(token_parts)))
-            head, tokens, token_parts, cotangent, there = flow.land(
-                head, tokens, token_parts, cotangent, there
-            )
-        else:
-            head = flow.land(head)
-        headed()
-    head, feeds = flow.land(head, feeds)
-    weights = [gather(feeds[0])]
+    for k in sorted(range(1, nm), key=lambda k: -min(k, nm - k)):
+        flow.fly(("head", k), ring(head[0], k, nm))
+    headed(0)
+    flow.launch()
+    token_parts = [pack(tokens[:, 0], k) for k in range(micro)]
+    view = lax.dynamic_index_in_dim(views[:, 0], mp % micro, 0, keepdims=True)
+    head, tokens, token_parts, cotangent, there, view, feeds, norm_gains, norm_biases = flow.land(
+        head, tokens, token_parts, cotangent, there, view, feeds, norm_gains, norm_biases
+    )
+    head += [flow.kept.pop(("head", k)) for k in range(1, nm)]
+    headed(1)
+    weights = []
     came = []
     head_names = [f"{name}{n}" for n in range(len(head_groups)) for name in ("kv", "qo")]
     while len(came) < micro or not all(n in halves or flow.whole(n) for n in head_names):
@@ -980,8 +958,9 @@
             core_halves(2, head_names)
         if len(came) == 1:
             grad_parts = [pack(cotangent[:, 0], k) for k in range(micro)]
-        came, token_parts, grad_parts, feeds, halves = flow.land(
-            came, token_parts, grad_parts, feeds, halves
+            gains, biases = by_place(norm_gains[0]), by_place(norm_biases[0])
+        came, token_parts, grad_parts, feeds, halves, gains, biases, view = flow.land(
+            came, token_parts, grad_parts, feeds, halves, gains, biases, view
         )
 
     def turn():
@@ -989,22 +968,18 @@
             feeds.append(ring(feeds[-1], 1, nm))
 
     def turned():
-        if len(weights) < firsts and len(weights) < len(feeds):
-            weights.append(gather(feeds[len(weights)]))
+        if not weights and len(feeds) >= firsts:
+            weights.append(gather(jnp.stack(feeds[:firsts])))
         for n, group in enumerate(groups):
             if f"up{n}" not in flow.order and group[-1] < len(feeds):
                 flow.add(f"up{n}", jnp.stack([feeds[k][0] for k in group]), forth)
                 flow.add(f"down{n}", jnp.stack([feeds[k][1] for k in group]), back)
 
     last = [f"{name}{n}" for n in range(len(groups)) for name in ("up", "down")]
-    slot = jnp.stack([(step_here - t) % micro for t in range(micro)])
-    within = (slot[:, None] * chunk + jnp.arange(chunk)[None]).reshape(-1)
-    position = jnp.stack([(rank ^ j) * rows + within for j in range(ranks)])
-    bias = jnp.where(position < TRI + view[0] * VIEW_TOK, 0.0, -1.0).astype(F32)
     core_halves(len(head_names), head_names)
     turn()
     x, normed, n_flip = first_norm(came, gains[:1], biases[:1])
-    x, normed, n_flip, bias, halves, feeds = flow.land(x, normed, n_flip, bias, halves, feeds)
+    x, normed, n_flip, halves, feeds, view = flow.land(x, normed, n_flip, halves, feeds, view)
     turned()
 
     def both(name):
@@ -1015,8 +990,9 @@
 
     turn()
     flow.launch()
+    views = lax.ppermute(view, ("dp", "mp"), routes(0))
     own_kv = project(normed, kv, 0, 2)
-    own_kv, normed, qo, feeds = flow.land(own_kv, normed, qo, feeds)
+    own_kv, normed, qo, feeds, views = flow.land(own_kv, normed, qo, feeds, views)
     turned()
 
     def swap_rank(value, bit):
@@ -1033,6 +1009,10 @@
     turn()
     flow.launch()
     query = project(normed, qo, 0, 1)
+    slot = jnp.stack([(step_here - t) % micro for t in range(micro)])
+    within = (slot[:, None] * chunk + jnp.arange(chunk)[None]).reshape(-1)
+    position = jnp.stack([(rank ^ j) * rows + within for j in range(ranks)])
+    bias = jnp.where(position < TRI + views[0] * VIEW_TOK, 0.0, -1.0).astype(F32)
     kvs, query, bias, grad_parts, feeds = flow.land(kvs, query, bias, grad_parts, feeds)
     turned()
 
@@ -1077,7 +1057,10 @@
     hid, gmid, attn, attn_flip, sums_two, flip_two, output, out_chunks = sums.land(
         hid, gmid, attn, attn_flip, sums_two, flip_two, output, out_chunks
     )
-    grads_up = over_dp(wide_grad(flip_two, hid, index))
+    grads_up = jnp.take(
+        over_dp(wide_grad(flip_two, hid, index))[0], (mp - jnp.arange(nm)) % nm, axis=0
+    )
+    grads_up = lax.psum_scatter(grads_up, "mp", scatter_dimension=0, tiled=True)
     grad_mixed = project(attn, qo, 1, 1)
 
     dqs, dkvs = {}, {}
@@ -1110,9 +1093,7 @@
     for k in list(reversed(range(nm))) + [-1]:
         if k == 0:
             sums.add_line("down", grads_down[0], rings=False)
-        if k < 0:
-            sums.add_line("up", grads_up[0], rings=True)
-        sums.launch(direct=1 if k >= 0 else 0)
+        sums.launch(direct=1 if k < 0 else 0, z=nm - 1)
         while k >= 0 and len(output) < min(micro, nm - k + 1):
             output.append(send_chunk(out_chunks, len(output)))
         ready = head_grads()
@@ -1130,19 +1111,20 @@
             add_heads(ready, outs)
 
     sums.launch()
+    ready = head_grads()
     first, sums_one = first_back(
         x,
         gmid,
         gains[:1],
         [dqs[k] for k in range(nm)],
-        [dkvs.get(k, dkv_part[k]) for k in range(nm)],
+        [dkvs[k] if k else dkv_part[k] for k in range(nm)],
         dkv_came[0],
         qo,
         kv,
     )
-    first, sums_one, dkv_part, dkv_came, output = sums.land(
-        first, sums_one, dkv_part, dkv_came, output
-    )
+    first, sums_one, outs, output = sums.land(first, sums_one, ready and ready[1], output)
+    if ready:
+        add_heads(ready, outs)
     first = first.reshape((micro, chunk, width))
     vectors = jnp.take(
         jnp.concatenate([sums_one, sums_two]).reshape(4, nd, width // nd),
@@ -1150,34 +1132,26 @@
         axis=1,
     ).reshape(4, width)
     hops = [lambda value, bit=1 << b: swap(value, bit, nd) for b in range(nd.bit_length() - 1)]
-    hops += [
-        lambda value, bit=1 << b: lax.ppermute(value, "mp", [(i, i ^ bit) for i in range(nm)])
-        for b in range(nm.bit_length() - 1)
-    ]
     grad_tokens = []
-    while sums.busy() or hops or len(grad_tokens) < micro:
-        z = 1 if not grad_tokens else 2
+    while sums.busy() or len(grad_tokens) < micro:
         if len(grad_tokens) < micro:
             grad_tokens.append(send_chunk(first, len(grad_tokens)))
-        sums.launch(direct=2, z=z)
-        if len(grad_tokens) == micro:
-            for _ in range(min(3, len(hops))):
-                vectors = vectors + hops.pop(0)(vectors)
-        ready = head_grads()
-        grad_tokens, first, outs, vectors, output = sums.land(
-            grad_tokens, first, ready and ready[1], vectors, output
-        )
-        if ready:
-            add_heads(ready, outs)
-    g_head, g_up, g_down = (sums.done[name] for name in ("head", "up", "down"))
+            if len(grad_tokens) == micro:
+                output = unpack(output)
+        sums.launch()
+        while hops:
+            vectors = vectors + hops.pop(0)(vectors)
+        grad_tokens, first, vectors, output = sums.land(grad_tokens, first, vectors, output)
+    g_head, g_down = sums.done["head"], sums.done["down"]
+    vectors = sum([ring(vectors, k, nm) for k in range(1, nm)], vectors)
     share = width // (nd * nm)
     vectors = lax.dynamic_slice_in_dim(vectors, (dp * nm + mp) * share, share, 1)
     return (
-        unpack(output)[:, None],
+        output[:, None],
         unpack(grad_tokens)[:, None],
         jnp.concatenate([g_head[:1], g_head[2:]])[None],
         g_head[1][None],
-        g_up[None],
+        grads_up.astype(F32),
         g_down[None],
         jnp.stack([vectors[0], vectors[2]])[None],
         vectors[1][None],

time: 541 us -> 515 us (0.952)
  waiting for transfers between devices: 88.1 us -> 67.5 us
  starting transfers between devices: 88.4 us -> 80.6 us
    ppermute x39 -> x42, waiting for transfers between devices: 35.4 us -> 21.1 us  [swap(): return lax.ppermute(value, 'dp', [(i, i ^ bit) for i in range(nd)])]
    ppermute x15, waiting for transfers between devices: 48.5 us -> 36.2 us  [ring(): return lax.ppermute(value, 'mp', [(i, (i + step) % nm) for i in range(nm)])]
    ppermute x4, waiting for transfers between devices: 0.01 us -> 10.2 us  [send(): return lax.ppermute(packed[k], ('dp', 'mp'), routes(k))]
    ppermute x39 -> x42, starting transfers between devices: 41.1 us -> 33.2 us  [swap(): return lax.ppermute(value, 'dp', [(i, i ^ bit) for i in range(nd)])]
    ppermute x4, starting transfers between devices: 9.61 us -> 15.4 us  [send(): return lax.ppermute(packed[k], ('dp', 'mp'), routes(k))]
    unnamed x120 -> x144, local copies, waits for them, and re-layouts: 11.3 us -> 12.6 us
  transfers between devices with their start and end apart: 69 -> 70, of which waited for: 23 -> 18; matrix products, arithmetic and copies ran while one was open for 6% -> 7% of each run, Pallas kernels for 45% -> 50%
where the time goes in v5:
time: 515 us; the launch traced here: 506 us
  Pallas kernels  288 us (56%)
  starting transfers between devices  80.6 us (16%)
  waiting for transfers between devices  67.5 us (13%)
  other arithmetic  27.6 us (5%)
  local copies, waits for them, and re-layouts  27.4 us (5%)
  between operations  15.7 us (3%)
    pallas_call x4, Pallas kernels, attend_back(): pl.pallas_call(functools.partial(attend_back_kernel, parts), grid=(count,...  69.8 us
    pallas_call x4, Pallas kernels, attend(): pl.pallas_call(functools.partial(attend_kernel, parts), grid=(count, rows...  46.1 us
    ppermute x15, waiting for transfers between devices, ring(): return lax.ppermute(value, 'mp', [(i, (i + step) % nm) for i in range(nm)])  36.2 us
    ppermute x42, starting transfers between devices, swap(): return lax.ppermute(value, 'dp', [(i, i ^ bit) for i in range(nd)])  33.2 us
    pallas_call x1, Pallas kernels, feed_back(): pl.pallas_call(functools.partial(feed_back_kernel, firsts, sizes), grid=(...  27.9 us
    pallas_call x2, Pallas kernels, wide_grad(): pl.pallas_call(wide_grad_kernel, grid=(nm, hidden // block), in_specs=[pl...  25.5 us
    pallas_call x1, Pallas kernels, feed(): pl.pallas_call(functools.partial(feed_kernel, firsts, sizes), grid=(nm,),...  23.4 us
    pallas_call x4, Pallas kernels, head_grad(): pl.pallas_call(head_grad_kernel, in_specs=[WHOLE] * 6, out_specs=[WHOLE]...  22.7 us
  transfers between devices with their start and end apart: 70, of which 18 were waited for; matrix products, arithmetic and copies ran while one was open for 7% of the time, Pallas kernels for 50%

profile of v5, /device:TPU:0, one launch (start us, length us, event | category | flops | bytes accessed | tf_op | source)
XLA Modules:
  0.0 506.3 jit_solution(12996889954569403929)
XLA Ops:
  9.9 4.1 collective-permute-start
  54.8 11.1 %collective-permute-start.14 = (bf16[384,1024]{1,0:T(8,128)(2,1)S(1)}, bf16[384,1024]{1,0:T(8,128)(2,1)S(1)}, u32[]{:S(2)}, u32[]{:S(2)}) collective-permute-start(bf16[384,1024]{1,0:T(8,128)(2,1)S(1)} %copy-done.20), channel_id=1, source_target_pairs={{0,2},{1,0},{2,6},{3,4},{4,3},{5,1},{6,7},{7,5},{8,10},{9,8},{10,1... | collective-permute-start | bytes 2359304 | tf_op jit(solution)/shard_map/ppermute | solution.py:905
  71.8 10.1 %collective-permute-done.14.refs_1_ = bf16[384,1024]{1,0:T(8,128)(2,1)S(1)} collective-permute-done((bf16[384,1024]{1,0:T(8,128)(2,1)S(1)}, bf16[384,1024]{1,0:T(8,128)(2,1)S(1)}, u32[]{:S(2)}, u32[]{:S(2)}) %collective-permute-start.14) | collective-permute-done | bytes 786464 | tf_op jit(solution)/shard_map/ppermute | solution.py:905
  86.1 4.8 first_norm.1
  90.9 10.1 %collective-permute-done.17 = bf16[2,128,1024]{2,1,0:T(8,128)(2,1)} collective-permute-done((bf16[2,128,1024]{2,1,0:T(8,128)(2,1)S(1)}, bf16[2,128,1024]{2,1,0:T(8,128)(2,1)}, u32[]{:S(2)}, u32[]{:S(2)}) %collective-permute-start.17) | collective-permute-done | bytes 524320 | tf_op jit(solution)/shard_map/ppermute | solution.py:53
  106.7 7.1 %project.3.refs_0_.refs_2_ = bf16[2,768,1024]{2,1,0:T(8,128)(2,1)} custom-call(bf16[768,1024]{1,0:T(8,128)(2,1)} %get-tuple-element.355.in_ref, bf16[4,1,2,128,256]{4,3,2,1,0:T(8,128)(2,1)} %copy-done.7, bf16[4,3,2,128,256]{4,3,2,1,0:T(8,128)(2,1)} %copy-done.6, bf16[4,1,2,128,256]{4,3,2,1,0:T(8,128)(2,1)} %copy-done.29, bf16[4,3,2,128,256]{4,3,2,1,0:T(8,128)(2,1)} %copy-done.15), custom_call_target="tpu_custom_call" | custom-call | flops 3221225472 | bytes 3145728 | tf_op jit(solution)/shard_map/project/pallas_call | solution.py:270
  113.8 6.5 %collective-permute-done.18 = bf16[2,128,1024]{2,1,0:T(8,128)(2,1)S(1)} collective-permute-done((bf16[2,128,1024]{2,1,0:T(8,128)(2,1)}, bf16[2,128,1024]{2,1,0:T(8,128)(2,1)S(1)}, u32[]{:S(2)}, u32[]{:S(2)}) %collective-permute-start.18) | collective-permute-done | bytes 524320 | tf_op jit(solution)/shard_map/ppermute | solution.py:53
  121.7 5.0 project.4.q_ref
  126.7 9.7 %collective-permute-done.21 = bf16[2,128,1024]{2,1,0:T(8,128)(2,1)S(1)} collective-permute-done((bf16[2,128,1024]{2,1,0:T(8,128)(2,1)S(1)}, bf16[2,128,1024]{2,1,0:T(8,128)(2,1)S(1)}, u32[]{:S(2)}, u32[]{:S(2)}) %collective-permute-start.21) | collective-permute-done | bytes 524320 | tf_op jit(solution)/shard_map/ppermute | solution.py:53
  139.3 11.5 %attend.4 = (bf16[768,256]{1,0:T(8,128)(2,1)}, f32[2,2,768]{2,1,0:T(2,128)}) custom-call(bf16[1,768,1024]{2,1,0:T(8,128)(2,1)} %project.4.q_ref, bf16[2,768,1024]{2,1,0:T(8,128)(2,1)} %project.3.refs_0_.refs_2_, bf16[2,768,1024]{2,1,0:T(8,128)(2,1)} %collective-permute-done.20.refs_1_.refs_3_, bf16[2,768,1024]{2,1,0:T(8,128)(2,1)} %project.3.refs_0_.refs_2_, ...), custom_call_target="tpu_custom_call" | custom-call | flops 4831838208 | bytes 3145728 | tf_op jit(solution)/shard_map/attend/pallas_call | solution.py:319
  150.8 11.5 %attend.5 = (bf16[768,256]{1,0:T(8,128)(2,1)}, f32[2,2,768]{2,1,0:T(2,128)}) custom-call(bf16[1,768,1024]{2,1,0:T(8,128)(2,1)} %project.4.q_ref, bf16[2,768,1024]{2,1,0:T(8,128)(2,1)} %project.3.refs_0_.refs_2_, bf16[2,768,1024]{2,1,0:T(8,128)(2,1)} %collective-permute-done.20.refs_1_.refs_3_, bf16[2,768,1024]{2,1,0:T(8,128)(2,1)} %project.3.refs_0_.refs_2_, ...), custom_call_target="tpu_custom_call" | custom-call | flops 4831838208 | bytes 3145728 | tf_op jit(solution)/shard_map/attend/pallas_call | solution.py:319
  168.0 11.5 %attend.6 = (bf16[768,256]{1,0:T(8,128)(2,1)}, f32[2,2,768]{2,1,0:T(2,128)}) custom-call(bf16[1,768,1024]{2,1,0:T(8,128)(2,1)} %project.4.q_ref, bf16[2,768,1024]{2,1,0:T(8,128)(2,1)} %project.3.refs_0_.refs_2_, bf16[2,768,1024]{2,1,0:T(8,128)(2,1)} %collective-permute-done.20.refs_1_.refs_3_, bf16[2,768,1024]{2,1,0:T(8,128)(2,1)} %project.3.refs_0_.refs_2_, ...), custom_call_target="tpu_custom_call" | custom-call | flops 4831838208 | bytes 3145728 | tf_op jit(solution)/shard_map/attend/pallas_call | solution.py:319
  179.5 11.5 %attend.7 = (bf16[768,256]{1,0:T(8,128)(2,1)}, f32[2,2,768]{2,1,0:T(2,128)}) custom-call(bf16[1,768,1024]{2,1,0:T(8,128)(2,1)} %project.4.q_ref, bf16[2,768,1024]{2,1,0:T(8,128)(2,1)} %project.3.refs_0_.refs_2_, bf16[2,768,1024]{2,1,0:T(8,128)(2,1)} %collective-permute-done.20.refs_1_.refs_3_, bf16[2,768,1024]{2,1,0:T(8,128)(2,1)} %project.3.refs_0_.refs_2_, ...), custom_call_target="tpu_custom_call" | custom-call | flops 4831838208 | bytes 3145728 | tf_op jit(solution)/shard_map/attend/pallas_call | solution.py:319
  193.3 4.3 flip.1
  197.6 6.7 %middle_norm.1 = (f32[768,1024]{1,0:T(8,128)}, bf16[768,1024]{1,0:T(8,128)(2,1)}, bf16[1024,768]{1,0:T(8,128)(2,1)}) custom-call(bf16[768,1024]{1,0:T(8,128)(2,1)} %get-tuple-element.391.x_ref, bf16[768,256]{1,0:T(8,128)(2,1)} %get-tuple-element.392.refs_0_.refs_6_.mixed_ref, bf16[768,256]{1,0:T(8,128)(2,1)} %get-tuple-element.393.refs_1_.refs_6_.mixed_ref, ...), custom_call_target="tpu_custom_call" | custom-call | flops 1610612736 | bytes 11010048 | tf_op jit(solution)/shard_map/middle_norm/pallas_call | solution.py:436
  205.7 23.4 %feed.1 = (bf16[768,1024]{1,0:T(8,128)(2,1)}, bf16[4,768,1024]{2,1,0:T(8,128)(2,1)}, bf16[4,768,1024]{2,1,0:T(8,128)(2,1)}) custom-call(s32[8]{0:T(128)} %copy-done.60, bf16[8,2,2,128,1024]{4,3,2,1,0:T(8,128)(2,1)} %bitcast.213, bf16[4,2,128,1024]{3,2,1,0:T(8,128)(2,1)} %copy-done.8, bf16[4,2,128,1024]{3,2,1,0:T(8,128)(2,1)} %collective-permute-done.28.refs_2_, ...), custom_call_target="tpu_custom_call" | custom-call | flops 12884901888 | bytes 16777216 | tf_op jit(solution)/shard_map/feed/pallas_call | solution.py:528
  229.1 12.4 %wide_grad.2 = bf16[8,4,128,1024]{3,2,1,0:T(8,128)(2,1)} custom-call(s32[8]{0:T(128)} %copy-done.60, bf16[1024,768]{1,0:T(8,128)(2,1)} %get-tuple-element.457.a_ref, bf16[4,768,1024]{2,1,0:T(8,128)(2,1)} %get-tuple-element.458.b_ref), custom_call_target="tpu_custom_call" | custom-call | flops 6442450944 | bytes 16777216 | tf_op jit(solution)/shard_map/wide_grad/pallas_call | solution.py:632
  243.9 27.9 %feed_back.1 = (bf16[4,768,1024]{2,1,0:T(8,128)(2,1)}, f32[768,1024]{1,0:T(8,128)}, bf16[768,1024]{1,0:T(8,128)(2,1)}, bf16[1024,768]{1,0:T(8,128)(2,1)}, f32[2,1024]{1,0:T(2,128)}) custom-call(s32[8]{0:T(128)} %copy-done.60, bf16[8,2,2,128,1024]{4,3,2,1,0:T(8,128)(2,1)} %bitcast.214, bf16[4,2,128,1024]{3,2,1,0:T(8,128)(2,1)} %copy-done.8, ...), custom_call_target="tpu_custom_call" | custom-call | flops 12884901888 | bytes 16777216 | tf_op jit(solution)/shard_map/feed_back/pallas_call | solution.py:589
  271.9 13.1 %wide_grad.3 = bf16[8,4,128,1024]{3,2,1,0:T(8,128)(2,1)} custom-call(s32[8]{0:T(128)} %copy-done.60, bf16[1024,768]{1,0:T(8,128)(2,1)} %get-tuple-element.562.a_ref, bf16[4,768,1024]{2,1,0:T(8,128)(2,1)} %get-tuple-element.563.b_ref), custom_call_target="tpu_custom_call" | custom-call | flops 6442450944 | bytes 16777216 | tf_op jit(solution)/shard_map/wide_grad/pallas_call | solution.py:632
  290.2 5.0 project.5.refs_7_
  295.2 17.4 %attend_back.4 = (bf16[768,256]{1,0:T(8,128)(2,1)}, bf16[2,768,256]{2,1,0:T(8,128)(2,1)}, bf16[2,768,256]{2,1,0:T(8,128)(2,1)}) custom-call(bf16[1,768,1024]{2,1,0:T(8,128)(2,1)} %project.4.q_ref, bf16[2,768,1024]{2,1,0:T(8,128)(2,1)} %project.3.refs_0_.refs_2_, bf16[2,768,1024]{2,1,0:T(8,128)(2,1)} %collective-permute-done.20.refs_1_.refs_3_, ...), custom_call_target="tpu_custom_call" | custom-call | flops 12079595520 | bytes 6291456 | tf_op jit(solution)/shard_map/attend_back/pallas_call | solution.py:387
  312.7 17.5 %attend_back.5 = (bf16[768,256]{1,0:T(8,128)(2,1)}, bf16[2,768,256]{2,1,0:T(8,128)(2,1)}, bf16[2,768,256]{2,1,0:T(8,128)(2,1)}) custom-call(bf16[1,768,1024]{2,1,0:T(8,128)(2,1)} %project.4.q_ref, bf16[2,768,1024]{2,1,0:T(8,128)(2,1)} %project.3.refs_0_.refs_2_, bf16[2,768,1024]{2,1,0:T(8,128)(2,1)} %collective-permute-done.20.refs_1_.refs_3_, ...), custom_call_target="tpu_custom_call" | custom-call | flops 12079595520 | bytes 6291456 | tf_op jit(solution)/shard_map/attend_back/pallas_call | solution.py:387
  331.2 5.7 %head_grad.4 = (bf16[2,768,256]{2,1,0:T(8,128)(2,1)}, bf16[4,4,128,256]{3,2,1,0:T(8,128)(2,1)}, bf16[4,4,128,256]{3,2,1,0:T(8,128)(2,1)}) custom-call(bf16[1024,768]{1,0:T(8,128)(2,1)} %get-tuple-element.341.n_ref, bf16[1024,768]{1,0:T(8,128)(2,1)} %get-tuple-element.418.g_ref, bf16[768,256]{1,0:T(8,128)(2,1)} %get-tuple-element.395.refs_3_.refs_6_.mixed_ref, ...), custom_call_target="tpu_custom_call" | custom-call | flops 1610612736 | bytes 2097152 | tf_op jit(solution)/shard_map/head_grad/pallas_call | solution.py:665
  336.8 17.5 %attend_back.6 = (bf16[768,256]{1,0:T(8,128)(2,1)}, bf16[2,768,256]{2,1,0:T(8,128)(2,1)}, bf16[2,768,256]{2,1,0:T(8,128)(2,1)}) custom-call(bf16[1,768,1024]{2,1,0:T(8,128)(2,1)} %project.4.q_ref, bf16[2,768,1024]{2,1,0:T(8,128)(2,1)} %project.3.refs_0_.refs_2_, bf16[2,768,1024]{2,1,0:T(8,128)(2,1)} %collective-permute-done.20.refs_1_.refs_3_, ...), custom_call_target="tpu_custom_call" | custom-call | flops 12079595520 | bytes 6291456 | tf_op jit(solution)/shard_map/attend_back/pallas_call | solution.py:387
  360.4 17.3 %attend_back.7 = (bf16[768,256]{1,0:T(8,128)(2,1)}, bf16[2,768,256]{2,1,0:T(8,128)(2,1)}, bf16[2,768,256]{2,1,0:T(8,128)(2,1)}) custom-call(bf16[1,768,1024]{2,1,0:T(8,128)(2,1)} %project.4.q_ref, bf16[2,768,1024]{2,1,0:T(8,128)(2,1)} %project.3.refs_0_.refs_2_, bf16[2,768,1024]{2,1,0:T(8,128)(2,1)} %collective-permute-done.20.refs_1_.refs_3_, ...), custom_call_target="tpu_custom_call" | custom-call | flops 12079595520 | bytes 6291456 | tf_op jit(solution)/shard_map/attend_back/pallas_call | solution.py:387
  377.8 5.7 %head_grad.5 = (bf16[2,768,256]{2,1,0:T(8,128)(2,1)}, bf16[4,4,128,256]{3,2,1,0:T(8,128)(2,1)}, bf16[4,4,128,256]{3,2,1,0:T(8,128)(2,1)}) custom-call(bf16[1024,768]{1,0:T(8,128)(2,1)} %get-tuple-element.341.n_ref, bf16[1024,768]{1,0:T(8,128)(2,1)} %get-tuple-element.418.g_ref, bf16[768,256]{1,0:T(8,128)(2,1)} %get-tuple-element.394.refs_2_.refs_6_.mixed_ref, ...), custom_call_target="tpu_custom_call" | custom-call | flops 1610612736 | bytes 2097152 | tf_op jit(solution)/shard_map/head_grad/pallas_call | solution.py:665
  390.5 5.7 %head_grad.6 = (bf16[2,768,256]{2,1,0:T(8,128)(2,1)}, bf16[4,4,128,256]{3,2,1,0:T(8,128)(2,1)}, bf16[4,4,128,256]{3,2,1,0:T(8,128)(2,1)}) custom-call(bf16[1024,768]{1,0:T(8,128)(2,1)} %get-tuple-element.341.n_ref, bf16[1024,768]{1,0:T(8,128)(2,1)} %get-tuple-element.418.g_ref, bf16[768,256]{1,0:T(8,128)(2,1)} %get-tuple-element.393.refs_1_.refs_6_.mixed_ref, ...), custom_call_target="tpu_custom_call" | custom-call | flops 1610612736 | bytes 2097152 | tf_op jit(solution)/shard_map/head_grad/pallas_call | solution.py:665
  413.9 11.6 %first_back.1 = (bf16[768,1024]{1,0:T(8,128)(2,1)}, f32[2,1024]{1,0:T(2,128)}) custom-call(bf16[768,1024]{1,0:T(8,128)(2,1)} %get-tuple-element.391.x_ref, f32[768,1024]{1,0:T(8,128)} %get-tuple-element.509.gmid_ref, f32[1,1024]{1,0:T(1,128)} %get-tuple-element.634.refs_2_.gain_ref, bf16[768,256]{1,0:T(8,128)(2,1)} %get-tuple-element.510.refs_0_.dq_ref, ...), custom_call_target="tpu_custom_call" | custom-call | flops 4831838208 | bytes 9437184 | tf_op jit(solution)/shard_map/first_back/pallas_call | solution.py:713
  425.5 5.7 %head_grad.7 = (bf16[2,768,256]{2,1,0:T(8,128)(2,1)}, bf16[4,4,128,256]{3,2,1,0:T(8,128)(2,1)}, bf16[4,4,128,256]{3,2,1,0:T(8,128)(2,1)}) custom-call(bf16[1024,768]{1,0:T(8,128)(2,1)} %get-tuple-element.341.n_ref, bf16[1024,768]{1,0:T(8,128)(2,1)} %get-tuple-element.418.g_ref, bf16[768,256]{1,0:T(8,128)(2,1)} %get-tuple-element.392.refs_0_.refs_6_.mixed_ref, ...), custom_call_target="tpu_custom_call" | custom-call | flops 1610612736 | bytes 2097152 | tf_op jit(solution)/shard_map/head_grad/pallas_call | solution.py:665
  444.5 5.9 %collective-permute-done.57 = f32[4,1024]{1,0:T(4,128)S(1)} collective-permute-done((f32[4,1024]{1,0:T(4,128)S(1)}, f32[4,1024]{1,0:T(4,128)S(1)}, u32[]{:S(2)}, u32[]{:S(2)}) %collective-permute-start.57) | collective-permute-done | bytes 16416 | tf_op jit(solution)/shard_map/ppermute | solution.py:49
  454.3 5.5 %collective-permute-done.52 = bf16[1,4,128,256]{3,2,1,0:T(8,128)(2,1)S(1)} collective-permute-done((bf16[1,4,128,256]{3,2,1,0:T(8,128)(2,1)S(1)}, bf16[1,4,128,256]{3,2,1,0:T(8,128)(2,1)S(1)}, u32[]{:S(2)}, u32[]{:S(2)}) %collective-permute-start.52) | collective-permute-done | bytes 262176 | tf_op jit(solution)/shard_map/ppermute | solution.py:49
  482.2 6.0 %collective-permute-done.61 = bf16[4,128,256]{2,1,0:T(8,128)(2,1)S(1)} collective-permute-done((bf16[4,128,256]{2,1,0:T(8,128)(2,1)S(1)}, bf16[4,128,256]{2,1,0:T(8,128)(2,1)S(1)}, u32[]{:S(2)}, u32[]{:S(2)}) %collective-permute-start.61) | collective-permute-done | bytes 262176 | tf_op jit(solution)/shard_map/ppermute | solution.py:53
  (367 shorter events, 161.7 us)
Async XLA Ops:
  7.2 198.5 %all-gather.3.cloned.1.call-start = ((), (), s32[]{:S(2)}) async-start(), calls=%async_computation.6 | async-start | bytes 9437184 | tf_op jit(solution)/shard_map/all_gather | solution.py:972
  9.9 22.5 %collective-permute-start = (bf16[4,128,256]{2,1,0:T(8,128)(2,1)S(1)}, bf16[4,128,256]{2,1,0:T(8,128)(2,1)S(1)}, u32[]{:S(2)}, u32[]{:S(2)}) collective-permute-start(bf16[4,128,256]{2,1,0:T(8,128)(2,1)S(1)} %pad_maximum_fusion.16), channel_id=1, source_target_pairs={{0,2},{1,3},{2,0},{3,1},{4,6},{5,7},{6,4},{7,5},{8,10},{9,11},{10,... | collective-permute-start | bytes 786440 | tf_op jit(solution)/shard_map/ppermute | solution.py:53
  14.0 18.4 %collective-permute-start.1 = (bf16[4,128,256]{2,1,0:T(8,128)(2,1)S(1)}, bf16[4,128,256]{2,1,0:T(8,128)(2,1)S(1)}, u32[]{:S(2)}, u32[]{:S(2)}) collective-permute-start(bf16[4,128,256]{2,1,0:T(8,128)(2,1)S(1)} %pad_maximum_fusion.16), channel_id=1, source_target_pairs={{0,1},{1,2},{2,3},{3,0},{4,5},{5,6},{6,7},{7,4},{8,9},{9,10},{10,1... | collective-permute-start | bytes 786440 | tf_op jit(solution)/shard_map/ppermute | solution.py:53
  51.5 20.3 %collective-permute-start.10 = (bf16[2,3,2,128,256]{4,3,2,1,0:T(8,128)(2,1)S(1)}, bf16[2,3,2,128,256]{4,3,2,1,0:T(8,128)(2,1)S(1)}, u32[]{:S(2)}, u32[]{:S(2)}) collective-permute-start(bf16[2,3,2,128,256]{4,3,2,1,0:T(8,128)(2,1)S(1)} %pad_maximum_fusion.7), channel_id=1, source_target_pairs={{0,8},{4,12},{8,0},{12,4},{16,24},{20,28},{24,16},{28,20},{1,9},{5... | collective-permute-start | bytes 2359304 | tf_op jit(solution)/shard_map/ppermute | solution.py:49
  53.2 18.6 %collective-permute-start.11 = (bf16[2,3,2,128,256]{4,3,2,1,0:T(8,128)(2,1)S(1)}, bf16[2,3,2,128,256]{4,3,2,1,0:T(8,128)(2,1)S(1)}, u32[]{:S(2)}, u32[]{:S(2)}) collective-permute-start(bf16[2,3,2,128,256]{4,3,2,1,0:T(8,128)(2,1)S(1)} %pad_maximum_fusion.8), channel_id=1, source_target_pairs={{0,16},{4,20},{8,24},{12,28},{16,0},{20,4},{24,8},{28,12},{1,17},{... | collective-permute-start | bytes 2359304 | tf_op jit(solution)/shard_map/ppermute | solution.py:49
  54.8 27.1 %collective-permute-start.14 = (bf16[384,1024]{1,0:T(8,128)(2,1)S(1)}, bf16[384,1024]{1,0:T(8,128)(2,1)S(1)}, u32[]{:S(2)}, u32[]{:S(2)}) collective-permute-start(bf16[384,1024]{1,0:T(8,128)(2,1)S(1)} %copy-done.20), channel_id=1, source_target_pairs={{0,2},{1,0},{2,6},{3,4},{4,3},{5,1},{6,7},{7,5},{8,10},{9,8},{10,1... | collective-permute-start | bytes 2359304 | tf_op jit(solution)/shard_map/ppermute | solution.py:905
  83.0 18.0 %collective-permute-start.15 = (bf16[4,3,2,128,256]{4,3,2,1,0:T(8,128)(2,1)S(1)}, bf16[4,3,2,128,256]{4,3,2,1,0:T(8,128)(2,1)S(1)}, u32[]{:S(2)}, u32[]{:S(2)}) collective-permute-start(bf16[4,3,2,128,256]{4,3,2,1,0:T(8,128)(2,1)S(1)} %pad_maximum_fusion.2.refs_1_.refs_14_), channel_id=1, source_target_pairs={{0,4},{4,0},{8,12},{12,8},{16,20},{20,16},{24,28},{28,24},{1,5},{5... | collective-permute-start | bytes 4718600 | tf_op jit(solution)/shard_map/ppermute | solution.py:49
  104.7 250.8 %reduce-scatter.4.cloned.1.call-start = ((), (), s32[]{:S(2)}) async-start(), calls=%async_computation.3 | async-start | bytes 9437184 | tf_op jit(solution)/shard_map/reduce_scatter | solution.py:1053
  136.5 25.8 %collective-permute-start.22 = (bf16[1,2,128,1024]{3,2,1,0:T(8,128)(2,1)S(1)}, bf16[1,2,128,1024]{3,2,1,0:T(8,128)(2,1)S(1)}, u32[]{:S(2)}, u32[]{:S(2)}) collective-permute-start(bf16[1,2,128,1024]{3,2,1,0:T(8,128)(2,1)S(1)} %get-tuple-element.608), channel_id=1, source_target_pairs={{0,8},{4,12},{8,0},{12,4},{16,24},{20,28},{24,16},{28,20},{1,9},{5... | collective-permute-start | bytes 1572872 | tf_op jit(solution)/shard_map/ppermute | solution.py:49
  137.8 25.6 %collective-permute-start.23 = (bf16[1,2,128,1024]{3,2,1,0:T(8,128)(2,1)S(1)}, bf16[1,2,128,1024]{3,2,1,0:T(8,128)(2,1)S(1)}, u32[]{:S(2)}, u32[]{:S(2)}) collective-permute-start(bf16[1,2,128,1024]{3,2,1,0:T(8,128)(2,1)S(1)} %get-tuple-element.606), channel_id=1, source_target_pairs={{0,16},{4,20},{8,24},{12,28},{16,0},{20,4},{24,8},{28,12},{1,17},{... | collective-permute-start | bytes 1572872 | tf_op jit(solution)/shard_map/ppermute | solution.py:49
  138.4 24.9 %collective-permute-start.24 = (bf16[384,1024]{1,0:T(8,128)(2,1)S(1)}, bf16[384,1024]{1,0:T(8,128)(2,1)S(1)}, u32[]{:S(2)}, u32[]{:S(2)}) collective-permute-start(bf16[384,1024]{1,0:T(8,128)(2,1)S(1)} %copy-done.19), channel_id=1, source_target_pairs={{0,0},{1,2},{2,4},{3,6},{4,1},{5,3},{6,5},{7,7},{8,8},{9,10},{10,1... | collective-permute-start | bytes 2359304 | tf_op jit(solution)/shard_map/ppermute | solution.py:905
  163.4 27.6 %collective-permute-start.25 = (bf16[2,2,128,1024]{3,2,1,0:T(8,128)(2,1)S(1)}, bf16[2,2,128,1024]{3,2,1,0:T(8,128)(2,1)S(1)}, u32[]{:S(2)}, u32[]{:S(2)}) collective-permute-start(bf16[2,2,128,1024]{3,2,1,0:T(8,128)(2,1)S(1)} %pad_maximum_fusion.5), channel_id=1, source_target_pairs={{0,8},{4,12},{8,0},{12,4},{16,24},{20,28},{24,16},{28,20},{1,9},{5... | collective-permute-start | bytes 3145736 | tf_op jit(solution)/shard_map/ppermute | solution.py:49
  164.6 26.5 %collective-permute-start.26 = (bf16[2,2,128,1024]{3,2,1,0:T(8,128)(2,1)S(1)}, bf16[2,2,128,1024]{3,2,1,0:T(8,128)(2,1)S(1)}, u32[]{:S(2)}, u32[]{:S(2)}) collective-permute-start(bf16[2,2,128,1024]{3,2,1,0:T(8,128)(2,1)S(1)} %pad_maximum_fusion.6), channel_id=1, source_target_pairs={{0,16},{4,20},{8,24},{12,28},{16,0},{20,4},{24,8},{28,12},{1,17},{... | collective-permute-start | bytes 3145736 | tf_op jit(solution)/shard_map/ppermute | solution.py:49
  165.4 25.7 %collective-permute-start.27 = (bf16[384,1024]{1,0:T(8,128)(2,1)S(1)}, bf16[384,1024]{1,0:T(8,128)(2,1)S(1)}, u32[]{:S(2)}, u32[]{:S(2)}) collective-permute-start(bf16[384,1024]{1,0:T(8,128)(2,1)S(1)} %copy-done.18), channel_id=1, source_target_pairs={{0,2},{1,0},{2,6},{3,4},{4,3},{5,1},{6,7},{7,5},{8,10},{9,8},{10,1... | collective-permute-start | bytes 2359304 | tf_op jit(solution)/shard_map/ppermute | solution.py:905
  241.6 154.6 %reduce-scatter.6.cloned.1.call-start = ((), (), s32[]{:S(2)}) async-start(), calls=%async_computation.4 | async-start | bytes 9437184 | tf_op jit(solution)/shard_map/reduce_scatter | solution.py:1061
  243.0 28.9 %collective-permute-start.30 = (bf16[384,1024]{1,0:T(8,128)(2,1)S(1)}, bf16[384,1024]{1,0:T(8,128)(2,1)S(1)}, u32[]{:S(2)}, u32[]{:S(2)}) collective-permute-start(bf16[384,1024]{1,0:T(8,128)(2,1)S(1)} %slice.176), channel_id=1, source_target_pairs={{0,0},{2,1},{4,2},{6,3},{1,4},{3,5},{5,6},{7,7},{8,8},{10,9},{12,1... | collective-permute-start | bytes 2359304 | tf_op jit(solution)/shard_map/ppermute | solution.py:908
  285.0 189.0 %reduce-scatter.8.cloned.1.call-start = ((), (), s32[]{:S(2)}) async-start(), calls=%async_computation.5 | async-start | bytes 1310720 | tf_op jit(solution)/shard_map/reduce_scatter | solution.py:1063
  286.9 25.6 %collective-permute-start.31 = (bf16[384,1024]{1,0:T(8,128)(2,1)S(1)}, bf16[384,1024]{1,0:T(8,128)(2,1)S(1)}, u32[]{:S(2)}, u32[]{:S(2)}) collective-permute-start(bf16[384,1024]{1,0:T(8,128)(2,1)S(1)} %slice_bitcast_fusion.1), channel_id=1, source_target_pairs={{2,0},{0,1},{6,2},{4,3},{3,4},{1,5},{7,6},{5,7},{10,8},{8,9},{14,1... | collective-permute-start | bytes 2359304 | tf_op jit(solution)/shard_map/ppermute | solution.py:908
  330.3 24.0 %collective-permute-start.33 = (bf16[2,768,256]{2,1,0:T(8,128)(2,1)}, bf16[2,768,256]{2,1,0:T(8,128)(2,1)S(1)}, u32[]{:S(2)}, u32[]{:S(2)}) collective-permute-start(bf16[2,768,256]{2,1,0:T(8,128)(2,1)} %get-tuple-element.451), channel_id=1, source_target_pairs={{0,4},{4,0},{8,12},{12,8},{16,20},{20,16},{24,28},{28,24},{1,5},{5... | collective-permute-start | bytes 2359304 | tf_op jit(solution)/shard_map/ppermute | solution.py:49
  354.4 29.1 %collective-permute-start.34 = (bf16[1,4,4,128,256]{4,3,2,1,0:T(8,128)(2,1)S(1)}, bf16[1,4,4,128,256]{4,3,2,1,0:T(8,128)(2,1)S(1)}, u32[]{:S(2)}, u32[]{:S(2)}) collective-permute-start(bf16[1,4,4,128,256]{4,3,2,1,0:T(8,128)(2,1)S(1)} %bitcast.218), channel_id=1, source_target_pairs={{0,4},{4,0},{8,12},{12,8},{16,20},{20,16},{24,28},{28,24},{1,5},{5... | collective-permute-start | bytes 3145736 | tf_op jit(solution)/shard_map/ppermute | solution.py:49
  355.2 28.2 %collective-permute-start.38 = (bf16[2,768,256]{2,1,0:T(8,128)(2,1)}, bf16[2,768,256]{2,1,0:T(8,128)(2,1)S(1)}, u32[]{:S(2)}, u32[]{:S(2)}) collective-permute-start(bf16[2,768,256]{2,1,0:T(8,128)(2,1)} %get-tuple-element.472), channel_id=1, source_target_pairs={{0,4},{4,0},{8,12},{12,8},{16,20},{20,16},{24,28},{28,24},{1,5},{5... | collective-permute-start | bytes 2359304 | tf_op jit(solution)/shard_map/ppermute | solution.py:49
  356.7 26.7 %collective-permute-start.35 = (bf16[128,1024]{1,0:T(8,128)(2,1)S(1)}, bf16[128,1024]{1,0:T(8,128)(2,1)S(1)}, u32[]{:S(2)}, u32[]{:S(2)}) collective-permute-start(bf16[128,1024]{1,0:T(8,128)(2,1)S(1)} %get-tuple-element.599), channel_id=1, source_target_pairs={{0,3},{1,0},{2,1},{3,2},{4,7},{5,4},{6,5},{7,6},{8,11},{9,8},{10,9... | collective-permute-start | bytes 786440 | tf_op jit(solution)/shard_map/ppermute | solution.py:53
  359.6 23.9 %collective-permute-start.36 = (bf16[128,1024]{1,0:T(8,128)(2,1)S(1)}, bf16[128,1024]{1,0:T(8,128)(2,1)S(1)}, u32[]{:S(2)}, u32[]{:S(2)}) collective-permute-start(bf16[128,1024]{1,0:T(8,128)(2,1)S(1)} %get-tuple-element.598), channel_id=1, source_target_pairs={{0,1},{1,2},{2,3},{3,0},{4,5},{5,6},{6,7},{7,4},{8,9},{9,10},{10,1... | collective-permute-start | bytes 786440 | tf_op jit(solution)/shard_map/ppermute | solution.py:53
  359.8 23.7 %collective-permute-start.37 = (bf16[128,1024]{1,0:T(8,128)(2,1)S(1)}, bf16[128,1024]{1,0:T(8,128)(2,1)S(1)}, u32[]{:S(2)}, u32[]{:S(2)}) collective-permute-start(bf16[128,1024]{1,0:T(8,128)(2,1)S(1)} %get-tuple-element.597), channel_id=1, source_target_pairs={{0,2},{1,3},{2,0},{3,1},{4,6},{5,7},{6,4},{7,5},{8,10},{9,11},{10,... | collective-permute-start | bytes 786440 | tf_op jit(solution)/shard_map/ppermute | solution.py:53
  402.1 30.6 %collective-permute-start.44 = (bf16[1,4,4,128,256]{4,3,2,1,0:T(8,128)(2,1)}, bf16[1,4,4,128,256]{4,3,2,1,0:T(8,128)(2,1)S(1)}, u32[]{:S(2)}, u32[]{:S(2)}) collective-permute-start(bf16[1,4,4,128,256]{4,3,2,1,0:T(8,128)(2,1)} %bitcast.216), channel_id=1, source_target_pairs={{0,4},{4,0},{8,12},{12,8},{16,20},{20,16},{24,28},{28,24},{1,5},{5... | collective-permute-start | bytes 3145736 | tf_op jit(solution)/shard_map/ppermute | solution.py:49
  405.9 25.4 %collective-permute-start.45 = (bf16[1,4,128,256]{3,2,1,0:T(8,128)(2,1)}, bf16[1,4,128,256]{3,2,1,0:T(8,128)(2,1)S(1)}, u32[]{:S(2)}, u32[]{:S(2)}) collective-permute-start(bf16[1,4,128,256]{3,2,1,0:T(8,128)(2,1)} %get-tuple-element.503), channel_id=1, source_target_pairs={{0,8},{4,12},{8,0},{12,4},{16,24},{20,28},{24,16},{28,20},{1,9},{5... | collective-permute-start | bytes 786440 | tf_op jit(solution)/shard_map/ppermute | solution.py:49
  407.3 24.0 %collective-permute-start.46 = (bf16[1,4,128,256]{3,2,1,0:T(8,128)(2,1)}, bf16[1,4,128,256]{3,2,1,0:T(8,128)(2,1)S(1)}, u32[]{:S(2)}, u32[]{:S(2)}) collective-permute-start(bf16[1,4,128,256]{3,2,1,0:T(8,128)(2,1)} %get-tuple-element.504), channel_id=1, source_target_pairs={{0,16},{4,20},{8,24},{12,28},{16,0},{20,4},{24,8},{28,12},{1,17},{... | collective-permute-start | bytes 786440 | tf_op jit(solution)/shard_map/ppermute | solution.py:49
  407.6 23.7 %collective-permute-start.47 = (bf16[1,4,128,256]{3,2,1,0:T(8,128)(2,1)}, bf16[1,4,128,256]{3,2,1,0:T(8,128)(2,1)S(1)}, u32[]{:S(2)}, u32[]{:S(2)}) collective-permute-start(bf16[1,4,128,256]{3,2,1,0:T(8,128)(2,1)} %get-tuple-element.505), channel_id=1, source_target_pairs={{0,24},{4,28},{8,16},{12,20},{16,8},{20,12},{24,0},{28,4},{1,25},{... | collective-permute-start | bytes 786440 | tf_op jit(solution)/shard_map/ppermute | solution.py:49
  410.7 22.0 %collective-permute-start.48 = (bf16[4,128,256]{2,1,0:T(8,128)(2,1)S(1)}, bf16[4,128,256]{2,1,0:T(8,128)(2,1)S(1)}, u32[]{:S(2)}, u32[]{:S(2)}) collective-permute-start(bf16[4,128,256]{2,1,0:T(8,128)(2,1)S(1)} %fusion.8), channel_id=1, source_target_pairs={{0,3},{1,0},{2,1},{3,2},{4,7},{5,4},{6,5},{7,6},{8,11},{9,8},{10,9... | collective-permute-start | bytes 786440 | tf_op jit(solution)/shard_map/ppermute | solution.py:53
  433.4 26.4 %collective-permute-start.49 = (bf16[1,4,4,128,256]{4,3,2,1,0:T(8,128)(2,1)}, bf16[1,4,4,128,256]{4,3,2,1,0:T(8,128)(2,1)S(1)}, u32[]{:S(2)}, u32[]{:S(2)}) collective-permute-start(bf16[1,4,4,128,256]{4,3,2,1,0:T(8,128)(2,1)} %bitcast.215), channel_id=1, source_target_pairs={{0,4},{4,0},{8,12},{12,8},{16,20},{20,16},{24,28},{28,24},{1,5},{5... | collective-permute-start | bytes 3145736 | tf_op jit(solution)/shard_map/ppermute | solution.py:49
  435.8 24.0 %collective-permute-start.54 = (bf16[384,1024]{1,0:T(8,128)(2,1)S(1)}, bf16[384,1024]{1,0:T(8,128)(2,1)S(1)}, u32[]{:S(2)}, u32[]{:S(2)}) collective-permute-start(bf16[384,1024]{1,0:T(8,128)(2,1)S(1)} %slice.185), channel_id=1, source_target_pairs={{0,0},{2,1},{4,2},{6,3},{1,4},{3,5},{5,6},{7,7},{8,8},{10,9},{12,1... | collective-permute-start | bytes 2359304 | tf_op jit(solution)/shard_map/ppermute | solution.py:908
  460.8 27.3 %collective-permute-start.62 = (bf16[384,1024]{1,0:T(8,128)(2,1)S(1)}, bf16[384,1024]{1,0:T(8,128)(2,1)}, u32[]{:S(2)}, u32[]{:S(2)}) collective-permute-start(bf16[384,1024]{1,0:T(8,128)(2,1)S(1)} %slice_bitcast_fusion), channel_id=1, source_target_pairs={{2,0},{0,1},{6,2},{4,3},{3,4},{1,5},{7,6},{5,7},{10,8},{8,9},{14,1... | collective-permute-start | bytes 2359304 | tf_op jit(solution)/shard_map/ppermute | solution.py:908
  (109 other events, 922.2 us)
Sparse Core Ops, SparseCore 0:
  104.8 62.4 all-gather.2
  241.7 68.1 reduce-scatter.3
  313.7 72.1 reduce-scatter.5
  403.4 33.2 reduce-scatter.7

commit v6 on v5

--- a/solution.py
+++ b/solution.py
@@ -193,15 +193,13 @@
 
 def first_norm_kernel(micro, *refs):
     chunks = refs[:micro]
-    gain_ref, bias_ref, x_ref, out_ref, flip_ref = refs[micro:]
+    gain_ref, bias_ref, x_ref, out_ref = refs[micro:]
     rows = chunks[0].shape[0]
     for k, ref in enumerate(chunks):
         here = slice(k * rows, (k + 1) * rows)
         x_ref[here] = ref[...]
         scaled, _ = standardize(ref[...].astype(F32))
-        normed = (scaled * gain_ref[...] + bias_ref[...]).astype(BF16)
-        out_ref[here] = normed
-        flip_ref[:, here] = normed.T
+        out_ref[here] = (scaled * gain_ref[...] + bias_ref[...]).astype(BF16)
 
 
 def first_norm(chunks, gain, bias):
@@ -210,35 +208,12 @@
     return pl.pallas_call(
         functools.partial(first_norm_kernel, len(chunks)),
         in_specs=[WHOLE] * (len(chunks) + 2),
-        out_specs=[WHOLE] * 3,
-        out_shape=[SHAPE((rows, width), BF16)] * 2 + [SHAPE((width, rows), BF16)],
+        out_specs=[WHOLE] * 2,
+        out_shape=[SHAPE((rows, width), BF16)] * 2,
         compiler_params=params(),
-        cost_estimate=cost(0, 10 * rows * width),
+        cost_estimate=cost(0, 8 * rows * width),
         name="first_norm",
     )(*chunks, gain, bias)
-
-
-def flip_kernel(*refs):
-    chunks, out_ref, flip_ref = refs[:-2], refs[-2], refs[-1]
-    rows = chunks[0].shape[0]
-    for k, ref in enumerate(chunks):
-        here = slice(k * rows, (k + 1) * rows)
-        out_ref[here] = ref[...]
-        flip_ref[:, here] = ref[...].T
-
-
-def flip(chunks):
-    rows, width = chunks[0].shape
-    rows = rows * len(chunks)
-    return pl.pallas_call(
-        flip_kernel,
-        in_specs=[WHOLE] * len(chunks),
-        out_specs=[WHOLE] * 2,
-        out_shape=[SHAPE((rows, width), BF16), SHAPE((width, rows), BF16)],
-        compiler_params=params(),
-        cost_estimate=cost(0, 6 * rows * width),
-        name="flip",
-    )(*chunks)
 
 
 def each_k(refs):
@@ -410,7 +385,7 @@
 def middle_kernel(nm, parts, x_ref, *refs):
     mixed_refs, refs = refs[:nm], refs[nm:]
     weights = refs[:parts], refs[parts : 2 * parts]
-    gain_ref, bias_ref, mid_ref, out_ref, flip_ref = refs[2 * parts :]
+    gain_ref, bias_ref, mid_ref, out_ref = refs[2 * parts :]
     half = x_ref.shape[1] // 2
     sides = []
     for side in weights:
@@ -421,9 +396,7 @@
     middle = x_ref[...].astype(F32) + jnp.concatenate(sides, axis=1)
     mid_ref[...] = middle
     scaled, _ = standardize(middle)
-    normed = (scaled * gain_ref[...] + bias_ref[...]).astype(BF16)
-    out_ref[...] = normed
-    flip_ref[...] = normed.T
+    out_ref[...] = (scaled * gain_ref[...] + bias_ref[...]).astype(BF16)
 
 
 def middle_norm(x, mixed, weights, which, gain, bias):
@@ -440,12 +413,8 @@
         + [pl.BlockSpec((block, wide), lambda i: (i, 0))] * nm
         + [head_spec(array, 1, lambda i: (0, 0, which, 0, 0)) for array in arrays]
         + [vector, vector],
-        out_specs=[line, line, pl.BlockSpec((width, block), lambda i: (0, i))],
-        out_shape=[
-            SHAPE((rows, width), F32),
-            SHAPE((rows, width), BF16),
-            SHAPE((width, rows), BF16),
-        ],
+        out_specs=[line, line],
+        out_shape=[SHAPE((rows, width), F32), SHAPE((rows, width), BF16)],
         compiler_params=params(),
         cost_estimate=cost(2 * rows * width * nm * wide, 14 * x.size),
         name="middle_norm",
@@ -547,7 +516,7 @@
 def feed_back_kernel(firsts, sizes, index_ref, *refs):
     nm, count = firsts + sum(sizes), 1 + 4 * len(sizes)
     g_ref, slope_ref, mid_ref, gain_ref = refs[count : count + 4]
-    hid_ref, gmid_ref, attn_ref, flip_ref, sums_ref, held, acc, sems = refs[count + 4 :]
+    hid_ref, gmid_ref, attn_ref, sums_ref, held, acc, sems = refs[count + 4 :]
     step = pl.program_id(0)
     load_weights(firsts, sizes, index_ref, refs[:count], held, sems)
     half = g_ref.shape[1] // 2
@@ -573,9 +542,7 @@
         into, sums = norm_back(acc[...], mid_ref[...], gain_ref[...])
         result = g_ref[...].astype(F32) + into
         gmid_ref[...] = result
-        attn = result.astype(BF16)
-        attn_ref[...] = attn
-        flip_ref[...] = attn.T
+        attn_ref[...] = result.astype(BF16)
         sums_ref[...] = sums
 
 
@@ -596,14 +563,12 @@
             wide,
             line,
             line,
-            pl.BlockSpec((width, rows), lambda k: (0, 0)),
             pl.BlockSpec((2, width), lambda k: (0, 0)),
         ],
         out_shape=[
             SHAPE((nm, rows, hidden), BF16),
             SHAPE((rows, width), F32),
             SHAPE((rows, width), BF16),
-            SHAPE((width, rows), BF16),
             SHAPE((2, width), F32),
         ],
         scratch_shapes=[
@@ -617,49 +582,58 @@
     )(index, *weights, grad, slope, middle, gain)
 
 
-def wide_grad_kernel(index_ref, a_ref, b_ref, out_ref):
-    part = dot_nn(a_ref[...], b_ref[0]).astype(BF16)
+def wide_grad_kernel(place_ref, a_ref, b_ref, out_ref):
+    part = dot_tn(a_ref[...], b_ref[0]).astype(BF16)
     nd, deep = out_ref.shape[0], out_ref.shape[2]
     for p in range(nd):
-        out_ref[index_ref[p], 0] = part[p * deep : (p + 1) * deep]
-
-
-def wide_grad(flipped, values, index):
-    width, rows = flipped.shape
+        out_ref[place_ref[p], 0] = part[p * deep : (p + 1) * deep]
+
+
+def wide_grad(rows_in, values, place, absolute):
+    rows, width = rows_in.shape
     nm, _, hidden = values.shape
-    nd = index.shape[0]
+    nd = place.shape[0] - 1
     block = min(512, hidden)
+
+    def out_map(k, i, place_ref):
+        return (0, lax.rem(place_ref[nd] + nm - k, nm) if absolute else k, 0, i)
+
     return pl.pallas_call(
         wide_grad_kernel,
-        grid=(nm, hidden // block),
-        in_specs=[
-            pl.BlockSpec(memory_space=pltpu.SMEM),
-            pl.BlockSpec((width, rows), lambda k, i: (0, 0)),
-            pl.BlockSpec((1, rows, block), lambda k, i: (k, 0, i)),
-        ],
-        out_specs=pl.BlockSpec((nd, 1, width // nd, block), lambda k, i: (0, k, 0, i)),
+        grid_spec=pltpu.PrefetchScalarGridSpec(
+            num_scalar_prefetch=1,
+            grid=(nm, hidden // block),
+            in_specs=[
+                pl.BlockSpec((rows, width), lambda k, i, place_ref: (0, 0)),
+                pl.BlockSpec((1, rows, block), lambda k, i, place_ref: (k, 0, i)),
+            ],
+            out_specs=pl.BlockSpec((nd, 1, width // nd, block), out_map),
+        ),
         out_shape=SHAPE((nd, nm, width // nd, hidden), BF16),
         compiler_params=params(),
         cost_estimate=cost(2 * nm * width * rows * hidden, 4 * nm * width * hidden),
         name="wide_grad",
-    )(index, flipped, values)
+    )(place, rows_in, values)
 
 
 def head_grad_kernel(
     n_ref, g_ref, mixed_ref, dq_ref, dkv_ref, came_ref, sum_ref, keep_ref, give_ref
 ):
-    half = n_ref.shape[0] // 2
     chips, _, deep, wide = keep_ref.shape
+    half = chips * deep
     total = (dkv_ref[...].astype(F32) + came_ref[...].astype(F32)).astype(BF16)
     sum_ref[...] = total
-    pairs = ((n_ref, dq_ref[...]), (g_ref, mixed_ref[...]), (n_ref, total[0]), (n_ref, total[1]))
-    for i, (left, right) in enumerate(pairs):
-        for out, side in ((keep_ref, left[:half]), (give_ref, left[half:])):
-            out[:, i] = dot_nn(side, right).astype(BF16).reshape(chips, deep, wide)
-
-
-def head_grad(n_flip, g_flip, mixed, dq, dkv, came, chips):
-    width, rows = n_flip.shape
+    three = dot_tn(n_ref[...], jnp.concatenate([dq_ref[...], total[0], total[1]], axis=1))
+    one = dot_tn(g_ref[...], mixed_ref[...])
+    parts = (three[:, :wide], one, three[:, wide : 2 * wide], three[:, 2 * wide :])
+    for i, part in enumerate(parts):
+        part = part.astype(BF16)
+        keep_ref[:, i] = part[:half].reshape(chips, deep, wide)
+        give_ref[:, i] = part[half:].reshape(chips, deep, wide)
+
+
+def head_grad(normed, attn, mixed, dq, dkv, came, chips):
+    rows, width = normed.shape
     wide = dq.shape[1]
     piece = SHAPE((chips, 4, width // 2 // chips, wide), BF16)
     total, keep, give = pl.pallas_call(
@@ -670,7 +644,7 @@
         compiler_params=params(),
         cost_estimate=cost(8 * width * rows * wide, 8 * width * wide),
         name="head_grad",
-    )(n_flip, g_flip, mixed, dq, dkv, came)
+    )(normed, attn, mixed, dq, dkv, came)
     return total, keep[None], give[None]
 
 
@@ -680,7 +654,6 @@
     kv = refs[2 * parts : 3 * parts], refs[3 * parts : 4 * parts]
     out_ref, sums_ref = refs[4 * parts :]
     last = (dkvs[0][...].astype(F32) + came_ref[...].astype(F32)).astype(BF16)
-    step = pl.program_id(0)
     half = x_ref.shape[1] // 2
     sides = []
     for side in range(2):
@@ -693,35 +666,30 @@
         sides.append(total)
     into, sums = norm_back(jnp.concatenate(sides, axis=1), x_ref[...].astype(F32), gain_ref[...])
     out_ref[...] = (gmid_ref[...] + into).astype(BF16)
-
-    @pl.when(step == 0)
-    def _():
-        sums_ref[...] = sums
-
-    @pl.when(step > 0)
-    def _():
-        sums_ref[...] += sums
-
-
-def first_back(x, gmid, gain, dqs, dkvs, came, qo, kv):
-    rows, width = x.shape
+    sums_ref[...] = sums
+
+
+def first_back(x, gmid, gain, dqs, dkvs, came, qo, kv, part, block):
+    width = x.shape[1]
     nm, wide = len(dqs), dqs[0].shape[1]
-    block = row_block(rows)
-    line = pl.BlockSpec((block, width), lambda i: (i, 0))
+    line = pl.BlockSpec((block, width), lambda i: (part, 0))
     still = lambda i: (0, 0, 0, 0, 0)
     qo_arrays, kv_arrays = [*qo[0], *qo[1]], [*kv[0], *kv[1]]
     return pl.pallas_call(
         functools.partial(first_back_kernel, nm, len(qo[0])),
-        grid=(rows // block,),
+        grid=(1,),
         in_specs=[line, line, pl.BlockSpec((1, width), lambda i: (0, 0))]
-        + [pl.BlockSpec((block, wide), lambda i: (i, 0))] * nm
-        + [pl.BlockSpec((2, block, wide), lambda i: (0, i, 0))] * (nm + 1)
+        + [pl.BlockSpec((block, wide), lambda i: (part, 0))] * nm
+        + [pl.BlockSpec((2, block, wide), lambda i: (0, part, 0))] * (nm + 1)
         + [head_spec(array, 1, still) for array in qo_arrays]
         + [head_spec(array, 2, still) for array in kv_arrays],
-        out_specs=[line, pl.BlockSpec((2, width), lambda i: (0, 0))],
-        out_shape=[SHAPE((rows, width), BF16), SHAPE((2, width), F32)],
+        out_specs=[
+            pl.BlockSpec((block, width), lambda i: (0, 0)),
+            pl.BlockSpec((2, width), lambda i: (0, 0)),
+        ],
+        out_shape=[SHAPE((block, width), BF16), SHAPE((2, width), F32)],
         compiler_params=params(),
-        cost_estimate=cost(6 * rows * width * nm * wide, 12 * x.size),
+        cost_estimate=cost(6 * block * width * nm * wide, 12 * block * width),
         name="first_back",
     )(x, gmid, gain, *dqs, *dkvs, came, *qo_arrays, *kv_arrays)
 
@@ -730,23 +698,29 @@
     return (a.astype(F32) + b.astype(F32)).astype(BF16)
 
 
-def add_parts_kernel(keep_ref, came_ref, *outs):
-    for n, out in enumerate(outs):
-        out[...] = add_low(keep_ref[:, n + 1], came_ref[:, n + 1])
-
-
-def add_parts(keep, came):
-    count = keep.shape[1] - 1
-    piece = SHAPE(keep.shape[:1] + keep.shape[2:], keep.dtype)
+def add_parts_kernel(pairs, *refs):
+    outs, row = refs[2 * pairs :], 0
+    for i in range(pairs):
+        keep_ref, came_ref = refs[2 * i : 2 * i + 2]
+        size = keep_ref.shape[0]
+        for n, out in enumerate(outs):
+            out[row : row + size] = add_low(keep_ref[:, n + 1], came_ref[:, n + 1])
+        row += size
+
+
+def add_parts(pairs):
+    keep = pairs[0][0]
+    rows = sum(pair[0].shape[0] for pair in pairs)
+    piece = SHAPE((rows,) + keep.shape[2:], keep.dtype)
     return pl.pallas_call(
-        add_parts_kernel,
-        in_specs=[WHOLE] * 2,
-        out_specs=[WHOLE] * count,
-        out_shape=[piece] * count,
+        functools.partial(add_parts_kernel, len(pairs)),
+        in_specs=[WHOLE] * (2 * len(pairs)),
+        out_specs=[WHOLE] * (keep.shape[1] - 1),
+        out_shape=[piece] * (keep.shape[1] - 1),
         compiler_params=params(),
-        cost_estimate=cost(0, 6 * keep.size),
+        cost_estimate=cost(0, 6 * len(pairs) * keep.size),
         name="add_parts",
-    )(keep, came)
+    )(*[array for pair in pairs for array in pair])
 
 
 class Scatter:
@@ -754,7 +728,7 @@
         self.nd, self.nm = nd, nm
         self.queue = {1: [], **{bit: [] for bit in bits}, "direct": [], "z": []}
         self.order, self.kept, self.waits, self.flying = {}, {}, {}, {}
-        self.ends, self.came, self.done, self.rings = {}, {}, {}, {}
+        self.ends, self.came, self.done, self.rings, self.joined = {}, {}, {}, {}, {}
 
     def add(self, name, ks, keep, give, order, rings=True):
         self.order[name, tuple(ks)], self.rings[name] = order, rings
@@ -788,9 +762,12 @@
                 elif link == "z":
                     value = ring(value, -1, self.nm)
                 elif link == "direct":
-                    value = [
-                        swap(part, 2 * n + 2, self.nd) for n, part in enumerate(add_parts(*value))
-                    ]
+                    more = [tasks.pop(0) for _ in range(min(direct - 1, len(tasks)))]
+                    self.joined[key] = more
+                    value = add_parts([value] + [self.waits.pop(other) for other in more])
+                    value = [swap(part, 2 * n + 2, self.nd) for n, part in enumerate(value)]
+                    self.flying[key] = value
+                    break
                 else:
                     value = swap(value, link, self.nd)
                 self.flying[key] = value
@@ -807,7 +784,12 @@
         came = dict(zip(flying, values[1]))
         self.flying = {}
         for key, value in came.items():
-            self.arrive(key, value)
+            if key not in self.joined:
+                self.arrive(key, value)
+                continue
+            for other in [key] + self.joined.pop(key):
+                self.arrive(other, [part[: len(other[1])] for part in value])
+                value = [part[len(other[1]) :] for part in value]
         extra = values[2]
         return extra[0] if len(extra) == 1 else extra
 
@@ -904,8 +886,11 @@
     def send(packed, k):
         return lax.ppermute(packed[k], ("dp", "mp"), routes(k))
 
+    def back_routes(k):
+        return [(b, a) for a, b in routes(k)]
+
     def send_chunk(chunks, k):
-        return lax.ppermute(chunks[k], ("dp", "mp"), [(b, a) for a, b in routes(k)])
+        return lax.ppermute(chunks[k], ("dp", "mp"), back_routes(k))
 
     def unpack(came):
         return unpack_features(came, there, [(k + mp) % micro for k in range(micro)])
@@ -918,14 +903,14 @@
     firsts = min(2, nm)
     groups = [list(range(k, min(k + 2, nm))) for k in range(firsts, nm, 2)]
     sizes = tuple(len(group) for group in groups)
-    head = [jnp.concatenate([w_proj[0, :1], w_out, w_proj[0, 1:]])]
+    head = [jnp.concatenate([w_proj[0], w_out])]
     feeds = [jnp.concatenate([w_up, w_down])]
     gather = functools.partial(lax.all_gather, axis_name="dp")
     head_groups = [[0], list(range(1, nm))]
 
     def headed(n):
-        flow.add(f"qo{n}", jnp.stack([head[k][:2] for k in head_groups[n]]), forth)
-        flow.add(f"kv{n}", jnp.stack([head[k][2:] for k in head_groups[n]]), back)
+        flow.add(f"qo{n}", jnp.stack([head[k][::3] for k in head_groups[n]]), forth)
+        flow.add(f"kv{n}", jnp.stack([head[k][1:3] for k in head_groups[n]]), back)
 
     halves = {}
 
@@ -978,8 +963,8 @@
     last = [f"{name}{n}" for n in range(len(groups)) for name in ("up", "down")]
     core_halves(len(head_names), head_names)
     turn()
-    x, normed, n_flip = first_norm(came, gains[:1], biases[:1])
-    x, normed, n_flip, halves, feeds, view = flow.land(x, normed, n_flip, halves, feeds, view)
+    x, normed = first_norm(came, gains[:1], biases[:1])
+    x, normed, halves, feeds, view = flow.land(x, normed, halves, feeds, view)
     turned()
 
     def both(name):
@@ -1035,11 +1020,9 @@
         )
         turned()
     core_halves(len(last), last)
-    middle, normed_two, flip_two = middle_norm(x, mixed, qo, 1, gains[1:], biases[1:])
-    grad, grad_flip = flip(grad_came)
-    middle, normed_two, flip_two, halves, grad, grad_flip = flow.land(
-        middle, normed_two, flip_two, halves, grad, grad_flip
-    )
+    middle, normed_two = middle_norm(x, mixed, qo, 1, gains[1:], biases[1:])
+    grad = jnp.concatenate(grad_came)
+    middle, normed_two, halves, grad = flow.land(middle, normed_two, halves, grad)
     for name in last:
         weights += [halves[name], flow.kept.pop(name)]
 
@@ -1050,16 +1033,15 @@
     sums = Scatter(nd, nm, flow.bits)
     output = [send_chunk(out_chunks, 0)]
     over_dp = functools.partial(lax.psum_scatter, axis_name="dp", scatter_dimension=0, tiled=True)
-    grads_down = over_dp(wide_grad(grad_flip, active, index))
-    hid, gmid, attn, attn_flip, sums_two = feed_back(
+    place = jnp.append(index, mp.astype(jnp.int32))
+    grads_down = over_dp(wide_grad(grad, active, place, False))
+    hid, gmid, attn, sums_two = feed_back(
         grad, slope, middle, gains[1:], index, firsts, sizes, weights
     )
-    hid, gmid, attn, attn_flip, sums_two, flip_two, output, out_chunks = sums.land(
-        hid, gmid, attn, attn_flip, sums_two, flip_two, output, out_chunks
+    hid, gmid, attn, sums_two, normed_two, output, out_chunks = sums.land(
+        hid, gmid, attn, sums_two, normed_two, output, out_chunks
     )
-    grads_up = jnp.take(
-        over_dp(wide_grad(flip_two, hid, index))[0], (mp - jnp.arange(nm)) % nm, axis=0
-    )
+    grads_up = over_dp(wide_grad(normed_two, hid, place, True))[0]
     grads_up = lax.psum_scatter(grads_up, "mp", scatter_dimension=0, tiled=True)
     grad_mixed = project(attn, qo, 1, 1)
 
@@ -1073,7 +1055,7 @@
             return None
         k = closing.pop()
         dkvs[k], keep, give = head_grad(
-            n_flip, attn_flip, mixed[k], dqs[k], dkv_part[k], dkv_came[k], chips
+            normed, attn, mixed[k], dqs[k], dkv_part[k], dkv_came[k], chips
         )
         return k, (keep, give)
 
@@ -1112,36 +1094,47 @@
 
     sums.launch()
     ready = head_grads()
-    first, sums_one = first_back(
-        x,
-        gmid,
-        gains[:1],
-        [dqs[k] for k in range(nm)],
-        [dkvs[k] if k else dkv_part[k] for k in range(nm)],
-        dkv_came[0],
-        qo,
-        kv,
-    )
-    first, sums_one, outs, output = sums.land(first, sums_one, ready and ready[1], output)
+
+    def first_part(part):
+        return first_back(
+            x,
+            gmid,
+            gains[:1],
+            [dqs[k] for k in range(nm)],
+            [dkvs[k] if k else dkv_part[k] for k in range(nm)],
+            dkv_came[0],
+            qo,
+            kv,
+            part,
+            chunk,
+        )
+
+    firsts_back = [first_part(0)]
+    firsts_back, outs, output, gmid = sums.land(firsts_back, ready and ready[1], output, gmid)
     if ready:
         add_heads(ready, outs)
-    first = first.reshape((micro, chunk, width))
-    vectors = jnp.take(
-        jnp.concatenate([sums_one, sums_two]).reshape(4, nd, width // nd),
-        jnp.argsort(index),
-        axis=1,
-    ).reshape(4, width)
     hops = [lambda value, bit=1 << b: swap(value, bit, nd) for b in range(nd.bit_length() - 1)]
-    grad_tokens = []
-    while sums.busy() or len(grad_tokens) < micro:
+    grad_tokens, vectors = [], None
+    while sums.busy() or hops or len(grad_tokens) < micro:
         if len(grad_tokens) < micro:
-            grad_tokens.append(send_chunk(first, len(grad_tokens)))
+            first = firsts_back[len(grad_tokens)][0]
+            grad_tokens.append(lax.ppermute(first, ("dp", "mp"), back_routes(len(grad_tokens))))
             if len(grad_tokens) == micro:
                 output = unpack(output)
         sums.launch()
-        while hops:
-            vectors = vectors + hops.pop(0)(vectors)
-        grad_tokens, first, vectors, output = sums.land(grad_tokens, first, vectors, output)
+        if len(firsts_back) < micro:
+            firsts_back.append(first_part(len(firsts_back)))
+        elif hops:
+            vectors = jnp.concatenate([sum(part[1] for part in firsts_back), sums_two])
+            vectors = jnp.take(
+                vectors.reshape(4, nd, width // nd), jnp.argsort(index), axis=1
+            ).reshape(4, width)
+            for hop in hops:
+                vectors = vectors + hop(vectors)
+            hops = []
+        grad_tokens, firsts_back, vectors, output, gmid = sums.land(
+            grad_tokens, firsts_back, vectors, output, gmid
+        )
     g_head, g_down = sums.done["head"], sums.done["down"]
     vectors = sum([ring(vectors, k, nm) for k in range(1, nm)], vectors)
     share = width // (nd * nm)

time: 515 us -> 507 us (0.984)
  waiting for transfers between devices: 67.5 us -> 59.9 us
  local copies, waits for them, and re-layouts: 27.4 us -> 21.7 us
    ppermute x42, starting transfers between devices: 33.2 us -> 41.9 us  [swap(): return lax.ppermute(value, 'dp', [(i, i ^ bit) for i in range(nd)])]
    ppermute x4, starting transfers between devices: 15.4 us -> 6.9 us  [send(): return lax.ppermute(packed[k], ('dp', 'mp'), routes(k))]
    ppermute x4, waiting for transfers between devices: 10.2 us -> 2.57 us  [send(): return lax.ppermute(packed[k], ('dp', 'mp'), routes(k))]
    ppermute x15, waiting for transfers between devices: 36.2 us -> 29.6 us  [ring(): return lax.ppermute(value, 'mp', [(i, (i + step) % nm) for i in range(nm)])]
    ppermute x42, waiting for transfers between devices: 21.1 us -> 27.6 us  [swap(): return lax.ppermute(value, 'dp', [(i, i ^ bit) for i in range(nd)])]
    pallas_call x1 -> x2, Pallas kernels: 11.6 us -> 17 us  [first_back(): pl.pallas_call(functools.partial(first_back_kernel, nm, len(qo[0])), grid...]
    pallas_call x7 -> x6, Pallas kernels: 39.9 us -> 36.7 us  [the longest x2 26.7 us: wide_grad(): pl.pallas_call(wide_grad_kernel, grid_spec=pltpu.PrefetchScalarGridSpec(n...]
    unnamed x144 -> x118, local copies, waits for them, and re-layouts: 12.6 us -> 10.5 us
  transfers between devices with their start and end apart: 70 -> 70, of which waited for: 18 -> 17; matrix products, arithmetic and copies ran while one was open for 7% -> 7% of each run, Pallas kernels for 50% -> 51%
where the time goes in v6:
time: 507 us; the launch traced here: 498 us
  Pallas kernels  289 us (57%)
  starting transfers between devices  81.3 us (16%)
  waiting for transfers between devices  59.9 us (12%)
  other arithmetic  30.3 us (6%)
  local copies, waits for them, and re-layouts  21.7 us (4%)
  between operations  15.8 us (3%)
    pallas_call x4, Pallas kernels, attend_back(): pl.pallas_call(functools.partial(attend_back_kernel, parts), grid=(count,...  70.5 us
    pallas_call x4, Pallas kernels, attend(): pl.pallas_call(functools.partial(attend_kernel, parts), grid=(count, rows...  46.1 us
    ppermute x42, starting transfers between devices, swap(): return lax.ppermute(value, 'dp', [(i, i ^ bit) for i in range(nd)])  41.9 us
    ppermute x15, waiting for transfers between devices, ring(): return lax.ppermute(value, 'mp', [(i, (i + step) % nm) for i in range(nm)])  29.6 us
    ppermute x42, waiting for transfers between devices, swap(): return lax.ppermute(value, 'dp', [(i, i ^ bit) for i in range(nd)])  27.6 us
    pallas_call x1, Pallas kernels, feed_back(): pl.pallas_call(functools.partial(feed_back_kernel, firsts, sizes), grid=(...  27 us
    pallas_call x2, Pallas kernels, wide_grad(): pl.pallas_call(wide_grad_kernel, grid_spec=pltpu.PrefetchScalarGridSpec(n...  26.7 us
    pallas_call x1, Pallas kernels, feed(): pl.pallas_call(functools.partial(feed_kernel, firsts, sizes), grid=(nm,),...  23.4 us
  transfers between devices with their start and end apart: 70, of which 17 were waited for; matrix products, arithmetic and copies ran while one was open for 7% of the time, Pallas kernels for 51%

profile of v6, /device:TPU:0, one launch (start us, length us, event | category | flops | bytes accessed | tf_op | source)
XLA Modules:
  0.0 497.9 jit_solution(4753671593065618693)
XLA Ops:
  8.2 4.1 collective-permute-start
  51.7 9.3 %collective-permute-start.13 = (bf16[4,1,2,128,256]{4,3,2,1,0:T(8,128)(2,1)S(1)}, bf16[4,1,2,128,256]{4,3,2,1,0:T(8,128)(2,1)S(1)}, u32[]{:S(2)}, u32[]{:S(2)}) collective-permute-start(bf16[4,1,2,128,256]{4,3,2,1,0:T(8,128)(2,1)S(1)} %pad_maximum_fusion.12.refs_0_.refs_4_.refs_9_), channel_id=1, source_target_pairs={{0,4},{4,0},{8,12},{12,8},{16,20},{20,16},{24,28},{28,24},{1,5},{5... | collective-permute-start | bytes 1572872 | tf_op jit(solution)/shard_map/ppermute | solution.py:49
  68.8 11.9 %collective-permute-done.11 = bf16[2,3,2,128,256]{4,3,2,1,0:T(8,128)(2,1)S(1)} collective-permute-done((bf16[2,3,2,128,256]{4,3,2,1,0:T(8,128)(2,1)S(1)}, bf16[2,3,2,128,256]{4,3,2,1,0:T(8,128)(2,1)S(1)}, u32[]{:S(2)}, u32[]{:S(2)}) %collective-permute-start.11) | collective-permute-done | bytes 786464 | tf_op jit(solution)/shard_map/ppermute | solution.py:49
  87.5 4.2 first_norm.1
  91.7 10.2 %collective-permute-done.17 = bf16[2,128,1024]{2,1,0:T(8,128)(2,1)S(1)} collective-permute-done((bf16[2,128,1024]{2,1,0:T(8,128)(2,1)S(1)}, bf16[2,128,1024]{2,1,0:T(8,128)(2,1)S(1)}, u32[]{:S(2)}, u32[]{:S(2)}) %collective-permute-start.17) | collective-permute-done | bytes 524320 | tf_op jit(solution)/shard_map/ppermute | solution.py:53
  106.3 7.0 %project.3.refs_0_.refs_2_ = bf16[2,768,1024]{2,1,0:T(8,128)(2,1)} custom-call(bf16[768,1024]{1,0:T(8,128)(2,1)} %get-tuple-element.347.in_ref.n_ref, bf16[4,1,2,128,256]{4,3,2,1,0:T(8,128)(2,1)} %copy-done.8, bf16[4,3,2,128,256]{4,3,2,1,0:T(8,128)(2,1)} %copy-done.5, bf16[4,1,2,128,256]{4,3,2,1,0:T(8,128)(2,1)} %copy-done.10, ...), custom_call_target="tpu_custom_call" | custom-call | flops 3221225472 | bytes 3145728 | tf_op jit(solution)/shard_map/project/pallas_call | solution.py:245
  113.2 6.2 %collective-permute-done.18 = bf16[2,128,1024]{2,1,0:T(8,128)(2,1)S(1)} collective-permute-done((bf16[2,128,1024]{2,1,0:T(8,128)(2,1)S(1)}, bf16[2,128,1024]{2,1,0:T(8,128)(2,1)S(1)}, u32[]{:S(2)}, u32[]{:S(2)}) %collective-permute-start.18) | collective-permute-done | bytes 524320 | tf_op jit(solution)/shard_map/ppermute | solution.py:53
  120.8 4.9 project.4.q_ref
  125.7 9.8 %collective-permute-done.21 = bf16[2,128,1024]{2,1,0:T(8,128)(2,1)S(1)} collective-permute-done((bf16[2,128,1024]{2,1,0:T(8,128)(2,1)S(1)}, bf16[2,128,1024]{2,1,0:T(8,128)(2,1)S(1)}, u32[]{:S(2)}, u32[]{:S(2)}) %collective-permute-start.21) | collective-permute-done | bytes 524320 | tf_op jit(solution)/shard_map/ppermute | solution.py:53
  138.9 11.5 %attend.5 = (bf16[768,256]{1,0:T(8,128)(2,1)}, f32[2,2,768]{2,1,0:T(2,128)}) custom-call(bf16[1,768,1024]{2,1,0:T(8,128)(2,1)} %project.4.q_ref, bf16[2,768,1024]{2,1,0:T(8,128)(2,1)} %project.3.refs_0_.refs_2_, bf16[2,768,1024]{2,1,0:T(8,128)(2,1)} %collective-permute-done.20.refs_1_.refs_3_, bf16[2,768,1024]{2,1,0:T(8,128)(2,1)} %project.3.refs_0_.refs_2_, ...), custom_call_target="tpu_custom_call" | custom-call | flops 4831838208 | bytes 3145728 | tf_op jit(solution)/shard_map/attend/pallas_call | solution.py:294
  150.4 11.5 %attend.4 = (bf16[768,256]{1,0:T(8,128)(2,1)}, f32[2,2,768]{2,1,0:T(2,128)}) custom-call(bf16[1,768,1024]{2,1,0:T(8,128)(2,1)} %project.4.q_ref, bf16[2,768,1024]{2,1,0:T(8,128)(2,1)} %project.3.refs_0_.refs_2_, bf16[2,768,1024]{2,1,0:T(8,128)(2,1)} %collective-permute-done.20.refs_1_.refs_3_, bf16[2,768,1024]{2,1,0:T(8,128)(2,1)} %project.3.refs_0_.refs_2_, ...), custom_call_target="tpu_custom_call" | custom-call | flops 4831838208 | bytes 3145728 | tf_op jit(solution)/shard_map/attend/pallas_call | solution.py:294
  167.2 11.5 %attend.7 = (bf16[768,256]{1,0:T(8,128)(2,1)}, f32[2,2,768]{2,1,0:T(2,128)}) custom-call(bf16[1,768,1024]{2,1,0:T(8,128)(2,1)} %project.4.q_ref, bf16[2,768,1024]{2,1,0:T(8,128)(2,1)} %project.3.refs_0_.refs_2_, bf16[2,768,1024]{2,1,0:T(8,128)(2,1)} %collective-permute-done.20.refs_1_.refs_3_, bf16[2,768,1024]{2,1,0:T(8,128)(2,1)} %project.3.refs_0_.refs_2_, ...), custom_call_target="tpu_custom_call" | custom-call | flops 4831838208 | bytes 3145728 | tf_op jit(solution)/shard_map/attend/pallas_call | solution.py:294
  178.7 11.5 %attend.6 = (bf16[768,256]{1,0:T(8,128)(2,1)}, f32[2,2,768]{2,1,0:T(2,128)}) custom-call(bf16[1,768,1024]{2,1,0:T(8,128)(2,1)} %project.4.q_ref, bf16[2,768,1024]{2,1,0:T(8,128)(2,1)} %project.3.refs_0_.refs_2_, bf16[2,768,1024]{2,1,0:T(8,128)(2,1)} %collective-permute-done.20.refs_1_.refs_3_, bf16[2,768,1024]{2,1,0:T(8,128)(2,1)} %project.3.refs_0_.refs_2_, ...), custom_call_target="tpu_custom_call" | custom-call | flops 4831838208 | bytes 3145728 | tf_op jit(solution)/shard_map/attend/pallas_call | solution.py:294
  192.0 7.1 %middle_norm.1 = (f32[768,1024]{1,0:T(8,128)}, bf16[768,1024]{1,0:T(8,128)(2,1)}) custom-call(bf16[768,1024]{1,0:T(8,128)(2,1)} %get-tuple-element.384.x_ref, bf16[768,256]{1,0:T(8,128)(2,1)} %get-tuple-element.385.refs_0_.refs_6_.mixed_ref, bf16[768,256]{1,0:T(8,128)(2,1)} %get-tuple-element.386.refs_1_.refs_6_.mixed_ref, ...), custom_call_target="tpu_custom_call" | custom-call | flops 1610612736 | bytes 11010048 | tf_op jit(solution)/shard_map/middle_norm/pallas_call | solution.py:409
  202.9 23.4 %feed.1 = (bf16[768,1024]{1,0:T(8,128)(2,1)}, bf16[4,768,1024]{2,1,0:T(8,128)(2,1)}, bf16[4,768,1024]{2,1,0:T(8,128)(2,1)}) custom-call(s32[8]{0:T(128)} %copy-done.45, bf16[8,2,2,128,1024]{4,3,2,1,0:T(8,128)(2,1)} %bitcast.207, bf16[4,2,128,1024]{3,2,1,0:T(8,128)(2,1)} %copy-done.12, bf16[4,2,128,1024]{3,2,1,0:T(8,128)(2,1)} %copy-done.49, ...), custom_call_target="tpu_custom_call" | custom-call | flops 12884901888 | bytes 16777216 | tf_op jit(solution)/shard_map/feed/pallas_call | solution.py:497
  226.4 13.2 %wide_grad.2 = bf16[8,4,128,1024]{3,2,1,0:T(8,128)(2,1)} custom-call(s32[9]{0:T(128)} %get-tuple-element.639.place_ref, bf16[768,1024]{1,0:T(8,128)(2,1)} %pad_maximum_fusion.4.refs_5_.a_ref, bf16[4,768,1024]{2,1,0:T(8,128)(2,1)} %get-tuple-element.444.b_ref), custom_call_target="tpu_custom_call" | custom-call | flops 6442450944 | bytes 16777216 | tf_op jit(solution)/shard_map/wide_grad/pallas_call | solution.py:601
  242.1 27.0 %feed_back.1 = (bf16[4,768,1024]{2,1,0:T(8,128)(2,1)}, f32[768,1024]{1,0:T(8,128)}, bf16[768,1024]{1,0:T(8,128)(2,1)}, f32[2,1024]{1,0:T(2,128)}) custom-call(s32[8]{0:T(128)} %copy-done.45, bf16[8,2,2,128,1024]{4,3,2,1,0:T(8,128)(2,1)} %bitcast.208, bf16[4,2,128,1024]{3,2,1,0:T(8,128)(2,1)} %copy-done.12, bf16[4,2,128,1024]{3,2,1,0:T(8,128)(2,1)} %copy-done.49, ...), custom_call_target="tpu_custom_call" | custom-call | flops 12884901888 | bytes 16777216 | tf_op jit(solution)/shard_map/feed_back/pallas_call | solution.py:556
  269.2 13.5 %wide_grad.3 = bf16[8,4,128,1024]{3,2,1,0:T(8,128)(2,1)} custom-call(s32[9]{0:T(128)} %get-tuple-element.639.place_ref, bf16[768,1024]{1,0:T(8,128)(2,1)} %get-tuple-element.552.refs_5_.a_ref, bf16[4,768,1024]{2,1,0:T(8,128)(2,1)} %get-tuple-element.553.b_ref), custom_call_target="tpu_custom_call" | custom-call | flops 6442450944 | bytes 16777216 | tf_op jit(solution)/shard_map/wide_grad/pallas_call | solution.py:601
  287.7 5.0 %project.5.refs_7_ = bf16[1,768,1024]{2,1,0:T(8,128)(2,1)} custom-call(bf16[768,1024]{1,0:T(8,128)(2,1)} %get-tuple-element.406.in_ref.g_ref, bf16[4,1,2,128,256]{4,3,2,1,0:T(8,128)(2,1)} %copy-done.4, bf16[4,3,2,128,256]{4,3,2,1,0:T(8,128)(2,1)} %copy-done.2, bf16[4,1,2,128,256]{4,3,2,1,0:T(8,128)(2,1)} %copy-done.6, bf16[4,3,2,128,256]{4,3,2,1,0:T(8,128)(2,1)} %copy-done.3), custom_call_target="tpu_custom_call" | custom-call | flops 1610612736 | bytes 1572864 | tf_op jit(solution)/shard_map/project/pallas_call | solution.py:245
  292.7 18.0 %attend_back.4 = (bf16[768,256]{1,0:T(8,128)(2,1)}, bf16[2,768,256]{2,1,0:T(8,128)(2,1)}, bf16[2,768,256]{2,1,0:T(8,128)(2,1)}) custom-call(bf16[1,768,1024]{2,1,0:T(8,128)(2,1)} %project.4.q_ref, bf16[2,768,1024]{2,1,0:T(8,128)(2,1)} %project.3.refs_0_.refs_2_, bf16[2,768,1024]{2,1,0:T(8,128)(2,1)} %collective-permute-done.20.refs_1_.refs_3_, ...), custom_call_target="tpu_custom_call" | custom-call | flops 12079595520 | bytes 6291456 | tf_op jit(solution)/shard_map/attend_back/pallas_call | solution.py:362
  310.8 17.6 %attend_back.5 = (bf16[768,256]{1,0:T(8,128)(2,1)}, bf16[2,768,256]{2,1,0:T(8,128)(2,1)}, bf16[2,768,256]{2,1,0:T(8,128)(2,1)}) custom-call(bf16[1,768,1024]{2,1,0:T(8,128)(2,1)} %project.4.q_ref, bf16[2,768,1024]{2,1,0:T(8,128)(2,1)} %project.3.refs_0_.refs_2_, bf16[2,768,1024]{2,1,0:T(8,128)(2,1)} %collective-permute-done.20.refs_1_.refs_3_, ...), custom_call_target="tpu_custom_call" | custom-call | flops 12079595520 | bytes 6291456 | tf_op jit(solution)/shard_map/attend_back/pallas_call | solution.py:362
  329.3 5.7 %head_grad.4 = (bf16[2,768,256]{2,1,0:T(8,128)(2,1)}, bf16[4,4,128,256]{3,2,1,0:T(8,128)(2,1)}, bf16[4,4,128,256]{3,2,1,0:T(8,128)(2,1)}) custom-call(bf16[768,1024]{1,0:T(8,128)(2,1)} %get-tuple-element.347.in_ref.n_ref, bf16[768,1024]{1,0:T(8,128)(2,1)} %get-tuple-element.406.in_ref.g_ref, bf16[768,256]{1,0:T(8,128)(2,1)} %get-tuple-element.388.refs_3_.refs_6_.mixed_ref, ...), custom_call_target="tpu_custom_call" | custom-call | flops 1610612736 | bytes 2097152 | tf_op jit(solution)/shard_map/head_grad/pallas_call | solution.py:639
  335.0 17.5 %attend_back.6 = (bf16[768,256]{1,0:T(8,128)(2,1)}, bf16[2,768,256]{2,1,0:T(8,128)(2,1)}, bf16[2,768,256]{2,1,0:T(8,128)(2,1)}) custom-call(bf16[1,768,1024]{2,1,0:T(8,128)(2,1)} %project.4.q_ref, bf16[2,768,1024]{2,1,0:T(8,128)(2,1)} %project.3.refs_0_.refs_2_, bf16[2,768,1024]{2,1,0:T(8,128)(2,1)} %collective-permute-done.20.refs_1_.refs_3_, ...), custom_call_target="tpu_custom_call" | custom-call | flops 12079595520 | bytes 6291456 | tf_op jit(solution)/shard_map/attend_back/pallas_call | solution.py:362
  357.6 17.4 %attend_back.7 = (bf16[768,256]{1,0:T(8,128)(2,1)}, bf16[2,768,256]{2,1,0:T(8,128)(2,1)}, bf16[2,768,256]{2,1,0:T(8,128)(2,1)}) custom-call(bf16[1,768,1024]{2,1,0:T(8,128)(2,1)} %project.4.q_ref, bf16[2,768,1024]{2,1,0:T(8,128)(2,1)} %project.3.refs_0_.refs_2_, bf16[2,768,1024]{2,1,0:T(8,128)(2,1)} %collective-permute-done.20.refs_1_.refs_3_, ...), custom_call_target="tpu_custom_call" | custom-call | flops 12079595520 | bytes 6291456 | tf_op jit(solution)/shard_map/attend_back/pallas_call | solution.py:362
  375.0 5.7 %head_grad.5 = (bf16[2,768,256]{2,1,0:T(8,128)(2,1)}, bf16[4,4,128,256]{3,2,1,0:T(8,128)(2,1)}, bf16[4,4,128,256]{3,2,1,0:T(8,128)(2,1)}) custom-call(bf16[768,1024]{1,0:T(8,128)(2,1)} %get-tuple-element.347.in_ref.n_ref, bf16[768,1024]{1,0:T(8,128)(2,1)} %get-tuple-element.406.in_ref.g_ref, bf16[768,256]{1,0:T(8,128)(2,1)} %get-tuple-element.387.refs_2_.refs_6_.mixed_ref, ...), custom_call_target="tpu_custom_call" | custom-call | flops 1610612736 | bytes 2097152 | tf_op jit(solution)/shard_map/head_grad/pallas_call | solution.py:639
  388.1 5.6 %head_grad.6 = (bf16[2,768,256]{2,1,0:T(8,128)(2,1)}, bf16[4,4,128,256]{3,2,1,0:T(8,128)(2,1)}, bf16[4,4,128,256]{3,2,1,0:T(8,128)(2,1)}) custom-call(bf16[768,1024]{1,0:T(8,128)(2,1)} %get-tuple-element.347.in_ref.n_ref, bf16[768,1024]{1,0:T(8,128)(2,1)} %get-tuple-element.406.in_ref.g_ref, bf16[768,256]{1,0:T(8,128)(2,1)} %get-tuple-element.386.refs_1_.refs_6_.mixed_ref, ...), custom_call_target="tpu_custom_call" | custom-call | flops 1610612736 | bytes 2097152 | tf_op jit(solution)/shard_map/head_grad/pallas_call | solution.py:639
  394.0 4.3 collective-permute-done.41
  411.1 5.6 %head_grad.7 = (bf16[2,768,256]{2,1,0:T(8,128)(2,1)}, bf16[4,4,128,256]{3,2,1,0:T(8,128)(2,1)}, bf16[4,4,128,256]{3,2,1,0:T(8,128)(2,1)}) custom-call(bf16[768,1024]{1,0:T(8,128)(2,1)} %get-tuple-element.347.in_ref.n_ref, bf16[768,1024]{1,0:T(8,128)(2,1)} %get-tuple-element.406.in_ref.g_ref, bf16[768,256]{1,0:T(8,128)(2,1)} %get-tuple-element.385.refs_0_.refs_6_.mixed_ref, ...), custom_call_target="tpu_custom_call" | custom-call | flops 1610612736 | bytes 2097152 | tf_op jit(solution)/shard_map/head_grad/pallas_call | solution.py:639
  416.7 8.6 %first_back.2 = (bf16[384,1024]{1,0:T(8,128)(2,1)}, f32[2,1024]{1,0:T(2,128)}) custom-call(bf16[768,1024]{1,0:T(8,128)(2,1)} %get-tuple-element.384.x_ref, f32[768,1024]{1,0:T(8,128)} %get-tuple-element.524.gmid_ref, f32[1,1024]{1,0:T(1,128)} %get-tuple-element.623.refs_2_.gain_ref, bf16[768,256]{1,0:T(8,128)(2,1)} %get-tuple-element.496.refs_0_.dq_ref, ...), custom_call_target="tpu_custom_call" | custom-call | flops 2415919104 | bytes 4718592 | tf_op jit(solution)/shard_map/first_back/pallas_call | solution.py:678
  437.3 8.5 %first_back.3 = (bf16[384,1024]{1,0:T(8,128)(2,1)}, f32[2,1024]{1,0:T(2,128)}) custom-call(bf16[768,1024]{1,0:T(8,128)(2,1)} %get-tuple-element.384.x_ref, f32[768,1024]{1,0:T(8,128)} %get-tuple-element.524.gmid_ref, f32[1,1024]{1,0:T(1,128)} %get-tuple-element.623.refs_2_.gain_ref, bf16[768,256]{1,0:T(8,128)(2,1)} %get-tuple-element.496.refs_0_.dq_ref, ...), custom_call_target="tpu_custom_call" | custom-call | flops 2415919104 | bytes 4718592 | tf_op jit(solution)/shard_map/first_back/pallas_call | solution.py:678
  448.8 6.5 %collective-permute-start.59 = (bf16[384,1024]{1,0:T(8,128)(2,1)}, bf16[384,1024]{1,0:T(8,128)(2,1)S(1)}, u32[]{:S(2)}, u32[]{:S(2)}) collective-permute-start(bf16[384,1024]{1,0:T(8,128)(2,1)} %get-tuple-element.538), channel_id=1, source_target_pairs={{2,0},{0,1},{6,2},{4,3},{3,4},{1,5},{7,6},{5,7},{10,8},{8,9},{14,1... | collective-permute-start | bytes 2359304 | tf_op jit(solution)/shard_map/ppermute | solution.py:1121
  476.5 3.2 collective-permute-done.56
  (336 shorter events, 155.2 us)
Async XLA Ops:
  7.2 195.7 %all-gather.3.cloned.1.call-start = ((), (), s32[]{:S(2)}) async-start(), calls=%async_computation.6 | async-start | bytes 9437184 | tf_op jit(solution)/shard_map/all_gather | solution.py:957
  8.2 23.5 %collective-permute-start = (bf16[4,128,256]{2,1,0:T(8,128)(2,1)S(1)}, bf16[4,128,256]{2,1,0:T(8,128)(2,1)S(1)}, u32[]{:S(2)}, u32[]{:S(2)}) collective-permute-start(bf16[4,128,256]{2,1,0:T(8,128)(2,1)S(1)} %pad_maximum_fusion.17), channel_id=1, source_target_pairs={{0,2},{1,3},{2,0},{3,1},{4,6},{5,7},{6,4},{7,5},{8,10},{9,11},{10,... | collective-permute-start | bytes 786440 | tf_op jit(solution)/shard_map/ppermute | solution.py:53
  12.3 19.4 %collective-permute-start.1 = (bf16[4,128,256]{2,1,0:T(8,128)(2,1)S(1)}, bf16[4,128,256]{2,1,0:T(8,128)(2,1)S(1)}, u32[]{:S(2)}, u32[]{:S(2)}) collective-permute-start(bf16[4,128,256]{2,1,0:T(8,128)(2,1)S(1)} %pad_maximum_fusion.17), channel_id=1, source_target_pairs={{0,1},{1,2},{2,3},{3,0},{4,5},{5,6},{6,7},{7,4},{8,9},{9,10},{10,1... | collective-permute-start | bytes 786440 | tf_op jit(solution)/shard_map/ppermute | solution.py:53
  13.9 17.9 %collective-permute-start.2 = (bf16[4,128,256]{2,1,0:T(8,128)(2,1)S(1)}, bf16[4,128,256]{2,1,0:T(8,128)(2,1)S(1)}, u32[]{:S(2)}, u32[]{:S(2)}) collective-permute-start(bf16[4,128,256]{2,1,0:T(8,128)(2,1)S(1)} %pad_maximum_fusion.17), channel_id=1, source_target_pairs={{0,3},{1,0},{2,1},{3,2},{4,7},{5,4},{6,5},{7,6},{8,11},{9,8},{10,9... | collective-permute-start | bytes 786440 | tf_op jit(solution)/shard_map/ppermute | solution.py:53
  61.1 19.5 %collective-permute-start.11 = (bf16[2,3,2,128,256]{4,3,2,1,0:T(8,128)(2,1)S(1)}, bf16[2,3,2,128,256]{4,3,2,1,0:T(8,128)(2,1)S(1)}, u32[]{:S(2)}, u32[]{:S(2)}) collective-permute-start(bf16[2,3,2,128,256]{4,3,2,1,0:T(8,128)(2,1)S(1)} %pad_maximum_fusion.9), channel_id=1, source_target_pairs={{0,16},{4,20},{8,24},{12,28},{16,0},{20,4},{24,8},{28,12},{1,17},{... | collective-permute-start | bytes 2359304 | tf_op jit(solution)/shard_map/ppermute | solution.py:49
  61.8 19.4 %collective-permute-start.10 = (bf16[2,3,2,128,256]{4,3,2,1,0:T(8,128)(2,1)S(1)}, bf16[2,3,2,128,256]{4,3,2,1,0:T(8,128)(2,1)S(1)}, u32[]{:S(2)}, u32[]{:S(2)}) collective-permute-start(bf16[2,3,2,128,256]{4,3,2,1,0:T(8,128)(2,1)S(1)} %pad_maximum_fusion.8), channel_id=1, source_target_pairs={{0,8},{4,12},{8,0},{12,4},{16,24},{20,28},{24,16},{28,20},{1,9},{5... | collective-permute-start | bytes 2359304 | tf_op jit(solution)/shard_map/ppermute | solution.py:49
  63.3 20.4 %collective-permute-start.14 = (bf16[384,1024]{1,0:T(8,128)(2,1)S(1)}, bf16[384,1024]{1,0:T(8,128)(2,1)S(1)}, u32[]{:S(2)}, u32[]{:S(2)}) collective-permute-start(bf16[384,1024]{1,0:T(8,128)(2,1)S(1)} %copy-done.21), channel_id=1, source_target_pairs={{0,2},{1,0},{2,6},{3,4},{4,3},{5,1},{6,7},{7,5},{8,10},{9,8},{10,1... | collective-permute-start | bytes 2359304 | tf_op jit(solution)/shard_map/ppermute | solution.py:887
  104.3 249.4 %reduce-scatter.4.cloned.1.call-start = ((), (), s32[]{:S(2)}) async-start(), calls=%async_computation.3 | async-start | bytes 9437184 | tf_op jit(solution)/shard_map/reduce_scatter | solution.py:1037
  135.7 26.2 %collective-permute-start.23 = (bf16[1,2,128,1024]{3,2,1,0:T(8,128)(2,1)S(1)}, bf16[1,2,128,1024]{3,2,1,0:T(8,128)(2,1)S(1)}, u32[]{:S(2)}, u32[]{:S(2)}) collective-permute-start(bf16[1,2,128,1024]{3,2,1,0:T(8,128)(2,1)S(1)} %get-tuple-element.596), channel_id=1, source_target_pairs={{0,16},{4,20},{8,24},{12,28},{16,0},{20,4},{24,8},{28,12},{1,17},{... | collective-permute-start | bytes 1572872 | tf_op jit(solution)/shard_map/ppermute | solution.py:49
  137.4 25.6 %collective-permute-start.22 = (bf16[1,2,128,1024]{3,2,1,0:T(8,128)(2,1)S(1)}, bf16[1,2,128,1024]{3,2,1,0:T(8,128)(2,1)S(1)}, u32[]{:S(2)}, u32[]{:S(2)}) collective-permute-start(bf16[1,2,128,1024]{3,2,1,0:T(8,128)(2,1)S(1)} %get-tuple-element.598), channel_id=1, source_target_pairs={{0,8},{4,12},{8,0},{12,4},{16,24},{20,28},{24,16},{28,20},{1,9},{5... | collective-permute-start | bytes 1572872 | tf_op jit(solution)/shard_map/ppermute | solution.py:49
  138.0 25.0 %collective-permute-start.24 = (bf16[384,1024]{1,0:T(8,128)(2,1)S(1)}, bf16[384,1024]{1,0:T(8,128)(2,1)S(1)}, u32[]{:S(2)}, u32[]{:S(2)}) collective-permute-start(bf16[384,1024]{1,0:T(8,128)(2,1)S(1)} %copy-done.20), channel_id=1, source_target_pairs={{0,0},{1,2},{2,4},{3,6},{4,1},{5,3},{6,5},{7,7},{8,8},{9,10},{10,1... | collective-permute-start | bytes 2359304 | tf_op jit(solution)/shard_map/ppermute | solution.py:887
  163.0 27.2 %collective-permute-start.26 = (bf16[2,2,128,1024]{3,2,1,0:T(8,128)(2,1)S(1)}, bf16[2,2,128,1024]{3,2,1,0:T(8,128)(2,1)S(1)}, u32[]{:S(2)}, u32[]{:S(2)}) collective-permute-start(bf16[2,2,128,1024]{3,2,1,0:T(8,128)(2,1)S(1)} %pad_maximum_fusion.7), channel_id=1, source_target_pairs={{0,16},{4,20},{8,24},{12,28},{16,0},{20,4},{24,8},{28,12},{1,17},{... | collective-permute-start | bytes 3145736 | tf_op jit(solution)/shard_map/ppermute | solution.py:49
  163.7 26.6 %collective-permute-start.25 = (bf16[2,2,128,1024]{3,2,1,0:T(8,128)(2,1)S(1)}, bf16[2,2,128,1024]{3,2,1,0:T(8,128)(2,1)S(1)}, u32[]{:S(2)}, u32[]{:S(2)}) collective-permute-start(bf16[2,2,128,1024]{3,2,1,0:T(8,128)(2,1)S(1)} %pad_maximum_fusion.6), channel_id=1, source_target_pairs={{0,8},{4,12},{8,0},{12,4},{16,24},{20,28},{24,16},{28,20},{1,9},{5... | collective-permute-start | bytes 3145736 | tf_op jit(solution)/shard_map/ppermute | solution.py:49
  164.3 25.9 %collective-permute-start.27 = (bf16[384,1024]{1,0:T(8,128)(2,1)S(1)}, bf16[384,1024]{1,0:T(8,128)(2,1)}, u32[]{:S(2)}, u32[]{:S(2)}) collective-permute-start(bf16[384,1024]{1,0:T(8,128)(2,1)S(1)} %copy-done.19), channel_id=1, source_target_pairs={{0,2},{1,0},{2,6},{3,4},{4,3},{5,1},{6,7},{7,5},{8,10},{9,8},{10,1... | collective-permute-start | bytes 2359304 | tf_op jit(solution)/shard_map/ppermute | solution.py:887
  239.6 161.1 %reduce-scatter.6.cloned.1.call-start = ((), (), s32[]{:S(2)}) async-start(), calls=%async_computation.4 | async-start | bytes 9437184 | tf_op jit(solution)/shard_map/reduce_scatter | solution.py:1044
  241.0 28.2 %collective-permute-start.30 = (bf16[384,1024]{1,0:T(8,128)(2,1)S(1)}, bf16[384,1024]{1,0:T(8,128)(2,1)S(1)}, u32[]{:S(2)}, u32[]{:S(2)}) collective-permute-start(bf16[384,1024]{1,0:T(8,128)(2,1)S(1)} %slice.169), channel_id=1, source_target_pairs={{0,0},{2,1},{4,2},{6,3},{1,4},{3,5},{5,6},{7,7},{8,8},{10,9},{12,1... | collective-permute-start | bytes 2359304 | tf_op jit(solution)/shard_map/ppermute | solution.py:893
  282.7 187.5 %reduce-scatter.8.cloned.1.call-start = ((), (), s32[]{:S(2)}) async-start(), calls=%async_computation.5 | async-start | bytes 1310720 | tf_op jit(solution)/shard_map/reduce_scatter | solution.py:1045
  284.6 26.1 %collective-permute-start.31 = (bf16[384,1024]{1,0:T(8,128)(2,1)S(1)}, bf16[384,1024]{1,0:T(8,128)(2,1)S(1)}, u32[]{:S(2)}, u32[]{:S(2)}) collective-permute-start(bf16[384,1024]{1,0:T(8,128)(2,1)S(1)} %slice_bitcast_fusion), channel_id=1, source_target_pairs={{2,0},{0,1},{6,2},{4,3},{3,4},{1,5},{7,6},{5,7},{10,8},{8,9},{14,1... | collective-permute-start | bytes 2359304 | tf_op jit(solution)/shard_map/ppermute | solution.py:893
  328.4 24.0 %collective-permute-start.33 = (bf16[2,768,256]{2,1,0:T(8,128)(2,1)}, bf16[2,768,256]{2,1,0:T(8,128)(2,1)S(1)}, u32[]{:S(2)}, u32[]{:S(2)}) collective-permute-start(bf16[2,768,256]{2,1,0:T(8,128)(2,1)} %get-tuple-element.438), channel_id=1, source_target_pairs={{0,4},{4,0},{8,12},{12,8},{16,20},{20,16},{24,28},{28,24},{1,5},{5... | collective-permute-start | bytes 2359304 | tf_op jit(solution)/shard_map/ppermute | solution.py:49
  352.5 28.3 %collective-permute-start.34 = (bf16[1,4,4,128,256]{4,3,2,1,0:T(8,128)(2,1)S(1)}, bf16[1,4,4,128,256]{4,3,2,1,0:T(8,128)(2,1)S(1)}, u32[]{:S(2)}, u32[]{:S(2)}) collective-permute-start(bf16[1,4,4,128,256]{4,3,2,1,0:T(8,128)(2,1)S(1)} %bitcast.212), channel_id=1, source_target_pairs={{0,4},{4,0},{8,12},{12,8},{16,20},{20,16},{24,28},{28,24},{1,5},{5... | collective-permute-start | bytes 3145736 | tf_op jit(solution)/shard_map/ppermute | solution.py:49
  353.3 27.4 %collective-permute-start.38 = (bf16[2,768,256]{2,1,0:T(8,128)(2,1)}, bf16[2,768,256]{2,1,0:T(8,128)(2,1)S(1)}, u32[]{:S(2)}, u32[]{:S(2)}) collective-permute-start(bf16[2,768,256]{2,1,0:T(8,128)(2,1)} %get-tuple-element.458), channel_id=1, source_target_pairs={{0,4},{4,0},{8,12},{12,8},{16,20},{20,16},{24,28},{28,24},{1,5},{5... | collective-permute-start | bytes 2359304 | tf_op jit(solution)/shard_map/ppermute | solution.py:49
  354.8 25.9 %collective-permute-start.35 = (bf16[128,1024]{1,0:T(8,128)(2,1)S(1)}, bf16[128,1024]{1,0:T(8,128)(2,1)S(1)}, u32[]{:S(2)}, u32[]{:S(2)}) collective-permute-start(bf16[128,1024]{1,0:T(8,128)(2,1)S(1)} %get-tuple-element.589), channel_id=1, source_target_pairs={{0,3},{1,0},{2,1},{3,2},{4,7},{5,4},{6,5},{7,6},{8,11},{9,8},{10,9... | collective-permute-start | bytes 786440 | tf_op jit(solution)/shard_map/ppermute | solution.py:53
  356.7 24.1 %collective-permute-start.36 = (bf16[128,1024]{1,0:T(8,128)(2,1)S(1)}, bf16[128,1024]{1,0:T(8,128)(2,1)S(1)}, u32[]{:S(2)}, u32[]{:S(2)}) collective-permute-start(bf16[128,1024]{1,0:T(8,128)(2,1)S(1)} %get-tuple-element.588), channel_id=1, source_target_pairs={{0,1},{1,2},{2,3},{3,0},{4,5},{5,6},{6,7},{7,4},{8,9},{9,10},{10,1... | collective-permute-start | bytes 786440 | tf_op jit(solution)/shard_map/ppermute | solution.py:53
  357.1 23.7 %collective-permute-start.37 = (bf16[128,1024]{1,0:T(8,128)(2,1)S(1)}, bf16[128,1024]{1,0:T(8,128)(2,1)S(1)}, u32[]{:S(2)}, u32[]{:S(2)}) collective-permute-start(bf16[128,1024]{1,0:T(8,128)(2,1)S(1)} %get-tuple-element.587), channel_id=1, source_target_pairs={{0,2},{1,3},{2,0},{3,1},{4,6},{5,7},{6,4},{7,5},{8,10},{9,11},{10,... | collective-permute-start | bytes 786440 | tf_op jit(solution)/shard_map/ppermute | solution.py:53
  381.6 18.0 %collective-permute-start.39 = (bf16[1,4,4,128,256]{4,3,2,1,0:T(8,128)(2,1)}, bf16[1,4,4,128,256]{4,3,2,1,0:T(8,128)(2,1)S(1)}, u32[]{:S(2)}, u32[]{:S(2)}) collective-permute-start(bf16[1,4,4,128,256]{4,3,2,1,0:T(8,128)(2,1)} %bitcast.211), channel_id=1, source_target_pairs={{0,4},{4,0},{8,12},{12,8},{16,20},{20,16},{24,28},{28,24},{1,5},{5... | collective-permute-start | bytes 3145736 | tf_op jit(solution)/shard_map/ppermute | solution.py:49
  381.6 18.0 %collective-permute-start.43 = (bf16[2,768,256]{2,1,0:T(8,128)(2,1)S(1)}, bf16[2,768,256]{2,1,0:T(8,128)(2,1)S(1)}, u32[]{:S(2)}, u32[]{:S(2)}) collective-permute-start(bf16[2,768,256]{2,1,0:T(8,128)(2,1)S(1)} %copy-done.54), channel_id=1, source_target_pairs={{0,4},{4,0},{8,12},{12,8},{16,20},{20,16},{24,28},{28,24},{1,5},{5... | collective-permute-start | bytes 2359304 | tf_op jit(solution)/shard_map/ppermute | solution.py:49
  400.7 24.7 %collective-permute-start.44 = (bf16[1,4,4,128,256]{4,3,2,1,0:T(8,128)(2,1)}, bf16[1,4,4,128,256]{4,3,2,1,0:T(8,128)(2,1)S(1)}, u32[]{:S(2)}, u32[]{:S(2)}) collective-permute-start(bf16[1,4,4,128,256]{4,3,2,1,0:T(8,128)(2,1)} %bitcast.210), channel_id=1, source_target_pairs={{0,4},{4,0},{8,12},{12,8},{16,20},{20,16},{24,28},{28,24},{1,5},{5... | collective-permute-start | bytes 3145736 | tf_op jit(solution)/shard_map/ppermute | solution.py:49
  402.1 23.3 %collective-permute-start.48 = (bf16[4,128,256]{2,1,0:T(8,128)(2,1)S(1)}, bf16[4,128,256]{2,1,0:T(8,128)(2,1)S(1)}, u32[]{:S(2)}, u32[]{:S(2)}) collective-permute-start(bf16[4,128,256]{2,1,0:T(8,128)(2,1)S(1)} %fusion.8), channel_id=1, source_target_pairs={{0,3},{1,0},{2,1},{3,2},{4,7},{5,4},{6,5},{7,6},{8,11},{9,8},{10,9... | collective-permute-start | bytes 786440 | tf_op jit(solution)/shard_map/ppermute | solution.py:53
  407.7 17.7 %collective-permute-start.45 = (bf16[1,4,128,256]{3,2,1,0:T(8,128)(2,1)}, bf16[1,4,128,256]{3,2,1,0:T(8,128)(2,1)S(1)}, u32[]{:S(2)}, u32[]{:S(2)}) collective-permute-start(bf16[1,4,128,256]{3,2,1,0:T(8,128)(2,1)} %get-tuple-element.489), channel_id=1, source_target_pairs={{0,8},{4,12},{8,0},{12,4},{16,24},{20,28},{24,16},{28,20},{1,9},{5... | collective-permute-start | bytes 786440 | tf_op jit(solution)/shard_map/ppermute | solution.py:49
  425.4 20.6 %collective-permute-start.49 = (bf16[1,4,4,128,256]{4,3,2,1,0:T(8,128)(2,1)S(1)}, bf16[1,4,4,128,256]{4,3,2,1,0:T(8,128)(2,1)S(1)}, u32[]{:S(2)}, u32[]{:S(2)}) collective-permute-start(bf16[1,4,4,128,256]{4,3,2,1,0:T(8,128)(2,1)S(1)} %bitcast.209), channel_id=1, source_target_pairs={{0,4},{4,0},{8,12},{12,8},{16,20},{20,16},{24,28},{28,24},{1,5},{5... | collective-permute-start | bytes 3145736 | tf_op jit(solution)/shard_map/ppermute | solution.py:49
  427.9 18.1 %collective-permute-start.54 = (bf16[384,1024]{1,0:T(8,128)(2,1)S(1)}, bf16[384,1024]{1,0:T(8,128)(2,1)S(1)}, u32[]{:S(2)}, u32[]{:S(2)}) collective-permute-start(bf16[384,1024]{1,0:T(8,128)(2,1)S(1)} %copy-done.52), channel_id=1, source_target_pairs={{0,0},{2,1},{4,2},{6,3},{1,4},{3,5},{5,6},{7,7},{8,8},{10,9},{12,1... | collective-permute-start | bytes 2359304 | tf_op jit(solution)/shard_map/ppermute | solution.py:1121
  448.8 30.9 %collective-permute-start.59 = (bf16[384,1024]{1,0:T(8,128)(2,1)}, bf16[384,1024]{1,0:T(8,128)(2,1)S(1)}, u32[]{:S(2)}, u32[]{:S(2)}) collective-permute-start(bf16[384,1024]{1,0:T(8,128)(2,1)} %get-tuple-element.538), channel_id=1, source_target_pairs={{2,0},{0,1},{6,2},{4,3},{3,4},{1,5},{7,6},{5,7},{10,8},{8,9},{14,1... | collective-permute-start | bytes 2359304 | tf_op jit(solution)/shard_map/ppermute | solution.py:1121
  (96 other events, 916.5 us)
Sparse Core Ops, SparseCore 0:
  104.4 63.1 all-gather.2
  239.7 68.7 reduce-scatter.3
  312.4 71.7 reduce-scatter.5
  400.8 29.5 reduce-scatter.7

commit v7 on v6

--- a/solution.py
+++ b/solution.py
@@ -516,7 +516,7 @@
 def feed_back_kernel(firsts, sizes, index_ref, *refs):
     nm, count = firsts + sum(sizes), 1 + 4 * len(sizes)
     g_ref, slope_ref, mid_ref, gain_ref = refs[count : count + 4]
-    hid_ref, gmid_ref, attn_ref, sums_ref, held, acc, sems = refs[count + 4 :]
+    hid_ref, attn_ref, sums_ref, held, acc, sems = refs[count + 4 :]
     step = pl.program_id(0)
     load_weights(firsts, sizes, index_ref, refs[:count], held, sems)
     half = g_ref.shape[1] // 2
@@ -540,9 +540,7 @@
     @pl.when(step == nm - 1)
     def _():
         into, sums = norm_back(acc[...], mid_ref[...], gain_ref[...])
-        result = g_ref[...].astype(F32) + into
-        gmid_ref[...] = result
-        attn_ref[...] = result.astype(BF16)
+        attn_ref[...] = (g_ref[...].astype(F32) + into).astype(BF16)
         sums_ref[...] = sums
 
 
@@ -562,12 +560,10 @@
         out_specs=[
             wide,
             line,
-            line,
             pl.BlockSpec((2, width), lambda k: (0, 0)),
         ],
         out_shape=[
             SHAPE((nm, rows, hidden), BF16),
-            SHAPE((rows, width), F32),
             SHAPE((rows, width), BF16),
             SHAPE((2, width), F32),
         ],
@@ -648,7 +644,7 @@
     return total, keep[None], give[None]
 
 
-def first_back_kernel(nm, parts, x_ref, gmid_ref, gain_ref, *refs):
+def first_back_kernel(nm, parts, x_ref, attn_ref, gain_ref, *refs):
     dqs, dkvs, came_ref, refs = refs[:nm], refs[nm : 2 * nm], refs[2 * nm], refs[2 * nm + 1 :]
     qo = refs[:parts], refs[parts : 2 * parts]
     kv = refs[2 * parts : 3 * parts], refs[3 * parts : 4 * parts]
@@ -665,11 +661,11 @@
                 total = total + dot_nt(dkv, kv_ref[:, n, i].reshape(half, -1))
         sides.append(total)
     into, sums = norm_back(jnp.concatenate(sides, axis=1), x_ref[...].astype(F32), gain_ref[...])
-    out_ref[...] = (gmid_ref[...] + into).astype(BF16)
+    out_ref[...] = (attn_ref[...].astype(F32) + into).astype(BF16)
     sums_ref[...] = sums
 
 
-def first_back(x, gmid, gain, dqs, dkvs, came, qo, kv, part, block):
+def first_back(x, attn, gain, dqs, dkvs, came, qo, kv, part, block):
     width = x.shape[1]
     nm, wide = len(dqs), dqs[0].shape[1]
     line = pl.BlockSpec((block, width), lambda i: (part, 0))
@@ -691,7 +687,7 @@
         compiler_params=params(),
         cost_estimate=cost(6 * block * width * nm * wide, 12 * block * width),
         name="first_back",
-    )(x, gmid, gain, *dqs, *dkvs, came, *qo_arrays, *kv_arrays)
+    )(x, attn, gain, *dqs, *dkvs, came, *qo_arrays, *kv_arrays)
 
 
 def add_low(a, b):
@@ -1035,11 +1031,11 @@
     over_dp = functools.partial(lax.psum_scatter, axis_name="dp", scatter_dimension=0, tiled=True)
     place = jnp.append(index, mp.astype(jnp.int32))
     grads_down = over_dp(wide_grad(grad, active, place, False))
-    hid, gmid, attn, sums_two = feed_back(
+    hid, attn, sums_two = feed_back(
         grad, slope, middle, gains[1:], index, firsts, sizes, weights
     )
-    hid, gmid, attn, sums_two, normed_two, output, out_chunks = sums.land(
-        hid, gmid, attn, sums_two, normed_two, output, out_chunks
+    hid, attn, sums_two, normed_two, output, out_chunks = sums.land(
+        hid, attn, sums_two, normed_two, output, out_chunks
     )
     grads_up = over_dp(wide_grad(normed_two, hid, place, True))[0]
     grads_up = lax.psum_scatter(grads_up, "mp", scatter_dimension=0, tiled=True)
@@ -1086,9 +1082,9 @@
             dqs[k], *parts = attend_back(
                 query, kvs, bias_tall, lses[k], mixed[k], grad_mixed, k * per_k, per_k
             )
-        live = (ready and ready[1], dqs, parts, query, dkv_part, dkv_came, dkvs, gmid)
+        live = (ready and ready[1], dqs, parts, query, dkv_part, dkv_came, dkvs, attn)
         live = sums.land(*live, output)
-        outs, dqs, parts, query, dkv_part, dkv_came, dkvs, gmid, output = live
+        outs, dqs, parts, query, dkv_part, dkv_came, dkvs, attn, output = live
         if ready:
             add_heads(ready, outs)
 
@@ -1098,7 +1094,7 @@
     def first_part(part):
         return first_back(
             x,
-            gmid,
+            attn,
             gains[:1],
             [dqs[k] for k in range(nm)],
             [dkvs[k] if k else dkv_part[k] for k in range(nm)],
@@ -1110,7 +1106,7 @@
         )
 
     firsts_back = [first_part(0)]
-    firsts_back, outs, output, gmid = sums.land(firsts_back, ready and ready[1], output, gmid)
+    firsts_back, outs, output, attn = sums.land(firsts_back, ready and ready[1], output, attn)
     if ready:
         add_heads(ready, outs)
     hops = [lambda value, bit=1 << b: swap(value, bit, nd) for b in range(nd.bit_length() - 1)]
@@ -1132,8 +1128,8 @@
             for hop in hops:
                 vectors = vectors + hop(vectors)
             hops = []
-        grad_tokens, firsts_back, vectors, output, gmid = sums.land(
-            grad_tokens, firsts_back, vectors, output, gmid
+        grad_tokens, firsts_back, vectors, output, attn = sums.land(
+            grad_tokens, firsts_back, vectors, output, attn
         )
     g_head, g_down = sums.done["head"], sums.done["down"]
     vectors = sum([ring(vectors, k, nm) for k in range(1, nm)], vectors)

time: 507 us -> 506 us (level)
  transfers between devices with their start and end apart: 70 -> 70, of which waited for: 17 -> 16; matrix products, arithmetic and copies ran while one was open for 7% -> 7% of each run, Pallas kernels for 51% -> 50%
where the time goes in v7:
time: 506 us; the launch traced here: 497 us
  Pallas kernels  287 us (57%)
  starting transfers between devices  81.6 us (16%)
  waiting for transfers between devices  60.6 us (12%)
  other arithmetic  30.2 us (6%)
  local copies, waits for them, and re-layouts  21.7 us (4%)
  between operations  15.8 us (3%)
    pallas_call x4, Pallas kernels, attend_back(): pl.pallas_call(functools.partial(attend_back_kernel, parts), grid=(count,...  69.7 us
    pallas_call x4, Pallas kernels, attend(): pl.pallas_call(functools.partial(attend_kernel, parts), grid=(count, rows...  46.1 us
    ppermute x42, starting transfers between devices, swap(): return lax.ppermute(value, 'dp', [(i, i ^ bit) for i in range(nd)])  40.9 us
    ppermute x15, waiting for transfers between devices, ring(): return lax.ppermute(value, 'mp', [(i, (i + step) % nm) for i in range(nm)])  29.5 us
    ppermute x42, waiting for transfers between devices, swap(): return lax.ppermute(value, 'dp', [(i, i ^ bit) for i in range(nd)])  28.5 us
    pallas_call x2, Pallas kernels, wide_grad(): pl.pallas_call(wide_grad_kernel, grid_spec=pltpu.PrefetchScalarGridSpec(n...  26.5 us
    pallas_call x1, Pallas kernels, feed_back(): pl.pallas_call(functools.partial(feed_back_kernel, firsts, sizes), grid=(...  26.1 us
    pallas_call x1, Pallas kernels, feed(): pl.pallas_call(functools.partial(feed_kernel, firsts, sizes), grid=(nm,),...  23.4 us
  transfers between devices with their start and end apart: 70, of which 16 were waited for; matrix products, arithmetic and copies ran while one was open for 7% of the time, Pallas kernels for 50%

profile of v7, /device:TPU:0, one launch (start us, length us, event | category | flops | bytes accessed | tf_op | source)
XLA Modules:
  0.0 496.9 jit_solution(5390231602291498083)
XLA Ops:
  8.2 4.1 collective-permute-start
  51.6 9.4 %collective-permute-start.13 = (bf16[4,1,2,128,256]{4,3,2,1,0:T(8,128)(2,1)S(1)}, bf16[4,1,2,128,256]{4,3,2,1,0:T(8,128)(2,1)S(1)}, u32[]{:S(2)}, u32[]{:S(2)}) collective-permute-start(bf16[4,1,2,128,256]{4,3,2,1,0:T(8,128)(2,1)S(1)} %pad_maximum_fusion.12.refs_0_.refs_4_.refs_9_), channel_id=1, source_target_pairs={{0,4},{4,0},{8,12},{12,8},{16,20},{20,16},{24,28},{28,24},{1,5},{5... | collective-permute-start | bytes 1572872 | tf_op jit(solution)/shard_map/ppermute | solution.py:49
  68.8 11.9 %collective-permute-done.11 = bf16[2,3,2,128,256]{4,3,2,1,0:T(8,128)(2,1)S(1)} collective-permute-done((bf16[2,3,2,128,256]{4,3,2,1,0:T(8,128)(2,1)S(1)}, bf16[2,3,2,128,256]{4,3,2,1,0:T(8,128)(2,1)S(1)}, u32[]{:S(2)}, u32[]{:S(2)}) %collective-permute-start.11) | collective-permute-done | bytes 786464 | tf_op jit(solution)/shard_map/ppermute | solution.py:49
  87.5 4.2 first_norm.1
  91.7 10.2 %collective-permute-done.17 = bf16[2,128,1024]{2,1,0:T(8,128)(2,1)S(1)} collective-permute-done((bf16[2,128,1024]{2,1,0:T(8,128)(2,1)S(1)}, bf16[2,128,1024]{2,1,0:T(8,128)(2,1)S(1)}, u32[]{:S(2)}, u32[]{:S(2)}) %collective-permute-start.17) | collective-permute-done | bytes 524320 | tf_op jit(solution)/shard_map/ppermute | solution.py:53
  106.1 6.9 %project.3.refs_0_.refs_2_ = bf16[2,768,1024]{2,1,0:T(8,128)(2,1)} custom-call(bf16[768,1024]{1,0:T(8,128)(2,1)} %get-tuple-element.345.in_ref.n_ref, bf16[4,1,2,128,256]{4,3,2,1,0:T(8,128)(2,1)} %copy-done.8, bf16[4,3,2,128,256]{4,3,2,1,0:T(8,128)(2,1)} %copy-done.5, bf16[4,1,2,128,256]{4,3,2,1,0:T(8,128)(2,1)} %copy-done.10, ...), custom_call_target="tpu_custom_call" | custom-call | flops 3221225472 | bytes 3145728 | tf_op jit(solution)/shard_map/project/pallas_call | solution.py:245
  113.0 6.3 %collective-permute-done.18 = bf16[2,128,1024]{2,1,0:T(8,128)(2,1)S(1)} collective-permute-done((bf16[2,128,1024]{2,1,0:T(8,128)(2,1)S(1)}, bf16[2,128,1024]{2,1,0:T(8,128)(2,1)S(1)}, u32[]{:S(2)}, u32[]{:S(2)}) %collective-permute-start.18) | collective-permute-done | bytes 524320 | tf_op jit(solution)/shard_map/ppermute | solution.py:53
  120.7 5.0 %project.4.q_ref = bf16[1,768,1024]{2,1,0:T(8,128)(2,1)} custom-call(bf16[768,1024]{1,0:T(8,128)(2,1)} %get-tuple-element.345.in_ref.n_ref, bf16[4,1,2,128,256]{4,3,2,1,0:T(8,128)(2,1)} %copy-done.4, bf16[4,3,2,128,256]{4,3,2,1,0:T(8,128)(2,1)} %copy-done.2, bf16[4,1,2,128,256]{4,3,2,1,0:T(8,128)(2,1)} %copy-done.6, bf16[4,3,2,128,256]{4,3,2,1,0:T(8,128)(2,1)} %copy-done.3), custom_call_target="tpu_custom_call" | custom-call | flops 1610612736 | bytes 1572864 | tf_op jit(solution)/shard_map/project/pallas_call | solution.py:245
  125.7 9.7 %collective-permute-done.21 = bf16[2,128,1024]{2,1,0:T(8,128)(2,1)S(1)} collective-permute-done((bf16[2,128,1024]{2,1,0:T(8,128)(2,1)S(1)}, bf16[2,128,1024]{2,1,0:T(8,128)(2,1)S(1)}, u32[]{:S(2)}, u32[]{:S(2)}) %collective-permute-start.21) | collective-permute-done | bytes 524320 | tf_op jit(solution)/shard_map/ppermute | solution.py:53
  138.7 11.5 %attend.5 = (bf16[768,256]{1,0:T(8,128)(2,1)}, f32[2,2,768]{2,1,0:T(2,128)}) custom-call(bf16[1,768,1024]{2,1,0:T(8,128)(2,1)} %project.4.q_ref, bf16[2,768,1024]{2,1,0:T(8,128)(2,1)} %project.3.refs_0_.refs_2_, bf16[2,768,1024]{2,1,0:T(8,128)(2,1)} %collective-permute-done.20.refs_1_.refs_3_, bf16[2,768,1024]{2,1,0:T(8,128)(2,1)} %project.3.refs_0_.refs_2_, ...), custom_call_target="tpu_custom_call" | custom-call | flops 4831838208 | bytes 3145728 | tf_op jit(solution)/shard_map/attend/pallas_call | solution.py:294
  150.3 11.5 %attend.4 = (bf16[768,256]{1,0:T(8,128)(2,1)}, f32[2,2,768]{2,1,0:T(2,128)}) custom-call(bf16[1,768,1024]{2,1,0:T(8,128)(2,1)} %project.4.q_ref, bf16[2,768,1024]{2,1,0:T(8,128)(2,1)} %project.3.refs_0_.refs_2_, bf16[2,768,1024]{2,1,0:T(8,128)(2,1)} %collective-permute-done.20.refs_1_.refs_3_, bf16[2,768,1024]{2,1,0:T(8,128)(2,1)} %project.3.refs_0_.refs_2_, ...), custom_call_target="tpu_custom_call" | custom-call | flops 4831838208 | bytes 3145728 | tf_op jit(solution)/shard_map/attend/pallas_call | solution.py:294
  167.1 11.5 %attend.7 = (bf16[768,256]{1,0:T(8,128)(2,1)}, f32[2,2,768]{2,1,0:T(2,128)}) custom-call(bf16[1,768,1024]{2,1,0:T(8,128)(2,1)} %project.4.q_ref, bf16[2,768,1024]{2,1,0:T(8,128)(2,1)} %project.3.refs_0_.refs_2_, bf16[2,768,1024]{2,1,0:T(8,128)(2,1)} %collective-permute-done.20.refs_1_.refs_3_, bf16[2,768,1024]{2,1,0:T(8,128)(2,1)} %project.3.refs_0_.refs_2_, ...), custom_call_target="tpu_custom_call" | custom-call | flops 4831838208 | bytes 3145728 | tf_op jit(solution)/shard_map/attend/pallas_call | solution.py:294
  178.6 11.5 %attend.6 = (bf16[768,256]{1,0:T(8,128)(2,1)}, f32[2,2,768]{2,1,0:T(2,128)}) custom-call(bf16[1,768,1024]{2,1,0:T(8,128)(2,1)} %project.4.q_ref, bf16[2,768,1024]{2,1,0:T(8,128)(2,1)} %project.3.refs_0_.refs_2_, bf16[2,768,1024]{2,1,0:T(8,128)(2,1)} %collective-permute-done.20.refs_1_.refs_3_, bf16[2,768,1024]{2,1,0:T(8,128)(2,1)} %project.3.refs_0_.refs_2_, ...), custom_call_target="tpu_custom_call" | custom-call | flops 4831838208 | bytes 3145728 | tf_op jit(solution)/shard_map/attend/pallas_call | solution.py:294
  191.8 7.1 %middle_norm.1 = (f32[768,1024]{1,0:T(8,128)}, bf16[768,1024]{1,0:T(8,128)(2,1)}) custom-call(bf16[768,1024]{1,0:T(8,128)(2,1)} %get-tuple-element.385.x_ref, bf16[768,256]{1,0:T(8,128)(2,1)} %get-tuple-element.386.refs_0_.refs_6_.mixed_ref, bf16[768,256]{1,0:T(8,128)(2,1)} %get-tuple-element.387.refs_1_.refs_6_.mixed_ref, ...), custom_call_target="tpu_custom_call" | custom-call | flops 1610612736 | bytes 11010048 | tf_op jit(solution)/shard_map/middle_norm/pallas_call | solution.py:409
  202.6 23.4 %feed.1 = (bf16[768,1024]{1,0:T(8,128)(2,1)}, bf16[4,768,1024]{2,1,0:T(8,128)(2,1)}, bf16[4,768,1024]{2,1,0:T(8,128)(2,1)}) custom-call(s32[8]{0:T(128)} %copy-done.45, bf16[8,2,2,128,1024]{4,3,2,1,0:T(8,128)(2,1)} %bitcast.207, bf16[4,2,128,1024]{3,2,1,0:T(8,128)(2,1)} %copy-done.12, bf16[4,2,128,1024]{3,2,1,0:T(8,128)(2,1)} %copy-done.49, ...), custom_call_target="tpu_custom_call" | custom-call | flops 12884901888 | bytes 16777216 | tf_op jit(solution)/shard_map/feed/pallas_call | solution.py:497
  226.0 13.2 %wide_grad.2 = bf16[8,4,128,1024]{3,2,1,0:T(8,128)(2,1)} custom-call(s32[9]{0:T(128)} %get-tuple-element.635.place_ref, bf16[768,1024]{1,0:T(8,128)(2,1)} %pad_maximum_fusion.4.refs_5_.a_ref, bf16[4,768,1024]{2,1,0:T(8,128)(2,1)} %get-tuple-element.440.b_ref), custom_call_target="tpu_custom_call" | custom-call | flops 6442450944 | bytes 16777216 | tf_op jit(solution)/shard_map/wide_grad/pallas_call | solution.py:597
  241.8 26.1 %feed_back.1 = (bf16[4,768,1024]{2,1,0:T(8,128)(2,1)}, bf16[768,1024]{1,0:T(8,128)(2,1)}, f32[2,1024]{1,0:T(2,128)}) custom-call(s32[8]{0:T(128)} %copy-done.45, bf16[8,2,2,128,1024]{4,3,2,1,0:T(8,128)(2,1)} %bitcast.208, bf16[4,2,128,1024]{3,2,1,0:T(8,128)(2,1)} %copy-done.12, bf16[4,2,128,1024]{3,2,1,0:T(8,128)(2,1)} %copy-done.49, ...), custom_call_target="tpu_custom_call" | custom-call | flops 12884901888 | bytes 16777216 | tf_op jit(solution)/shard_map/feed_back/pallas_call | solution.py:554
  267.9 13.3 %wide_grad.3 = bf16[8,4,128,1024]{3,2,1,0:T(8,128)(2,1)} custom-call(s32[9]{0:T(128)} %get-tuple-element.635.place_ref, bf16[768,1024]{1,0:T(8,128)(2,1)} %get-tuple-element.548.refs_5_.a_ref, bf16[4,768,1024]{2,1,0:T(8,128)(2,1)} %get-tuple-element.549.b_ref), custom_call_target="tpu_custom_call" | custom-call | flops 6442450944 | bytes 16777216 | tf_op jit(solution)/shard_map/wide_grad/pallas_call | solution.py:597
  286.4 5.0 %project.5.refs_7_ = bf16[1,768,1024]{2,1,0:T(8,128)(2,1)} custom-call(bf16[768,1024]{1,0:T(8,128)(2,1)} %get-tuple-element.520.in_ref.g_ref.attn_ref, bf16[4,1,2,128,256]{4,3,2,1,0:T(8,128)(2,1)} %copy-done.4, bf16[4,3,2,128,256]{4,3,2,1,0:T(8,128)(2,1)} %copy-done.2, bf16[4,1,2,128,256]{4,3,2,1,0:T(8,128)(2,1)} %copy-done.6, ...), custom_call_target="tpu_custom_call" | custom-call | flops 1610612736 | bytes 1572864 | tf_op jit(solution)/shard_map/project/pallas_call | solution.py:245
  291.4 17.4 %attend_back.4 = (bf16[768,256]{1,0:T(8,128)(2,1)}, bf16[2,768,256]{2,1,0:T(8,128)(2,1)}, bf16[2,768,256]{2,1,0:T(8,128)(2,1)}) custom-call(bf16[1,768,1024]{2,1,0:T(8,128)(2,1)} %project.4.q_ref, bf16[2,768,1024]{2,1,0:T(8,128)(2,1)} %project.3.refs_0_.refs_2_, bf16[2,768,1024]{2,1,0:T(8,128)(2,1)} %collective-permute-done.20.refs_1_.refs_3_, ...), custom_call_target="tpu_custom_call" | custom-call | flops 12079595520 | bytes 6291456 | tf_op jit(solution)/shard_map/attend_back/pallas_call | solution.py:362
  309.1 17.4 %attend_back.5 = (bf16[768,256]{1,0:T(8,128)(2,1)}, bf16[2,768,256]{2,1,0:T(8,128)(2,1)}, bf16[2,768,256]{2,1,0:T(8,128)(2,1)}) custom-call(bf16[1,768,1024]{2,1,0:T(8,128)(2,1)} %project.4.q_ref, bf16[2,768,1024]{2,1,0:T(8,128)(2,1)} %project.3.refs_0_.refs_2_, bf16[2,768,1024]{2,1,0:T(8,128)(2,1)} %collective-permute-done.20.refs_1_.refs_3_, ...), custom_call_target="tpu_custom_call" | custom-call | flops 12079595520 | bytes 6291456 | tf_op jit(solution)/shard_map/attend_back/pallas_call | solution.py:362
  327.4 5.8 %head_grad.4 = (bf16[2,768,256]{2,1,0:T(8,128)(2,1)}, bf16[4,4,128,256]{3,2,1,0:T(8,128)(2,1)}, bf16[4,4,128,256]{3,2,1,0:T(8,128)(2,1)}) custom-call(bf16[768,1024]{1,0:T(8,128)(2,1)} %get-tuple-element.345.in_ref.n_ref, bf16[768,1024]{1,0:T(8,128)(2,1)} %get-tuple-element.520.in_ref.g_ref.attn_ref, ...), custom_call_target="tpu_custom_call" | custom-call | flops 1610612736 | bytes 2097152 | tf_op jit(solution)/shard_map/head_grad/pallas_call | solution.py:635
  333.2 17.5 %attend_back.6 = (bf16[768,256]{1,0:T(8,128)(2,1)}, bf16[2,768,256]{2,1,0:T(8,128)(2,1)}, bf16[2,768,256]{2,1,0:T(8,128)(2,1)}) custom-call(bf16[1,768,1024]{2,1,0:T(8,128)(2,1)} %project.4.q_ref, bf16[2,768,1024]{2,1,0:T(8,128)(2,1)} %project.3.refs_0_.refs_2_, bf16[2,768,1024]{2,1,0:T(8,128)(2,1)} %collective-permute-done.20.refs_1_.refs_3_, ...), custom_call_target="tpu_custom_call" | custom-call | flops 12079595520 | bytes 6291456 | tf_op jit(solution)/shard_map/attend_back/pallas_call | solution.py:362
  356.5 17.3 %attend_back.7 = (bf16[768,256]{1,0:T(8,128)(2,1)}, bf16[2,768,256]{2,1,0:T(8,128)(2,1)}, bf16[2,768,256]{2,1,0:T(8,128)(2,1)}) custom-call(bf16[1,768,1024]{2,1,0:T(8,128)(2,1)} %project.4.q_ref, bf16[2,768,1024]{2,1,0:T(8,128)(2,1)} %project.3.refs_0_.refs_2_, bf16[2,768,1024]{2,1,0:T(8,128)(2,1)} %collective-permute-done.20.refs_1_.refs_3_, ...), custom_call_target="tpu_custom_call" | custom-call | flops 12079595520 | bytes 6291456 | tf_op jit(solution)/shard_map/attend_back/pallas_call | solution.py:362
  373.9 5.7 %head_grad.5 = (bf16[2,768,256]{2,1,0:T(8,128)(2,1)}, bf16[4,4,128,256]{3,2,1,0:T(8,128)(2,1)}, bf16[4,4,128,256]{3,2,1,0:T(8,128)(2,1)}) custom-call(bf16[768,1024]{1,0:T(8,128)(2,1)} %get-tuple-element.345.in_ref.n_ref, bf16[768,1024]{1,0:T(8,128)(2,1)} %get-tuple-element.520.in_ref.g_ref.attn_ref, ...), custom_call_target="tpu_custom_call" | custom-call | flops 1610612736 | bytes 2097152 | tf_op jit(solution)/shard_map/head_grad/pallas_call | solution.py:635
  387.0 5.6 %head_grad.6 = (bf16[2,768,256]{2,1,0:T(8,128)(2,1)}, bf16[4,4,128,256]{3,2,1,0:T(8,128)(2,1)}, bf16[4,4,128,256]{3,2,1,0:T(8,128)(2,1)}) custom-call(bf16[768,1024]{1,0:T(8,128)(2,1)} %get-tuple-element.345.in_ref.n_ref, bf16[768,1024]{1,0:T(8,128)(2,1)} %get-tuple-element.520.in_ref.g_ref.attn_ref, ...), custom_call_target="tpu_custom_call" | custom-call | flops 1610612736 | bytes 2097152 | tf_op jit(solution)/shard_map/head_grad/pallas_call | solution.py:635
  392.9 5.7 %collective-permute-done.41 = bf16[1,4,128,256]{3,2,1,0:T(8,128)(2,1)S(1)} collective-permute-done((bf16[1,4,128,256]{3,2,1,0:T(8,128)(2,1)}, bf16[1,4,128,256]{3,2,1,0:T(8,128)(2,1)S(1)}, u32[]{:S(2)}, u32[]{:S(2)}) %collective-permute-start.41) | collective-permute-done | bytes 262176 | tf_op jit(solution)/shard_map/ppermute | solution.py:49
  410.3 5.6 %head_grad.7 = (bf16[2,768,256]{2,1,0:T(8,128)(2,1)}, bf16[4,4,128,256]{3,2,1,0:T(8,128)(2,1)}, bf16[4,4,128,256]{3,2,1,0:T(8,128)(2,1)}) custom-call(bf16[768,1024]{1,0:T(8,128)(2,1)} %get-tuple-element.345.in_ref.n_ref, bf16[768,1024]{1,0:T(8,128)(2,1)} %get-tuple-element.520.in_ref.g_ref.attn_ref, ...), custom_call_target="tpu_custom_call" | custom-call | flops 1610612736 | bytes 2097152 | tf_op jit(solution)/shard_map/head_grad/pallas_call | solution.py:635
  415.9 8.4 %first_back.2 = (bf16[384,1024]{1,0:T(8,128)(2,1)}, f32[2,1024]{1,0:T(2,128)}) custom-call(bf16[768,1024]{1,0:T(8,128)(2,1)} %get-tuple-element.385.x_ref, bf16[768,1024]{1,0:T(8,128)(2,1)} %get-tuple-element.520.in_ref.g_ref.attn_ref, f32[1,1024]{1,0:T(1,128)} %get-tuple-element.619.refs_2_.gain_ref, bf16[768,256]{1,0:T(8,128)(2,1)} %get-tuple-element.492.refs_0_.dq_ref, ...), custom_call_target="tpu_custom_call" | custom-call | flops 2415919104 | bytes 4718592 | tf_op jit(solution)/shard_map/first_back/pallas_call | solution.py:674
  436.0 8.3 %first_back.3 = (bf16[384,1024]{1,0:T(8,128)(2,1)}, f32[2,1024]{1,0:T(2,128)}) custom-call(bf16[768,1024]{1,0:T(8,128)(2,1)} %get-tuple-element.385.x_ref, bf16[768,1024]{1,0:T(8,128)(2,1)} %get-tuple-element.520.in_ref.g_ref.attn_ref, f32[1,1024]{1,0:T(1,128)} %get-tuple-element.619.refs_2_.gain_ref, bf16[768,256]{1,0:T(8,128)(2,1)} %get-tuple-element.492.refs_0_.dq_ref, ...), custom_call_target="tpu_custom_call" | custom-call | flops 2415919104 | bytes 4718592 | tf_op jit(solution)/shard_map/first_back/pallas_call | solution.py:674
  447.5 6.9 %collective-permute-start.59 = (bf16[384,1024]{1,0:T(8,128)(2,1)}, bf16[384,1024]{1,0:T(8,128)(2,1)S(1)}, u32[]{:S(2)}, u32[]{:S(2)}) collective-permute-start(bf16[384,1024]{1,0:T(8,128)(2,1)} %get-tuple-element.534), channel_id=1, source_target_pairs={{2,0},{0,1},{6,2},{4,3},{3,4},{1,5},{7,6},{5,7},{10,8},{8,9},{14,1... | collective-permute-start | bytes 2359304 | tf_op jit(solution)/shard_map/ppermute | solution.py:1117
  475.2 3.4 collective-permute-done.56
  (336 shorter events, 154.1 us)
Async XLA Ops:
  7.2 195.4 %all-gather.3.cloned.1.call-start = ((), (), s32[]{:S(2)}) async-start(), calls=%async_computation.6 | async-start | bytes 9437184 | tf_op jit(solution)/shard_map/all_gather | solution.py:953
  8.2 23.5 %collective-permute-start = (bf16[4,128,256]{2,1,0:T(8,128)(2,1)S(1)}, bf16[4,128,256]{2,1,0:T(8,128)(2,1)S(1)}, u32[]{:S(2)}, u32[]{:S(2)}) collective-permute-start(bf16[4,128,256]{2,1,0:T(8,128)(2,1)S(1)} %pad_maximum_fusion.17), channel_id=1, source_target_pairs={{0,2},{1,3},{2,0},{3,1},{4,6},{5,7},{6,4},{7,5},{8,10},{9,11},{10,... | collective-permute-start | bytes 786440 | tf_op jit(solution)/shard_map/ppermute | solution.py:53
  12.3 19.4 %collective-permute-start.1 = (bf16[4,128,256]{2,1,0:T(8,128)(2,1)S(1)}, bf16[4,128,256]{2,1,0:T(8,128)(2,1)S(1)}, u32[]{:S(2)}, u32[]{:S(2)}) collective-permute-start(bf16[4,128,256]{2,1,0:T(8,128)(2,1)S(1)} %pad_maximum_fusion.17), channel_id=1, source_target_pairs={{0,1},{1,2},{2,3},{3,0},{4,5},{5,6},{6,7},{7,4},{8,9},{9,10},{10,1... | collective-permute-start | bytes 786440 | tf_op jit(solution)/shard_map/ppermute | solution.py:53
  13.9 17.8 %collective-permute-start.2 = (bf16[4,128,256]{2,1,0:T(8,128)(2,1)S(1)}, bf16[4,128,256]{2,1,0:T(8,128)(2,1)S(1)}, u32[]{:S(2)}, u32[]{:S(2)}) collective-permute-start(bf16[4,128,256]{2,1,0:T(8,128)(2,1)S(1)} %pad_maximum_fusion.17), channel_id=1, source_target_pairs={{0,3},{1,0},{2,1},{3,2},{4,7},{5,4},{6,5},{7,6},{8,11},{9,8},{10,9... | collective-permute-start | bytes 786440 | tf_op jit(solution)/shard_map/ppermute | solution.py:53
  61.1 19.5 %collective-permute-start.11 = (bf16[2,3,2,128,256]{4,3,2,1,0:T(8,128)(2,1)S(1)}, bf16[2,3,2,128,256]{4,3,2,1,0:T(8,128)(2,1)S(1)}, u32[]{:S(2)}, u32[]{:S(2)}) collective-permute-start(bf16[2,3,2,128,256]{4,3,2,1,0:T(8,128)(2,1)S(1)} %pad_maximum_fusion.9), channel_id=1, source_target_pairs={{0,16},{4,20},{8,24},{12,28},{16,0},{20,4},{24,8},{28,12},{1,17},{... | collective-permute-start | bytes 2359304 | tf_op jit(solution)/shard_map/ppermute | solution.py:49
  61.8 19.4 %collective-permute-start.10 = (bf16[2,3,2,128,256]{4,3,2,1,0:T(8,128)(2,1)S(1)}, bf16[2,3,2,128,256]{4,3,2,1,0:T(8,128)(2,1)S(1)}, u32[]{:S(2)}, u32[]{:S(2)}) collective-permute-start(bf16[2,3,2,128,256]{4,3,2,1,0:T(8,128)(2,1)S(1)} %pad_maximum_fusion.8), channel_id=1, source_target_pairs={{0,8},{4,12},{8,0},{12,4},{16,24},{20,28},{24,16},{28,20},{1,9},{5... | collective-permute-start | bytes 2359304 | tf_op jit(solution)/shard_map/ppermute | solution.py:49
  63.3 20.4 %collective-permute-start.14 = (bf16[384,1024]{1,0:T(8,128)(2,1)S(1)}, bf16[384,1024]{1,0:T(8,128)(2,1)S(1)}, u32[]{:S(2)}, u32[]{:S(2)}) collective-permute-start(bf16[384,1024]{1,0:T(8,128)(2,1)S(1)} %copy-done.21), channel_id=1, source_target_pairs={{0,2},{1,0},{2,6},{3,4},{4,3},{5,1},{6,7},{7,5},{8,10},{9,8},{10,1... | collective-permute-start | bytes 2359304 | tf_op jit(solution)/shard_map/ppermute | solution.py:883
  104.2 247.7 %reduce-scatter.4.cloned.1.call-start = ((), (), s32[]{:S(2)}) async-start(), calls=%async_computation.3 | async-start | bytes 9437184 | tf_op jit(solution)/shard_map/reduce_scatter | solution.py:1033
  135.6 26.2 %collective-permute-start.23 = (bf16[1,2,128,1024]{3,2,1,0:T(8,128)(2,1)S(1)}, bf16[1,2,128,1024]{3,2,1,0:T(8,128)(2,1)S(1)}, u32[]{:S(2)}, u32[]{:S(2)}) collective-permute-start(bf16[1,2,128,1024]{3,2,1,0:T(8,128)(2,1)S(1)} %get-tuple-element.592), channel_id=1, source_target_pairs={{0,16},{4,20},{8,24},{12,28},{16,0},{20,4},{24,8},{28,12},{1,17},{... | collective-permute-start | bytes 1572872 | tf_op jit(solution)/shard_map/ppermute | solution.py:49
  137.2 25.6 %collective-permute-start.22 = (bf16[1,2,128,1024]{3,2,1,0:T(8,128)(2,1)S(1)}, bf16[1,2,128,1024]{3,2,1,0:T(8,128)(2,1)S(1)}, u32[]{:S(2)}, u32[]{:S(2)}) collective-permute-start(bf16[1,2,128,1024]{3,2,1,0:T(8,128)(2,1)S(1)} %get-tuple-element.594), channel_id=1, source_target_pairs={{0,8},{4,12},{8,0},{12,4},{16,24},{20,28},{24,16},{28,20},{1,9},{5... | collective-permute-start | bytes 1572872 | tf_op jit(solution)/shard_map/ppermute | solution.py:49
  137.8 25.0 %collective-permute-start.24 = (bf16[384,1024]{1,0:T(8,128)(2,1)S(1)}, bf16[384,1024]{1,0:T(8,128)(2,1)S(1)}, u32[]{:S(2)}, u32[]{:S(2)}) collective-permute-start(bf16[384,1024]{1,0:T(8,128)(2,1)S(1)} %copy-done.20), channel_id=1, source_target_pairs={{0,0},{1,2},{2,4},{3,6},{4,1},{5,3},{6,5},{7,7},{8,8},{9,10},{10,1... | collective-permute-start | bytes 2359304 | tf_op jit(solution)/shard_map/ppermute | solution.py:883
  162.9 27.2 %collective-permute-start.26 = (bf16[2,2,128,1024]{3,2,1,0:T(8,128)(2,1)S(1)}, bf16[2,2,128,1024]{3,2,1,0:T(8,128)(2,1)S(1)}, u32[]{:S(2)}, u32[]{:S(2)}) collective-permute-start(bf16[2,2,128,1024]{3,2,1,0:T(8,128)(2,1)S(1)} %pad_maximum_fusion.6), channel_id=1, source_target_pairs={{0,16},{4,20},{8,24},{12,28},{16,0},{20,4},{24,8},{28,12},{1,17},{... | collective-permute-start | bytes 3145736 | tf_op jit(solution)/shard_map/ppermute | solution.py:49
  163.6 26.5 %collective-permute-start.25 = (bf16[2,2,128,1024]{3,2,1,0:T(8,128)(2,1)S(1)}, bf16[2,2,128,1024]{3,2,1,0:T(8,128)(2,1)S(1)}, u32[]{:S(2)}, u32[]{:S(2)}) collective-permute-start(bf16[2,2,128,1024]{3,2,1,0:T(8,128)(2,1)S(1)} %pad_maximum_fusion.5), channel_id=1, source_target_pairs={{0,8},{4,12},{8,0},{12,4},{16,24},{20,28},{24,16},{28,20},{1,9},{5... | collective-permute-start | bytes 3145736 | tf_op jit(solution)/shard_map/ppermute | solution.py:49
  164.2 25.9 %collective-permute-start.27 = (bf16[384,1024]{1,0:T(8,128)(2,1)S(1)}, bf16[384,1024]{1,0:T(8,128)(2,1)}, u32[]{:S(2)}, u32[]{:S(2)}) collective-permute-start(bf16[384,1024]{1,0:T(8,128)(2,1)S(1)} %copy-done.19), channel_id=1, source_target_pairs={{0,2},{1,0},{2,6},{3,4},{4,3},{5,1},{6,7},{7,5},{8,10},{9,8},{10,1... | collective-permute-start | bytes 2359304 | tf_op jit(solution)/shard_map/ppermute | solution.py:883
  239.3 160.4 %reduce-scatter.6.cloned.1.call-start = ((), (), s32[]{:S(2)}) async-start(), calls=%async_computation.4 | async-start | bytes 9437184 | tf_op jit(solution)/shard_map/reduce_scatter | solution.py:1040
  240.7 27.2 %collective-permute-start.30 = (bf16[384,1024]{1,0:T(8,128)(2,1)S(1)}, bf16[384,1024]{1,0:T(8,128)(2,1)S(1)}, u32[]{:S(2)}, u32[]{:S(2)}) collective-permute-start(bf16[384,1024]{1,0:T(8,128)(2,1)S(1)} %slice.169), channel_id=1, source_target_pairs={{0,0},{2,1},{4,2},{6,3},{1,4},{3,5},{5,6},{7,7},{8,8},{10,9},{12,1... | collective-permute-start | bytes 2359304 | tf_op jit(solution)/shard_map/ppermute | solution.py:889
  281.2 188.0 %reduce-scatter.8.cloned.1.call-start = ((), (), s32[]{:S(2)}) async-start(), calls=%async_computation.5 | async-start | bytes 1310720 | tf_op jit(solution)/shard_map/reduce_scatter | solution.py:1041
  283.2 25.6 %collective-permute-start.31 = (bf16[384,1024]{1,0:T(8,128)(2,1)S(1)}, bf16[384,1024]{1,0:T(8,128)(2,1)S(1)}, u32[]{:S(2)}, u32[]{:S(2)}) collective-permute-start(bf16[384,1024]{1,0:T(8,128)(2,1)S(1)} %slice_bitcast_fusion), channel_id=1, source_target_pairs={{2,0},{0,1},{6,2},{4,3},{3,4},{1,5},{7,6},{5,7},{10,8},{8,9},{14,1... | collective-permute-start | bytes 2359304 | tf_op jit(solution)/shard_map/ppermute | solution.py:889
  308.8 17.7 %collective-permute-start.32 = (bf16[2,768,256]{2,1,0:T(8,128)(2,1)}, bf16[2,768,256]{2,1,0:T(8,128)(2,1)S(1)}, u32[]{:S(2)}, u32[]{:S(2)}) collective-permute-start(bf16[2,768,256]{2,1,0:T(8,128)(2,1)} %get-tuple-element.418), channel_id=1, source_target_pairs={{0,4},{4,0},{8,12},{12,8},{16,20},{20,16},{24,28},{28,24},{1,5},{5... | collective-permute-start | bytes 2359304 | tf_op jit(solution)/shard_map/ppermute | solution.py:49
  326.5 24.2 %collective-permute-start.33 = (bf16[2,768,256]{2,1,0:T(8,128)(2,1)}, bf16[2,768,256]{2,1,0:T(8,128)(2,1)S(1)}, u32[]{:S(2)}, u32[]{:S(2)}) collective-permute-start(bf16[2,768,256]{2,1,0:T(8,128)(2,1)} %get-tuple-element.435), channel_id=1, source_target_pairs={{0,4},{4,0},{8,12},{12,8},{16,20},{20,16},{24,28},{28,24},{1,5},{5... | collective-permute-start | bytes 2359304 | tf_op jit(solution)/shard_map/ppermute | solution.py:49
  350.8 28.8 %collective-permute-start.34 = (bf16[1,4,4,128,256]{4,3,2,1,0:T(8,128)(2,1)S(1)}, bf16[1,4,4,128,256]{4,3,2,1,0:T(8,128)(2,1)S(1)}, u32[]{:S(2)}, u32[]{:S(2)}) collective-permute-start(bf16[1,4,4,128,256]{4,3,2,1,0:T(8,128)(2,1)S(1)} %bitcast.212), channel_id=1, source_target_pairs={{0,4},{4,0},{8,12},{12,8},{16,20},{20,16},{24,28},{28,24},{1,5},{5... | collective-permute-start | bytes 3145736 | tf_op jit(solution)/shard_map/ppermute | solution.py:49
  351.6 28.0 %collective-permute-start.38 = (bf16[2,768,256]{2,1,0:T(8,128)(2,1)}, bf16[2,768,256]{2,1,0:T(8,128)(2,1)S(1)}, u32[]{:S(2)}, u32[]{:S(2)}) collective-permute-start(bf16[2,768,256]{2,1,0:T(8,128)(2,1)} %get-tuple-element.455), channel_id=1, source_target_pairs={{0,4},{4,0},{8,12},{12,8},{16,20},{20,16},{24,28},{28,24},{1,5},{5... | collective-permute-start | bytes 2359304 | tf_op jit(solution)/shard_map/ppermute | solution.py:49
  353.2 26.5 %collective-permute-start.35 = (bf16[128,1024]{1,0:T(8,128)(2,1)S(1)}, bf16[128,1024]{1,0:T(8,128)(2,1)S(1)}, u32[]{:S(2)}, u32[]{:S(2)}) collective-permute-start(bf16[128,1024]{1,0:T(8,128)(2,1)S(1)} %get-tuple-element.585), channel_id=1, source_target_pairs={{0,3},{1,0},{2,1},{3,2},{4,7},{5,4},{6,5},{7,6},{8,11},{9,8},{10,9... | collective-permute-start | bytes 786440 | tf_op jit(solution)/shard_map/ppermute | solution.py:53
  355.7 24.0 %collective-permute-start.36 = (bf16[128,1024]{1,0:T(8,128)(2,1)S(1)}, bf16[128,1024]{1,0:T(8,128)(2,1)S(1)}, u32[]{:S(2)}, u32[]{:S(2)}) collective-permute-start(bf16[128,1024]{1,0:T(8,128)(2,1)S(1)} %get-tuple-element.584), channel_id=1, source_target_pairs={{0,1},{1,2},{2,3},{3,0},{4,5},{5,6},{6,7},{7,4},{8,9},{9,10},{10,1... | collective-permute-start | bytes 786440 | tf_op jit(solution)/shard_map/ppermute | solution.py:53
  355.9 23.8 %collective-permute-start.37 = (bf16[128,1024]{1,0:T(8,128)(2,1)S(1)}, bf16[128,1024]{1,0:T(8,128)(2,1)S(1)}, u32[]{:S(2)}, u32[]{:S(2)}) collective-permute-start(bf16[128,1024]{1,0:T(8,128)(2,1)S(1)} %get-tuple-element.583), channel_id=1, source_target_pairs={{0,2},{1,3},{2,0},{3,1},{4,6},{5,7},{6,4},{7,5},{8,10},{9,11},{10,... | collective-permute-start | bytes 786440 | tf_op jit(solution)/shard_map/ppermute | solution.py:53
  380.5 18.2 %collective-permute-start.39 = (bf16[1,4,4,128,256]{4,3,2,1,0:T(8,128)(2,1)}, bf16[1,4,4,128,256]{4,3,2,1,0:T(8,128)(2,1)S(1)}, u32[]{:S(2)}, u32[]{:S(2)}) collective-permute-start(bf16[1,4,4,128,256]{4,3,2,1,0:T(8,128)(2,1)} %bitcast.211), channel_id=1, source_target_pairs={{0,4},{4,0},{8,12},{12,8},{16,20},{20,16},{24,28},{28,24},{1,5},{5... | collective-permute-start | bytes 3145736 | tf_op jit(solution)/shard_map/ppermute | solution.py:49
  380.5 18.2 %collective-permute-start.43 = (bf16[2,768,256]{2,1,0:T(8,128)(2,1)S(1)}, bf16[2,768,256]{2,1,0:T(8,128)(2,1)S(1)}, u32[]{:S(2)}, u32[]{:S(2)}) collective-permute-start(bf16[2,768,256]{2,1,0:T(8,128)(2,1)S(1)} %copy-done.54), channel_id=1, source_target_pairs={{0,4},{4,0},{8,12},{12,8},{16,20},{20,16},{24,28},{28,24},{1,5},{5... | collective-permute-start | bytes 2359304 | tf_op jit(solution)/shard_map/ppermute | solution.py:49
  399.7 24.7 %collective-permute-start.44 = (bf16[1,4,4,128,256]{4,3,2,1,0:T(8,128)(2,1)}, bf16[1,4,4,128,256]{4,3,2,1,0:T(8,128)(2,1)S(1)}, u32[]{:S(2)}, u32[]{:S(2)}) collective-permute-start(bf16[1,4,4,128,256]{4,3,2,1,0:T(8,128)(2,1)} %bitcast.210), channel_id=1, source_target_pairs={{0,4},{4,0},{8,12},{12,8},{16,20},{20,16},{24,28},{28,24},{1,5},{5... | collective-permute-start | bytes 3145736 | tf_op jit(solution)/shard_map/ppermute | solution.py:49
  401.1 23.3 %collective-permute-start.48 = (bf16[4,128,256]{2,1,0:T(8,128)(2,1)S(1)}, bf16[4,128,256]{2,1,0:T(8,128)(2,1)S(1)}, u32[]{:S(2)}, u32[]{:S(2)}) collective-permute-start(bf16[4,128,256]{2,1,0:T(8,128)(2,1)S(1)} %fusion.8), channel_id=1, source_target_pairs={{0,3},{1,0},{2,1},{3,2},{4,7},{5,4},{6,5},{7,6},{8,11},{9,8},{10,9... | collective-permute-start | bytes 786440 | tf_op jit(solution)/shard_map/ppermute | solution.py:53
  424.4 20.6 %collective-permute-start.49 = (bf16[1,4,4,128,256]{4,3,2,1,0:T(8,128)(2,1)S(1)}, bf16[1,4,4,128,256]{4,3,2,1,0:T(8,128)(2,1)S(1)}, u32[]{:S(2)}, u32[]{:S(2)}) collective-permute-start(bf16[1,4,4,128,256]{4,3,2,1,0:T(8,128)(2,1)S(1)} %bitcast.209), channel_id=1, source_target_pairs={{0,4},{4,0},{8,12},{12,8},{16,20},{20,16},{24,28},{28,24},{1,5},{5... | collective-permute-start | bytes 3145736 | tf_op jit(solution)/shard_map/ppermute | solution.py:49
  426.9 18.1 %collective-permute-start.54 = (bf16[384,1024]{1,0:T(8,128)(2,1)S(1)}, bf16[384,1024]{1,0:T(8,128)(2,1)S(1)}, u32[]{:S(2)}, u32[]{:S(2)}) collective-permute-start(bf16[384,1024]{1,0:T(8,128)(2,1)S(1)} %copy-done.52), channel_id=1, source_target_pairs={{0,0},{2,1},{4,2},{6,3},{1,4},{3,5},{5,6},{7,7},{8,8},{10,9},{12,1... | collective-permute-start | bytes 2359304 | tf_op jit(solution)/shard_map/ppermute | solution.py:1117
  447.5 31.1 %collective-permute-start.59 = (bf16[384,1024]{1,0:T(8,128)(2,1)}, bf16[384,1024]{1,0:T(8,128)(2,1)S(1)}, u32[]{:S(2)}, u32[]{:S(2)}) collective-permute-start(bf16[384,1024]{1,0:T(8,128)(2,1)} %get-tuple-element.534), channel_id=1, source_target_pairs={{2,0},{0,1},{6,2},{4,3},{3,4},{1,5},{7,6},{5,7},{10,8},{8,9},{14,1... | collective-permute-start | bytes 2359304 | tf_op jit(solution)/shard_map/ppermute | solution.py:1117
  (96 other events, 915.9 us)
Sparse Core Ops, SparseCore 0:
  104.3 63.1 all-gather.2
  239.4 68.8 reduce-scatter.3
  312.1 71.6 reduce-scatter.5
  399.9 29.7 reduce-scatter.7

commit v8 on v7

--- a/solution.py
+++ b/solution.py
@@ -1069,7 +1069,7 @@
 
     parts = None
     for k in list(reversed(range(nm))) + [-1]:
-        if k == 0:
+        if k == 1:
             sums.add_line("down", grads_down[0], rings=False)
         sums.launch(direct=1 if k < 0 else 0, z=nm - 1)
         while k >= 0 and len(output) < min(micro, nm - k + 1):

time: 506 us -> 510 us (level)
  starting transfers between devices: 81.6 us -> 90.7 us
    ppermute x15, starting transfers between devices: 19.6 us -> 28.1 us  [ring(): return lax.ppermute(value, 'mp', [(i, (i + step) % nm) for i in range(nm)])]
where the time goes in v8:
time: 510 us; the launch traced here: 501 us
  Pallas kernels  287 us (56%)
  starting transfers between devices  90.7 us (18%)
  waiting for transfers between devices  56.3 us (11%)
  other arithmetic  30.2 us (6%)
  local copies, waits for them, and re-layouts  21.2 us (4%)
  between operations  15.5 us (3%)
    pallas_call x4, Pallas kernels, attend_back(): pl.pallas_call(functools.partial(attend_back_kernel, parts), grid=(count,...  69.8 us
    pallas_call x4, Pallas kernels, attend(): pl.pallas_call(functools.partial(attend_kernel, parts), grid=(count, rows...  46.1 us
    ppermute x42, starting transfers between devices, swap(): return lax.ppermute(value, 'dp', [(i, i ^ bit) for i in range(nd)])  42 us
    ppermute x15, waiting for transfers between devices, ring(): return lax.ppermute(value, 'mp', [(i, (i + step) % nm) for i in range(nm)])  29.7 us
    ppermute x15, starting transfers between devices, ring(): return lax.ppermute(value, 'mp', [(i, (i + step) % nm) for i in range(nm)])  28.1 us
    pallas_call x2, Pallas kernels, wide_grad(): pl.pallas_call(wide_grad_kernel, grid_spec=pltpu.PrefetchScalarGridSpec(n...  26.5 us
    pallas_call x1, Pallas kernels, feed_back(): pl.pallas_call(functools.partial(feed_back_kernel, firsts, sizes), grid=(...  26 us
    ppermute x42, waiting for transfers between devices, swap(): return lax.ppermute(value, 'dp', [(i, i ^ bit) for i in range(nd)])  23.9 us
  transfers between devices with their start and end apart: 70, of which 16 were waited for; matrix products, arithmetic and copies ran while one was open for 7% of the time, Pallas kernels for 50%

profile of v8, /device:TPU:0, one launch (start us, length us, event | category | flops | bytes accessed | tf_op | source)
XLA Modules:
  0.0 500.9 jit_solution(17564421635497995395)
XLA Ops:
  8.2 4.1 collective-permute-start
  51.6 9.4 %collective-permute-start.13 = (bf16[4,1,2,128,256]{4,3,2,1,0:T(8,128)(2,1)S(1)}, bf16[4,1,2,128,256]{4,3,2,1,0:T(8,128)(2,1)S(1)}, u32[]{:S(2)}, u32[]{:S(2)}) collective-permute-start(bf16[4,1,2,128,256]{4,3,2,1,0:T(8,128)(2,1)S(1)} %pad_maximum_fusion.12.refs_0_.refs_4_.refs_9_), channel_id=1, source_target_pairs={{0,4},{4,0},{8,12},{12,8},{16,20},{20,16},{24,28},{28,24},{1,5},{5... | collective-permute-start | bytes 1572872 | tf_op jit(solution)/shard_map/ppermute | solution.py:49
  68.8 11.9 %collective-permute-done.11 = bf16[2,3,2,128,256]{4,3,2,1,0:T(8,128)(2,1)S(1)} collective-permute-done((bf16[2,3,2,128,256]{4,3,2,1,0:T(8,128)(2,1)S(1)}, bf16[2,3,2,128,256]{4,3,2,1,0:T(8,128)(2,1)S(1)}, u32[]{:S(2)}, u32[]{:S(2)}) %collective-permute-start.11) | collective-permute-done | bytes 786464 | tf_op jit(solution)/shard_map/ppermute | solution.py:49
  87.5 4.2 first_norm.1
  91.7 10.2 %collective-permute-done.17 = bf16[2,128,1024]{2,1,0:T(8,128)(2,1)S(1)} collective-permute-done((bf16[2,128,1024]{2,1,0:T(8,128)(2,1)S(1)}, bf16[2,128,1024]{2,1,0:T(8,128)(2,1)S(1)}, u32[]{:S(2)}, u32[]{:S(2)}) %collective-permute-start.17) | collective-permute-done | bytes 524320 | tf_op jit(solution)/shard_map/ppermute | solution.py:53
  106.1 6.9 %project.3.refs_0_.refs_2_ = bf16[2,768,1024]{2,1,0:T(8,128)(2,1)} custom-call(bf16[768,1024]{1,0:T(8,128)(2,1)} %get-tuple-element.346.in_ref.n_ref, bf16[4,1,2,128,256]{4,3,2,1,0:T(8,128)(2,1)} %copy-done.8, bf16[4,3,2,128,256]{4,3,2,1,0:T(8,128)(2,1)} %copy-done.5, bf16[4,1,2,128,256]{4,3,2,1,0:T(8,128)(2,1)} %copy-done.10, ...), custom_call_target="tpu_custom_call" | custom-call | flops 3221225472 | bytes 3145728 | tf_op jit(solution)/shard_map/project/pallas_call | solution.py:245
  113.0 6.3 %collective-permute-done.18 = bf16[2,128,1024]{2,1,0:T(8,128)(2,1)S(1)} collective-permute-done((bf16[2,128,1024]{2,1,0:T(8,128)(2,1)S(1)}, bf16[2,128,1024]{2,1,0:T(8,128)(2,1)S(1)}, u32[]{:S(2)}, u32[]{:S(2)}) %collective-permute-start.18) | collective-permute-done | bytes 524320 | tf_op jit(solution)/shard_map/ppermute | solution.py:53
  120.7 5.0 project.4.q_ref
  125.7 9.7 %collective-permute-done.21 = bf16[2,128,1024]{2,1,0:T(8,128)(2,1)S(1)} collective-permute-done((bf16[2,128,1024]{2,1,0:T(8,128)(2,1)S(1)}, bf16[2,128,1024]{2,1,0:T(8,128)(2,1)S(1)}, u32[]{:S(2)}, u32[]{:S(2)}) %collective-permute-start.21) | collective-permute-done | bytes 524320 | tf_op jit(solution)/shard_map/ppermute | solution.py:53
  139.0 11.5 %attend.5 = (bf16[768,256]{1,0:T(8,128)(2,1)}, f32[2,2,768]{2,1,0:T(2,128)}) custom-call(bf16[1,768,1024]{2,1,0:T(8,128)(2,1)} %project.4.q_ref, bf16[2,768,1024]{2,1,0:T(8,128)(2,1)} %project.3.refs_0_.refs_2_, bf16[2,768,1024]{2,1,0:T(8,128)(2,1)} %collective-permute-done.20.refs_1_.refs_3_, bf16[2,768,1024]{2,1,0:T(8,128)(2,1)} %project.3.refs_0_.refs_2_, ...), custom_call_target="tpu_custom_call" | custom-call | flops 4831838208 | bytes 3145728 | tf_op jit(solution)/shard_map/attend/pallas_call | solution.py:294
  150.5 11.5 %attend.4 = (bf16[768,256]{1,0:T(8,128)(2,1)}, f32[2,2,768]{2,1,0:T(2,128)}) custom-call(bf16[1,768,1024]{2,1,0:T(8,128)(2,1)} %project.4.q_ref, bf16[2,768,1024]{2,1,0:T(8,128)(2,1)} %project.3.refs_0_.refs_2_, bf16[2,768,1024]{2,1,0:T(8,128)(2,1)} %collective-permute-done.20.refs_1_.refs_3_, bf16[2,768,1024]{2,1,0:T(8,128)(2,1)} %project.3.refs_0_.refs_2_, ...), custom_call_target="tpu_custom_call" | custom-call | flops 4831838208 | bytes 3145728 | tf_op jit(solution)/shard_map/attend/pallas_call | solution.py:294
  167.3 11.5 %attend.7 = (bf16[768,256]{1,0:T(8,128)(2,1)}, f32[2,2,768]{2,1,0:T(2,128)}) custom-call(bf16[1,768,1024]{2,1,0:T(8,128)(2,1)} %project.4.q_ref, bf16[2,768,1024]{2,1,0:T(8,128)(2,1)} %project.3.refs_0_.refs_2_, bf16[2,768,1024]{2,1,0:T(8,128)(2,1)} %collective-permute-done.20.refs_1_.refs_3_, bf16[2,768,1024]{2,1,0:T(8,128)(2,1)} %project.3.refs_0_.refs_2_, ...), custom_call_target="tpu_custom_call" | custom-call | flops 4831838208 | bytes 3145728 | tf_op jit(solution)/shard_map/attend/pallas_call | solution.py:294
  178.8 11.5 %attend.6 = (bf16[768,256]{1,0:T(8,128)(2,1)}, f32[2,2,768]{2,1,0:T(2,128)}) custom-call(bf16[1,768,1024]{2,1,0:T(8,128)(2,1)} %project.4.q_ref, bf16[2,768,1024]{2,1,0:T(8,128)(2,1)} %project.3.refs_0_.refs_2_, bf16[2,768,1024]{2,1,0:T(8,128)(2,1)} %collective-permute-done.20.refs_1_.refs_3_, bf16[2,768,1024]{2,1,0:T(8,128)(2,1)} %project.3.refs_0_.refs_2_, ...), custom_call_target="tpu_custom_call" | custom-call | flops 4831838208 | bytes 3145728 | tf_op jit(solution)/shard_map/attend/pallas_call | solution.py:294
  192.0 7.1 %middle_norm.1 = (f32[768,1024]{1,0:T(8,128)}, bf16[768,1024]{1,0:T(8,128)(2,1)}) custom-call(bf16[768,1024]{1,0:T(8,128)(2,1)} %get-tuple-element.382.x_ref, bf16[768,256]{1,0:T(8,128)(2,1)} %get-tuple-element.383.refs_0_.refs_6_.mixed_ref, bf16[768,256]{1,0:T(8,128)(2,1)} %get-tuple-element.384.refs_1_.refs_6_.mixed_ref, ...), custom_call_target="tpu_custom_call" | custom-call | flops 1610612736 | bytes 11010048 | tf_op jit(solution)/shard_map/middle_norm/pallas_call | solution.py:409
  202.9 23.4 %feed.1 = (bf16[768,1024]{1,0:T(8,128)(2,1)}, bf16[4,768,1024]{2,1,0:T(8,128)(2,1)}, bf16[4,768,1024]{2,1,0:T(8,128)(2,1)}) custom-call(s32[8]{0:T(128)} %copy-done.45, bf16[8,2,2,128,1024]{4,3,2,1,0:T(8,128)(2,1)} %bitcast.207, bf16[4,2,128,1024]{3,2,1,0:T(8,128)(2,1)} %copy-done.12, bf16[4,2,128,1024]{3,2,1,0:T(8,128)(2,1)} %copy-done.49, ...), custom_call_target="tpu_custom_call" | custom-call | flops 12884901888 | bytes 16777216 | tf_op jit(solution)/shard_map/feed/pallas_call | solution.py:497
  226.3 13.2 %wide_grad.2 = bf16[8,4,128,1024]{3,2,1,0:T(8,128)(2,1)} custom-call(s32[9]{0:T(128)} %get-tuple-element.635.place_ref, bf16[768,1024]{1,0:T(8,128)(2,1)} %pad_maximum_fusion.4.a_ref.refs_5_, bf16[4,768,1024]{2,1,0:T(8,128)(2,1)} %get-tuple-element.398.b_ref), custom_call_target="tpu_custom_call" | custom-call | flops 6442450944 | bytes 16777216 | tf_op jit(solution)/shard_map/wide_grad/pallas_call | solution.py:597
  241.9 26.0 %feed_back.1 = (bf16[4,768,1024]{2,1,0:T(8,128)(2,1)}, bf16[768,1024]{1,0:T(8,128)(2,1)}, f32[2,1024]{1,0:T(2,128)}) custom-call(s32[8]{0:T(128)} %copy-done.45, bf16[8,2,2,128,1024]{4,3,2,1,0:T(8,128)(2,1)} %bitcast.208, bf16[4,2,128,1024]{3,2,1,0:T(8,128)(2,1)} %copy-done.12, bf16[4,2,128,1024]{3,2,1,0:T(8,128)(2,1)} %copy-done.49, ...), custom_call_target="tpu_custom_call" | custom-call | flops 12884901888 | bytes 16777216 | tf_op jit(solution)/shard_map/feed_back/pallas_call | solution.py:554
  267.9 13.3 %wide_grad.3 = bf16[8,4,128,1024]{3,2,1,0:T(8,128)(2,1)} custom-call(s32[9]{0:T(128)} %get-tuple-element.635.place_ref, bf16[768,1024]{1,0:T(8,128)(2,1)} %get-tuple-element.548.refs_5_.a_ref, bf16[4,768,1024]{2,1,0:T(8,128)(2,1)} %get-tuple-element.549.b_ref), custom_call_target="tpu_custom_call" | custom-call | flops 6442450944 | bytes 16777216 | tf_op jit(solution)/shard_map/wide_grad/pallas_call | solution.py:597
  286.3 5.0 project.5.refs_7_
  291.2 17.4 %attend_back.4 = (bf16[768,256]{1,0:T(8,128)(2,1)}, bf16[2,768,256]{2,1,0:T(8,128)(2,1)}, bf16[2,768,256]{2,1,0:T(8,128)(2,1)}) custom-call(bf16[1,768,1024]{2,1,0:T(8,128)(2,1)} %project.4.q_ref, bf16[2,768,1024]{2,1,0:T(8,128)(2,1)} %project.3.refs_0_.refs_2_, bf16[2,768,1024]{2,1,0:T(8,128)(2,1)} %collective-permute-done.20.refs_1_.refs_3_, ...), custom_call_target="tpu_custom_call" | custom-call | flops 12079595520 | bytes 6291456 | tf_op jit(solution)/shard_map/attend_back/pallas_call | solution.py:362
  308.7 17.6 %attend_back.5 = (bf16[768,256]{1,0:T(8,128)(2,1)}, bf16[2,768,256]{2,1,0:T(8,128)(2,1)}, bf16[2,768,256]{2,1,0:T(8,128)(2,1)}) custom-call(bf16[1,768,1024]{2,1,0:T(8,128)(2,1)} %project.4.q_ref, bf16[2,768,1024]{2,1,0:T(8,128)(2,1)} %project.3.refs_0_.refs_2_, bf16[2,768,1024]{2,1,0:T(8,128)(2,1)} %collective-permute-done.20.refs_1_.refs_3_, ...), custom_call_target="tpu_custom_call" | custom-call | flops 12079595520 | bytes 6291456 | tf_op jit(solution)/shard_map/attend_back/pallas_call | solution.py:362
  331.6 17.4 %attend_back.6 = (bf16[768,256]{1,0:T(8,128)(2,1)}, bf16[2,768,256]{2,1,0:T(8,128)(2,1)}, bf16[2,768,256]{2,1,0:T(8,128)(2,1)}) custom-call(bf16[1,768,1024]{2,1,0:T(8,128)(2,1)} %project.4.q_ref, bf16[2,768,1024]{2,1,0:T(8,128)(2,1)} %project.3.refs_0_.refs_2_, bf16[2,768,1024]{2,1,0:T(8,128)(2,1)} %collective-permute-done.20.refs_1_.refs_3_, ...), custom_call_target="tpu_custom_call" | custom-call | flops 12079595520 | bytes 6291456 | tf_op jit(solution)/shard_map/attend_back/pallas_call | solution.py:362
  349.0 6.0 %head_grad.4 = (bf16[2,768,256]{2,1,0:T(8,128)(2,1)}, bf16[4,4,128,256]{3,2,1,0:T(8,128)(2,1)}, bf16[4,4,128,256]{3,2,1,0:T(8,128)(2,1)}) custom-call(bf16[768,1024]{1,0:T(8,128)(2,1)} %get-tuple-element.346.in_ref.n_ref, bf16[768,1024]{1,0:T(8,128)(2,1)} %get-tuple-element.520.in_ref.g_ref.attn_ref, ...), custom_call_target="tpu_custom_call" | custom-call | flops 1610612736 | bytes 2097152 | tf_op jit(solution)/shard_map/head_grad/pallas_call | solution.py:635
  356.5 5.6 %head_grad.5 = (bf16[2,768,256]{2,1,0:T(8,128)(2,1)}, bf16[4,4,128,256]{3,2,1,0:T(8,128)(2,1)}, bf16[4,4,128,256]{3,2,1,0:T(8,128)(2,1)}) custom-call(bf16[768,1024]{1,0:T(8,128)(2,1)} %get-tuple-element.346.in_ref.n_ref, bf16[768,1024]{1,0:T(8,128)(2,1)} %get-tuple-element.520.in_ref.g_ref.attn_ref, ...), custom_call_target="tpu_custom_call" | custom-call | flops 1610612736 | bytes 2097152 | tf_op jit(solution)/shard_map/head_grad/pallas_call | solution.py:635
  362.1 17.4 %attend_back.7 = (bf16[768,256]{1,0:T(8,128)(2,1)}, bf16[2,768,256]{2,1,0:T(8,128)(2,1)}, bf16[2,768,256]{2,1,0:T(8,128)(2,1)}) custom-call(bf16[1,768,1024]{2,1,0:T(8,128)(2,1)} %project.4.q_ref, bf16[2,768,1024]{2,1,0:T(8,128)(2,1)} %project.3.refs_0_.refs_2_, bf16[2,768,1024]{2,1,0:T(8,128)(2,1)} %collective-permute-done.20.refs_1_.refs_3_, ...), custom_call_target="tpu_custom_call" | custom-call | flops 12079595520 | bytes 6291456 | tf_op jit(solution)/shard_map/attend_back/pallas_call | solution.py:362
  386.6 5.6 %head_grad.6 = (bf16[2,768,256]{2,1,0:T(8,128)(2,1)}, bf16[4,4,128,256]{3,2,1,0:T(8,128)(2,1)}, bf16[4,4,128,256]{3,2,1,0:T(8,128)(2,1)}) custom-call(bf16[768,1024]{1,0:T(8,128)(2,1)} %get-tuple-element.346.in_ref.n_ref, bf16[768,1024]{1,0:T(8,128)(2,1)} %get-tuple-element.520.in_ref.g_ref.attn_ref, ...), custom_call_target="tpu_custom_call" | custom-call | flops 1610612736 | bytes 2097152 | tf_op jit(solution)/shard_map/head_grad/pallas_call | solution.py:635
  392.7 5.2 %collective-permute-done.42 = bf16[1,4,128,256]{3,2,1,0:T(8,128)(2,1)S(1)} collective-permute-done((bf16[1,4,128,256]{3,2,1,0:T(8,128)(2,1)}, bf16[1,4,128,256]{3,2,1,0:T(8,128)(2,1)S(1)}, u32[]{:S(2)}, u32[]{:S(2)}) %collective-permute-start.42) | collective-permute-done | bytes 262176 | tf_op jit(solution)/shard_map/ppermute | solution.py:49
  409.7 5.6 %head_grad.7 = (bf16[2,768,256]{2,1,0:T(8,128)(2,1)}, bf16[4,4,128,256]{3,2,1,0:T(8,128)(2,1)}, bf16[4,4,128,256]{3,2,1,0:T(8,128)(2,1)}) custom-call(bf16[768,1024]{1,0:T(8,128)(2,1)} %get-tuple-element.346.in_ref.n_ref, bf16[768,1024]{1,0:T(8,128)(2,1)} %get-tuple-element.520.in_ref.g_ref.attn_ref, ...), custom_call_target="tpu_custom_call" | custom-call | flops 1610612736 | bytes 2097152 | tf_op jit(solution)/shard_map/head_grad/pallas_call | solution.py:635
  415.3 8.4 %first_back.2 = (bf16[384,1024]{1,0:T(8,128)(2,1)}, f32[2,1024]{1,0:T(2,128)}) custom-call(bf16[768,1024]{1,0:T(8,128)(2,1)} %get-tuple-element.382.x_ref, bf16[768,1024]{1,0:T(8,128)(2,1)} %get-tuple-element.520.in_ref.g_ref.attn_ref, f32[1,1024]{1,0:T(1,128)} %get-tuple-element.619.refs_2_.gain_ref, bf16[768,256]{1,0:T(8,128)(2,1)} %get-tuple-element.492.refs_0_.dq_ref, ...), custom_call_target="tpu_custom_call" | custom-call | flops 2415919104 | bytes 4718592 | tf_op jit(solution)/shard_map/first_back/pallas_call | solution.py:674
  435.8 8.3 %first_back.3 = (bf16[384,1024]{1,0:T(8,128)(2,1)}, f32[2,1024]{1,0:T(2,128)}) custom-call(bf16[768,1024]{1,0:T(8,128)(2,1)} %get-tuple-element.382.x_ref, bf16[768,1024]{1,0:T(8,128)(2,1)} %get-tuple-element.520.in_ref.g_ref.attn_ref, f32[1,1024]{1,0:T(1,128)} %get-tuple-element.619.refs_2_.gain_ref, bf16[768,256]{1,0:T(8,128)(2,1)} %get-tuple-element.492.refs_0_.dq_ref, ...), custom_call_target="tpu_custom_call" | custom-call | flops 2415919104 | bytes 4718592 | tf_op jit(solution)/shard_map/first_back/pallas_call | solution.py:674
  447.0 6.7 %collective-permute-start.59 = (bf16[384,1024]{1,0:T(8,128)(2,1)}, bf16[384,1024]{1,0:T(8,128)(2,1)S(1)}, u32[]{:S(2)}, u32[]{:S(2)}) collective-permute-start(bf16[384,1024]{1,0:T(8,128)(2,1)} %get-tuple-element.534), channel_id=1, source_target_pairs={{2,0},{0,1},{6,2},{4,3},{3,4},{1,5},{7,6},{5,7},{10,8},{8,9},{14,1... | collective-permute-start | bytes 2359304 | tf_op jit(solution)/shard_map/ppermute | solution.py:1117
  478.5 7.6 %collective-permute-start.64 = (f32[4,1024]{1,0:T(4,128)S(1)}, f32[4,1024]{1,0:T(4,128)S(1)}, u32[]{:S(2)}, u32[]{:S(2)}) collective-permute-start(f32[4,1024]{1,0:T(4,128)S(1)} %add.256), channel_id=1, source_target_pairs={{0,2},{1,3},{2,0},{3,1},{4,6},{5,7},{6,4},{7,5},{8,10},{9,11},{10,... | collective-permute-start | bytes 49160 | tf_op jit(solution)/shard_map/ppermute | solution.py:53
  (336 shorter events, 154.8 us)
Async XLA Ops:
  7.2 195.7 %all-gather.3.cloned.1.call-start = ((), (), s32[]{:S(2)}) async-start(), calls=%async_computation.6 | async-start | bytes 9437184 | tf_op jit(solution)/shard_map/all_gather | solution.py:953
  8.2 23.5 %collective-permute-start = (bf16[4,128,256]{2,1,0:T(8,128)(2,1)S(1)}, bf16[4,128,256]{2,1,0:T(8,128)(2,1)S(1)}, u32[]{:S(2)}, u32[]{:S(2)}) collective-permute-start(bf16[4,128,256]{2,1,0:T(8,128)(2,1)S(1)} %pad_maximum_fusion.17), channel_id=1, source_target_pairs={{0,2},{1,3},{2,0},{3,1},{4,6},{5,7},{6,4},{7,5},{8,10},{9,11},{10,... | collective-permute-start | bytes 786440 | tf_op jit(solution)/shard_map/ppermute | solution.py:53
  12.3 19.4 %collective-permute-start.1 = (bf16[4,128,256]{2,1,0:T(8,128)(2,1)S(1)}, bf16[4,128,256]{2,1,0:T(8,128)(2,1)S(1)}, u32[]{:S(2)}, u32[]{:S(2)}) collective-permute-start(bf16[4,128,256]{2,1,0:T(8,128)(2,1)S(1)} %pad_maximum_fusion.17), channel_id=1, source_target_pairs={{0,1},{1,2},{2,3},{3,0},{4,5},{5,6},{6,7},{7,4},{8,9},{9,10},{10,1... | collective-permute-start | bytes 786440 | tf_op jit(solution)/shard_map/ppermute | solution.py:53
  13.9 17.8 %collective-permute-start.2 = (bf16[4,128,256]{2,1,0:T(8,128)(2,1)S(1)}, bf16[4,128,256]{2,1,0:T(8,128)(2,1)S(1)}, u32[]{:S(2)}, u32[]{:S(2)}) collective-permute-start(bf16[4,128,256]{2,1,0:T(8,128)(2,1)S(1)} %pad_maximum_fusion.17), channel_id=1, source_target_pairs={{0,3},{1,0},{2,1},{3,2},{4,7},{5,4},{6,5},{7,6},{8,11},{9,8},{10,9... | collective-permute-start | bytes 786440 | tf_op jit(solution)/shard_map/ppermute | solution.py:53
  61.1 19.5 %collective-permute-start.11 = (bf16[2,3,2,128,256]{4,3,2,1,0:T(8,128)(2,1)S(1)}, bf16[2,3,2,128,256]{4,3,2,1,0:T(8,128)(2,1)S(1)}, u32[]{:S(2)}, u32[]{:S(2)}) collective-permute-start(bf16[2,3,2,128,256]{4,3,2,1,0:T(8,128)(2,1)S(1)} %pad_maximum_fusion.9), channel_id=1, source_target_pairs={{0,16},{4,20},{8,24},{12,28},{16,0},{20,4},{24,8},{28,12},{1,17},{... | collective-permute-start | bytes 2359304 | tf_op jit(solution)/shard_map/ppermute | solution.py:49
  61.8 19.4 %collective-permute-start.10 = (bf16[2,3,2,128,256]{4,3,2,1,0:T(8,128)(2,1)S(1)}, bf16[2,3,2,128,256]{4,3,2,1,0:T(8,128)(2,1)S(1)}, u32[]{:S(2)}, u32[]{:S(2)}) collective-permute-start(bf16[2,3,2,128,256]{4,3,2,1,0:T(8,128)(2,1)S(1)} %pad_maximum_fusion.8), channel_id=1, source_target_pairs={{0,8},{4,12},{8,0},{12,4},{16,24},{20,28},{24,16},{28,20},{1,9},{5... | collective-permute-start | bytes 2359304 | tf_op jit(solution)/shard_map/ppermute | solution.py:49
  63.3 20.4 %collective-permute-start.14 = (bf16[384,1024]{1,0:T(8,128)(2,1)S(1)}, bf16[384,1024]{1,0:T(8,128)(2,1)S(1)}, u32[]{:S(2)}, u32[]{:S(2)}) collective-permute-start(bf16[384,1024]{1,0:T(8,128)(2,1)S(1)} %copy-done.21), channel_id=1, source_target_pairs={{0,2},{1,0},{2,6},{3,4},{4,3},{5,1},{6,7},{7,5},{8,10},{9,8},{10,1... | collective-permute-start | bytes 2359304 | tf_op jit(solution)/shard_map/ppermute | solution.py:883
  104.2 222.6 %reduce-scatter.4.cloned.1.call-start = ((), (), s32[]{:S(2)}) async-start(), calls=%async_computation.3 | async-start | bytes 9437184 | tf_op jit(solution)/shard_map/reduce_scatter | solution.py:1033
  135.6 26.5 %collective-permute-start.23 = (bf16[1,2,128,1024]{3,2,1,0:T(8,128)(2,1)S(1)}, bf16[1,2,128,1024]{3,2,1,0:T(8,128)(2,1)S(1)}, u32[]{:S(2)}, u32[]{:S(2)}) collective-permute-start(bf16[1,2,128,1024]{3,2,1,0:T(8,128)(2,1)S(1)} %get-tuple-element.592), channel_id=1, source_target_pairs={{0,16},{4,20},{8,24},{12,28},{16,0},{20,4},{24,8},{28,12},{1,17},{... | collective-permute-start | bytes 1572872 | tf_op jit(solution)/shard_map/ppermute | solution.py:49
  137.2 25.6 %collective-permute-start.22 = (bf16[1,2,128,1024]{3,2,1,0:T(8,128)(2,1)S(1)}, bf16[1,2,128,1024]{3,2,1,0:T(8,128)(2,1)S(1)}, u32[]{:S(2)}, u32[]{:S(2)}) collective-permute-start(bf16[1,2,128,1024]{3,2,1,0:T(8,128)(2,1)S(1)} %get-tuple-element.594), channel_id=1, source_target_pairs={{0,8},{4,12},{8,0},{12,4},{16,24},{20,28},{24,16},{28,20},{1,9},{5... | collective-permute-start | bytes 1572872 | tf_op jit(solution)/shard_map/ppermute | solution.py:49
  137.8 25.0 %collective-permute-start.24 = (bf16[384,1024]{1,0:T(8,128)(2,1)S(1)}, bf16[384,1024]{1,0:T(8,128)(2,1)S(1)}, u32[]{:S(2)}, u32[]{:S(2)}) collective-permute-start(bf16[384,1024]{1,0:T(8,128)(2,1)S(1)} %copy-done.20), channel_id=1, source_target_pairs={{0,0},{1,2},{2,4},{3,6},{4,1},{5,3},{6,5},{7,7},{8,8},{9,10},{10,1... | collective-permute-start | bytes 2359304 | tf_op jit(solution)/shard_map/ppermute | solution.py:883
  162.9 27.5 %collective-permute-start.26 = (bf16[2,2,128,1024]{3,2,1,0:T(8,128)(2,1)S(1)}, bf16[2,2,128,1024]{3,2,1,0:T(8,128)(2,1)S(1)}, u32[]{:S(2)}, u32[]{:S(2)}) collective-permute-start(bf16[2,2,128,1024]{3,2,1,0:T(8,128)(2,1)S(1)} %pad_maximum_fusion.6), channel_id=1, source_target_pairs={{0,16},{4,20},{8,24},{12,28},{16,0},{20,4},{24,8},{28,12},{1,17},{... | collective-permute-start | bytes 3145736 | tf_op jit(solution)/shard_map/ppermute | solution.py:49
  163.6 26.8 %collective-permute-start.25 = (bf16[2,2,128,1024]{3,2,1,0:T(8,128)(2,1)S(1)}, bf16[2,2,128,1024]{3,2,1,0:T(8,128)(2,1)S(1)}, u32[]{:S(2)}, u32[]{:S(2)}) collective-permute-start(bf16[2,2,128,1024]{3,2,1,0:T(8,128)(2,1)S(1)} %pad_maximum_fusion.5), channel_id=1, source_target_pairs={{0,8},{4,12},{8,0},{12,4},{16,24},{20,28},{24,16},{28,20},{1,9},{5... | collective-permute-start | bytes 3145736 | tf_op jit(solution)/shard_map/ppermute | solution.py:49
  164.4 25.9 %collective-permute-start.27 = (bf16[384,1024]{1,0:T(8,128)(2,1)S(1)}, bf16[384,1024]{1,0:T(8,128)(2,1)}, u32[]{:S(2)}, u32[]{:S(2)}) collective-permute-start(bf16[384,1024]{1,0:T(8,128)(2,1)S(1)} %copy-done.19), channel_id=1, source_target_pairs={{0,2},{1,0},{2,6},{3,4},{4,3},{5,1},{6,7},{7,5},{8,10},{9,8},{10,1... | collective-permute-start | bytes 2359304 | tf_op jit(solution)/shard_map/ppermute | solution.py:883
  239.5 159.5 %reduce-scatter.6.cloned.1.call-start = ((), (), s32[]{:S(2)}) async-start(), calls=%async_computation.4 | async-start | bytes 9437184 | tf_op jit(solution)/shard_map/reduce_scatter | solution.py:1040
  241.0 27.0 %collective-permute-start.33 = (bf16[384,1024]{1,0:T(8,128)(2,1)S(1)}, bf16[384,1024]{1,0:T(8,128)(2,1)S(1)}, u32[]{:S(2)}, u32[]{:S(2)}) collective-permute-start(bf16[384,1024]{1,0:T(8,128)(2,1)S(1)} %slice.172), channel_id=1, source_target_pairs={{0,0},{2,1},{4,2},{6,3},{1,4},{3,5},{5,6},{7,7},{8,8},{10,9},{12,1... | collective-permute-start | bytes 2359304 | tf_op jit(solution)/shard_map/ppermute | solution.py:889
  281.2 187.3 %reduce-scatter.8.cloned.1.call-start = ((), (), s32[]{:S(2)}) async-start(), calls=%async_computation.5 | async-start | bytes 1310720 | tf_op jit(solution)/shard_map/reduce_scatter | solution.py:1041
  283.2 25.5 %collective-permute-start.34 = (bf16[384,1024]{1,0:T(8,128)(2,1)S(1)}, bf16[384,1024]{1,0:T(8,128)(2,1)S(1)}, u32[]{:S(2)}, u32[]{:S(2)}) collective-permute-start(bf16[384,1024]{1,0:T(8,128)(2,1)S(1)} %slice_bitcast_fusion), channel_id=1, source_target_pairs={{2,0},{0,1},{6,2},{4,3},{3,4},{1,5},{7,6},{5,7},{10,8},{8,9},{14,1... | collective-permute-start | bytes 2359304 | tf_op jit(solution)/shard_map/ppermute | solution.py:889
  326.4 28.6 %collective-permute-start.36 = (bf16[2,768,256]{2,1,0:T(8,128)(2,1)}, bf16[2,768,256]{2,1,0:T(8,128)(2,1)S(1)}, u32[]{:S(2)}, u32[]{:S(2)}) collective-permute-start(bf16[2,768,256]{2,1,0:T(8,128)(2,1)} %get-tuple-element.436), channel_id=1, source_target_pairs={{0,4},{4,0},{8,12},{12,8},{16,20},{20,16},{24,28},{28,24},{1,5},{5... | collective-permute-start | bytes 2359304 | tf_op jit(solution)/shard_map/ppermute | solution.py:49
  328.1 27.0 %collective-permute-start.30 = (bf16[128,1024]{1,0:T(8,128)(2,1)S(1)}, bf16[128,1024]{1,0:T(8,128)(2,1)S(1)}, u32[]{:S(2)}, u32[]{:S(2)}) collective-permute-start(bf16[128,1024]{1,0:T(8,128)(2,1)S(1)} %get-tuple-element.585), channel_id=1, source_target_pairs={{0,3},{1,0},{2,1},{3,2},{4,7},{5,4},{6,5},{7,6},{8,11},{9,8},{10,9... | collective-permute-start | bytes 786440 | tf_op jit(solution)/shard_map/ppermute | solution.py:53
  330.6 24.5 %collective-permute-start.31 = (bf16[128,1024]{1,0:T(8,128)(2,1)S(1)}, bf16[128,1024]{1,0:T(8,128)(2,1)S(1)}, u32[]{:S(2)}, u32[]{:S(2)}) collective-permute-start(bf16[128,1024]{1,0:T(8,128)(2,1)S(1)} %get-tuple-element.584), channel_id=1, source_target_pairs={{0,1},{1,2},{2,3},{3,0},{4,5},{5,6},{6,7},{7,4},{8,9},{9,10},{10,1... | collective-permute-start | bytes 786440 | tf_op jit(solution)/shard_map/ppermute | solution.py:53
  331.0 24.1 %collective-permute-start.32 = (bf16[128,1024]{1,0:T(8,128)(2,1)S(1)}, bf16[128,1024]{1,0:T(8,128)(2,1)S(1)}, u32[]{:S(2)}, u32[]{:S(2)}) collective-permute-start(bf16[128,1024]{1,0:T(8,128)(2,1)S(1)} %get-tuple-element.583), channel_id=1, source_target_pairs={{0,2},{1,3},{2,0},{3,1},{4,6},{5,7},{6,4},{7,5},{8,10},{9,11},{10,... | collective-permute-start | bytes 786440 | tf_op jit(solution)/shard_map/ppermute | solution.py:53
  356.0 23.6 %collective-permute-start.37 = (bf16[1,4,4,128,256]{4,3,2,1,0:T(8,128)(2,1)}, bf16[1,4,4,128,256]{4,3,2,1,0:T(8,128)(2,1)S(1)}, u32[]{:S(2)}, u32[]{:S(2)}) collective-permute-start(bf16[1,4,4,128,256]{4,3,2,1,0:T(8,128)(2,1)} %bitcast.212), channel_id=1, source_target_pairs={{0,4},{4,0},{8,12},{12,8},{16,20},{20,16},{24,28},{28,24},{1,5},{5... | collective-permute-start | bytes 3145736 | tf_op jit(solution)/shard_map/ppermute | solution.py:49
  356.0 23.5 %collective-permute-start.38 = (bf16[2,768,256]{2,1,0:T(8,128)(2,1)S(1)}, bf16[2,768,256]{2,1,0:T(8,128)(2,1)S(1)}, u32[]{:S(2)}, u32[]{:S(2)}) collective-permute-start(bf16[2,768,256]{2,1,0:T(8,128)(2,1)S(1)} %copy-done.55), channel_id=1, source_target_pairs={{0,4},{4,0},{8,12},{12,8},{16,20},{20,16},{24,28},{28,24},{1,5},{5... | collective-permute-start | bytes 2359304 | tf_op jit(solution)/shard_map/ppermute | solution.py:49
  379.5 18.4 %collective-permute-start.39 = (bf16[1,4,4,128,256]{4,3,2,1,0:T(8,128)(2,1)S(1)}, bf16[1,4,4,128,256]{4,3,2,1,0:T(8,128)(2,1)S(1)}, u32[]{:S(2)}, u32[]{:S(2)}) collective-permute-start(bf16[1,4,4,128,256]{4,3,2,1,0:T(8,128)(2,1)S(1)} %bitcast.211), channel_id=1, source_target_pairs={{0,4},{4,0},{8,12},{12,8},{16,20},{20,16},{24,28},{28,24},{1,5},{5... | collective-permute-start | bytes 3145736 | tf_op jit(solution)/shard_map/ppermute | solution.py:49
  379.6 18.3 %collective-permute-start.43 = (bf16[2,768,256]{2,1,0:T(8,128)(2,1)}, bf16[2,768,256]{2,1,0:T(8,128)(2,1)S(1)}, u32[]{:S(2)}, u32[]{:S(2)}) collective-permute-start(bf16[2,768,256]{2,1,0:T(8,128)(2,1)} %get-tuple-element.476), channel_id=1, source_target_pairs={{0,4},{4,0},{8,12},{12,8},{16,20},{20,16},{24,28},{28,24},{1,5},{5... | collective-permute-start | bytes 2359304 | tf_op jit(solution)/shard_map/ppermute | solution.py:49
  399.0 24.8 %collective-permute-start.44 = (bf16[1,4,4,128,256]{4,3,2,1,0:T(8,128)(2,1)}, bf16[1,4,4,128,256]{4,3,2,1,0:T(8,128)(2,1)S(1)}, u32[]{:S(2)}, u32[]{:S(2)}) collective-permute-start(bf16[1,4,4,128,256]{4,3,2,1,0:T(8,128)(2,1)} %bitcast.210), channel_id=1, source_target_pairs={{0,4},{4,0},{8,12},{12,8},{16,20},{20,16},{24,28},{28,24},{1,5},{5... | collective-permute-start | bytes 3145736 | tf_op jit(solution)/shard_map/ppermute | solution.py:49
  400.3 23.4 %collective-permute-start.48 = (bf16[4,128,256]{2,1,0:T(8,128)(2,1)S(1)}, bf16[4,128,256]{2,1,0:T(8,128)(2,1)S(1)}, u32[]{:S(2)}, u32[]{:S(2)}) collective-permute-start(bf16[4,128,256]{2,1,0:T(8,128)(2,1)S(1)} %fusion.8), channel_id=1, source_target_pairs={{0,3},{1,0},{2,1},{3,2},{4,7},{5,4},{6,5},{7,6},{8,11},{9,8},{10,9... | collective-permute-start | bytes 786440 | tf_op jit(solution)/shard_map/ppermute | solution.py:53
  423.8 20.6 %collective-permute-start.49 = (bf16[1,4,4,128,256]{4,3,2,1,0:T(8,128)(2,1)S(1)}, bf16[1,4,4,128,256]{4,3,2,1,0:T(8,128)(2,1)S(1)}, u32[]{:S(2)}, u32[]{:S(2)}) collective-permute-start(bf16[1,4,4,128,256]{4,3,2,1,0:T(8,128)(2,1)S(1)} %bitcast.209), channel_id=1, source_target_pairs={{0,4},{4,0},{8,12},{12,8},{16,20},{20,16},{24,28},{28,24},{1,5},{5... | collective-permute-start | bytes 3145736 | tf_op jit(solution)/shard_map/ppermute | solution.py:49
  426.3 18.1 %collective-permute-start.54 = (bf16[384,1024]{1,0:T(8,128)(2,1)S(1)}, bf16[384,1024]{1,0:T(8,128)(2,1)S(1)}, u32[]{:S(2)}, u32[]{:S(2)}) collective-permute-start(bf16[384,1024]{1,0:T(8,128)(2,1)S(1)} %copy-done.52), channel_id=1, source_target_pairs={{0,0},{2,1},{4,2},{6,3},{1,4},{3,5},{5,6},{7,7},{8,8},{10,9},{12,1... | collective-permute-start | bytes 2359304 | tf_op jit(solution)/shard_map/ppermute | solution.py:1117
  447.0 27.7 %collective-permute-start.59 = (bf16[384,1024]{1,0:T(8,128)(2,1)}, bf16[384,1024]{1,0:T(8,128)(2,1)S(1)}, u32[]{:S(2)}, u32[]{:S(2)}) collective-permute-start(bf16[384,1024]{1,0:T(8,128)(2,1)} %get-tuple-element.534), channel_id=1, source_target_pairs={{2,0},{0,1},{6,2},{4,3},{3,4},{1,5},{7,6},{5,7},{10,8},{8,9},{14,1... | collective-permute-start | bytes 2359304 | tf_op jit(solution)/shard_map/ppermute | solution.py:1117
  474.8 18.2 %collective-permute-start.63 = (f32[4,1024]{1,0:T(4,128)S(1)}, f32[4,1024]{1,0:T(4,128)S(1)}, u32[]{:S(2)}, u32[]{:S(2)}) collective-permute-start(f32[4,1024]{1,0:T(4,128)S(1)} %add.256), channel_id=1, source_target_pairs={{0,1},{1,2},{2,3},{3,0},{4,5},{5,6},{6,7},{7,4},{8,9},{9,10},{10,1... | collective-permute-start | bytes 49160 | tf_op jit(solution)/shard_map/ppermute | solution.py:53
  (96 other events, 914.6 us)
Sparse Core Ops, SparseCore 0:
  104.3 62.8 all-gather.2
  239.6 68.5 reduce-scatter.3
  312.1 72.1 reduce-scatter.5
  399.1 29.7 reduce-scatter.7
